TPU v7x, 32 devices: a whole 2x2x4 slice. The times are simulated.
32 devices in a mesh: sec: 2 (over y), rad: 4 (over z), ax: 4 (over x, core).
Axes of the slice: x: 2, y: 2, z: 4, core: 2. Of those that a mesh axis runs over, the one named last changes fastest.
Arguments:
- state: float32 [5, 8, 1024, 2048], P(None, 'ax', 'rad', 'sec'), may hold values from -1.6 to 4, as said below
- coarsen: int32 [16], replicated, may hold values from 1 to 16, as said below
Outputs:
- tendency: float32 [5, 8, 1024, 2048], P(None, 'ax', 'rad', 'sec')
Inputs may be any that keep to these rules, and one draw needn't show every extreme that they name: `coarsen`: each entry is a power of two; cycle 0 takes 16 and cycle 16 - 1 takes 1. state[0] (density) lies in 0.6 to 1.4, the momenta in -1.6 to 1.6, state[4] (energy) in 2.5 to 4.0.
All inputs are finite; a program needn't handle non-finite values.
Results may differ from a plain program's by a relative error of at most 0.0003.
Values sent between devices are 32-bit elements; how exact they have to be, the bound alone decides.
No kernel may reach another device: no remote copies, remote signals or barrier semaphores. Data moves between devices by JAX's collectives and lax.ppermute only.
A program may use at most 256 MiB of HBM per device.

v0:
```python
import math

import jax
import jax.numpy as jnp
from jax import lax
from jax.sharding import PartitionSpec as P

R_NEAR = 16


GAMMA = 1.4
KAPPA = 1.44


def padded_2(value, sides, width):
    for axis, dim in sides:
        size, length = (lax.axis_size(axis), value.shape[dim])
        up = [(i, (i + 1) % size) for i in range(size)]
        down = [(j, i) for i, j in up]
        last = lax.slice_in_dim(value, length - width, length, axis=dim)
        first = lax.slice_in_dim(value, 0, width, axis=dim)
        before = lax.ppermute(last, axis, up)
        after = lax.ppermute(first, axis, down)
        value = jnp.concatenate([before, value, after], axis=dim)
    return value


def spread(value, axis, root):
    mine = lax.axis_index(axis) == root
    return lax.psum(jnp.where(mine, value, jnp.zeros_like(value)), axis)


def body(state, coarsen):
    fields, planes, cycles_dev, cells_dev = state.shape
    sec_count = lax.axis_size("sec")
    rad_count = lax.axis_size("rad")
    ax_count = lax.axis_size("ax")
    sec_index = lax.axis_index("sec")
    rad_index = lax.axis_index("rad")
    ax_index = lax.axis_index("ax")
    total_cells = cells_dev * sec_count
    dtheta = 2.0 * math.pi / total_cells
    padded = padded_2(state, (("sec", 3), ("rad", 2), ("ax", 1)), 1)
    plane_pos = ax_index * planes + jnp.arange(-1, planes + 1, dtype=jnp.int32)
    cycle_pos = rad_index * cycles_dev + jnp.arange(-1, cycles_dev + 1, dtype=jnp.int32)
    inside_ax = ((plane_pos >= 0) & (plane_pos < planes * ax_count)).astype(jnp.float32)
    inside_rad = ((cycle_pos >= 0) & (cycle_pos < cycles_dev * rad_count)).astype(jnp.float32)
    ghost_plane = jnp.arange(planes + 2) % (planes + 1) == 0
    ghost_cycle = jnp.arange(cycles_dev + 2) % (cycles_dev + 1) == 0
    ghost_cell = jnp.arange(cells_dev + 2) % (cells_dev + 1) == 0
    ghosts = (
        ghost_plane.astype(jnp.int32)[:, None, None]
        + ghost_cycle.astype(jnp.int32)[None, :, None]
        + ghost_cell.astype(jnp.int32)[None, None, :]
    )
    corner = ghosts >= 2
    density = jnp.where(corner, 1.0, padded[0])
    mom_ax = padded[1]
    mom_rad = padded[2]
    mom_az = padded[3]
    energy = padded[4]
    vel_ax = mom_ax / density
    vel_rad = mom_rad / density
    vel_az = mom_az / density
    pressure = (GAMMA - 1.0) * (
        energy - 0.5 * (mom_ax * vel_ax + mom_rad * vel_rad + mom_az * vel_az)
    )
    radius_pad = cycle_pos.astype(jnp.float32) + 0.5
    flux_ax = jnp.stack(
        [
            mom_ax,
            mom_ax * vel_ax + pressure,
            mom_rad * vel_ax,
            mom_az * vel_ax,
            (energy + pressure) * vel_ax,
        ]
    )
    flux_ax = flux_ax * inside_ax[None, :, None, None]
    flux_rad = jnp.stack(
        [
            mom_rad,
            mom_ax * vel_rad,
            mom_rad * vel_rad + pressure,
            mom_az * vel_rad,
            (energy + pressure) * vel_rad,
        ]
    )
    flux_rad = flux_rad * (radius_pad * inside_rad)[None, None, :, None]
    flux_az = jnp.stack(
        [
            mom_az,
            mom_ax * vel_az,
            mom_rad * vel_az,
            mom_az * vel_az + pressure,
            (energy + pressure) * vel_az,
        ]
    )
    radius = radius_pad[1:-1][:, None]
    tendency = -(flux_ax[:, 2:, 1:-1, 1:-1] - flux_ax[:, :-2, 1:-1, 1:-1]) * 0.5
    tendency = (
        tendency - (flux_rad[:, 1:-1, 2:, 1:-1] - flux_rad[:, 1:-1, :-2, 1:-1]) * 0.5 / radius
    )
    tendency = tendency - (flux_az[:, 1:-1, 1:-1, 2:] - flux_az[:, 1:-1, 1:-1, :-2]) * 0.5 / (
        radius * dtheta
    )
    inner_press = pressure[1:-1, 1:-1, 1:-1]
    inner_mom_az = mom_az[1:-1, 1:-1, 1:-1]
    inner_mom_rad = mom_rad[1:-1, 1:-1, 1:-1]
    inner_vel_az = vel_az[1:-1, 1:-1, 1:-1]
    zero_part = jnp.zeros_like(inner_press)
    source = jnp.stack(
        [
            zero_part,
            zero_part,
            (inner_press + inner_mom_az * inner_vel_az) / radius,
            -(inner_mom_rad * inner_vel_az) / radius,
            zero_part,
        ]
    )
    tendency = tendency + source
    own_pos = sec_index * cells_dev + jnp.arange(cells_dev, dtype=jnp.int32)

    def kernel(cycle_factor, cycle_blocks, log_ratio, scale_const, columns):
        rows_coarse = own_pos // cycle_factor
        columns_coarse = columns // cycle_factor
        distance = ((rows_coarse[:, None] - columns_coarse[None, :]) % cycle_blocks).astype(
            jnp.float32
        )
        blocks_f = cycle_blocks.astype(jnp.float32)
        return (jnp.exp(distance * log_ratio) + jnp.exp((blocks_f - distance) * log_ratio)) / (
            scale_const * cycle_factor.astype(jnp.float32)
        )

    near_axis = tendency[:, :, :R_NEAR, :]
    cycle_lines = jnp.transpose(near_axis, (2, 0, 1, 3)).reshape(R_NEAR, fields * planes, cells_dev)
    shared = spread(cycle_lines, "rad", 0)
    per_device = R_NEAR // rad_count
    my_cycles = lax.dynamic_slice_in_dim(shared, rad_index * per_device, per_device, 0)
    selector = (rad_index * per_device + jnp.arange(per_device, dtype=jnp.int32))[
        :, None
    ] == jnp.arange(coarsen.shape[0], dtype=jnp.int32)[None, :]
    factor = jnp.sum(jnp.where(selector, coarsen[None, :], 0), axis=1)
    blocks = total_cells // factor
    factor_f = factor.astype(jnp.float32)
    stiffness = KAPPA / (factor_f * dtheta) ** 2
    inverse_half = 0.5 / stiffness
    one_minus = jnp.sqrt(inverse_half * (2.0 + inverse_half)) - inverse_half
    log_ratio = jnp.log1p(-one_minus)
    scale_const = (
        stiffness
        * one_minus
        * (2.0 - one_minus)
        / (1.0 - one_minus)
        * -jnp.expm1(blocks.astype(jnp.float32) * log_ratio)
    )
    portion = lax.all_gather(my_cycles, "sec", axis=2, tiled=True)
    columns = jnp.arange(portion.shape[2], dtype=jnp.int32)

    def per_cycle(cycle_item):
        lines_one, cycle_factor, cycle_blocks, cycle_log, cycle_scale = cycle_item
        table = kernel(cycle_factor, cycle_blocks, cycle_log, cycle_scale, columns)
        return jnp.einsum("lq,pq->lp", lines_one, table, precision=lax.Precision.HIGHEST)

    smoothed = lax.map(per_cycle, (portion, factor, blocks, log_ratio, scale_const))
    result = lax.all_gather(smoothed, "rad", axis=0, tiled=True)
    restored = jnp.transpose(result.reshape(R_NEAR, fields, planes, cells_dev), (1, 2, 0, 3))
    near_new = jnp.where(rad_index == 0, restored, near_axis)
    return jnp.concatenate([near_new, tendency[:, :, R_NEAR:, :]], axis=2)


def solution(mesh):
    return jax.shard_map(
        body,
        mesh=mesh,
        in_specs=(P(None, "ax", "rad", "sec"), P()),
        out_specs=P(None, "ax", "rad", "sec"),
        check_vma=False,
    )
```

profile of v0, /device:TPU:1, one launch (start us, length us, event | category | flops | bytes accessed | tf_op | source)
XLA Modules:
  0.0 1013.9 jit_solution(10305879099743430704)
XLA Ops:
  6.5 2.2 fusion.71
  9.1 2.1 collective-permute-start
  11.6 0.6 collective-permute-done
  12.7 1.4 collective-permute-done.1
  14.6 14.7 %concatenate.12 = f32[5,2,256,1026]{3,2,1,0:T(8,128)} concatenate(f32[5,2,256,1]{3,2,1,0:T(8,128)S(1)} %copy.25, f32[5,2,256,1024]{3,2,1,0:T(8,128)} %param.4, f32[5,2,256,1]{3,2,1,0:T(8,128)S(1)} %copy.26), dimensions={3} | concatenate | bytes 21012480 | tf_op jit(solution)/shard_map/concatenate | solution.py:24
  29.3 1.2 fusion.70
  30.5 1.3 collective-permute-start.2
  31.8 2.1 collective-permute-start.3
  33.9 1.4 collective-permute-done.2
  35.3 10.4 %pad_maximum_fusion.1 = f32[5,2,258,1026]{3,2,1,0:T(8,128)} fusion(f32[5,2,1,1026]{3,2,1,0:T(1,128)S(1)} %collective-permute-done.3, f32[5,2,256,1026]{3,2,1,0:T(8,128)} %concatenate.12, f32[5,2,1,1026]{3,2,1,0:T(1,128)S(1)} %collective-permute-done.2), kind=kLoop, calls=%fused_computation.40 | loop fusion | flops 5294160 | bytes 21176640 | tf_op jit(solution)/shard_map/concatenate | solution.py:24
  45.7 7.9 fusion.69
  53.6 8.6 copy.27
  62.2 4.6 collective-permute-start.4
  66.8 9.0 copy.28
  76.4 108.5 %collective-permute-done.4 = f32[5,1,258,1026]{3,1,2,0:T(1,128)} collective-permute-done((f32[5,1,258,1026]{3,1,2,0:T(1,128)}, f32[5,1,258,1026]{3,1,2,0:T(1,128)}, u32[]{:S(2)}, u32[]{:S(2)}) %collective-permute-start.4) | collective-permute-done | bytes 5294192 | tf_op jit(solution)/shard_map/ppermute | solution.py:22
  184.9 3.2 copy.29
  188.1 7.6 collective-permute-done.5
  195.7 3.1 copy.30
  198.8 10.8 %pad_maximum_fusion = f32[5,4,258,1026]{3,2,1,0:T(8,128)} fusion(f32[5,1,258,1026]{3,2,1,0:T(8,128)S(1)} %copy.30, f32[5,2,1,1026]{3,2,1,0:T(1,128)S(1)} %collective-permute-done.3, f32[5,2,256,1026]{3,2,1,0:T(8,128)S(1)} %bitcast.57, f32[5,2,1,1026]{3,2,1,0:T(1,128)S(1)} %collective-permute-done.2, f32[5,1,258,1026]{3,2,1,0:T(8,128)S(1)} %copy.29), kind=kLoop, calls=%fused_computation.39 | loop fusion | flops 21176640 | bytes 42353280 | tf_op jit(solution)/shard_map/concatenate | solution.py:24
  209.6 16.3 %slice_bitcast_fusion.3 = (f32[4,258,1026]{2,1,0:T(8,128)}, f32[5,4,258,1026]{3,2,1,0:T(8,128)}, f32[5,4,258,1026]{3,2,1,0:T(8,128)}, f32[4,258,1026]{2,1,0:T(8,...) fusion(f32[5,4,258,1026]{3,2,1,0:T(8,128)} %pad_maximum_fusion), kind=kLoop, calls=%fused_computation.83 | loop fusion | bytes 51003648 | tf_op jit(solution)/shard_map/squeeze | solution.py:58
  225.9 12.8 %fusion.44 = (f32[4,258,1026]{2,1,0:T(8,128)}, f32[4,258,1026]{2,1,0:T(8,128)}, f32[4,258,1026]{2,1,0:T(8,128)}) fusion(f32[5,4,258,1026]{3,2,1,0:T(8,128)} %pad_maximum_fusion, s32[1026]{0:T(1024)S(1)} %fusion.56, s32[4,258]{1,0:T(4,128)S(1)} %broadcast_add_fusion), kind=kLoop, calls=%fused_computation.89 | loop fusion | flops 6352992 | bytes 29655528 | tf_op jit(solution)/shard_map/div | solution.py:62
  238.7 13.2 %add_dynamic-update-slice_fusion.2 = (f32[5,4,258,1026]{3,2,1,0:T(8,128)}, f32[1,4,258,1026]{3,2,1,0:T(8,128)}, f32[1,4,258,1026]{3,2,1,0:T(8,128)S(1)}, f32[1,4...) fusion(f32[5,4,258,1026]{3,2,1,0:T(8,128)} %get-tuple-element.282, f32[5,4,258,1026]{3,2,1,0:T(8,128)} %pad_maximum_fusion, ...), kind=kLoop, calls=%fused_computation.69 | loop fusion | flops 15882480 | bytes 46776552
  251.9 6.9 multiply_dynamic-update-slice_fusion.8
  258.7 10.4 %multiply_dynamic-update-slice_fusion.7 = (f32[5,4,258,1026]{3,2,1,0:T(8,128)}, f32[5,4,258,1026]{3,2,1,0:T(8,128)}, f32[5,4,258,1026]{3,2,1,0:T(8,128)}) fusion(f32[5,4,258,1026]{3,2,1,0:T(8,128)} %multiply_dynamic-update-slice_fusion.8, f32[1,4,258,1026]{3,2,1,0:T(8,128)} %copy-done, f32[5,4,258,1026]{3,2,1,0:T(8,128)} %pad_maximum_fusion, ...), kind=kLoop, calls=%fused_computation.67 | loop fusion | flops 3176496 | bytes 37666944
  269.2 5.1 multiply_dynamic-update-slice_fusion.1
  274.2 6.8 add_dynamic-update-slice_fusion
  281.0 12.7 %multiply_dynamic-update-slice_fusion.6 = (f32[5,4,258,1026]{3,2,1,0:T(8,128)}, f32[5,4,258,1026]{3,2,1,0:T(8,128)}, f32[5,4,258,1026]{3,2,1,0:T(8,128)}) fusion(f32[5,4,258,1026]{3,2,1,0:T(8,128)} %get-tuple-element.288, f32[1,4,258,1026]{3,2,1,0:T(8,128)} %copy-done, f32[1,4,258,1026]{3,2,1,0:T(8,128)} %get-tuple-element.271, ...), kind=kLoop, calls=%fused_computation.66 | loop fusion | flops 5294160 | bytes 42532992 | tf_op jit(solution)/shard_map/stack | solution.py:69
  293.7 5.0 multiply_dynamic-update-slice_fusion.4
  298.7 6.8 multiply_dynamic-update-slice_fusion.3
  305.6 32.1 %broadcast_multiply_fusion = (f32[5,4,258,1026]{3,2,1,0:T(8,128)}, f32[5,4,258,1026]{3,2,1,0:T(8,128)}) fusion(f32[5,4,258,1026]{3,2,1,0:T(8,128)} %multiply_dynamic-update-slice_fusion.3, f32[258]{0:T(512)S(1)} %fusion.63, f32[5,4,258,1026]{3,2,1,0:T(8,128)} %get-tuple-element.275, f32[4]{0:T(128)S(1)} %and_convert_fusion), kind=kLoop, calls=%fused_computation.41 | loop fusion | flops 10588320 | bytes 84707608 | tf_op jit(solution)/shard_map/mul | solution.py:88
  337.6 9.9 fusion.48
  347.5 26.9 %fusion.35 = f32[5,2,256,1024]{3,2,1,0:T(8,128)S(1)} fusion(f32[5,4,258,1026]{3,2,1,0:T(8,128)} %get-tuple-element.276, f32[5,4,258,1026]{3,2,1,0:T(8,128)} %get-tuple-element.302, f32[5,4,258,1026]{3,2,1,0:T(8,128)} %get-tuple-element.303, f32[1,2,256,1024]{3,2,1,0:T(8,128)} %get-tuple-element.298, f32[1,2,256,1024]{3,2,1,0:T(8,128)S(1)} %get-tuple-element.297, ...), kind=kLoop, calls=%fused_computation.47 | loop fusion | flops 39321600 | bytes 77596712 | tf_op jit(solution)/shard_map/add | solution.py:120
  374.4 4.1 copy-done.1
  378.5 0.9 slice_select_fusion.1
  379.8 9.6 slice.122
  389.4 30.4 %all-reduce.2.cloned.1.call-done = f32[16,10,1024]{2,0,1:T(8,128)} async-done(((f32[16,10,1024]{2,0,1:T(8,128)}), f32[16,10,1024]{2,0,1:T(8,128)}) %all-reduce.2.cloned.1.call-update) | async-done | bytes 655376 | tf_op jit(solution)/shard_map/psum | solution.py:30
  419.8 1.0 constant_dynamic-slice_fusion.1
  420.8 5.7 all_gather.6
  426.6 549.2 %while.16 = (s32[]{:T(128)}, f32[4,10,1024]{2,1,0:T(8,128)S(1)}, f32[4,10,2048]{2,0,1:T(4,128)S(1)}, s32[4]{0:T(128)S(1)}, s32[4]{0:T(128)S(1)}, /*index=5*/f32[...) while((s32[]{:T(128)}, f32[4,10,1024]{2,1,0:T(8,128)S(1)}, ...), condition=%wide.region_3.4_spmd.clone.clone.clone, body=%wide.region_2.3_spmd.clone.clone.clone.sunk | while | flops 281044992 | bytes 342281 | solution.py:164
  427.1 0.6 dynamic_slice.66
  428.5 0.8 add_select_fusion.8
  429.3 0.8 add_select_fusion.7
  432.6 0.7 dynamic_slice.65
  435.3 138.4 %fusion.73 = f32[4,10,1024]{2,1,0:T(8,128)S(1)} fusion(f32[4,10,1024]{2,1,0:T(8,128)S(1)} %get-tuple-element.364, s32[]{:T(128)} %get-tuple-element.363, f32[]{:T(128)S(6)} %mul.406, f32[]{:T(128)S(6)} %convert_element_type.115, f32[]{:T(128)} %bitcast.55, s32[]{:T(128)S(6)} %select_n.210, s32[2048]{0:T(1024)S(1)} %add_select_fusion.7, ...), kind=kOutput, calls=%fused_computation.22.clone.1 | convolution fusion | flops 281018368 | bytes 159765 | tf_op jit(solution)/shard_map/while/body/eval_jaxpr/lq,pq->lp/dot_general | solution.py:162
  575.1 0.6 dynamic_slice.66
  576.4 0.8 add_select_fusion.8
  577.2 0.8 add_select_fusion.7
  578.0 0.6 dynamic_slice.67
  580.6 0.7 dynamic_slice.65
  582.6 0.6 dynamic_slice.68
  583.2 119.9 %fusion.73 = f32[4,10,1024]{2,1,0:T(8,128)S(1)} fusion(f32[4,10,1024]{2,1,0:T(8,128)S(1)} %get-tuple-element.364, s32[]{:T(128)} %get-tuple-element.363, f32[]{:T(128)S(6)} %mul.406, f32[]{:T(128)S(6)} %convert_element_type.115, f32[]{:T(128)} %bitcast.55, s32[]{:T(128)S(6)} %select_n.210, s32[2048]{0:T(1024)S(1)} %add_select_fusion.7, ...), kind=kOutput, calls=%fused_computation.22.clone.1 | convolution fusion | flops 281018368 | bytes 159765 | tf_op jit(solution)/shard_map/while/body/eval_jaxpr/lq,pq->lp/dot_general | solution.py:162
  704.5 0.6 dynamic_slice.66
  705.9 0.8 add_select_fusion.8
  706.7 0.8 add_select_fusion.7
  710.0 0.7 dynamic_slice.65
  712.7 121.0 %fusion.73 = f32[4,10,1024]{2,1,0:T(8,128)S(1)} fusion(f32[4,10,1024]{2,1,0:T(8,128)S(1)} %get-tuple-element.364, s32[]{:T(128)} %get-tuple-element.363, f32[]{:T(128)S(6)} %mul.406, f32[]{:T(128)S(6)} %convert_element_type.115, f32[]{:T(128)} %bitcast.55, s32[]{:T(128)S(6)} %select_n.210, s32[2048]{0:T(1024)S(1)} %add_select_fusion.7, ...), kind=kOutput, calls=%fused_computation.22.clone.1 | convolution fusion | flops 281018368 | bytes 159765 | tf_op jit(solution)/shard_map/while/body/eval_jaxpr/lq,pq->lp/dot_general | solution.py:162
  834.9 0.6 dynamic_slice.66
  836.3 0.8 add_select_fusion.8
  837.1 0.8 add_select_fusion.7
  840.4 0.7 dynamic_slice.65
  843.1 129.3 %fusion.73 = f32[4,10,1024]{2,1,0:T(8,128)S(1)} fusion(f32[4,10,1024]{2,1,0:T(8,128)S(1)} %get-tuple-element.364, s32[]{:T(128)} %get-tuple-element.363, f32[]{:T(128)S(6)} %mul.406, f32[]{:T(128)S(6)} %convert_element_type.115, f32[]{:T(128)} %bitcast.55, s32[]{:T(128)S(6)} %select_n.210, s32[2048]{0:T(1024)S(1)} %add_select_fusion.7, ...), kind=kOutput, calls=%fused_computation.22.clone.1 | convolution fusion | flops 281018368 | bytes 159765 | tf_op jit(solution)/shard_map/while/body/eval_jaxpr/lq,pq->lp/dot_general | solution.py:162
  975.8 19.2 %all_gather.7 = f32[16,10,1024]{2,1,0:T(8,128)S(1)} all-gather(f32[4,10,1024]{2,1,0:T(8,128)S(1)} %get-tuple-element.161), channel_id=1, replica_groups=mesh['sec'=2,'rad'=4,'ax'=4] {'rad'}, dimensions={0}, use_global_device_ids=true | all-gather | bytes 819200 | tf_op jit(solution)/shard_map/all_gather | solution.py:165
  995.4 1.2 slice_select_fusion
  996.6 10.1 pad_maximum_fusion.2
  (55 shorter events, 7.3 us)
Async XLA Ops:
  6.5 413.3 %all-reduce.2.cloned.1.call-start = ((), (), s32[]{:S(2)}) async-start(), calls=%async_computation | async-start | bytes 1310720 | tf_op jit(solution)/shard_map/psum | solution.py:30
  9.1 3.2 collective-permute-start
  11.6 2.6 collective-permute-start.1
  30.5 4.8 collective-permute-start.2
  31.8 3.5 collective-permute-start.3
  62.2 122.6 %collective-permute-start.4 = (f32[5,1,258,1026]{3,1,2,0:T(1,128)}, f32[5,1,258,1026]{3,1,2,0:T(1,128)}, u32[]{:S(2)}, u32[]{:S(2)}) collective-permute-start(f32[5,1,258,1026]{3,1,2,0:T(1,128)} %copy.27), channel_id=1, source_target_pairs={{0,1},{1,2},{2,3},{3,0},{4,5},{5,6},{6,7},{7,4},{8,9},{9,10},{10,1... | collective-permute-start | bytes 15882488 | tf_op jit(solution)/shard_map/ppermute | solution.py:22
  75.7 119.9 %collective-permute-start.5 = (f32[5,1,258,1026]{3,1,2,0:T(1,128)}, f32[5,1,258,1026]{3,1,2,0:T(1,128)}, u32[]{:S(2)}, u32[]{:S(2)}) collective-permute-start(f32[5,1,258,1026]{3,1,2,0:T(1,128)} %copy.28), channel_id=1, source_target_pairs={{1,0},{2,1},{3,2},{0,3},{5,4},{6,5},{7,6},{4,7},{9,8},{10,9},{11,1... | collective-permute-start | bytes 15882488 | tf_op jit(solution)/shard_map/ppermute | solution.py:23
  184.8 13.9 %slice-start = ((s8[11796480]{0:T(1024)(128)(4,1)}), s8[4194304]{0:T(1024)(128)(4,1)S(1)}, s32[]{:S(2)}) async-start(s8[11796480]{0:T(1024)(128)(4,1)} %bitcast.56), calls=%async_computation.1 | async-start | bytes 8388608
  184.9 13.9 %slice-start.1 = ((s8[11796480]{0:T(1024)(128)(4,1)}), s8[4194304]{0:T(1024)(128)(4,1)S(1)}, s32[]{:S(2)}) async-start(s8[11796480]{0:T(1024)(128)(4,1)} %bitcast.56), calls=%async_computation.2 | async-start | bytes 8388608
  188.1 10.7 %slice-start.2 = ((s8[11796480]{0:T(1024)(128)(4,1)}), s8[3407872]{0:T(1024)(128)(4,1)S(1)}, s32[]{:S(2)}) async-start(s8[11796480]{0:T(1024)(128)(4,1)} %bitcast.56), calls=%async_computation.3 | async-start | bytes 6815744
  251.9 6.9 copy-start
  347.5 32.0 %copy-start.2 = (s32[16]{0:T(128)S(1)}, s32[16]{0:T(128)}, u32[]{:S(2)}) copy-start(s32[16]{0:T(128)} %param.5) | copy-start | bytes 196
  374.4 4.1 copy-start.1
Sparse Core Ops, SparseCore 0:
  379.6 40.2 all-reduce.1
where the time goes:
time: 1020 us; the launch traced here: 1010 us
  matrix products  509 us (50%)
  other arithmetic  189 us (19%)
  waiting for transfers between devices  150 us (15%)
  local copies, waits for them, and re-layouts  93.4 us (9%)
  blocking collectives  24.9 us (2%)
  loops' own time  23.5 us (2%)
  between operations  14 us (1%)
  starting transfers between devices  10.4 us (1%)
    dot_general x4, matrix products, per_cycle(): jnp.einsum('lq,pq->lp', lines_one, table, precision=lax.Precision.HIGHEST)  509 us
    ppermute x3, waiting for transfers between devices, padded_2(): before = lax.ppermute(last, axis, up)  110 us
    unnamed x7, other arithmetic  47.3 us
    mul x2, other arithmetic, body(): flux_rad = flux_rad * (radius_pad * inside_rad)[None, None, :, None]  32.1 us
    psum x1, waiting for transfers between devices, spread(): return lax.psum(jnp.where(mine, value, jnp.zeros_like(value)), axis)  30.4 us
    add x1, other arithmetic, body(): tendency = tendency + source  26.9 us
    another operation x1, loops' own time, body(): lax.map(per_cycle, (portion, factor, blocks, log_ratio, scale_const))  23.5 us
    concatenate x2, other arithmetic, padded_2(): value = jnp.concatenate([before, value, after], axis=dim)  21.2 us
  transfers between devices with their start and end apart: 7, of which 6 were waited for; matrix products, arithmetic and copies ran while one was open for 2% of the time, Pallas kernels for 0%

commit v1 on v0

v1 whole, which is shorter than its diff:
```python
import functools
import math

import jax
import jax.numpy as jnp
from jax import lax
from jax.experimental import pallas as pl
from jax.experimental.pallas import tpu as pltpu
from jax.sharding import PartitionSpec as P

R_NEAR = 16
FMAX = 16

GAMMA = 1.4
KAPPA = 1.44

FIELDS = 5
PLANES = 2
ROWS = 16
LANES = 128
VMEM_LIMIT = 40 * 1024 * 1024

COL_LOG = 32
COL_GAIN = 33

PARITY, OUTER, FIRST, LAST, BASE, PLANE = range(6)


def primitives(fields):
    density, mom_ax, mom_rad, mom_az, energy = fields
    inverse = 1.0 / density
    vel_ax = mom_ax * inverse
    vel_rad = mom_rad * inverse
    vel_az = mom_az * inverse
    pressure = (GAMMA - 1.0) * (
        energy - 0.5 * (mom_ax * vel_ax + mom_rad * vel_rad + mom_az * vel_az)
    )
    return vel_ax, vel_rad, vel_az, pressure


def flux(fields, velocity, pressure, along):
    _, mom_ax, mom_rad, mom_az, energy = fields
    out = [fields[along], mom_ax * velocity, mom_rad * velocity, mom_az * velocity]
    out[along] = out[along] + pressure
    return out + [(energy + pressure) * velocity]


def stencil(flags, first_row, fields, above, below, edges, inner, outer, dtheta):
    rows, cells = fields[0][0].shape
    row = lax.broadcasted_iota(jnp.int32, (rows, 1), 0)
    lane = lax.broadcasted_iota(jnp.int32, (rows, cells), 1)
    sub = lax.broadcasted_iota(jnp.int32, (rows, cells), 0)
    start = flags[BASE] + first_row
    radius = (start + row).astype(jnp.float32) + 0.5
    inv_radius = 1.0 / radius
    half_inv = 0.5 * inv_radius
    half_arc = 0.5 / (radius * dtheta)
    radius_above = jnp.maximum(start - 1, 0).astype(jnp.float32) + 0.5
    radius_below = (start + rows).astype(jnp.float32) + 0.5
    radius_above = jnp.where((flags[FIRST] == 1) & (first_row == 0), 0.0, radius_above)
    out = []
    axial = []
    for plane in range(PLANES):
        mine = fields[plane]
        vel_ax, vel_rad, vel_az, pressure = primitives(mine)
        axial.append(flux(mine, vel_ax, pressure, 1))
        flux_rad = [g * radius for g in flux(mine, vel_rad, pressure, 2)]
        _, vel, _, press = primitives(above[plane])
        flux_above = [g * radius_above for g in flux(above[plane], vel, press, 2)]
        _, vel, _, press = primitives(below[plane][0])
        flux_below = [g * radius_below * below[plane][1] for g in flux(below[plane][0], vel, press, 2)]
        flux_az = flux(mine, vel_az, pressure, 3)
        _, _, vel, press = primitives(edges[plane][0])
        flux_left = flux(edges[plane][0], vel, press, 3)
        _, _, vel, press = primitives(edges[plane][1])
        flux_right = flux(edges[plane][1], vel, press, 3)
        result = []
        for f in range(FIELDS):
            up = jnp.where(sub == 0, flux_above[f], pltpu.roll(flux_rad[f], 1, 0))
            down = jnp.where(sub == rows - 1, flux_below[f], pltpu.roll(flux_rad[f], rows - 1, 0))
            left = jnp.where(lane == 0, flux_left[f], pltpu.roll(flux_az[f], 1, 1))
            right = jnp.where(lane == cells - 1, flux_right[f], pltpu.roll(flux_az[f], cells - 1, 1))
            result.append((up - down) * half_inv + (left - right) * half_arc)
        result[2] = result[2] + (pressure + mine[3] * vel_az) * inv_radius
        result[3] = result[3] - (mine[2] * vel_az) * inv_radius
        out.append(result)
    vel, _, _, press = primitives(inner)
    flux_inner = flux(inner, vel, press, 1)
    odd = flags[PARITY].astype(jnp.float32)
    low = [g * odd for g in flux_inner]
    high = [g * (1.0 - odd) for g in flux_inner]
    if outer is not None:
        flux_outer = outer_flux(flags, outer)
        low = [a + g * (1.0 - odd) for a, g in zip(low, flux_outer)]
        high = [a + g * odd for a, g in zip(high, flux_outer)]
    for f in range(FIELDS):
        out[0][f] = out[0][f] - 0.5 * (axial[1][f] - low[f])
        out[1][f] = out[1][f] - 0.5 * (high[f] - axial[0][f])
    return out


def outer_flux(flags, outer):
    present = flags[OUTER] == 1
    outer = [jnp.where(present, outer[0], 1.0)] + [jnp.where(present, g, 0.0) for g in outer[1:]]
    vel, _, _, press = primitives(outer)
    return flux(outer, vel, press, 1)


def edge_columns(edge_ref):
    edges = []
    for plane in range(PLANES):
        sides = []
        for side in range(2):
            at = [(side * FIELDS + f) * PLANES + plane for f in range(FIELDS)]
            sides.append([edge_ref[:, c : c + 1] for c in at])
        edges.append(sides)
    return edges


def bulk_kernel(dtheta, blocks, flags, state, before, after, halo_low, halo_high, inner, edge, out):
    block = pl.program_id(0) + 1
    last = block == blocks - 1
    fields = [[state[f, p] for f in range(FIELDS)] for p in range(PLANES)]
    above = [[before[f, p, 7:8, :] for f in range(FIELDS)] for p in range(PLANES)]
    keep = jnp.where((flags[LAST] == 1) & last, 0.0, 1.0)
    present = jnp.logical_not((flags[LAST] == 1) & last)
    below = []
    for p in range(PLANES):
        rows = []
        for f in range(FIELDS):
            k = f * PLANES + p
            value = jnp.where(last, halo_high[k : k + 1, :], after[f, p, 0:1, :])
            rows.append(jnp.where(present, value, 1.0))
        below.append((rows, keep))
    inner_fields = [inner[f] for f in range(FIELDS)]
    result = stencil(
        flags, block * ROWS, fields, above, below, edge_columns(edge), inner_fields, None, dtheta
    )
    for p in range(PLANES):
        for f in range(FIELDS):
            out[f, p] = result[p][f]


def near_kernel(dtheta, flags, state, after, halo_low, inner, outer, edge, table, rhs, local, carry):
    cells = state.shape[-1]
    steps = int(math.log2(cells))
    fields = [[state[f, p] for f in range(FIELDS)] for p in range(PLANES)]
    present = flags[FIRST] == 0
    above = []
    for p in range(PLANES):
        at = [f * PLANES + p for f in range(FIELDS)]
        above.append([jnp.where(present, halo_low[k : k + 1, :], 1.0) for k in at])
    below = [([after[f, p, 0:1, :] for f in range(FIELDS)], 1.0) for p in range(PLANES)]
    inner_fields = [inner[f] for f in range(FIELDS)]
    outer_fields = [outer[f] for f in range(FIELDS)]
    result = stencil(
        flags, 0, fields, above, below, edge_columns(edge), inner_fields, outer_fields, dtheta
    )
    for p in range(PLANES):
        for f in range(FIELDS):
            rhs[f * PLANES + p] = result[p][f]
    lane = lax.broadcasted_iota(jnp.int32, (R_NEAR, cells), 1)
    column = lax.broadcasted_iota(jnp.int32, (R_NEAR, LANES), 1)
    coefs = [table[:, k : k + 1] for k in range(steps)]

    def line(k, ends):
        mean = rhs[k]
        for level in range(FMAX.bit_length() - 1):
            width = 1 << level
            partner = jnp.where(
                (lane & width) == 0,
                pltpu.roll(mean, cells - width, 1),
                pltpu.roll(mean, width, 1),
            )
            mean = jnp.where(table[:, level : level + 1] == 0.0, 0.5 * (mean + partner), mean)
        ahead = mean
        behind = mean
        for step in range(steps):
            width = 1 << step
            moved = jnp.where(lane >= width, pltpu.roll(ahead, width, 1), 0.0)
            ahead = ahead + coefs[step] * moved
            moved = jnp.where(lane < cells - width, pltpu.roll(behind, cells - width, 1), 0.0)
            behind = behind + coefs[step] * moved
        local[k] = ahead + behind - mean
        ends = jnp.where(column == k, ahead[:, cells - 1 : cells], ends)
        return jnp.where(column == k + FIELDS * PLANES, behind[:, 0:1], ends)

    ends = lax.fori_loop(0, FIELDS * PLANES, line, jnp.zeros((R_NEAR, LANES), jnp.float32))
    carry[...] = ends


def finish_kernel(flags, factor, rhs, local, carry, table, held, out):
    cells = out.shape[-1]
    lane = lax.broadcasted_iota(jnp.int32, (R_NEAR, cells), 1).astype(jnp.float32)
    width = factor[:, 0:1].astype(jnp.float32)
    block = jnp.floor((lane + 0.5) / width)
    count = cells / width
    log_ratio = table[:, COL_LOG : COL_LOG + 1]
    gain = table[:, COL_GAIN : COL_GAIN + 1]
    from_left = jnp.exp(log_ratio * (block + 1.0))
    from_right = jnp.exp(log_ratio * (count - block))
    near = flags[FIRST] == 1
    for f in range(FIELDS):
        for p in range(PLANES):
            k = f * PLANES + p
            j = k + FIELDS * PLANES
            smooth = gain * (
                local[k] + from_left * carry[:, k : k + 1] + from_right * carry[:, j : j + 1]
            )
            out[f, p] = jnp.where(near, smooth, rhs[k])


def outer_kernel(flags, outer, held, out):
    values = outer_flux(flags, [outer[f] for f in range(FIELDS)])
    sign = jnp.where(flags[PARITY] == 1, -0.5, 0.5)
    for f in range(FIELDS):
        out[f, 0] = held[f, 0] + sign * values[f]


def cost(flops, nbytes):
    return pl.CostEstimate(flops=flops, bytes_accessed=nbytes, transcendentals=0)


def bulk(flags, state, halo_low, halo_high, inner, edge, dtheta):
    _, _, rows, cells = state.shape
    blocks = rows // ROWS
    eights = ROWS // 8
    size = state.size * 4
    return pl.pallas_call(
        functools.partial(bulk_kernel, dtheta, blocks),
        grid_spec=pltpu.PrefetchScalarGridSpec(
            num_scalar_prefetch=1,
            grid=(blocks - 1,),
            in_specs=[
                pl.BlockSpec((FIELDS, PLANES, ROWS, cells), lambda i, s: (0, 0, i + 1, 0)),
                pl.BlockSpec(
                    (FIELDS, PLANES, 8, cells), lambda i, s: (0, 0, (i + 1) * eights - 1, 0)
                ),
                pl.BlockSpec(
                    (FIELDS, PLANES, 8, cells),
                    lambda i, s: (0, 0, jnp.minimum((i + 2) * eights, rows // 8 - 1), 0),
                ),
                pl.BlockSpec((FIELDS * PLANES, cells), lambda i, s: (0, 0)),
                pl.BlockSpec((FIELDS * PLANES, cells), lambda i, s: (0, 0)),
                pl.BlockSpec((FIELDS, ROWS, cells), lambda i, s: (0, i + 1, 0)),
                pl.BlockSpec((ROWS, LANES), lambda i, s: (i + 1, 0)),
            ],
            out_specs=pl.BlockSpec((FIELDS, PLANES, ROWS, cells), lambda i, s: (0, 0, i + 1, 0)),
        ),
        out_shape=jax.ShapeDtypeStruct(state.shape, jnp.float32),
        compiler_params=pltpu.CompilerParams(vmem_limit_bytes=VMEM_LIMIT),
        cost_estimate=cost(state.size * 40, size * 3),
        name="bulk",
    )(flags, state, state, state, halo_low, halo_high, inner, edge)


def near(flags, state, halo_low, inner, outer, edge, table, dtheta):
    _, _, rows, cells = state.shape
    lines = FIELDS * PLANES
    whole = lambda *shape: pl.BlockSpec(shape, lambda i, s: (0,) * len(shape))
    out = jax.ShapeDtypeStruct((lines, R_NEAR, cells), jnp.float32)
    return pl.pallas_call(
        functools.partial(near_kernel, dtheta),
        grid_spec=pltpu.PrefetchScalarGridSpec(
            num_scalar_prefetch=1,
            grid=(1,),
            in_specs=[
                whole(FIELDS, PLANES, R_NEAR, cells),
                pl.BlockSpec((FIELDS, PLANES, 8, cells), lambda i, s: (0, 0, R_NEAR // 8, 0)),
                whole(lines, cells),
                whole(FIELDS, R_NEAR, cells),
                whole(FIELDS, R_NEAR, cells),
                whole(R_NEAR, LANES),
                whole(R_NEAR, LANES),
            ],
            out_specs=[
                whole(lines, R_NEAR, cells),
                whole(lines, R_NEAR, cells),
                whole(R_NEAR, LANES),
            ],
        ),
        out_shape=[out, out, jax.ShapeDtypeStruct((R_NEAR, LANES), jnp.float32)],
        compiler_params=pltpu.CompilerParams(vmem_limit_bytes=VMEM_LIMIT),
        cost_estimate=cost(lines * R_NEAR * cells * 200, lines * R_NEAR * cells * 20),
        name="near",
    )(flags, state, state, halo_low, inner, outer, edge, table)


def finish(flags, factor, rhs, local, carry, table, held):
    lines, _, cells = rhs.shape
    whole = lambda *shape: pl.BlockSpec(shape, lambda i, s: (0,) * len(shape))
    return pl.pallas_call(
        finish_kernel,
        grid_spec=pltpu.PrefetchScalarGridSpec(
            num_scalar_prefetch=1,
            grid=(1,),
            in_specs=[
                whole(R_NEAR, LANES),
                whole(lines, R_NEAR, cells),
                whole(lines, R_NEAR, cells),
                whole(R_NEAR, LANES),
                whole(R_NEAR, LANES),
                pl.BlockSpec(memory_space=pl.ANY),
            ],
            out_specs=whole(FIELDS, PLANES, R_NEAR, cells),
        ),
        out_shape=jax.ShapeDtypeStruct(held.shape, jnp.float32),
        input_output_aliases={6: 0},
        compiler_params=pltpu.CompilerParams(vmem_limit_bytes=VMEM_LIMIT),
        cost_estimate=cost(lines * R_NEAR * cells * 10, lines * R_NEAR * cells * 12),
        name="finish",
    )(flags, factor, rhs, local, carry, table, held)


def add_outer(flags, outer, first, held):
    _, count, cells = outer.shape
    at = first // ROWS
    place = pl.BlockSpec((FIELDS, 1, ROWS, cells), lambda i, s: (0, s[PLANE], i + at, 0))
    return pl.pallas_call(
        outer_kernel,
        grid_spec=pltpu.PrefetchScalarGridSpec(
            num_scalar_prefetch=1,
            grid=(count // ROWS,),
            in_specs=[pl.BlockSpec((FIELDS, ROWS, cells), lambda i, s: (0, i, 0)), place],
            out_specs=place,
        ),
        out_shape=jax.ShapeDtypeStruct(held.shape, jnp.float32),
        input_output_aliases={2: 0},
        compiler_params=pltpu.CompilerParams(vmem_limit_bytes=VMEM_LIMIT),
        cost_estimate=cost(outer.size * 6, outer.size * 12),
        name="add_outer",
    )(flags, outer, held)


def chunk_bounds(rows):
    units = rows // ROWS
    cuts = {1, units}
    for share in (0.4, 0.8):
        cuts.add(max(1, min(units, round(1 + share * (units - 1)))))
    return [0] + [c * ROWS for c in sorted(cuts)]


def smoothing_table(coarsen, cells, total_cells, dtheta):
    factor = coarsen.astype(jnp.float32)[:, None]
    stiffness = KAPPA / (factor * dtheta) ** 2
    inverse_half = 0.5 / stiffness
    one_minus = jnp.sqrt(inverse_half * (2.0 + inverse_half)) - inverse_half
    log_ratio = jnp.log1p(-one_minus)
    gain = (1.0 - one_minus) / (stiffness * one_minus * (2.0 - one_minus))
    closing = 1.0 / -jnp.expm1((total_cells / factor) * log_ratio)
    across = jnp.exp((cells / factor) * log_ratio)
    column = jnp.arange(LANES, dtype=jnp.int32)[None, :]
    width = jnp.left_shift(1, jnp.minimum(column, 20)).astype(jnp.float32)
    table = jnp.where(width >= factor, jnp.exp(log_ratio * (width / factor)), 0.0)
    table = jnp.where(column == COL_LOG, log_ratio, table)
    table = jnp.where(column == COL_GAIN, gain, table)
    return table, closing, across


def ring(value, axis, shift):
    size = lax.axis_size(axis)
    return lax.ppermute(value, axis, [(i, (i + shift) % size) for i in range(size)])


def body(state, coarsen):
    fields, planes, rows, cells = state.shape
    sec_count = lax.axis_size("sec")
    rad_count = lax.axis_size("rad")
    ax_count = lax.axis_size("ax")
    assert fields == FIELDS and planes == PLANES and ax_count % 2 == 0
    rad_index = lax.axis_index("rad")
    ax_index = lax.axis_index("ax")
    total_cells = cells * sec_count
    dtheta = 2.0 * math.pi / total_cells
    odd = ax_index % 2
    outer_pairs = []
    for i in range(1, ax_count - 1, 2):
        outer_pairs += [(i, i + 1), (i + 1, i)]
    inner_pairs = []
    for i in range(0, ax_count, 2):
        inner_pairs += [(i, i + 1), (i + 1, i)]
    flags = jnp.stack(
        [
            odd,
            ((ax_index > 0) & (ax_index < ax_count - 1)).astype(jnp.int32),
            (rad_index == 0).astype(jnp.int32),
            (rad_index == rad_count - 1).astype(jnp.int32),
            rad_index * rows,
            odd,
        ]
    ).astype(jnp.int32)

    bounds = chunk_bounds(rows)
    outer = []
    for first, end in zip(bounds[:-1], bounds[1:]):
        part = lax.dynamic_slice(
            state, (0, odd, first, 0), (FIELDS, 1, end - first, cells)
        ).reshape(FIELDS, end - first, cells)
        outer.append(lax.ppermute(part, "ax", outer_pairs))
    part = lax.dynamic_slice(state, (0, 1 - odd, 0, 0), (FIELDS, 1, rows, cells))
    inner = lax.ppermute(part.reshape(FIELDS, rows, cells), "ax", inner_pairs)

    lines = FIELDS * PLANES
    up = [(i, i + 1) for i in range(rad_count - 1)]
    down = [(i + 1, i) for i in range(rad_count - 1)]
    halo_low = lax.ppermute(state[:, :, rows - 1, :].reshape(lines, cells), "rad", up)
    halo_high = lax.ppermute(state[:, :, 0, :].reshape(lines, cells), "rad", down)

    first_column = state[:, :, :, 0].reshape(lines, rows)
    last_column = state[:, :, :, cells - 1].reshape(lines, rows)
    if sec_count == 2:
        edge = ring(jnp.concatenate([last_column, first_column], axis=0), "sec", 1)
    else:
        edge = jnp.concatenate([ring(last_column, "sec", 1), ring(first_column, "sec", -1)], axis=0)
    edge = jnp.pad(edge.T, ((0, 0), (0, LANES - 2 * lines)), constant_values=1.0)

    table, closing, across = smoothing_table(coarsen, cells, total_cells, dtheta)
    factor = jnp.broadcast_to(coarsen[:, None], (R_NEAR, LANES))

    rhs, local, ends = near(flags, state, halo_low, inner, outer[0], edge, table, dtheta)
    arrived = [ends] + [ring(ends, "sec", k) for k in range(1, sec_count)] + [ends]
    from_left = jnp.arange(LANES)[None, :] < lines
    carry = jnp.zeros_like(ends)
    for k in range(sec_count, 0, -1):
        carry = carry * across + jnp.where(from_left, arrived[k], arrived[sec_count - k])
    carry = carry * closing

    out = bulk(flags, state, halo_low, halo_high, inner, edge, dtheta)
    for k in range(1, len(outer) - 1):
        out = add_outer(flags, outer[k], bounds[k], out)
    out = finish(flags, factor, rhs, local, carry, table, out)
    return add_outer(flags, outer[-1], bounds[-2], out)


def solution(mesh):
    return jax.shard_map(
        body,
        mesh=mesh,
        in_specs=(P(None, "ax", "rad", "sec"), P()),
        out_specs=P(None, "ax", "rad", "sec"),
        check_vma=False,
    )
```

time: 1020 us -> 128 us (0.13)
  matrix products: 509 us -> 0 us
  other arithmetic: 189 us -> 2.95 us
  waiting for transfers between devices: 150 us -> 33.3 us
  local copies, waits for them, and re-layouts: 93.4 us -> 19.5 us
  Pallas kernels: 0 us -> 50.4 us
  blocking collectives: 24.9 us -> 0 us
  loops' own time: 23.5 us -> 0 us
  between operations: 14 us -> 0.18 us
  starting transfers between devices: 10.4 us -> 20.7 us
    dot_general x4 -> x0, matrix products: 509 us -> none  [per_cycle(): jnp.einsum('lq,pq->lp', lines_one, table, precision=lax.Precision.HIGHEST)]
    ppermute x6 -> x9, waiting for transfers between devices: 120 us -> 33.3 us  [the longest x4 33.3 us: body(): outer.append(lax.ppermute(part, 'ax', outer_pairs))]
    pallas_call x0 -> x6, Pallas kernels: none -> 50.4 us  [the longest x1 20.4 us: bulk(): pl.pallas_call(functools.partial(bulk_kernel, dtheta, blocks), grid_spec=...]
    unnamed x7 -> x0, other arithmetic: 47.3 us -> none
    slice x6 -> x2, local copies, waits for them, and re-layouts: 38.4 us -> 4.18 us  [the longest x1 2.85 us: body(): last_column = state[:, :, :, cells - 1].reshape(lines, rows)]
    mul x4 -> x1, other arithmetic: 32.3 us -> 0.08 us  [body(): carry = carry * closing]
    concatenate x3 -> x1, other arithmetic: 31.3 us -> 0.01 us  [body(): edge = ring(jnp.concatenate([last_column, first_column], axis=0), 'sec', 1)]
    psum x1 -> x0, waiting for transfers between devices: 30.4 us -> none  [spread(): return lax.psum(jnp.where(mine, value, jnp.zeros_like(value)), axis)]
  transfers between devices with their start and end apart: 7 -> 9, of which waited for: 6 -> 1; matrix products, arithmetic and copies ran while one was open for 2% -> 13% of each run, Pallas kernels for 0% -> 37%
where the time goes in v1:
time: 128 us; the launch traced here: 127 us
  Pallas kernels  50.4 us (39%)
  waiting for transfers between devices  33.3 us (26%)
  starting transfers between devices  20.7 us (16%)
  local copies, waits for them, and re-layouts  19.5 us (15%)
  other arithmetic  2.95 us (2%)
    ppermute x4, waiting for transfers between devices, body(): outer.append(lax.ppermute(part, 'ax', outer_pairs))  33.3 us
    pallas_call x1, Pallas kernels, bulk(): pl.pallas_call(functools.partial(bulk_kernel, dtheta, blocks), grid_spec=...  20.4 us
    pallas_call x3, Pallas kernels, add_outer(): pl.pallas_call(outer_kernel, grid_spec=pltpu.PrefetchScalarGridSpec(num_s...  14.9 us
    pallas_call x1, Pallas kernels, near(): pl.pallas_call(functools.partial(near_kernel, dtheta), grid_spec=pltpu.Pr...  13.4 us
    ppermute x4, starting transfers between devices, body(): outer.append(lax.ppermute(part, 'ax', outer_pairs))  12.4 us
    reshape x3, local copies, waits for them, and re-layouts, body(): part = lax.dynamic_slice(state, (0, odd, first, 0), (FIELDS, 1, end - fir...  8.62 us
    reshape x1, local copies, waits for them, and re-layouts, body(): inner = lax.ppermute(part.reshape(FIELDS, rows, cells), 'ax', inner_pairs)  5.71 us
    ppermute x2, starting transfers between devices, ring(): lax.ppermute(value, axis, [(i, (i + shift) % size) for i in range(size)])  3.82 us
  transfers between devices with their start and end apart: 9, of which 1 were waited for; matrix products, arithmetic and copies ran while one was open for 13% of the time, Pallas kernels for 37%

profile of v1, /device:TPU:1, one launch (start us, length us, event | category | flops | bytes accessed | tf_op | source)
XLA Modules:
  0.0 127.1 jit_solution(2578747658614351905)
XLA Ops:
  0.0 0.0 copy-start
  0.0 5.7 %dynamic-slice_bitcast_fusion = f32[5,256,1024]{2,1,0:T(8,128)} fusion(f32[5,2,256,1024]{3,2,1,0:T(8,128)} %after.3, s32[]{:T(128)S(6)} %select_n.32), kind=kLoop, calls=%fused_computation | loop fusion | bytes 10485764 | tf_op jit(solution)/shard_map/reshape | solution.py:401
  5.7 0.1 collective-permute-start.2
  5.8 4.6 %dynamic-slice_bitcast_fusion.1 = (f32[5,96,1024]{2,1,0:T(8,128)}, f32[5,96,1024]{2,1,0:T(8,128)}) fusion(f32[5,2,256,1024]{3,2,1,0:T(8,128)} %after.3, s32[]{:T(128)S(6)} %select_n.31), kind=kLoop, calls=%fused_computation.1 | loop fusion | bytes 7864324 | tf_op jit(solution)/shard_map/reshape | solution.py:398
  10.4 4.4 %collective-permute-start.7 = (f32[5,96,1024]{2,1,0:T(8,128)}, f32[5,96,1024]{2,1,0:T(8,128)}, u32[]{:S(2)}, u32[]{:S(2)}) collective-permute-start(f32[5,96,1024]{2,1,0:T(8,128)} %get-tuple-element.18), channel_id=1, source_target_pairs={{1,2},{2,1},{5,6},{6,5},{9,10},{10,9},{13,14},{14,13},{17,18},{18,... | collective-permute-start | bytes 5898248 | tf_op jit(solution)/shard_map/ppermute | solution.py:399
  14.8 1.9 %collective-permute-start.6 = (f32[5,96,1024]{2,1,0:T(8,128)}, f32[5,96,1024]{2,1,0:T(8,128)S(1)}, u32[]{:S(2)}, u32[]{:S(2)}) collective-permute-start(f32[5,96,1024]{2,1,0:T(8,128)} %get-tuple-element.19), channel_id=1, source_target_pairs={{1,2},{2,1},{5,6},{6,5},{9,10},{10,9},{13,14},{14,13},{17,18},{18,... | collective-permute-start | bytes 5898248 | tf_op jit(solution)/shard_map/ppermute | solution.py:399
  16.8 2.9 %slice_reduce_fusion.1 = (f32[5,2,256]{2,1,0:T(2,128)S(1)}, f32[5,2,256]{2,1,0:T(2,128)S(1)}) fusion(f32[5,2,256,1024]{3,2,1,0:T(8,128)} %after.3), kind=kLoop, calls=%fused_computation.4 | loop fusion | bytes 40960 | tf_op jit(solution)/shard_map/slice | solution.py:410
  19.7 0.1 copy.11
  19.8 1.9 %collective-permute-start.4 = (f32[20,256]{0,1:T(8,128)S(1)}, f32[20,256]{0,1:T(8,128)S(1)}, u32[]{:S(2)}, u32[]{:S(2)}) collective-permute-start(f32[20,256]{0,1:T(8,128)S(1)} %copy.11), channel_id=1, source_target_pairs={{0,16},{16,0},{1,17},{17,1},{2,18},{18,2},{3,19},{19,3},{4,20},{20... | collective-permute-start | bytes 61448 | tf_op jit(solution)/shard_map/ppermute | solution.py:362
  21.7 2.3 %dynamic-slice_bitcast_fusion.3 = f32[5,48,1024]{2,1,0:T(8,128)} fusion(f32[5,2,256,1024]{3,2,1,0:T(8,128)} %after.3, s32[]{:T(128)S(6)} %select_n.31), kind=kLoop, calls=%fused_computation.5 | loop fusion | bytes 1966084 | tf_op jit(solution)/shard_map/reshape | solution.py:398
  24.0 3.3 %collective-permute-start = (f32[5,48,1024]{2,1,0:T(8,128)}, f32[5,48,1024]{2,1,0:T(8,128)S(1)}, u32[]{:S(2)}, u32[]{:S(2)}) collective-permute-start(f32[5,48,1024]{2,1,0:T(8,128)} %dynamic-slice_bitcast_fusion.3), channel_id=1, source_target_pairs={{1,2},{2,1},{5,6},{6,5},{9,10},{10,9},{13,14},{14,13},{17,18},{18,... | collective-permute-start | bytes 2949128 | tf_op jit(solution)/shard_map/ppermute | solution.py:399
  27.3 1.3 %slice_reduce_fusion.2 = (f32[5,2,1024]{2,1,0:T(2,128)S(1)}, f32[5,2,1024]{2,1,0:T(2,128)S(1)}) fusion(f32[5,2,256,1024]{3,2,1,0:T(8,128)} %after.3), kind=kLoop, calls=%fused_computation.7 | loop fusion | bytes 163840 | tf_op jit(solution)/shard_map/slice | solution.py:407
  28.6 0.0 copy-done
  28.6 0.6 broadcast_multiply_fusion
  29.2 1.7 %dynamic-slice_bitcast_fusion.4 = f32[5,16,1024]{2,1,0:T(8,128)} fusion(f32[5,2,256,1024]{3,2,1,0:T(8,128)} %after.3, s32[]{:T(128)S(6)} %select_n.31), kind=kLoop, calls=%fused_computation.6 | loop fusion | bytes 655364 | tf_op jit(solution)/shard_map/reshape | solution.py:398
  31.0 0.0 collective-permute-done.4
  31.0 3.2 %collective-permute-start.1 = (f32[10,1024]{1,0:T(8,128)S(1)}, f32[10,1024]{1,0:T(8,128)S(1)}, u32[]{:S(2)}, u32[]{:S(2)}) collective-permute-start(f32[10,1024]{1,0:T(8,128)S(1)} %reshape_squeeze.12), channel_id=1, source_target_pairs={{0,4},{4,8},{8,12},{1,5},{5,9},{9,13},{2,6},{6,10},{10,14},{3,7},{... | collective-permute-start | bytes 122888 | tf_op jit(solution)/shard_map/ppermute | solution.py:406
  34.2 0.5 iota_compare_fusion
  34.7 0.5 convert_element_type.16
  35.2 0.7 reshape_squeeze.15
  35.9 0.0 collective-permute-done.1.halo_low
  35.9 2.7 %collective-permute-start.3 = (f32[5,16,1024]{2,1,0:T(8,128)}, f32[5,16,1024]{2,1,0:T(8,128)S(1)}, u32[]{:S(2)}, u32[]{:S(2)}) collective-permute-start(f32[5,16,1024]{2,1,0:T(8,128)} %dynamic-slice_bitcast_fusion.4), channel_id=1, source_target_pairs={{1,2},{2,1},{5,6},{6,5},{9,10},{10,9},{13,14},{14,13},{17,18},{18,... | collective-permute-start | bytes 983048 | tf_op jit(solution)/shard_map/ppermute | solution.py:399
  38.6 0.6 negate_divide_fusion
  39.2 33.3 %collective-permute-done.3.outer = f32[5,16,1024]{2,1,0:T(8,128)S(1)} collective-permute-done((f32[5,16,1024]{2,1,0:T(8,128)}, f32[5,16,1024]{2,1,0:T(8,128)S(1)}, u32[]{:S(2)}, u32[]{:S(2)}) %collective-permute-start.3) | collective-permute-done | bytes 327712 | tf_op jit(solution)/shard_map/ppermute | solution.py:399
  72.5 1.3 %collective-permute-start.8 = (f32[10,1024]{1,0:T(8,128)}, f32[10,1024]{1,0:T(8,128)S(1)}, u32[]{:S(2)}, u32[]{:S(2)}) collective-permute-start(f32[10,1024]{1,0:T(8,128)} %reshape_squeeze.15), channel_id=1, source_target_pairs={{4,0},{8,4},{12,8},{5,1},{9,5},{13,9},{6,2},{10,6},{14,10},{7,3},{... | collective-permute-start | bytes 122888 | tf_op jit(solution)/shard_map/ppermute | solution.py:407
  73.7 0.7 fusion.3.table
  74.5 0.1 stack.36.flags
  74.6 0.0 collective-permute-done.2.inner
  74.6 13.4 %near.1 = (f32[10,16,1024]{2,1,0:T(8,128)S(1)}, f32[10,16,1024]{2,1,0:T(8,128)S(1)}, f32[16,128]{1,0:T(8,128)S(1)}) custom-call(s32[6]{0:T(128)S(1)} %stack.36.flags, f32[5,2,256,1024]{3,2,1,0:T(8,128)} %after.3, f32[5,2,256,1024]{3,2,1,0:T(8,128)} %after.3, f32[10,1024]{1,0:T(8,128)S(1)} %collective-permute-done.1.halo_low, ...), custom_call_target="tpu_custom_call" | custom-call | flops 32768000 | bytes 3276800 | tf_op jit(solution)/shard_map/near/pallas_call | solution.py:262
  88.0 1.9 %collective-permute-start.5 = (f32[16,128]{1,0:T(8,128)S(1)}, f32[16,128]{1,0:T(8,128)S(1)}, u32[]{:S(2)}, u32[]{:S(2)}) collective-permute-start(f32[16,128]{1,0:T(8,128)S(1)} %get-tuple-element.10), channel_id=1, source_target_pairs={{0,16},{16,0},{1,17},{17,1},{2,18},{18,2},{3,19},{19,3},{4,20},{20... | collective-permute-start | bytes 24584 | tf_op jit(solution)/shard_map/ppermute | solution.py:362
  89.9 0.0 collective-permute-done.8.halo_high
  89.9 20.4 %bulk.1.held = f32[5,2,256,1024]{3,2,1,0:T(8,128)} custom-call(s32[6]{0:T(128)S(1)} %stack.36.flags, f32[5,2,256,1024]{3,2,1,0:T(8,128)} %after.3, f32[5,2,256,1024]{3,2,1,0:T(8,128)} %after.3, f32[5,2,256,1024]{3,2,1,0:T(8,128)} %after.3, f32[10,1024]{1,0:T(8,128)S(1)} %collective-permute-done.1.halo_low, f32[10,1024]{1,0:T(8,128)S(1)} %collective-permute-done.8.halo_high, ...), custom_call_target="tpu_custom_call" | custom-call | flops 104857600 | bytes 31457280 | tf_op jit(solution)/shard_map/bulk/pallas_call | solution.py:229
  110.4 0.0 collective-permute-done.7.outer
  110.4 5.8 %add_outer.3.held = f32[5,2,256,1024]{3,2,1,0:T(8,128)} custom-call(s32[6]{0:T(128)S(1)} %stack.36.flags, f32[5,96,1024]{2,1,0:T(8,128)} %collective-permute-done.7.outer, f32[5,2,256,1024]{3,2,1,0:T(8,128)} %bulk.1.held), custom_call_target="tpu_custom_call", output_to_operand_aliasing={{}: (2, {})} | custom-call | flops 2949120 | bytes 5898240 | tf_op jit(solution)/shard_map/add_outer/pallas_call | solution.py:319
  116.1 0.0 copy-start.1
  116.1 0.0 copy-start.2
  116.1 0.0 copy-start.3
  116.1 0.0 collective-permute-done.6.outer
  116.2 5.5 %add_outer.4.held = f32[5,2,256,1024]{3,2,1,0:T(8,128)} custom-call(s32[6]{0:T(128)S(1)} %stack.36.flags, f32[5,96,1024]{2,1,0:T(8,128)S(1)} %collective-permute-done.6.outer, f32[5,2,256,1024]{3,2,1,0:T(8,128)} %add_outer.3.held), custom_call_target="tpu_custom_call", output_to_operand_aliasing={{}: (2, {})} | custom-call | flops 2949120 | bytes 5898240 | tf_op jit(solution)/shard_map/add_outer/pallas_call | solution.py:319
  121.6 0.0 collective-permute-done.5
  121.6 0.0 copy-done.1
  121.6 0.0 copy-done.2
  121.6 0.0 copy-done.3
  121.6 0.1 add_multiply_fusion.carry
  121.7 0.1 broadcast_in_dim.51.factor
  121.8 1.6 %finish.1.held = f32[5,2,256,1024]{3,2,1,0:T(8,128)} custom-call(s32[6]{0:T(128)S(1)} %stack.36.flags, s32[16,128]{1,0:T(8,128)S(1)} %broadcast_in_dim.51.factor, f32[10,16,1024]{2,1,0:T(8,128)S(1)} %get-tuple-element.8.rhs, f32[10,16,1024]{2,1,0:T(8,128)S(1)} %get-tuple-element.9.local, ...), custom_call_target="tpu_custom_call", output_to_operand_aliasing={{}: (6, {})} | custom-call | flops 1638400 | bytes 1966080 | tf_op jit(solution)/shard_map/finish/pallas_call | solution.py:292
  123.4 0.0 collective-permute-done.outer
  123.4 3.7 %add_outer.5 = f32[5,2,256,1024]{3,2,1,0:T(8,128)} custom-call(s32[6]{0:T(128)S(1)} %stack.36.flags, f32[5,48,1024]{2,1,0:T(8,128)S(1)} %collective-permute-done.outer, f32[5,2,256,1024]{3,2,1,0:T(8,128)} %finish.1.held), custom_call_target="tpu_custom_call", output_to_operand_aliasing={{}: (2, {})} | custom-call | flops 1474560 | bytes 2949120 | tf_op jit(solution)/shard_map/add_outer/pallas_call | solution.py:319
  (6 shorter events, 0.1 us)
Async XLA Ops:
  0.0 28.6 %copy-start = (s32[16]{0:T(128)S(1)}, s32[16]{0:T(128)}, u32[]{:S(2)}) copy-start(s32[16]{0:T(128)} %param.3) | copy-start | bytes 196
  5.7 68.9 %collective-permute-start.2 = (f32[5,256,1024]{2,1,0:T(8,128)}, f32[5,256,1024]{2,1,0:T(8,128)}, u32[]{:S(2)}, u32[]{:S(2)}) collective-permute-start(f32[5,256,1024]{2,1,0:T(8,128)} %dynamic-slice_bitcast_fusion), channel_id=1, source_target_pairs={{0,1},{1,0},{2,3},{3,2},{4,5},{5,4},{6,7},{7,6},{8,9},{9,8},{10,11... | collective-permute-start | bytes 15728648 | tf_op jit(solution)/shard_map/ppermute | solution.py:401
  10.4 100.0 %collective-permute-start.7 = (f32[5,96,1024]{2,1,0:T(8,128)}, f32[5,96,1024]{2,1,0:T(8,128)}, u32[]{:S(2)}, u32[]{:S(2)}) collective-permute-start(f32[5,96,1024]{2,1,0:T(8,128)} %get-tuple-element.18), channel_id=1, source_target_pairs={{1,2},{2,1},{5,6},{6,5},{9,10},{10,9},{13,14},{14,13},{17,18},{18,... | collective-permute-start | bytes 5898248 | tf_op jit(solution)/shard_map/ppermute | solution.py:399
  14.8 101.3 %collective-permute-start.6 = (f32[5,96,1024]{2,1,0:T(8,128)}, f32[5,96,1024]{2,1,0:T(8,128)S(1)}, u32[]{:S(2)}, u32[]{:S(2)}) collective-permute-start(f32[5,96,1024]{2,1,0:T(8,128)} %get-tuple-element.19), channel_id=1, source_target_pairs={{1,2},{2,1},{5,6},{6,5},{9,10},{10,9},{13,14},{14,13},{17,18},{18,... | collective-permute-start | bytes 5898248 | tf_op jit(solution)/shard_map/ppermute | solution.py:399
  19.8 11.2 %collective-permute-start.4 = (f32[20,256]{0,1:T(8,128)S(1)}, f32[20,256]{0,1:T(8,128)S(1)}, u32[]{:S(2)}, u32[]{:S(2)}) collective-permute-start(f32[20,256]{0,1:T(8,128)S(1)} %copy.11), channel_id=1, source_target_pairs={{0,16},{16,0},{1,17},{17,1},{2,18},{18,2},{3,19},{19,3},{4,20},{20... | collective-permute-start | bytes 61448 | tf_op jit(solution)/shard_map/ppermute | solution.py:362
  24.0 99.4 %collective-permute-start = (f32[5,48,1024]{2,1,0:T(8,128)}, f32[5,48,1024]{2,1,0:T(8,128)S(1)}, u32[]{:S(2)}, u32[]{:S(2)}) collective-permute-start(f32[5,48,1024]{2,1,0:T(8,128)} %dynamic-slice_bitcast_fusion.3), channel_id=1, source_target_pairs={{1,2},{2,1},{5,6},{6,5},{9,10},{10,9},{13,14},{14,13},{17,18},{18,... | collective-permute-start | bytes 2949128 | tf_op jit(solution)/shard_map/ppermute | solution.py:399
  31.0 4.9 %collective-permute-start.1 = (f32[10,1024]{1,0:T(8,128)S(1)}, f32[10,1024]{1,0:T(8,128)S(1)}, u32[]{:S(2)}, u32[]{:S(2)}) collective-permute-start(f32[10,1024]{1,0:T(8,128)S(1)} %reshape_squeeze.12), channel_id=1, source_target_pairs={{0,4},{4,8},{8,12},{1,5},{5,9},{9,13},{2,6},{6,10},{10,14},{3,7},{... | collective-permute-start | bytes 122888 | tf_op jit(solution)/shard_map/ppermute | solution.py:406
  35.9 36.6 %collective-permute-start.3 = (f32[5,16,1024]{2,1,0:T(8,128)}, f32[5,16,1024]{2,1,0:T(8,128)S(1)}, u32[]{:S(2)}, u32[]{:S(2)}) collective-permute-start(f32[5,16,1024]{2,1,0:T(8,128)} %dynamic-slice_bitcast_fusion.4), channel_id=1, source_target_pairs={{1,2},{2,1},{5,6},{6,5},{9,10},{10,9},{13,14},{14,13},{17,18},{18,... | collective-permute-start | bytes 983048 | tf_op jit(solution)/shard_map/ppermute | solution.py:399
  72.5 17.5 %collective-permute-start.8 = (f32[10,1024]{1,0:T(8,128)}, f32[10,1024]{1,0:T(8,128)S(1)}, u32[]{:S(2)}, u32[]{:S(2)}) collective-permute-start(f32[10,1024]{1,0:T(8,128)} %reshape_squeeze.15), channel_id=1, source_target_pairs={{4,0},{8,4},{12,8},{5,1},{9,5},{13,9},{6,2},{10,6},{14,10},{7,3},{... | collective-permute-start | bytes 122888 | tf_op jit(solution)/shard_map/ppermute | solution.py:407
  88.0 33.6 %collective-permute-start.5 = (f32[16,128]{1,0:T(8,128)S(1)}, f32[16,128]{1,0:T(8,128)S(1)}, u32[]{:S(2)}, u32[]{:S(2)}) collective-permute-start(f32[16,128]{1,0:T(8,128)S(1)} %get-tuple-element.10), channel_id=1, source_target_pairs={{0,16},{16,0},{1,17},{17,1},{2,18},{18,2},{3,19},{19,3},{4,20},{20... | collective-permute-start | bytes 24584 | tf_op jit(solution)/shard_map/ppermute | solution.py:362
  116.1 5.5 %copy-start.1 = (f32[16]{0:T(128)S(1)}, f32[16]{0:T(128)}, u32[]{:S(2)}) copy-start(f32[16]{0:T(128)} %get-tuple-element.20) | copy-start | bytes 196
  116.1 5.5 %copy-start.2 = (f32[16]{0:T(128)S(1)}, f32[16]{0:T(128)}, u32[]{:S(2)}) copy-start(f32[16]{0:T(128)} %get-tuple-element.15) | copy-start | bytes 196
  116.1 5.5 %copy-start.3 = (f32[16]{0:T(128)S(1)}, f32[16]{0:T(128)}, u32[]{:S(2)}) copy-start(f32[16]{0:T(128)} %get-tuple-element.16) | copy-start | bytes 196

commit v2 on v1

v2 whole, which is shorter than its diff:
```python
import functools
import math

import jax
import jax.numpy as jnp
from jax import lax
from jax.experimental import pallas as pl
from jax.experimental.pallas import tpu as pltpu
from jax.sharding import PartitionSpec as P

R_NEAR = 16
FMAX = 16

GAMMA = 1.4
KAPPA = 1.44

FIELDS = 5
PLANES = 2
LINES = FIELDS * PLANES
EIGHT = 8
LANES = 128
VMEM_LIMIT = 28 * 1024 * 1024

COL_LOG = 32
COL_GAIN = 33

ODD, OUTER, FIRST, LAST, BASE = range(5)


def plane_of(odd, q):
    return odd if q else 1 - odd


def primitives(fields):
    density, mom_ax, mom_rad, mom_az, energy = fields
    inverse = 1.0 / density
    vel_ax = mom_ax * inverse
    vel_rad = mom_rad * inverse
    vel_az = mom_az * inverse
    pressure = (GAMMA - 1.0) * (
        energy - 0.5 * (mom_ax * vel_ax + mom_rad * vel_rad + mom_az * vel_az)
    )
    return vel_ax, vel_rad, vel_az, pressure


def flux(fields, velocity, pressure, along):
    _, mom_ax, mom_rad, mom_az, energy = fields
    out = [fields[along], mom_ax * velocity, mom_rad * velocity, mom_az * velocity]
    out[along] = out[along] + pressure
    return out + [(energy + pressure) * velocity]


def flux_along(fields, along):
    velocities = primitives(fields)
    return flux(fields, velocities[along - 1], velocities[3], along)


def outer_flux(flags, outer):
    present = flags[OUTER] == 1
    outer = [jnp.where(present, outer[0], 1.0)] + [jnp.where(present, g, 0.0) for g in outer[1:]]
    return flux_along(outer, 1)


def stencil(flags, first_row, rows, dtheta, load, above, below, edge, inner, outer, store):
    strips = rows // EIGHT
    cells = load(0, 0, 0).shape[-1]
    row = lax.broadcasted_iota(jnp.int32, (EIGHT, 1), 0)
    sub = lax.broadcasted_iota(jnp.int32, (EIGHT, cells), 0)
    lane = lax.broadcasted_iota(jnp.int32, (EIGHT, LANES), 1)
    start = flags[BASE] + first_row
    axial_sign = jnp.where(flags[ODD] == 1, 0.5, -0.5)
    no_above = (flags[FIRST] == 1) & (first_row == 0)
    radius_above = jnp.where(no_above, 0.0, (start - 1).astype(jnp.float32) + 0.5)
    radius_below = (start + rows).astype(jnp.float32) + 0.5
    radii = [(start + EIGHT * t + row).astype(jnp.float32) + 0.5 for t in range(strips)]

    flux_above = []
    flux_below = []
    for q in range(PLANES):
        values = [above(f, q) for f in range(FIELDS)]
        values[0] = jnp.where(no_above, 1.0, values[0])
        flux_above.append([g * radius_above for g in flux_along(values, 2)])
        values, present = below(q)
        flux_below.append([g * (radius_below * present) for g in flux_along(values, 2)])

    def parts(t):
        axial, radial, azimuthal, source = [], [], [], []
        for q in range(PLANES):
            fields = [load(f, q, EIGHT * t) for f in range(FIELDS)]
            vel_ax, vel_rad, vel_az, pressure = primitives(fields)
            axial.append(flux(fields, vel_ax, pressure, 1))
            radial.append([g * radii[t] for g in flux(fields, vel_rad, pressure, 2)])
            azimuthal.append(flux(fields, vel_az, pressure, 3))
            source.append((pressure + fields[3] * vel_az, fields[2] * vel_az))
        return axial, radial, azimuthal, source

    last = None
    current = parts(0)
    for t in range(strips):
        following = parts(t + 1) if t + 1 < strips else None
        axial, radial, azimuthal, source = current
        half_inv = 0.5 / radii[t]
        inner_flux = flux_along([inner(f, EIGHT * t) for f in range(FIELDS)], 1)
        beside = [[a - b for a, b in zip(inner_flux, axial[1])], axial[0]]
        if outer is not None:
            far = outer_flux(flags, [outer(f, EIGHT * t) for f in range(FIELDS)])
            beside[1] = [a - b for a, b in zip(axial[0], far)]
        for q in range(PLANES):
            sides = []
            for side in range(2):
                at = [side * LINES + f * PLANES + q for f in range(FIELDS)]
                sides.append(flux_along([edge(c, EIGHT * t) for c in at], 3))
            for f in range(FIELDS):
                here = radial[q][f]
                before = flux_above[q][f] if last is None else pltpu.roll(last[1][q][f], 1, 0)
                after = (
                    flux_below[q][f]
                    if following is None
                    else pltpu.roll(following[1][q][f], EIGHT - 1, 0)
                )
                up = jnp.where(sub == 0, before, pltpu.roll(here, 1, 0))
                down = jnp.where(sub == EIGHT - 1, after, pltpu.roll(here, EIGHT - 1, 0))
                round_ = azimuthal[q][f]
                left = pltpu.roll(round_, 1, 1)
                left = jnp.concatenate(
                    [jnp.where(lane == 0, sides[0][f], left[:, :LANES]), left[:, LANES:]], axis=1
                )
                right = pltpu.roll(round_, cells - 1, 1)
                end = cells - LANES
                right = jnp.concatenate(
                    [right[:, :end], jnp.where(lane == LANES - 1, sides[1][f], right[:, end:])],
                    axis=1,
                )
                total = (up - down) + (left - right) * (1.0 / dtheta)
                if f == 2:
                    total = total + 2.0 * source[q][0]
                if f == 3:
                    total = total - 2.0 * source[q][1]
                store(f, q, EIGHT * t, total * half_inv + axial_sign * beside[q][f])
        last, current = current, following


def bulk_kernel(dtheta, rows, first, total_rows, fused, part, flags, state, before, after, low, high, inner, edge, *rest):
    rest = list(rest)
    outer = rest.pop(0) if fused else None
    token, held = rest.pop(0), rest.pop(0)
    hbm = rest.pop(0)
    out = rest.pop(0)
    odd = flags[ODD]
    step = pl.program_id(0)
    if part is not None:
        sent, sem = rest
        copy = pltpu.make_async_copy(hbm.at[:, lax.axis_index("ax") % 2, part[0] : part[1], :], sent, sem)
        pl.when(step == 0)(copy.start)
    first_row = first + step * rows
    at_end = first_row + rows == total_rows
    present = jnp.logical_not((flags[LAST] == 1) & at_end)

    def load(f, q, r):
        return state[f, plane_of(odd, q), r : r + EIGHT, :]

    def above(f, q):
        return before[f, plane_of(odd, q), EIGHT - 1 : EIGHT, :]

    def below(q):
        rows_ = []
        for f in range(FIELDS):
            k = f * PLANES + q
            value = jnp.where(at_end, high[k : k + 1, :], after[f, plane_of(odd, q), 0:1, :])
            rows_.append(jnp.where(present, value, 1.0))
        return rows_, jnp.where(present, 1.0, 0.0)

    def store(f, q, r, value):
        out[f, plane_of(odd, q), r : r + EIGHT, :] = value

    stencil(
        flags,
        first_row,
        rows,
        dtheta,
        load,
        above,
        below,
        lambda c, r: edge[r : r + EIGHT, c : c + 1],
        lambda f, r: inner[f, r : r + EIGHT, :],
        None if outer is None else lambda f, r: outer[f, r : r + EIGHT, :],
        store,
    )
    if part is not None:
        pl.when(step == pl.num_programs(0) - 1)(copy.wait)


def near_kernel(
    dtheta, total_rows, flags, state, after, low, high, inner, outer, edge, factor, table, token, rhs, local, carry
):
    cells = state.shape[-1]
    odd = flags[ODD]
    at_end = total_rows == R_NEAR
    present = jnp.logical_not((flags[LAST] == 1) & at_end)

    def below(q):
        rows_ = []
        for f in range(FIELDS):
            k = f * PLANES + q
            value = high[k : k + 1, :] if at_end else after[f, plane_of(odd, q), 0:1, :]
            rows_.append(jnp.where(present, value, 1.0))
        return rows_, jnp.where(present, 1.0, 0.0)

    def store(f, q, r, value):
        rhs[f * PLANES + q, r : r + EIGHT, :] = value

    stencil(
        flags,
        0,
        R_NEAR,
        dtheta,
        lambda f, q, r: state[f, plane_of(odd, q), r : r + EIGHT, :],
        lambda f, q: low[f * PLANES + q : f * PLANES + q + 1, :],
        below,
        lambda c, r: edge[r : r + EIGHT, c : c + 1],
        lambda f, r: inner[f, r : r + EIGHT, :],
        lambda f, r: outer[f, r : r + EIGHT, :],
        store,
    )

    pieces = cells // LANES
    steps = LANES.bit_length() - 1
    lane = lax.broadcasted_iota(jnp.int32, (R_NEAR, LANES), 1)
    width = factor[...]
    ahead_coef = []
    behind_coef = []
    for k in range(steps):
        coef = jnp.broadcast_to(table[:, k : k + 1], (R_NEAR, LANES))
        ahead_coef.append(jnp.where(lane >= (1 << k), coef, 0.0))
        behind_coef.append(jnp.where(lane < LANES - (1 << k), coef, 0.0))
    log_ratio = table[:, COL_LOG : COL_LOG + 1]
    block = jnp.floor((lane.astype(jnp.float32) + 0.5) / width)
    ahead_entry = jnp.exp(log_ratio * (block + 1.0))
    behind_entry = jnp.exp(log_ratio * (LANES / width - block))
    across = jnp.exp(log_ratio * (LANES / width))

    def line(k, ends):
        ahead = []
        behind = []
        means = []
        for b in range(pieces):
            mean = rhs[k, :, b * LANES : (b + 1) * LANES]
            for level in range(FMAX.bit_length() - 1):
                size = 1 << level
                partner = jnp.where(
                    (lane & size) == 0, pltpu.roll(mean, LANES - size, 1), pltpu.roll(mean, size, 1)
                )
                mean = jnp.where(width > size, 0.5 * (mean + partner), mean)
            up = mean
            down = mean
            for step in range(steps):
                up = up + ahead_coef[step] * pltpu.roll(up, 1 << step, 1)
                down = down + behind_coef[step] * pltpu.roll(down, LANES - (1 << step), 1)
            means.append(mean)
            ahead.append(up)
            behind.append(down)
        enter = jnp.zeros((R_NEAR, LANES), jnp.float32)
        for b in range(pieces):
            leave = jnp.broadcast_to(ahead[b][:, LANES - 1 : LANES], (R_NEAR, LANES))
            ahead[b] = ahead[b] + ahead_entry * enter
            enter = leave + across * enter
        ends = jnp.where(lane == k, enter, ends)
        enter = jnp.zeros((R_NEAR, LANES), jnp.float32)
        for b in reversed(range(pieces)):
            leave = jnp.broadcast_to(behind[b][:, 0:1], (R_NEAR, LANES))
            behind[b] = behind[b] + behind_entry * enter
            enter = leave + across * enter
        for b in range(pieces):
            local[k, :, b * LANES : (b + 1) * LANES] = ahead[b] + behind[b] - means[b]
        return jnp.where(lane == k + LINES, enter, ends)

    carry[...] = lax.fori_loop(
        0, LINES, line, jnp.zeros((R_NEAR, LANES), jnp.float32)
    )


def finish_kernel(flags, factor, rhs, local, carry, table, held, out):
    cells = out.shape[-1]
    lane = lax.broadcasted_iota(jnp.int32, (R_NEAR, cells), 1).astype(jnp.float32)
    width = factor[:, 0:1]
    block = jnp.floor((lane + 0.5) / width)
    count = cells / width
    log_ratio = table[:, COL_LOG : COL_LOG + 1]
    gain = table[:, COL_GAIN : COL_GAIN + 1]
    from_left = jnp.exp(log_ratio * (block + 1.0))
    from_right = jnp.exp(log_ratio * (count - block))
    near = flags[FIRST] == 1
    for f in range(FIELDS):
        for q in range(PLANES):
            k = f * PLANES + q
            j = k + LINES
            smooth = gain * (
                local[k] + from_left * carry[:, k : k + 1] + from_right * carry[:, j : j + 1]
            )
            out[f, plane_of(flags[ODD], q)] = jnp.where(near, smooth, rhs[k])


def outer_kernel(flags, outer, held, out):
    sign = jnp.where(flags[ODD] == 1, -0.5, 0.5)
    for r in range(0, outer.shape[1], EIGHT):
        values = outer_flux(flags, [outer[f, r : r + EIGHT, :] for f in range(FIELDS)])
        for f in range(FIELDS):
            out[f, 0, r : r + EIGHT, :] = held[f, 0, r : r + EIGHT, :] + sign * values[f]


def pack_edges_kernel(count, state, part, low, high, edge, left, right, top, bottom, sems):
    _, _, rows, cells = state.shape
    odd = lax.axis_index("ax") % 2
    copies = [
        pltpu.make_async_copy(state.at[:, odd, 0:count, :], part, sems.at[0]),
        pltpu.make_async_copy(state.at[:, :, :, cells - LANES : cells], left, sems.at[1]),
        pltpu.make_async_copy(state.at[:, :, :, 0:LANES], right, sems.at[2]),
        pltpu.make_async_copy(state.at[:, :, rows - EIGHT : rows, :], top, sems.at[3]),
        pltpu.make_async_copy(state.at[:, :, 0:EIGHT, :], bottom, sems.at[4]),
    ]
    for copy in copies:
        copy.start()
    for copy in copies[1:]:
        copy.wait()
    lane = lax.broadcasted_iota(jnp.int32, (rows, LANES), 1)
    columns = jnp.ones((rows, LANES), jnp.float32)
    for f in range(FIELDS):
        for q in range(PLANES):
            k = f * PLANES + q
            p = plane_of(odd, q)
            low[k : k + 1, :] = top[f, p, EIGHT - 1 : EIGHT, :]
            high[k : k + 1, :] = bottom[f, p, 0:1, :]
            columns = jnp.where(lane == k, left[f, p, :, LANES - 1 : LANES], columns)
            columns = jnp.where(lane == k + LINES, right[f, p, :, 0:1], columns)
    edge[...] = columns
    copies[0].wait()


def pack_planes_kernel(part, state, token, side, *rest):
    odd = lax.axis_index("ax") % 2
    sems = rest[-1]
    copies = [pltpu.make_async_copy(state.at[:, 1 - odd, :, :], side, sems.at[0])]
    if part is not None:
        source = state.at[:, odd, part[0] : part[1], :]
        copies.insert(0, pltpu.make_async_copy(source, rest[0], sems.at[1]))
    for copy in copies:
        copy.start()
    for copy in copies:
        copy.wait()


ANY = pl.BlockSpec(memory_space=pl.ANY)
PARAMS = pltpu.CompilerParams(vmem_limit_bytes=VMEM_LIMIT)


def whole(*shape):
    return pl.BlockSpec(shape, lambda i, s: (0,) * len(shape))


def rows_from(shape, axis, first, step):
    def place(i, s):
        row = (first // EIGHT + i * (step // EIGHT)) * EIGHT
        return tuple(row if d == axis else 0 for d in range(len(shape)))

    return pl.BlockSpec(tuple(pl.Element(n) for n in shape), place)


def in_hbm(value):
    return pltpu.with_memory_space_constraint(value, pltpu.HBM)


def cost(flops, nbytes):
    return pl.CostEstimate(flops=flops, bytes_accessed=nbytes, transcendentals=0)


def pack_edges(state, count):
    fields, planes, rows, cells = state.shape
    vmem = pl.BlockSpec(memory_space=pltpu.VMEM)
    row = jax.ShapeDtypeStruct((LINES, cells), jnp.float32)
    return pl.pallas_call(
        functools.partial(pack_edges_kernel, count),
        in_specs=[ANY],
        out_specs=[ANY, vmem, vmem, vmem],
        out_shape=[
            pltpu.VMEM((fields, count, cells), jnp.float32),
            row,
            row,
            jax.ShapeDtypeStruct((rows, LANES), jnp.float32),
        ],
        scratch_shapes=[
            pltpu.VMEM((fields, planes, rows, LANES), jnp.float32),
            pltpu.VMEM((fields, planes, rows, LANES), jnp.float32),
            pltpu.VMEM((fields, planes, EIGHT, cells), jnp.float32),
            pltpu.VMEM((fields, planes, EIGHT, cells), jnp.float32),
            pltpu.SemaphoreType.DMA((5,)),
        ],
        compiler_params=PARAMS,
        cost_estimate=cost(0, fields * count * cells * 8),
        name="pack_edges",
    )(in_hbm(state))


def pack_planes(state, part, token):
    fields, _, rows, cells = state.shape
    shapes = [pltpu.VMEM((fields, rows, cells), jnp.float32)]
    if part is not None:
        shapes.append(pltpu.VMEM((fields, part[1] - part[0], cells), jnp.float32))
    out = pl.pallas_call(
        functools.partial(pack_planes_kernel, part),
        in_specs=[ANY, ANY],
        out_specs=[ANY] * len(shapes),
        out_shape=shapes,
        scratch_shapes=[pltpu.SemaphoreType.DMA((2,))],
        compiler_params=PARAMS,
        cost_estimate=cost(0, sum(math.prod(x.shape) for x in shapes) * 8),
        name="pack_planes",
    )(in_hbm(state), token)
    return out if part is not None else (out[0], None)


def bulk(flags, state, low, high, inner, edge, dtheta, span, rows, token, held, outer=None, part=None):
    fields, planes, total_rows, cells = state.shape
    first, end = span
    fused = outer is not None
    tail = total_rows // EIGHT - 1
    eights = rows // EIGHT
    at = first // EIGHT
    row_block = (fields, planes, EIGHT, cells)
    in_specs = [
        rows_from((fields, planes, rows, cells), 2, first, rows),
        pl.BlockSpec(row_block, lambda i, s: (0, 0, at + i * eights - 1, 0)),
        pl.BlockSpec(row_block, lambda i, s: (0, 0, jnp.minimum(at + (i + 1) * eights, tail), 0)),
        whole(LINES, cells),
        whole(LINES, cells),
        rows_from((fields, rows, cells), 1, first, rows),
        rows_from((rows, LANES), 0, first, rows),
    ]
    state = in_hbm(state)
    operands = [state, state, state, low, high, inner, edge]
    if fused:
        in_specs.append(rows_from((fields, rows, cells), 1, first, rows))
        operands.append(outer)
    in_specs += [ANY, ANY, ANY]
    operands += [token, state if held is None else held, state]
    out_specs = [rows_from((fields, planes, rows, cells), 2, first, rows)]
    out_shape = [pltpu.HBM(state.shape, jnp.float32)]
    scratch = []
    if part is not None:
        out_specs.append(ANY)
        out_shape.append(pltpu.VMEM((fields, part[1] - part[0], cells), jnp.float32))
        scratch.append(pltpu.SemaphoreType.DMA)
    size = fields * planes * (end - first) * cells
    out = pl.pallas_call(
        functools.partial(bulk_kernel, dtheta, rows, first, total_rows, fused, part),
        grid_spec=pltpu.PrefetchScalarGridSpec(
            num_scalar_prefetch=1,
            grid=((end - first) // rows,),
            in_specs=in_specs,
            out_specs=out_specs,
            scratch_shapes=scratch,
        ),
        out_shape=out_shape,
        input_output_aliases={} if held is None else {len(operands) - 1: 0},
        compiler_params=PARAMS,
        cost_estimate=cost(size * 60, size * 24),
        name="bulk",
    )(flags, *operands)
    return out if part is not None else (out[0], None)


def near(flags, state, low, high, inner, outer, edge, factor, table, dtheta, token):
    fields, planes, rows, cells = state.shape
    out = jax.ShapeDtypeStruct((LINES, R_NEAR, cells), jnp.float32)
    tail = min(R_NEAR // EIGHT, rows // EIGHT - 1)
    state = in_hbm(state)
    return pl.pallas_call(
        functools.partial(near_kernel, dtheta, rows),
        grid_spec=pltpu.PrefetchScalarGridSpec(
            num_scalar_prefetch=1,
            grid=(1,),
            in_specs=[
                whole(fields, planes, R_NEAR, cells),
                pl.BlockSpec((fields, planes, EIGHT, cells), lambda i, s: (0, 0, tail, 0)),
                whole(LINES, cells),
                whole(LINES, cells),
                whole(fields, R_NEAR, cells),
                whole(fields, R_NEAR, cells),
                whole(R_NEAR, LANES),
                whole(R_NEAR, LANES),
                whole(R_NEAR, LANES),
                ANY,
            ],
            out_specs=[
                whole(LINES, R_NEAR, cells),
                whole(LINES, R_NEAR, cells),
                whole(R_NEAR, LANES),
            ],
        ),
        out_shape=[out, out, jax.ShapeDtypeStruct((R_NEAR, LANES), jnp.float32)],
        compiler_params=PARAMS,
        cost_estimate=cost(LINES * R_NEAR * cells * 200, LINES * R_NEAR * cells * 80),
        name="near",
    )(flags, state, state, low, high, inner, outer, edge, factor, table, token)


def finish(flags, factor, rhs, local, carry, table, held):
    _, _, cells = rhs.shape
    return pl.pallas_call(
        finish_kernel,
        grid_spec=pltpu.PrefetchScalarGridSpec(
            num_scalar_prefetch=1,
            grid=(1,),
            in_specs=[
                whole(R_NEAR, LANES),
                whole(LINES, R_NEAR, cells),
                whole(LINES, R_NEAR, cells),
                whole(R_NEAR, LANES),
                whole(R_NEAR, LANES),
                ANY,
            ],
            out_specs=whole(FIELDS, PLANES, R_NEAR, cells),
        ),
        out_shape=pltpu.HBM(held.shape, jnp.float32),
        input_output_aliases={6: 0},
        compiler_params=PARAMS,
        cost_estimate=cost(LINES * R_NEAR * cells * 10, LINES * R_NEAR * cells * 20),
        name="finish",
    )(flags, factor, rhs, local, carry, table, held)


def add_outer(flags, outer, span, rows, held):
    fields, _, cells = outer.shape
    first, end = span
    place = pl.BlockSpec(
        tuple(pl.Element(n) for n in (fields, 1, rows, cells)),
        lambda i, s: (0, s[ODD], (first // EIGHT + i * (rows // EIGHT)) * EIGHT, 0),
    )
    return pl.pallas_call(
        outer_kernel,
        grid_spec=pltpu.PrefetchScalarGridSpec(
            num_scalar_prefetch=1,
            grid=((end - first) // rows,),
            in_specs=[rows_from((fields, rows, cells), 1, 0, rows), place],
            out_specs=place,
        ),
        out_shape=pltpu.HBM(held.shape, jnp.float32),
        input_output_aliases={2: 0},
        compiler_params=PARAMS,
        cost_estimate=cost(outer.size * 6, outer.size * 16),
        name="add_outer",
    )(flags, outer, held)


def chunks(rows):
    size = 48 if (rows - R_NEAR) % 48 == 0 else EIGHT
    blocks = (rows - R_NEAR) // size
    cuts = sorted({1, 1 + (blocks - 1) // 2, blocks - (blocks - 1) // 4, blocks})
    ends = [R_NEAR + c * size for c in cuts]
    return size, list(zip([0] + ends[:-1], ends))


def smoothing_table(coarsen, cells, total_cells, dtheta):
    factor = coarsen.astype(jnp.float32)[:, None]
    stiffness = KAPPA / (factor * dtheta) ** 2
    inverse_half = 0.5 / stiffness
    one_minus = jnp.sqrt(inverse_half * (2.0 + inverse_half)) - inverse_half
    log_ratio = jnp.log1p(-one_minus)
    gain = (1.0 - one_minus) / (stiffness * one_minus * (2.0 - one_minus))
    closing = 1.0 / -jnp.expm1((total_cells / factor) * log_ratio)
    across = jnp.exp((cells / factor) * log_ratio)
    column = jnp.arange(LANES, dtype=jnp.int32)[None, :]
    width = jnp.left_shift(1, jnp.minimum(column, 20)).astype(jnp.float32)
    table = jnp.where(width >= factor, jnp.exp(log_ratio * (width / factor)), 0.0)
    table = jnp.where(column == COL_LOG, log_ratio, table)
    table = jnp.where(column == COL_GAIN, gain, table)
    return table, closing, across


def ring(value, axis, shift):
    size = lax.axis_size(axis)
    return lax.ppermute(value, axis, [(i, (i + shift) % size) for i in range(size)])


def body(state, coarsen):
    fields, planes, rows, cells = state.shape
    sec_count = lax.axis_size("sec")
    rad_count = lax.axis_size("rad")
    ax_count = lax.axis_size("ax")
    assert fields == FIELDS and planes == PLANES and ax_count % 2 == 0
    rad_index = lax.axis_index("rad")
    ax_index = lax.axis_index("ax")
    total_cells = cells * sec_count
    dtheta = 2.0 * math.pi / total_cells
    outer_pairs = []
    for i in range(1, ax_count - 1, 2):
        outer_pairs += [(i, i + 1), (i + 1, i)]
    inner_pairs = []
    for i in range(0, ax_count, 2):
        inner_pairs += [(i, i + 1), (i + 1, i)]
    up = [(i, i + 1) for i in range(rad_count - 1)]
    down = [(i + 1, i) for i in range(rad_count - 1)]
    flags = jnp.stack(
        [
            ax_index % 2,
            ((ax_index > 0) & (ax_index < ax_count - 1)).astype(jnp.int32),
            (rad_index == 0).astype(jnp.int32),
            (rad_index == rad_count - 1).astype(jnp.int32),
            rad_index * rows,
        ]
    ).astype(jnp.int32)
    size, spans = chunks(rows)
    count = len(spans)

    part, low, high, columns = pack_edges(state, spans[0][1])
    outer = [lax.ppermute(part, "ax", outer_pairs)]
    low = lax.ppermute(low, "rad", up)
    high = lax.ppermute(high, "rad", down)
    if sec_count == 2:
        edge = ring(columns, "sec", 1)
    else:
        from_left = jnp.arange(LANES)[None, :] < LINES
        edge = jnp.where(from_left, ring(columns, "sec", 1), ring(columns, "sec", -1))
    side, part = pack_planes(state, spans[1] if count > 1 else None, part)
    inner = lax.ppermute(side, "ax", inner_pairs)
    if count > 1:
        outer.append(lax.ppermute(part, "ax", outer_pairs))

    table, closing, across = smoothing_table(coarsen, cells, total_cells, dtheta)
    factor = jnp.broadcast_to(coarsen.astype(jnp.float32)[:, None], (R_NEAR, LANES))

    given = (flags, state, low, high, inner, edge, dtheta)
    out = None
    token = side
    if count > 1:
        out, part = bulk(*given, spans[1], size, token, None, part=spans[2] if count > 2 else None)
        if part is not None:
            outer.append(lax.ppermute(part, "ax", outer_pairs))
            token = part
    rhs, local, ends = near(
        flags, state, low, high, inner, outer[0], edge, factor, table, dtheta, token
    )
    arrived = [ends] + [ring(ends, "sec", k) for k in range(1, sec_count)] + [ends]
    from_left = jnp.arange(LANES)[None, :] < LINES
    carry = jnp.zeros_like(ends)
    for k in range(sec_count, 0, -1):
        carry = carry * across + jnp.where(from_left, arrived[k], arrived[sec_count - k])
    carry = carry * closing

    first_span = (R_NEAR, spans[0][1])
    part = spans[3] if count > 3 else None
    out, part = bulk(*given, first_span, size, ends, out, outer=outer[0], part=part)
    if part is not None:
        outer.append(lax.ppermute(part, "ax", outer_pairs))
    if count > 2:
        out, _ = bulk(*given, (spans[2][0], rows), size, ends, out)
    out = finish(flags, factor, rhs, local, carry, table, out)
    for k in range(1, count):
        out = add_outer(flags, outer[k], spans[k], size, out)
    return out


def solution(mesh):
    return jax.shard_map(
        body,
        mesh=mesh,
        in_specs=(P(None, "ax", "rad", "sec"), P()),
        out_specs=P(None, "ax", "rad", "sec"),
        check_vma=False,
    )
```

time: 128 us -> 341 us (2.66)
  Pallas kernels: 50.4 us -> 316 us
  waiting for transfers between devices: 33.3 us -> 2.6 us
  local copies, waits for them, and re-layouts: 19.5 us -> 0.17 us
    pallas_call x2 -> x6, Pallas kernels: 33.9 us -> 305 us  [the longest x1 220 us: pack_planes(): pl.pallas_call(functools.partial(pack_planes_kernel, part), in_specs=[ANY...]
    ppermute x4 -> x3, waiting for transfers between devices: 33.3 us -> 0.01 us  [body(): outer.append(lax.ppermute(part, 'ax', outer_pairs))]
    reshape x4 -> x0, local copies, waits for them, and re-layouts: 14.3 us -> none  [the longest x3 8.62 us: body(): part = lax.dynamic_slice(state, (0, odd, first, 0), (FIELDS, 1, end - fir...]
    pallas_call x3, Pallas kernels: 14.9 us -> 9.1 us  [add_outer(): pl.pallas_call(outer_kernel, grid_spec=pltpu.PrefetchScalarGridSpec(num_s...]
    ppermute x3 -> x4, starting transfers between devices: 4.54 us -> 9.7 us  [the longest x1 4.47 us: body(): outer = [lax.ppermute(part, 'ax', outer_pairs)]]
    slice x2 -> x0, local copies, waits for them, and re-layouts: 4.18 us -> none  [the longest x1 2.85 us: body(): last_column = state[:, :, :, cells - 1].reshape(lines, rows)]
    ppermute x4 -> x3, starting transfers between devices: 12.4 us -> 8.48 us  [body(): outer.append(lax.ppermute(part, 'ax', outer_pairs))]
  transfers between devices with their start and end apart: 9 -> 9, of which waited for: 1 -> 2; matrix products, arithmetic and copies ran while one was open for 13% -> 0% of each run, Pallas kernels for 37% -> 15%
where the time goes in v2:
time: 341 us; the launch traced here: 340 us
  Pallas kernels  316 us (93%)
  starting transfers between devices  20.8 us (6%)
    pallas_call x1, Pallas kernels, pack_planes(): pl.pallas_call(functools.partial(pack_planes_kernel, part), in_specs=[ANY...  220 us
    pallas_call x1, Pallas kernels, pack_edges(): pl.pallas_call(functools.partial(pack_edges_kernel, count), in_specs=[ANY...  41.5 us
    pallas_call x3, Pallas kernels, bulk(): pl.pallas_call(functools.partial(bulk_kernel, dtheta, rows, first, total_...  31.2 us
    pallas_call x1, Pallas kernels, near(): pl.pallas_call(functools.partial(near_kernel, dtheta, rows), grid_spec=pl...  12.6 us
    pallas_call x3, Pallas kernels, add_outer(): pl.pallas_call(outer_kernel, grid_spec=pltpu.PrefetchScalarGridSpec(num_s...  9.1 us
    ppermute x3, starting transfers between devices, body(): outer.append(lax.ppermute(part, 'ax', outer_pairs))  8.48 us
  transfers between devices with their start and end apart: 9, of which 2 were waited for; matrix products, arithmetic and copies ran while one was open for 0% of the time, Pallas kernels for 15%

profile of v2, /device:TPU:1, one launch (start us, length us, event | category | flops | bytes accessed | tf_op | source)
XLA Modules:
  0.0 340.1 jit_solution(5789580503984454509)
XLA Ops:
  0.0 0.0 copy-start.2
  0.0 41.5 %pack_edges.1 = (f32[5,64,1024]{2,1,0:T(8,128)}, f32[10,1024]{1,0:T(8,128)S(1)}, f32[10,1024]{1,0:T(8,128)}, f32[256,128]{1,0:T(8,128)}) custom-call(f32[5,2,256,1024]{3,2,1,0:T(8,128)} %rest_2_.3), custom_call_target="tpu_custom_call" | custom-call | bytes 2621440 | tf_op jit(solution)/shard_map/pack_edges/pallas_call | solution.py:380
  41.5 219.5 %pack_planes.1 = (f32[5,256,1024]{2,1,0:T(8,128)}, f32[5,96,1024]{2,1,0:T(8,128)}) custom-call(f32[5,2,256,1024]{3,2,1,0:T(8,128)} %rest_2_.3, f32[5,64,1024]{2,1,0:T(8,128)} %get-tuple-element.20.token), custom_call_target="tpu_custom_call" | custom-call | bytes 14417920 | tf_op jit(solution)/shard_map/pack_planes/pallas_call | solution.py:408
  261.1 0.1 collective-permute-start.2
  261.2 4.5 %collective-permute-start.4 = (f32[5,64,1024]{2,1,0:T(8,128)}, f32[5,64,1024]{2,1,0:T(8,128)S(1)}, u32[]{:S(2)}, u32[]{:S(2)}) collective-permute-start(f32[5,64,1024]{2,1,0:T(8,128)} %get-tuple-element.20.token), channel_id=1, source_target_pairs={{1,2},{2,1},{5,6},{6,5},{9,10},{10,9},{13,14},{14,13},{17,18},{18,... | collective-permute-start | bytes 3932168 | tf_op jit(solution)/shard_map/ppermute | solution.py:615
  265.6 1.9 collective-permute-start.7
  267.6 3.8 %collective-permute-start = (f32[10,1024]{1,0:T(8,128)S(1)}, f32[10,1024]{1,0:T(8,128)S(1)}, u32[]{:S(2)}, u32[]{:S(2)}) collective-permute-start(f32[10,1024]{1,0:T(8,128)S(1)} %get-tuple-element.18), channel_id=1, source_target_pairs={{0,4},{4,8},{8,12},{1,5},{5,9},{9,13},{2,6},{6,10},{10,14},{3,7},{... | collective-permute-start | bytes 122888 | tf_op jit(solution)/shard_map/ppermute | solution.py:616
  271.4 1.3 collective-permute-start.1
  272.7 0.0 copy-done.2
  272.7 0.6 broadcast_multiply_fusion
  273.4 0.0 copy-start
  273.4 0.0 collective-permute-done.low
  273.4 1.3 collective-permute-start.3
  274.7 0.1 fusion.3.table
  274.8 0.0 copy-done
  274.8 0.1 stack.35.flags
  274.9 0.0 copy-start.1
  274.9 1.7 collective-permute-done.1.high
  276.6 0.9 collective-permute-done.3.edge
  277.5 0.0 collective-permute-done.2.inner
  277.5 11.3 %bulk.3 = (f32[5,2,256,1024]{3,2,1,0:T(8,128)}, f32[5,48,1024]{2,1,0:T(8,128)S(1)}) custom-call(s32[5]{0:T(128)S(1)} %stack.35.flags, f32[5,2,256,1024]{3,2,1,0:T(8,128)} %rest_2_.3, f32[5,2,256,1024]{3,2,1,0:T(8,128)} %rest_2_.3, f32[5,2,256,1024]{3,2,1,0:T(8,128)} %rest_2_.3, f32[10,1024]{1,0:T(8,128)S(1)} %collective-permute-done.low, ...), custom_call_target="tpu_custom_call" | custom-call | flops 58982400 | bytes 23592960 | tf_op jit(solution)/shard_map/bulk/pallas_call | solution.py:453
  288.8 4.5 %collective-permute-start.6 = (f32[5,48,1024]{2,1,0:T(8,128)S(1)}, f32[5,48,1024]{2,1,0:T(8,128)S(1)}, u32[]{:S(2)}, u32[]{:S(2)}) collective-permute-start(f32[5,48,1024]{2,1,0:T(8,128)S(1)} %get-tuple-element.23.token), channel_id=1, source_target_pairs={{1,2},{2,1},{5,6},{6,5},{9,10},{10,9},{13,14},{14,13},{17,18},{18,... | collective-permute-start | bytes 2949128 | tf_op jit(solution)/shard_map/ppermute | solution.py:637
  293.3 0.0 collective-permute-done.4.outer.rest_0_
  293.3 0.0 copy-done.1
  293.3 0.1 broadcast_in_dim.51.factor
  293.4 12.6 %near.1 = (f32[10,16,1024]{2,1,0:T(8,128)S(1)}, f32[10,16,1024]{2,1,0:T(8,128)S(1)}, f32[16,128]{1,0:T(8,128)S(1)}) custom-call(s32[5]{0:T(128)S(1)} %stack.35.flags, f32[5,2,256,1024]{3,2,1,0:T(8,128)} %rest_2_.3, f32[5,2,256,1024]{3,2,1,0:T(8,128)} %rest_2_.3, f32[10,1024]{1,0:T(8,128)S(1)} %collective-permute-done.low, ...), custom_call_target="tpu_custom_call" | custom-call | flops 32768000 | bytes 13107200 | tf_op jit(solution)/shard_map/near/pallas_call | solution.py:476
  306.0 8.6 %bulk.4 = (f32[5,2,256,1024]{3,2,1,0:T(8,128)}, f32[5,48,1024]{2,1,0:T(8,128)S(1)}) custom-call(s32[5]{0:T(128)S(1)} %stack.35.flags, f32[5,2,256,1024]{3,2,1,0:T(8,128)} %rest_2_.3, f32[5,2,256,1024]{3,2,1,0:T(8,128)} %rest_2_.3, f32[5,2,256,1024]{3,2,1,0:T(8,128)} %rest_2_.3, ...), custom_call_target="tpu_custom_call", output_to_operand_aliasing={{0}: (10, {})} | custom-call | flops 29491200 | bytes 11796480 | tf_op jit(solution)/shard_map/bulk/pallas_call | solution.py:453
  314.5 2.1 collective-permute-start.5
  316.6 1.3 collective-permute-start.8
  317.9 0.0 copy-start.3
  318.0 0.0 copy-start.4
  318.0 11.3 %bulk.5.held = f32[5,2,256,1024]{3,2,1,0:T(8,128)} custom-call(s32[5]{0:T(128)S(1)} %stack.35.flags, f32[5,2,256,1024]{3,2,1,0:T(8,128)} %rest_2_.3, f32[5,2,256,1024]{3,2,1,0:T(8,128)} %rest_2_.3, f32[5,2,256,1024]{3,2,1,0:T(8,128)} %rest_2_.3, f32[10,1024]{1,0:T(8,128)S(1)} %collective-permute-done.low, ...), custom_call_target="tpu_custom_call", output_to_operand_aliasing={{}: (9, {})} | custom-call | flops 58982400 | bytes 23592960 | tf_op jit(solution)/shard_map/bulk/pallas_call | solution.py:453
  329.3 0.0 collective-permute-done.8
  329.3 0.0 copy-done.3
  329.3 0.0 copy-done.4
  329.3 0.1 add_multiply_fusion.carry
  329.4 1.6 finish.1.held
  331.0 0.0 collective-permute-done.7.outer
  331.0 3.3 add_outer.3.held
  334.3 0.0 collective-permute-done.6.outer
  334.3 2.9 add_outer.4.held
  337.2 0.0 collective-permute-done.5.outer
  337.2 2.9 add_outer.5
  (4 shorter events, 0.0 us)
Async XLA Ops:
  0.0 272.7 %copy-start.2 = (s32[16]{0:T(128)S(1)}, s32[16]{0:T(128)}, u32[]{:S(2)}) copy-start(s32[16]{0:T(128)} %param.3) | copy-start | bytes 196
  261.1 16.4 %collective-permute-start.2 = (f32[5,256,1024]{2,1,0:T(8,128)}, f32[5,256,1024]{2,1,0:T(8,128)}, u32[]{:S(2)}, u32[]{:S(2)}) collective-permute-start(f32[5,256,1024]{2,1,0:T(8,128)} %get-tuple-element.21.rest_0_), channel_id=1, source_target_pairs={{0,1},{1,0},{2,3},{3,2},{4,5},{5,4},{6,7},{7,6},{8,9},{9,8},{10,11... | collective-permute-start | bytes 15728648 | tf_op jit(solution)/shard_map/ppermute | solution.py:624
  261.2 32.1 %collective-permute-start.4 = (f32[5,64,1024]{2,1,0:T(8,128)}, f32[5,64,1024]{2,1,0:T(8,128)S(1)}, u32[]{:S(2)}, u32[]{:S(2)}) collective-permute-start(f32[5,64,1024]{2,1,0:T(8,128)} %get-tuple-element.20.token), channel_id=1, source_target_pairs={{1,2},{2,1},{5,6},{6,5},{9,10},{10,9},{13,14},{14,13},{17,18},{18,... | collective-permute-start | bytes 3932168 | tf_op jit(solution)/shard_map/ppermute | solution.py:615
  265.6 65.3 %collective-permute-start.7 = (f32[5,96,1024]{2,1,0:T(8,128)}, f32[5,96,1024]{2,1,0:T(8,128)S(1)}, u32[]{:S(2)}, u32[]{:S(2)}) collective-permute-start(f32[5,96,1024]{2,1,0:T(8,128)} %get-tuple-element.27), channel_id=1, source_target_pairs={{1,2},{2,1},{5,6},{6,5},{9,10},{10,9},{13,14},{14,13},{17,18},{18,... | collective-permute-start | bytes 5898248 | tf_op jit(solution)/shard_map/ppermute | solution.py:626
  267.6 5.8 %collective-permute-start = (f32[10,1024]{1,0:T(8,128)S(1)}, f32[10,1024]{1,0:T(8,128)S(1)}, u32[]{:S(2)}, u32[]{:S(2)}) collective-permute-start(f32[10,1024]{1,0:T(8,128)S(1)} %get-tuple-element.18), channel_id=1, source_target_pairs={{0,4},{4,8},{8,12},{1,5},{5,9},{9,13},{2,6},{6,10},{10,14},{3,7},{... | collective-permute-start | bytes 122888 | tf_op jit(solution)/shard_map/ppermute | solution.py:616
  271.4 5.2 %collective-permute-start.1 = (f32[10,1024]{1,0:T(8,128)}, f32[10,1024]{1,0:T(8,128)S(1)}, u32[]{:S(2)}, u32[]{:S(2)}) collective-permute-start(f32[10,1024]{1,0:T(8,128)} %get-tuple-element.19), channel_id=1, source_target_pairs={{4,0},{8,4},{12,8},{5,1},{9,5},{13,9},{6,2},{10,6},{14,10},{7,3},{... | collective-permute-start | bytes 122888 | tf_op jit(solution)/shard_map/ppermute | solution.py:617
  273.4 1.4 copy-start
  273.4 4.1 %collective-permute-start.3 = (f32[256,128]{1,0:T(8,128)}, f32[256,128]{1,0:T(8,128)S(1)}, u32[]{:S(2)}, u32[]{:S(2)}) collective-permute-start(f32[256,128]{1,0:T(8,128)} %get-tuple-element.22), channel_id=1, source_target_pairs={{0,16},{16,0},{1,17},{17,1},{2,18},{18,2},{3,19},{19,3},{4,20},{20... | collective-permute-start | bytes 393224 | tf_op jit(solution)/shard_map/ppermute | solution.py:581
  274.9 18.4 %copy-start.1 = (f32[16]{0:T(128)S(1)}, f32[16]{0:T(128)}, u32[]{:S(2)}) copy-start(f32[16]{0:T(128)} %copy-done) | copy-start | bytes 196
  288.8 45.5 %collective-permute-start.6 = (f32[5,48,1024]{2,1,0:T(8,128)S(1)}, f32[5,48,1024]{2,1,0:T(8,128)S(1)}, u32[]{:S(2)}, u32[]{:S(2)}) collective-permute-start(f32[5,48,1024]{2,1,0:T(8,128)S(1)} %get-tuple-element.23.token), channel_id=1, source_target_pairs={{1,2},{2,1},{5,6},{6,5},{9,10},{10,9},{13,14},{14,13},{17,18},{18,... | collective-permute-start | bytes 2949128 | tf_op jit(solution)/shard_map/ppermute | solution.py:637
  314.5 22.7 %collective-permute-start.5 = (f32[5,48,1024]{2,1,0:T(8,128)S(1)}, f32[5,48,1024]{2,1,0:T(8,128)S(1)}, u32[]{:S(2)}, u32[]{:S(2)}) collective-permute-start(f32[5,48,1024]{2,1,0:T(8,128)S(1)} %get-tuple-element.26), channel_id=1, source_target_pairs={{1,2},{2,1},{5,6},{6,5},{9,10},{10,9},{13,14},{14,13},{17,18},{18,... | collective-permute-start | bytes 2949128 | tf_op jit(solution)/shard_map/ppermute | solution.py:653
  316.6 12.6 %collective-permute-start.8 = (f32[16,128]{1,0:T(8,128)S(1)}, f32[16,128]{1,0:T(8,128)S(1)}, u32[]{:S(2)}, u32[]{:S(2)}) collective-permute-start(f32[16,128]{1,0:T(8,128)S(1)} %get-tuple-element.24.rest_1_.rest_0_), channel_id=1, source_target_pairs={{0,16},{16,0},{1,17},{17,1},{2,18},{18,2},{3,19},{19,3},{4,20},{20... | collective-permute-start | bytes 24584 | tf_op jit(solution)/shard_map/ppermute | solution.py:581
  317.9 11.3 %copy-start.3 = (f32[16]{0:T(128)S(1)}, f32[16]{0:T(128)}, u32[]{:S(2)}) copy-start(f32[16]{0:T(128)} %get-tuple-element.31) | copy-start | bytes 196
  318.0 11.3 %copy-start.4 = (f32[16]{0:T(128)S(1)}, f32[16]{0:T(128)}, u32[]{:S(2)}) copy-start(f32[16]{0:T(128)} %get-tuple-element.32) | copy-start | bytes 196

commit v3 on v2

v3 whole, which is shorter than its diff:
```python
import functools
import math

import jax
import jax.numpy as jnp
from jax import lax
from jax.experimental import pallas as pl
from jax.experimental.pallas import tpu as pltpu
from jax.sharding import PartitionSpec as P

R_NEAR = 16
FMAX = 16

GAMMA = 1.4
KAPPA = 1.44

FIELDS = 5
PLANES = 2
LINES = FIELDS * PLANES
EIGHT = 8
LANES = 128
VMEM_LIMIT = 28 * 1024 * 1024

COL_LOG = 32
COL_GAIN = 33

ODD, OUTER, FIRST, LAST, BASE = range(5)


def plane_of(odd, q):
    return odd if q else 1 - odd


def primitives(fields):
    density, mom_ax, mom_rad, mom_az, energy = fields
    inverse = 1.0 / density
    vel_ax = mom_ax * inverse
    vel_rad = mom_rad * inverse
    vel_az = mom_az * inverse
    pressure = (GAMMA - 1.0) * (
        energy - 0.5 * (mom_ax * vel_ax + mom_rad * vel_rad + mom_az * vel_az)
    )
    return vel_ax, vel_rad, vel_az, pressure


def flux(fields, velocity, pressure, along):
    _, mom_ax, mom_rad, mom_az, energy = fields
    out = [fields[along], mom_ax * velocity, mom_rad * velocity, mom_az * velocity]
    out[along] = out[along] + pressure
    return out + [(energy + pressure) * velocity]


def flux_along(fields, along):
    velocities = primitives(fields)
    return flux(fields, velocities[along - 1], velocities[3], along)


def outer_flux(flags, outer):
    present = flags[OUTER] == 1
    outer = [jnp.where(present, outer[0], 1.0)] + [jnp.where(present, g, 0.0) for g in outer[1:]]
    return flux_along(outer, 1)


def stencil(flags, first_row, rows, dtheta, load, above, below, edge, inner, outer, place, scratch):
    strips = rows // EIGHT
    pieces = scratch.shape[2]
    row = lax.broadcasted_iota(jnp.int32, (EIGHT, 1), 0)
    lane = lax.broadcasted_iota(jnp.int32, (EIGHT, LANES), 1)
    start = flags[BASE] + first_row
    axial_sign = jnp.where(flags[ODD] == 1, 0.5, -0.5)
    no_above = (flags[FIRST] == 1) & (first_row == 0)
    radius_above = jnp.where(no_above, 0.0, (start - 1).astype(jnp.float32) + 0.5)
    radius_below = (start + rows).astype(jnp.float32) + 0.5
    at = [slice(b * LANES, (b + 1) * LANES) for b in range(pieces)]

    for q in range(PLANES):
        for b in range(pieces):
            values = [above(f, q, at[b]) for f in range(FIELDS)]
            values[0] = jnp.where(no_above, 1.0, values[0])
            flux_above = flux_along(values, 2)
            values, present = below(q, at[b])
            flux_below = flux_along(values, 2)
            for f in range(FIELDS):
                scratch[q, f, b, EIGHT - 1 : EIGHT, :] = flux_above[f] * radius_above
                scratch[q, f, b, EIGHT + rows : EIGHT + rows + 1, :] = flux_below[f] * (
                    radius_below * present
                )

    def across(t, carry):
        r = pl.multiple_of(EIGHT * t, EIGHT)
        radius = (start + r + row).astype(jnp.float32) + 0.5
        half_inv = 0.5 / radius
        half_arc = half_inv * (1.0 / dtheta)
        side = []
        for q in range(PLANES):
            columns = [[(s * FIELDS + f) * PLANES + q for f in range(FIELDS)] for s in range(2)]
            side.append([flux_along([edge(c, r) for c in cs], 3) for cs in columns])

        def piece(b):
            fields = [[load(f, q, r, at[b]) for f in range(FIELDS)] for q in range(PLANES)]
            base, left, right = [], [], []
            axial = []
            for q in range(PLANES):
                vel_ax, vel_rad, vel_az, pressure = primitives(fields[q])
                axial.append(flux(fields[q], vel_ax, pressure, 1))
                radial = flux(fields[q], vel_rad, pressure, 2)
                for f in range(FIELDS):
                    scratch[q, f, b, pl.ds(r + EIGHT, EIGHT), :] = radial[f] * radius
                azimuthal = flux(fields[q], vel_az, pressure, 3)
                left.append([pltpu.roll(g, 1, 1) for g in azimuthal])
                right.append([pltpu.roll(g, LANES - 1, 1) for g in azimuthal])
                source = (pressure + fields[q][3] * vel_az) * (2.0 * half_inv)
                swirl = (fields[q][2] * vel_az) * (2.0 * half_inv)
                base.append([None, None, source, -swirl, None])
            inner_flux = flux_along([inner(f, r, at[b]) for f in range(FIELDS)], 1)
            beside = [[x - y for x, y in zip(inner_flux, axial[1])], axial[0]]
            if outer is not None:
                far = outer_flux(flags, [outer(f, r, at[b]) for f in range(FIELDS)])
                beside[1] = [x - y for x, y in zip(axial[0], far)]
            for q in range(PLANES):
                for f in range(FIELDS):
                    value = axial_sign * beside[q][f]
                    base[q][f] = value if base[q][f] is None else base[q][f] + value
            return base, left, right

        before = [side[q][0] for q in range(PLANES)]
        here = piece(0)
        for b in range(pieces):
            following = piece(b + 1) if b + 1 < pieces else None
            base, left, right = here
            for q in range(PLANES):
                for f in range(FIELDS):
                    after = side[q][1][f] if following is None else following[2][q][f]
                    ahead = jnp.where(lane == LANES - 1, after, right[q][f])
                    behind = jnp.where(lane == 0, before[q][f], left[q][f])
                    place(f, q, r)[:, at[b]] = base[q][f] + (behind - ahead) * half_arc
            before, here = left, following
        return carry

    lax.fori_loop(0, strips, across, 0)

    def along(t, carry):
        r = pl.multiple_of(EIGHT * t, EIGHT)
        radius = (start + r + row).astype(jnp.float32) + 0.5
        half_inv = 0.5 / radius
        for q in range(PLANES):
            for f in range(FIELDS):
                out = place(f, q, r)
                for b in range(pieces):
                    up = scratch[q, f, b, pl.ds(r + EIGHT - 1, EIGHT), :]
                    down = scratch[q, f, b, pl.ds(r + EIGHT + 1, EIGHT), :]
                    out[:, at[b]] = out[:, at[b]] + (up - down) * half_inv
        return carry

    lax.fori_loop(0, strips, along, 0)


def bulk_kernel(
    dtheta, rows, first, total_rows, flags, state, before, after, low, high, inner, edge, outer, token, held, out, scratch
):
    odd = flags[ODD]
    step = pl.program_id(0)
    first_row = first + step * rows
    at_end = first_row + rows == total_rows
    present = jnp.logical_not((flags[LAST] == 1) & at_end)

    def load(f, q, r, at):
        return state[f, plane_of(odd, q), pl.ds(r, EIGHT), at]

    def above(f, q, at):
        return before[f, plane_of(odd, q), EIGHT - 1 : EIGHT, at]

    def below(q, at):
        values = []
        for f in range(FIELDS):
            k = f * PLANES + q
            value = jnp.where(at_end, high[k : k + 1, at], after[f, plane_of(odd, q), 0:1, at])
            values.append(jnp.where(present, value, 1.0))
        return values, jnp.where(present, 1.0, 0.0)

    stencil(
        flags,
        first_row,
        rows,
        dtheta,
        load,
        above,
        below,
        lambda c, r: edge[pl.ds(r, EIGHT), c : c + 1],
        lambda f, r, at: inner[f, pl.ds(r, EIGHT), at],
        lambda f, r, at: outer[f, pl.ds(r, EIGHT), at],
        lambda f, q, r: out.at[f, plane_of(odd, q), pl.ds(r, EIGHT), :],
        scratch,
    )


def near_kernel(
    dtheta,
    total_rows,
    part_first,
    flags,
    state,
    after,
    low,
    high,
    inner,
    outer,
    edge,
    factor,
    table,
    token,
    hbm,
    rhs,
    local,
    carry,
    *rest,
):
    cells = state.shape[-1]
    odd = flags[ODD]
    at_end = total_rows == R_NEAR
    present = jnp.logical_not((flags[LAST] == 1) & at_end)
    part = rest[0] if len(rest) > 1 else None
    scratch = rest[-1 if part is None else -2]
    if part is not None:
        source = hbm.at[:, lax.axis_index("ax") % 2, part_first : part_first + part.shape[1], :]
        copy = pltpu.make_async_copy(source, part, rest[-1])
        copy.start()

    def below(q, at):
        values = []
        for f in range(FIELDS):
            k = f * PLANES + q
            value = high[k : k + 1, at] if at_end else after[f, plane_of(odd, q), 0:1, at]
            values.append(jnp.where(present, value, 1.0))
        return values, jnp.where(present, 1.0, 0.0)

    stencil(
        flags,
        0,
        R_NEAR,
        dtheta,
        lambda f, q, r, at: state[f, plane_of(odd, q), pl.ds(r, EIGHT), at],
        lambda f, q, at: low[f * PLANES + q : f * PLANES + q + 1, at],
        below,
        lambda c, r: edge[pl.ds(r, EIGHT), c : c + 1],
        lambda f, r, at: inner[f, pl.ds(r, EIGHT), at],
        lambda f, r, at: outer[f, pl.ds(r, EIGHT), at],
        lambda f, q, r: rhs.at[f * PLANES + q, pl.ds(r, EIGHT), :],
        scratch,
    )

    pieces = cells // LANES
    steps = LANES.bit_length() - 1
    lane = lax.broadcasted_iota(jnp.int32, (R_NEAR, LANES), 1)
    width = factor[...]
    ahead_coef = []
    behind_coef = []
    for k in range(steps):
        coef = jnp.broadcast_to(table[:, k : k + 1], (R_NEAR, LANES))
        ahead_coef.append(jnp.where(lane >= (1 << k), coef, 0.0))
        behind_coef.append(jnp.where(lane < LANES - (1 << k), coef, 0.0))
    log_ratio = table[:, COL_LOG : COL_LOG + 1]
    block = jnp.floor((lane.astype(jnp.float32) + 0.5) / width)
    ahead_entry = jnp.exp(log_ratio * (block + 1.0))
    behind_entry = jnp.exp(log_ratio * (LANES / width - block))
    across = jnp.exp(log_ratio * (LANES / width))

    def line(k, ends):
        ahead = []
        behind = []
        means = []
        for b in range(pieces):
            mean = rhs[k, :, b * LANES : (b + 1) * LANES]
            for level in range(FMAX.bit_length() - 1):
                size = 1 << level
                partner = jnp.where(
                    (lane & size) == 0, pltpu.roll(mean, LANES - size, 1), pltpu.roll(mean, size, 1)
                )
                mean = jnp.where(width > size, 0.5 * (mean + partner), mean)
            up = mean
            down = mean
            for step in range(steps):
                up = up + ahead_coef[step] * pltpu.roll(up, 1 << step, 1)
                down = down + behind_coef[step] * pltpu.roll(down, LANES - (1 << step), 1)
            means.append(mean)
            ahead.append(up)
            behind.append(down)
        enter = jnp.zeros((R_NEAR, LANES), jnp.float32)
        for b in range(pieces):
            leave = jnp.broadcast_to(ahead[b][:, LANES - 1 : LANES], (R_NEAR, LANES))
            ahead[b] = ahead[b] + ahead_entry * enter
            enter = leave + across * enter
        ends = jnp.where(lane == k, enter, ends)
        enter = jnp.zeros((R_NEAR, LANES), jnp.float32)
        for b in reversed(range(pieces)):
            leave = jnp.broadcast_to(behind[b][:, 0:1], (R_NEAR, LANES))
            behind[b] = behind[b] + behind_entry * enter
            enter = leave + across * enter
        for b in range(pieces):
            local[k, :, b * LANES : (b + 1) * LANES] = ahead[b] + behind[b] - means[b]
        return jnp.where(lane == k + LINES, enter, ends)

    carry[...] = lax.fori_loop(
        0, LINES, line, jnp.zeros((R_NEAR, LANES), jnp.float32)
    )
    if part is not None:
        copy.wait()


def finish_kernel(flags, factor, rhs, local, carry, table, held, out):
    cells = out.shape[-1]
    lane = lax.broadcasted_iota(jnp.int32, (R_NEAR, cells), 1).astype(jnp.float32)
    width = factor[:, 0:1]
    block = jnp.floor((lane + 0.5) / width)
    count = cells / width
    log_ratio = table[:, COL_LOG : COL_LOG + 1]
    gain = table[:, COL_GAIN : COL_GAIN + 1]
    from_left = jnp.exp(log_ratio * (block + 1.0))
    from_right = jnp.exp(log_ratio * (count - block))
    near = flags[FIRST] == 1
    for f in range(FIELDS):
        for q in range(PLANES):
            k = f * PLANES + q
            j = k + LINES
            smooth = gain * (
                local[k] + from_left * carry[:, k : k + 1] + from_right * carry[:, j : j + 1]
            )
            out[f, plane_of(flags[ODD], q)] = jnp.where(near, smooth, rhs[k])


def pack_first_kernel(count, state, part, low, high, top, bottom, sems):
    _, _, rows, _ = state.shape
    odd = lax.axis_index("ax") % 2
    copies = [
        pltpu.make_async_copy(state.at[:, odd, 0:count, :], part, sems.at[0]),
        pltpu.make_async_copy(state.at[:, :, rows - EIGHT : rows, :], top, sems.at[1]),
        pltpu.make_async_copy(state.at[:, :, 0:EIGHT, :], bottom, sems.at[2]),
    ]
    for copy in copies:
        copy.start()
    for copy in copies[1:]:
        copy.wait()
    for f in range(FIELDS):
        for q in range(PLANES):
            k = f * PLANES + q
            p = plane_of(odd, q)
            low[k : k + 1, :] = top[f, p, EIGHT - 1 : EIGHT, :]
            high[k : k + 1, :] = bottom[f, p, 0:1, :]
    copies[0].wait()


def pack_edges_kernel(state, token, edge, side, left, right, sems):
    _, _, rows, cells = state.shape
    odd = lax.axis_index("ax") % 2
    copies = [
        pltpu.make_async_copy(state.at[:, :, :, cells - LANES : cells], left, sems.at[0]),
        pltpu.make_async_copy(state.at[:, :, :, 0:LANES], right, sems.at[1]),
        pltpu.make_async_copy(state.at[:, 1 - odd, 0:R_NEAR, :], side, sems.at[2]),
    ]
    for copy in copies:
        copy.start()
    for copy in copies[:2]:
        copy.wait()
    lane = lax.broadcasted_iota(jnp.int32, (rows, LANES), 1)
    columns = jnp.ones((rows, LANES), jnp.float32)
    for f in range(FIELDS):
        for q in range(PLANES):
            k = f * PLANES + q
            p = plane_of(odd, q)
            columns = jnp.where(lane == k, left[f, p, :, LANES - 1 : LANES], columns)
            columns = jnp.where(lane == k + LINES, right[f, p, :, 0:1], columns)
    edge[...] = columns
    copies[2].wait()


def pack_rest_kernel(parts, state, token, *rest):
    odd = lax.axis_index("ax") % 2
    sems = rest[-1]
    copies = []
    for k, (q, first, last) in enumerate(parts):
        source = state.at[:, plane_of(odd, q), first:last, :]
        copies.append(pltpu.make_async_copy(source, rest[k], sems.at[k]))
    for copy in copies:
        copy.start()
    for copy in copies:
        copy.wait()


ANY = pl.BlockSpec(memory_space=pl.ANY)
PARAMS = pltpu.CompilerParams(vmem_limit_bytes=VMEM_LIMIT)


def whole(*shape):
    return pl.BlockSpec(shape, lambda i, s: (0,) * len(shape))


def rows_from(shape, axis, first, step):
    def place(i, s):
        row = (first // EIGHT + i * (step // EIGHT)) * EIGHT
        return tuple(row if d == axis else 0 for d in range(len(shape)))

    return pl.BlockSpec(tuple(pl.Element(n) for n in shape), place)


def in_hbm(value):
    return pltpu.with_memory_space_constraint(value, pltpu.HBM)


def cost(flops, nbytes):
    return pl.CostEstimate(flops=flops, bytes_accessed=nbytes, transcendentals=0)


def pack_first(state, count):
    fields, planes, _, cells = state.shape
    vmem = pl.BlockSpec(memory_space=pltpu.VMEM)
    row = jax.ShapeDtypeStruct((LINES, cells), jnp.float32)
    rows = pltpu.VMEM((fields, planes, EIGHT, cells), jnp.float32)
    return pl.pallas_call(
        functools.partial(pack_first_kernel, count),
        in_specs=[ANY],
        out_specs=[vmem, vmem, vmem],
        out_shape=[jax.ShapeDtypeStruct((fields, count, cells), jnp.float32), row, row],
        scratch_shapes=[rows, rows, pltpu.SemaphoreType.DMA((3,))],
        compiler_params=PARAMS,
        cost_estimate=cost(0, fields * count * cells * 8),
        name="pack_first",
    )(in_hbm(state))


def pack_edges(state, token):
    fields, planes, rows, cells = state.shape
    vmem = pl.BlockSpec(memory_space=pltpu.VMEM)
    tiles = pltpu.VMEM((fields, planes, rows, LANES), jnp.float32)
    return pl.pallas_call(
        pack_edges_kernel,
        in_specs=[ANY, ANY],
        out_specs=[vmem, vmem],
        out_shape=[
            jax.ShapeDtypeStruct((rows, LANES), jnp.float32),
            jax.ShapeDtypeStruct((fields, R_NEAR, cells), jnp.float32),
        ],
        scratch_shapes=[tiles, tiles, pltpu.SemaphoreType.DMA((3,))],
        compiler_params=PARAMS,
        cost_estimate=cost(0, fields * planes * rows * LANES * 16),
        name="pack_edges",
    )(in_hbm(state), token)


def pack_rest(state, parts, token):
    fields, _, _, cells = state.shape
    shapes = [jax.ShapeDtypeStruct((fields, last - first, cells), jnp.float32) for _, first, last in parts]
    return pl.pallas_call(
        functools.partial(pack_rest_kernel, parts),
        in_specs=[ANY, ANY],
        out_specs=[pl.BlockSpec(memory_space=pltpu.VMEM)] * len(shapes),
        out_shape=shapes,
        scratch_shapes=[pltpu.SemaphoreType.DMA((len(parts),))],
        compiler_params=PARAMS,
        cost_estimate=cost(0, sum(math.prod(x.shape) for x in shapes) * 8),
        name="pack_rest",
    )(in_hbm(state), token)


def flux_scratch(rows, cells):
    return pltpu.VMEM((PLANES, FIELDS, cells // LANES, rows + 2 * EIGHT, LANES), jnp.float32)


def bulk(flags, state, low, high, inner, edge, dtheta, outer, span, first, rows, token, held):
    fields, planes, total_rows, cells = state.shape
    end = span[1]
    tail = total_rows // EIGHT - 1
    eights = rows // EIGHT
    at = first // EIGHT
    row_block = (fields, planes, EIGHT, cells)
    in_specs = [
        rows_from((fields, planes, rows, cells), 2, first, rows),
        pl.BlockSpec(row_block, lambda i, s: (0, 0, at + i * eights - 1, 0)),
        pl.BlockSpec(row_block, lambda i, s: (0, 0, jnp.minimum(at + (i + 1) * eights, tail), 0)),
        whole(LINES, cells),
        whole(LINES, cells),
        rows_from((fields, rows, cells), 1, 0, rows),
        rows_from((rows, LANES), 0, first, rows),
        rows_from((fields, rows, cells), 1, first - span[0], rows),
        ANY,
        ANY,
    ]
    state = in_hbm(state)
    operands = [state, state, state, low, high, inner, edge, outer]
    operands += [token, state if held is None else held]
    size = fields * planes * (end - first) * cells
    return pl.pallas_call(
        functools.partial(bulk_kernel, dtheta, rows, first, total_rows),
        grid_spec=pltpu.PrefetchScalarGridSpec(
            num_scalar_prefetch=1,
            grid=((end - first) // rows,),
            in_specs=in_specs,
            out_specs=rows_from((fields, planes, rows, cells), 2, first, rows),
            scratch_shapes=[flux_scratch(rows, cells)],
        ),
        out_shape=pltpu.HBM(state.shape, jnp.float32),
        input_output_aliases={} if held is None else {len(operands): 0},
        compiler_params=PARAMS,
        cost_estimate=cost(size * 60, size * 60),
        name="bulk",
    )(flags, *operands)


def near(flags, state, low, high, inner, edge, dtheta, outer, factor, table, token, part=None):
    fields, planes, rows, cells = state.shape
    out = jax.ShapeDtypeStruct((LINES, R_NEAR, cells), jnp.float32)
    tail = min(R_NEAR // EIGHT, rows // EIGHT - 1)
    state = in_hbm(state)
    out_specs = [whole(LINES, R_NEAR, cells), whole(LINES, R_NEAR, cells), whole(R_NEAR, LANES)]
    out_shape = [out, out, jax.ShapeDtypeStruct((R_NEAR, LANES), jnp.float32)]
    scratch = [flux_scratch(R_NEAR, cells)]
    if part is not None:
        out_specs.append(whole(fields, part[1] - part[0], cells))
        out_shape.append(jax.ShapeDtypeStruct((fields, part[1] - part[0], cells), jnp.float32))
        scratch.append(pltpu.SemaphoreType.DMA)
    result = pl.pallas_call(
        functools.partial(near_kernel, dtheta, rows, part[0] if part else 0),
        grid_spec=pltpu.PrefetchScalarGridSpec(
            num_scalar_prefetch=1,
            grid=(1,),
            in_specs=[
                whole(fields, planes, R_NEAR, cells),
                pl.BlockSpec((fields, planes, EIGHT, cells), lambda i, s: (0, 0, tail, 0)),
                whole(LINES, cells),
                whole(LINES, cells),
                whole(fields, R_NEAR, cells),
                whole(fields, R_NEAR, cells),
                whole(R_NEAR, LANES),
                whole(R_NEAR, LANES),
                whole(R_NEAR, LANES),
                ANY,
                ANY,
            ],
            out_specs=out_specs,
            scratch_shapes=scratch,
        ),
        out_shape=out_shape,
        compiler_params=PARAMS,
        cost_estimate=cost(LINES * R_NEAR * cells * 200, LINES * R_NEAR * cells * 250),
        name="near",
    )(flags, state, state, low, high, inner, outer, edge, factor, table, token, state)
    return result if part is not None else (*result, None)


def finish(flags, factor, rhs, local, carry, table, held):
    _, _, cells = rhs.shape
    return pl.pallas_call(
        finish_kernel,
        grid_spec=pltpu.PrefetchScalarGridSpec(
            num_scalar_prefetch=1,
            grid=(1,),
            in_specs=[
                whole(R_NEAR, LANES),
                whole(LINES, R_NEAR, cells),
                whole(LINES, R_NEAR, cells),
                whole(R_NEAR, LANES),
                whole(R_NEAR, LANES),
                ANY,
            ],
            out_specs=whole(FIELDS, PLANES, R_NEAR, cells),
        ),
        out_shape=pltpu.HBM(held.shape, jnp.float32),
        input_output_aliases={6: 0},
        compiler_params=PARAMS,
        cost_estimate=cost(LINES * R_NEAR * cells * 10, LINES * R_NEAR * cells * 20),
        name="finish",
    )(flags, factor, rhs, local, carry, table, held)


def chunks(rows):
    size = 48 if (rows - R_NEAR) % 48 == 0 else EIGHT
    blocks = (rows - R_NEAR) // size
    cuts = sorted({-(-2 * blocks // 5), -(-4 * blocks // 5), blocks})
    ends = [R_NEAR + c * size for c in cuts]
    return size, list(zip([0] + ends[:-1], ends))


def smoothing_table(coarsen, cells, total_cells, dtheta):
    factor = coarsen.astype(jnp.float32)[:, None]
    stiffness = KAPPA / (factor * dtheta) ** 2
    inverse_half = 0.5 / stiffness
    one_minus = jnp.sqrt(inverse_half * (2.0 + inverse_half)) - inverse_half
    log_ratio = jnp.log1p(-one_minus)
    gain = (1.0 - one_minus) / (stiffness * one_minus * (2.0 - one_minus))
    closing = 1.0 / -jnp.expm1((total_cells / factor) * log_ratio)
    across = jnp.exp((cells / factor) * log_ratio)
    column = jnp.arange(LANES, dtype=jnp.int32)[None, :]
    width = jnp.left_shift(1, jnp.minimum(column, 20)).astype(jnp.float32)
    table = jnp.where(width >= factor, jnp.exp(log_ratio * (width / factor)), 0.0)
    table = jnp.where(column == COL_LOG, log_ratio, table)
    table = jnp.where(column == COL_GAIN, gain, table)
    return table, closing, across


def ring(value, axis, shift):
    size = lax.axis_size(axis)
    return lax.ppermute(value, axis, [(i, (i + shift) % size) for i in range(size)])


def body(state, coarsen):
    fields, planes, rows, cells = state.shape
    sec_count = lax.axis_size("sec")
    rad_count = lax.axis_size("rad")
    ax_count = lax.axis_size("ax")
    assert fields == FIELDS and planes == PLANES and ax_count % 2 == 0
    rad_index = lax.axis_index("rad")
    ax_index = lax.axis_index("ax")
    total_cells = cells * sec_count
    dtheta = 2.0 * math.pi / total_cells
    outer_pairs = []
    for i in range(1, ax_count - 1, 2):
        outer_pairs += [(i, i + 1), (i + 1, i)]
    inner_pairs = []
    for i in range(0, ax_count, 2):
        inner_pairs += [(i, i + 1), (i + 1, i)]
    up = [(i, i + 1) for i in range(rad_count - 1)]
    down = [(i + 1, i) for i in range(rad_count - 1)]
    flags = jnp.stack(
        [
            ax_index % 2,
            ((ax_index > 0) & (ax_index < ax_count - 1)).astype(jnp.int32),
            (rad_index == 0).astype(jnp.int32),
            (rad_index == rad_count - 1).astype(jnp.int32),
            rad_index * rows,
        ]
    ).astype(jnp.int32)
    size, spans = chunks(rows)
    count = len(spans)

    part, low, high = pack_first(state, spans[0][1])
    outer = [lax.ppermute(part, "ax", outer_pairs)]
    columns, side = pack_edges(state, high)
    low = lax.ppermute(low, "rad", up)
    high = lax.ppermute(high, "rad", down)
    inner = [lax.ppermute(side, "ax", inner_pairs)]
    wanted = [(0, R_NEAR, spans[0][1])] + [(0, *span) for span in spans[1:]]
    if count > 1:
        wanted.insert(1, (1, *spans[1]))
    parts = pack_rest(state, wanted, columns)
    for k, value in enumerate(parts):
        if wanted[k][0]:
            outer.append(lax.ppermute(value, "ax", outer_pairs))
        else:
            inner.append(lax.ppermute(value, "ax", inner_pairs))
    if sec_count == 2:
        edge = ring(columns, "sec", 1)
    else:
        from_left = jnp.arange(LANES)[None, :] < LINES
        edge = jnp.where(from_left, ring(columns, "sec", 1), ring(columns, "sec", -1))

    table, closing, across = smoothing_table(coarsen, cells, total_cells, dtheta)
    factor = jnp.broadcast_to(coarsen.astype(jnp.float32)[:, None], (R_NEAR, LANES))

    given = (flags, state, low, high)
    part = spans[2] if count > 2 else None
    rhs, local, ends, part = near(
        *given, inner[0], edge, dtheta, outer[0], factor, table, parts[0], part
    )
    if part is not None:
        outer.append(lax.ppermute(part, "ax", outer_pairs))
    arrived = [ends] + [ring(ends, "sec", k) for k in range(1, sec_count)] + [ends]
    from_left = jnp.arange(LANES)[None, :] < LINES
    carry = jnp.zeros_like(ends)
    for k in range(sec_count, 0, -1):
        carry = carry * across + jnp.where(from_left, arrived[k], arrived[sec_count - k])
    carry = carry * closing

    out = None
    for k in range(count):
        first = spans[k][0] if k else R_NEAR
        if k == count - 1 and k:
            out = finish(flags, factor, rhs, local, carry, table, out)
        out = bulk(*given, inner[k + 1], edge, dtheta, outer[k], spans[k], first, size, ends, out)
    return out if count > 1 else finish(flags, factor, rhs, local, carry, table, out)


def solution(mesh):
    return jax.shard_map(
        body,
        mesh=mesh,
        in_specs=(P(None, "ax", "rad", "sec"), P()),
        out_specs=P(None, "ax", "rad", "sec"),
        check_vma=False,
    )
```

time: 341 us -> 85 us (0.25)
  Pallas kernels: 316 us -> 53.3 us
  waiting for transfers between devices: 2.6 us -> 9.12 us
    pallas_call x6 -> x4, Pallas kernels: 283 us -> 23.9 us  [the longest x1 12.6 us: near(): pl.pallas_call(functools.partial(near_kernel, dtheta, rows, part[0] if pa...]
    ppermute x1 -> x5, starting transfers between devices: 0.12 us -> 5.65 us  [the longest x1 2.85 us: body(): inner = [lax.ppermute(side, 'ax', inner_pairs)]]
    ppermute x3 -> x1, starting transfers between devices: 8.48 us -> 3.54 us  [body(): outer.append(lax.ppermute(part, 'ax', outer_pairs))]
  transfers between devices with their start and end apart: 9 -> 11, of which waited for: 2 -> 4; matrix products, arithmetic and copies ran while one was open for 0% -> 0% of each run, Pallas kernels for 15% -> 51%
where the time goes in v3:
time: 85 us; the launch traced here: 84.7 us
  Pallas kernels  53.3 us (63%)
  starting transfers between devices  20.7 us (24%)
  waiting for transfers between devices  9.12 us (11%)
  local copies, waits for them, and re-layouts  1.13 us (1%)
    pallas_call x3, Pallas kernels, bulk(): pl.pallas_call(functools.partial(bulk_kernel, dtheta, rows, first, total_...  27.8 us
    pallas_call x1, Pallas kernels, near(): pl.pallas_call(functools.partial(near_kernel, dtheta, rows, part[0] if pa...  12.6 us
    pallas_call x1, Pallas kernels, pack_rest(): pl.pallas_call(functools.partial(pack_rest_kernel, parts), in_specs=[ANY,...  5.5 us
    ppermute x1, starting transfers between devices, body(): outer = [lax.ppermute(part, 'ax', outer_pairs)]  4.51 us
    ppermute x1, waiting for transfers between devices, body(): high = lax.ppermute(high, 'rad', down)  4.25 us
    ppermute x1, starting transfers between devices, body(): outer.append(lax.ppermute(part, 'ax', outer_pairs))  3.54 us
    pallas_call x1, Pallas kernels, pack_first(): pl.pallas_call(functools.partial(pack_first_kernel, count), in_specs=[ANY...  3.19 us
    ppermute x1, starting transfers between devices, body(): low = lax.ppermute(low, 'rad', up)  3.19 us
  transfers between devices with their start and end apart: 11, of which 4 were waited for; matrix products, arithmetic and copies ran while one was open for 0% of the time, Pallas kernels for 51%

profile of v3, /device:TPU:1, one launch (start us, length us, event | category | flops | bytes accessed | tf_op | source)
XLA Modules:
  0.0 84.7 jit_solution(3573307086250854657)
XLA Ops:
  0.0 3.2 %pack_first.1 = (f32[5,112,1024]{2,1,0:T(8,128)}, f32[10,1024]{1,0:T(8,128)S(1)}, f32[10,1024]{1,0:T(8,128)S(1)}) custom-call(f32[5,2,256,1024]{3,2,1,0:T(8,128)} %after.7), custom_call_target="tpu_custom_call" | custom-call | bytes 4587520 | tf_op jit(solution)/shard_map/pack_first/pallas_call | solution.py:418
  3.2 4.5 %collective-permute-start.5 = (f32[5,112,1024]{2,1,0:T(8,128)}, f32[5,112,1024]{2,1,0:T(8,128)S(1)}, u32[]{:S(2)}, u32[]{:S(2)}) collective-permute-start(f32[5,112,1024]{2,1,0:T(8,128)} %get-tuple-element.23), channel_id=1, source_target_pairs={{1,2},{2,1},{5,6},{6,5},{9,10},{10,9},{13,14},{14,13},{17,18},{18,... | collective-permute-start | bytes 6881288 | tf_op jit(solution)/shard_map/ppermute | solution.py:635
  7.7 2.6 %pack_edges.1 = (f32[256,128]{1,0:T(8,128)S(1)}, f32[5,16,1024]{2,1,0:T(8,128)S(1)}) custom-call(f32[5,2,256,1024]{3,2,1,0:T(8,128)} %after.7, f32[10,1024]{1,0:T(8,128)S(1)} %get-tuple-element.19.token), custom_call_target="tpu_custom_call" | custom-call | bytes 5242880 | tf_op jit(solution)/shard_map/pack_edges/pallas_call | solution.py:434
  10.3 0.0 copy-start.1
  10.3 5.5 %pack_rest.1 = (f32[5,96,1024]{2,1,0:T(8,128)}, f32[5,96,1024]{2,1,0:T(8,128)}, f32[5,96,1024]{2,1,0:T(8,128)}, f32[5,48,1024]{2,1,0:T(8,128)S(1)}) custom-call(f32[5,2,256,1024]{3,2,1,0:T(8,128)} %after.7, f32[256,128]{1,0:T(8,128)S(1)} %get-tuple-element.20.token), custom_call_target="tpu_custom_call" | custom-call | bytes 13762560 | tf_op jit(solution)/shard_map/pack_rest/pallas_call | solution.py:452
  15.8 0.0 copy-start
  15.8 1.0 %copy-done = f32[5,48,1024]{2,1,0:T(8,128)} copy-done((f32[5,48,1024]{2,1,0:T(8,128)}, f32[5,48,1024]{2,1,0:T(8,128)S(1)}, u32[]{:S(2)}) %copy-start) | copy-done | bytes 983064
  16.8 0.0 collective-permute-start.10
  16.8 0.5 collective-permute-start.8
  17.3 1.9 %collective-permute-start.9 = (f32[5,96,1024]{2,1,0:T(8,128)}, f32[5,96,1024]{2,1,0:T(8,128)}, u32[]{:S(2)}, u32[]{:S(2)}) collective-permute-start(f32[5,96,1024]{2,1,0:T(8,128)} %get-tuple-element.30), channel_id=1, source_target_pairs={{1,2},{2,1},{5,6},{6,5},{9,10},{10,9},{13,14},{14,13},{17,18},{18,... | collective-permute-start | bytes 5898248 | tf_op jit(solution)/shard_map/ppermute | solution.py:646
  19.2 1.3 %collective-permute-start.1 = (f32[10,1024]{1,0:T(8,128)S(1)}, f32[10,1024]{1,0:T(8,128)S(1)}, u32[]{:S(2)}, u32[]{:S(2)}) collective-permute-start(f32[10,1024]{1,0:T(8,128)S(1)} %get-tuple-element.19.token), channel_id=1, source_target_pairs={{4,0},{8,4},{12,8},{5,1},{9,5},{13,9},{6,2},{10,6},{14,10},{7,3},{... | collective-permute-start | bytes 122888 | tf_op jit(solution)/shard_map/ppermute | solution.py:638
  20.5 4.3 %collective-permute-done.1.high = f32[10,1024]{1,0:T(8,128)S(1)} collective-permute-done((f32[10,1024]{1,0:T(8,128)S(1)}, f32[10,1024]{1,0:T(8,128)S(1)}, u32[]{:S(2)}, u32[]{:S(2)}) %collective-permute-start.1) | collective-permute-done | bytes 40992 | tf_op jit(solution)/shard_map/ppermute | solution.py:638
  24.8 3.2 %collective-permute-start = (f32[10,1024]{1,0:T(8,128)S(1)}, f32[10,1024]{1,0:T(8,128)S(1)}, u32[]{:S(2)}, u32[]{:S(2)}) collective-permute-start(f32[10,1024]{1,0:T(8,128)S(1)} %get-tuple-element.18), channel_id=1, source_target_pairs={{0,4},{4,8},{8,12},{1,5},{5,9},{9,13},{2,6},{6,10},{10,14},{3,7},{... | collective-permute-start | bytes 122888 | tf_op jit(solution)/shard_map/ppermute | solution.py:637
  28.0 0.0 copy-done.1
  28.0 1.3 %collective-permute-done.low = f32[10,1024]{1,0:T(8,128)S(1)} collective-permute-done((f32[10,1024]{1,0:T(8,128)S(1)}, f32[10,1024]{1,0:T(8,128)S(1)}, u32[]{:S(2)}, u32[]{:S(2)}) %collective-permute-start) | collective-permute-done | bytes 40992 | tf_op jit(solution)/shard_map/ppermute | solution.py:637
  29.3 1.2 %collective-permute-start.3 = (f32[256,128]{1,0:T(8,128)S(1)}, f32[256,128]{1,0:T(8,128)S(1)}, u32[]{:S(2)}, u32[]{:S(2)}) collective-permute-start(f32[256,128]{1,0:T(8,128)S(1)} %get-tuple-element.20.token), channel_id=1, source_target_pairs={{0,16},{16,0},{1,17},{17,1},{2,18},{18,2},{3,19},{19,3},{4,20},{20... | collective-permute-start | bytes 393224 | tf_op jit(solution)/shard_map/ppermute | solution.py:601
  30.6 0.1 stack.35.flags
  30.7 2.4 %collective-permute-done.3.edge = f32[256,128]{1,0:T(8,128)S(1)} collective-permute-done((f32[256,128]{1,0:T(8,128)S(1)}, f32[256,128]{1,0:T(8,128)S(1)}, u32[]{:S(2)}, u32[]{:S(2)}) %collective-permute-start.3) | collective-permute-done | bytes 131104 | tf_op jit(solution)/shard_map/ppermute | solution.py:601
  33.1 2.9 %collective-permute-start.4 = (f32[5,16,1024]{2,1,0:T(8,128)S(1)}, f32[5,16,1024]{2,1,0:T(8,128)S(1)}, u32[]{:S(2)}, u32[]{:S(2)}) collective-permute-start(f32[5,16,1024]{2,1,0:T(8,128)S(1)} %get-tuple-element.22), channel_id=1, source_target_pairs={{0,1},{1,0},{2,3},{3,2},{4,5},{5,4},{6,7},{7,6},{8,9},{9,8},{10,11... | collective-permute-start | bytes 983048 | tf_op jit(solution)/shard_map/ppermute | solution.py:639
  35.9 0.1 fusion.3.table
  36.0 1.2 %collective-permute-done.4.inner = f32[5,16,1024]{2,1,0:T(8,128)S(1)} collective-permute-done((f32[5,16,1024]{2,1,0:T(8,128)S(1)}, f32[5,16,1024]{2,1,0:T(8,128)S(1)}, u32[]{:S(2)}, u32[]{:S(2)}) %collective-permute-start.4) | collective-permute-done | bytes 327712 | tf_op jit(solution)/shard_map/ppermute | solution.py:639
  37.2 0.4 collective-permute-start.2
  37.6 0.0 collective-permute-done.5.outer
  37.6 0.1 broadcast_in_dim.51.factor
  37.6 12.6 %near.1 = (f32[10,16,1024]{2,1,0:T(8,128)S(1)}, f32[10,16,1024]{2,1,0:T(8,128)S(1)}, f32[16,128]{1,0:T(8,128)S(1)}, f32[5,48,1024]{2,1,0:T(8,128)S(1)}) custom-call(s32[5]{0:T(128)S(1)} %stack.35.flags, f32[5,2,256,1024]{3,2,1,0:T(8,128)} %after.7, f32[5,2,256,1024]{3,2,1,0:T(8,128)} %after.7, f32[10,1024]{1,0:T(8,128)S(1)} %collective-permute-done.low, ...), custom_call_target="tpu_custom_call" | custom-call | flops 32768000 | bytes 40960000 | tf_op jit(solution)/shard_map/near/pallas_call | solution.py:520
  50.3 3.5 %collective-permute-start.6 = (f32[5,48,1024]{2,1,0:T(8,128)S(1)}, f32[5,48,1024]{2,1,0:T(8,128)S(1)}, u32[]{:S(2)}, u32[]{:S(2)}) collective-permute-start(f32[5,48,1024]{2,1,0:T(8,128)S(1)} %get-tuple-element.25), channel_id=1, source_target_pairs={{1,2},{2,1},{5,6},{6,5},{9,10},{10,9},{13,14},{14,13},{17,18},{18,... | collective-permute-start | bytes 2949128 | tf_op jit(solution)/shard_map/ppermute | solution.py:664
  53.8 0.0 collective-permute-done.10.inner
  53.8 1.3 %collective-permute-start.7 = (f32[16,128]{1,0:T(8,128)S(1)}, f32[16,128]{1,0:T(8,128)S(1)}, u32[]{:S(2)}, u32[]{:S(2)}) collective-permute-start(f32[16,128]{1,0:T(8,128)S(1)} %get-tuple-element.26.token), channel_id=1, source_target_pairs={{0,16},{16,0},{1,17},{17,1},{2,18},{18,2},{3,19},{19,3},{4,20},{20... | collective-permute-start | bytes 24584 | tf_op jit(solution)/shard_map/ppermute | solution.py:601
  55.1 10.4 %bulk.3.held = f32[5,2,256,1024]{3,2,1,0:T(8,128)} custom-call(s32[5]{0:T(128)S(1)} %stack.35.flags, f32[5,2,256,1024]{3,2,1,0:T(8,128)} %after.7, f32[5,2,256,1024]{3,2,1,0:T(8,128)} %after.7, f32[5,2,256,1024]{3,2,1,0:T(8,128)} %after.7, f32[10,1024]{1,0:T(8,128)S(1)} %collective-permute-done.low, f32[10,1024]{1,0:T(8,128)S(1)} %collective-permute-done.1.high, ...), custom_call_target="tpu_custom_call" | custom-call | flops 58982400 | bytes 58982400 | tf_op jit(solution)/shard_map/bulk/pallas_call | solution.py:491
  65.5 0.0 collective-permute-done.8.inner
  65.5 0.0 collective-permute-done.9.outer
  65.6 10.7 %bulk.4.held = f32[5,2,256,1024]{3,2,1,0:T(8,128)} custom-call(s32[5]{0:T(128)S(1)} %stack.35.flags, f32[5,2,256,1024]{3,2,1,0:T(8,128)} %after.7, f32[5,2,256,1024]{3,2,1,0:T(8,128)} %after.7, f32[5,2,256,1024]{3,2,1,0:T(8,128)} %after.7, f32[10,1024]{1,0:T(8,128)S(1)} %collective-permute-done.low, ...), custom_call_target="tpu_custom_call", output_to_operand_aliasing={{}: (10, {})} | custom-call | flops 58982400 | bytes 58982400 | tf_op jit(solution)/shard_map/bulk/pallas_call | solution.py:491
  76.3 0.0 collective-permute-done.7
  76.3 0.1 add_multiply_fusion.carry
  76.4 1.6 %finish.1.held = f32[5,2,256,1024]{3,2,1,0:T(8,128)} custom-call(s32[5]{0:T(128)S(1)} %stack.35.flags, f32[16,128]{1,0:T(8,128)S(1)} %broadcast_in_dim.51.factor, f32[10,16,1024]{2,1,0:T(8,128)S(1)} %get-tuple-element.27.rhs, f32[10,16,1024]{2,1,0:T(8,128)S(1)} %get-tuple-element.28.local, ...), custom_call_target="tpu_custom_call", output_to_operand_aliasing={{}: (6, {})} | custom-call | flops 1638400 | bytes 3276800 | tf_op jit(solution)/shard_map/finish/pallas_call | solution.py:551
  78.0 0.0 collective-permute-done.2.inner
  78.0 0.0 collective-permute-done.6.outer
  78.0 6.7 %bulk.5 = f32[5,2,256,1024]{3,2,1,0:T(8,128)} custom-call(s32[5]{0:T(128)S(1)} %stack.35.flags, f32[5,2,256,1024]{3,2,1,0:T(8,128)} %after.7, f32[5,2,256,1024]{3,2,1,0:T(8,128)} %after.7, f32[5,2,256,1024]{3,2,1,0:T(8,128)} %after.7, f32[10,1024]{1,0:T(8,128)S(1)} %collective-permute-done.low, ...), custom_call_target="tpu_custom_call", output_to_operand_aliasing={{}: (10, {})} | custom-call | flops 29491200 | bytes 29491200 | tf_op jit(solution)/shard_map/bulk/pallas_call | solution.py:491
  (5 shorter events, 0.1 us)
Async XLA Ops:
  3.2 34.4 %collective-permute-start.5 = (f32[5,112,1024]{2,1,0:T(8,128)}, f32[5,112,1024]{2,1,0:T(8,128)S(1)}, u32[]{:S(2)}, u32[]{:S(2)}) collective-permute-start(f32[5,112,1024]{2,1,0:T(8,128)} %get-tuple-element.23), channel_id=1, source_target_pairs={{1,2},{2,1},{5,6},{6,5},{9,10},{10,9},{13,14},{14,13},{17,18},{18,... | collective-permute-start | bytes 6881288 | tf_op jit(solution)/shard_map/ppermute | solution.py:635
  10.3 17.7 %copy-start.1 = (s32[16]{0:T(128)S(1)}, s32[16]{0:T(128)}, u32[]{:S(2)}) copy-start(s32[16]{0:T(128)} %param.3) | copy-start | bytes 196
  15.8 1.0 %copy-start = (f32[5,48,1024]{2,1,0:T(8,128)}, f32[5,48,1024]{2,1,0:T(8,128)S(1)}, u32[]{:S(2)}) copy-start(f32[5,48,1024]{2,1,0:T(8,128)S(1)} %get-tuple-element.21) | copy-start | bytes 2949124
  16.8 37.0 %collective-permute-start.10 = (f32[5,96,1024]{2,1,0:T(8,128)}, f32[5,96,1024]{2,1,0:T(8,128)}, u32[]{:S(2)}, u32[]{:S(2)}) collective-permute-start(f32[5,96,1024]{2,1,0:T(8,128)} %get-tuple-element.24.token), channel_id=1, source_target_pairs={{0,1},{1,0},{2,3},{3,2},{4,5},{5,4},{6,7},{7,6},{8,9},{9,8},{10,11... | collective-permute-start | bytes 5898248 | tf_op jit(solution)/shard_map/ppermute | solution.py:648
  16.8 48.8 %collective-permute-start.8 = (f32[5,96,1024]{2,1,0:T(8,128)}, f32[5,96,1024]{2,1,0:T(8,128)}, u32[]{:S(2)}, u32[]{:S(2)}) collective-permute-start(f32[5,96,1024]{2,1,0:T(8,128)} %get-tuple-element.29), channel_id=1, source_target_pairs={{0,1},{1,0},{2,3},{3,2},{4,5},{5,4},{6,7},{7,6},{8,9},{9,8},{10,11... | collective-permute-start | bytes 5898248 | tf_op jit(solution)/shard_map/ppermute | solution.py:648
  17.3 48.3 %collective-permute-start.9 = (f32[5,96,1024]{2,1,0:T(8,128)}, f32[5,96,1024]{2,1,0:T(8,128)}, u32[]{:S(2)}, u32[]{:S(2)}) collective-permute-start(f32[5,96,1024]{2,1,0:T(8,128)} %get-tuple-element.30), channel_id=1, source_target_pairs={{1,2},{2,1},{5,6},{6,5},{9,10},{10,9},{13,14},{14,13},{17,18},{18,... | collective-permute-start | bytes 5898248 | tf_op jit(solution)/shard_map/ppermute | solution.py:646
  19.2 5.6 %collective-permute-start.1 = (f32[10,1024]{1,0:T(8,128)S(1)}, f32[10,1024]{1,0:T(8,128)S(1)}, u32[]{:S(2)}, u32[]{:S(2)}) collective-permute-start(f32[10,1024]{1,0:T(8,128)S(1)} %get-tuple-element.19.token), channel_id=1, source_target_pairs={{4,0},{8,4},{12,8},{5,1},{9,5},{13,9},{6,2},{10,6},{14,10},{7,3},{... | collective-permute-start | bytes 122888 | tf_op jit(solution)/shard_map/ppermute | solution.py:638
  24.8 4.5 %collective-permute-start = (f32[10,1024]{1,0:T(8,128)S(1)}, f32[10,1024]{1,0:T(8,128)S(1)}, u32[]{:S(2)}, u32[]{:S(2)}) collective-permute-start(f32[10,1024]{1,0:T(8,128)S(1)} %get-tuple-element.18), channel_id=1, source_target_pairs={{0,4},{4,8},{8,12},{1,5},{5,9},{9,13},{2,6},{6,10},{10,14},{3,7},{... | collective-permute-start | bytes 122888 | tf_op jit(solution)/shard_map/ppermute | solution.py:637
  29.3 3.8 %collective-permute-start.3 = (f32[256,128]{1,0:T(8,128)S(1)}, f32[256,128]{1,0:T(8,128)S(1)}, u32[]{:S(2)}, u32[]{:S(2)}) collective-permute-start(f32[256,128]{1,0:T(8,128)S(1)} %get-tuple-element.20.token), channel_id=1, source_target_pairs={{0,16},{16,0},{1,17},{17,1},{2,18},{18,2},{3,19},{19,3},{4,20},{20... | collective-permute-start | bytes 393224 | tf_op jit(solution)/shard_map/ppermute | solution.py:601
  33.1 4.1 %collective-permute-start.4 = (f32[5,16,1024]{2,1,0:T(8,128)S(1)}, f32[5,16,1024]{2,1,0:T(8,128)S(1)}, u32[]{:S(2)}, u32[]{:S(2)}) collective-permute-start(f32[5,16,1024]{2,1,0:T(8,128)S(1)} %get-tuple-element.22), channel_id=1, source_target_pairs={{0,1},{1,0},{2,3},{3,2},{4,5},{5,4},{6,7},{7,6},{8,9},{9,8},{10,11... | collective-permute-start | bytes 983048 | tf_op jit(solution)/shard_map/ppermute | solution.py:639
  37.2 40.8 %collective-permute-start.2 = (f32[5,48,1024]{2,1,0:T(8,128)}, f32[5,48,1024]{2,1,0:T(8,128)S(1)}, u32[]{:S(2)}, u32[]{:S(2)}) collective-permute-start(f32[5,48,1024]{2,1,0:T(8,128)} %copy-done), channel_id=1, source_target_pairs={{0,1},{1,0},{2,3},{3,2},{4,5},{5,4},{6,7},{7,6},{8,9},{9,8},{10,11... | collective-permute-start | bytes 2949128 | tf_op jit(solution)/shard_map/ppermute | solution.py:648
  50.3 27.7 %collective-permute-start.6 = (f32[5,48,1024]{2,1,0:T(8,128)S(1)}, f32[5,48,1024]{2,1,0:T(8,128)S(1)}, u32[]{:S(2)}, u32[]{:S(2)}) collective-permute-start(f32[5,48,1024]{2,1,0:T(8,128)S(1)} %get-tuple-element.25), channel_id=1, source_target_pairs={{1,2},{2,1},{5,6},{6,5},{9,10},{10,9},{13,14},{14,13},{17,18},{18,... | collective-permute-start | bytes 2949128 | tf_op jit(solution)/shard_map/ppermute | solution.py:664
  53.8 22.5 %collective-permute-start.7 = (f32[16,128]{1,0:T(8,128)S(1)}, f32[16,128]{1,0:T(8,128)S(1)}, u32[]{:S(2)}, u32[]{:S(2)}) collective-permute-start(f32[16,128]{1,0:T(8,128)S(1)} %get-tuple-element.26.token), channel_id=1, source_target_pairs={{0,16},{16,0},{1,17},{17,1},{2,18},{18,2},{3,19},{19,3},{4,20},{20... | collective-permute-start | bytes 24584 | tf_op jit(solution)/shard_map/ppermute | solution.py:601

commit v4 on v3

--- a/solution.py
+++ b/solution.py
@@ -3,6 +3,7 @@
 
 import jax
 import jax.numpy as jnp
+import numpy as np
 from jax import lax
 from jax.experimental import pallas as pl
 from jax.experimental.pallas import tpu as pltpu
@@ -31,28 +32,34 @@
     return odd if q else 1 - odd
 
 
-def primitives(fields):
-    density, mom_ax, mom_rad, mom_az, energy = fields
-    inverse = 1.0 / density
-    vel_ax = mom_ax * inverse
-    vel_rad = mom_rad * inverse
-    vel_az = mom_az * inverse
-    pressure = (GAMMA - 1.0) * (
-        energy - 0.5 * (mom_ax * vel_ax + mom_rad * vel_rad + mom_az * vel_az)
-    )
-    return vel_ax, vel_rad, vel_az, pressure
-
-
-def flux(fields, velocity, pressure, along):
-    _, mom_ax, mom_rad, mom_az, energy = fields
-    out = [fields[along], mom_ax * velocity, mom_rad * velocity, mom_az * velocity]
-    out[along] = out[along] + pressure
-    return out + [(energy + pressure) * velocity]
+def reciprocal(x):
+    y = pl.reciprocal(x, approx=True)
+    y = y * (2.0 - x * y)
+    return y * (2.0 - x * y)
+
+
+def fluxes(fields, want):
+    density, energy = fields[0], fields[4]
+    momentum = fields[1:4]
+    inverse = reciprocal(density)
+    velocity = [m * inverse for m in momentum]
+    square = {}
+    for i in range(3):
+        for j in range(i, 3):
+            if i == j or i + 1 in want or j + 1 in want or (i, j) == (1, 2):
+                square[i, j] = square[j, i] = momentum[i] * velocity[j]
+    pressure = (GAMMA - 1.0) * (energy - 0.5 * (square[0, 0] + square[1, 1] + square[2, 2]))
+    enthalpy = energy + pressure
+    out = {}
+    for d in want:
+        k = d - 1
+        flow = [square[i, k] + pressure if i == k else square[i, k] for i in range(3)]
+        out[d] = [momentum[k]] + flow + [enthalpy * velocity[k]]
+    return out, (pressure, square[2, 2], square[1, 2])
 
 
 def flux_along(fields, along):
-    velocities = primitives(fields)
-    return flux(fields, velocities[along - 1], velocities[3], along)
+    return fluxes(fields, (along,))[0][along]
 
 
 def outer_flux(flags, outer):
@@ -89,29 +96,26 @@
     def across(t, carry):
         r = pl.multiple_of(EIGHT * t, EIGHT)
         radius = (start + r + row).astype(jnp.float32) + 0.5
-        half_inv = 0.5 / radius
-        half_arc = half_inv * (1.0 / dtheta)
-        side = []
-        for q in range(PLANES):
-            columns = [[(s * FIELDS + f) * PLANES + q for f in range(FIELDS)] for s in range(2)]
-            side.append([flux_along([edge(c, r) for c in cs], 3) for cs in columns])
+        inv_radius = 1.0 / radius
+        half_arc = inv_radius * (0.5 / dtheta)
+        beyond = [edge(r)] + [pltpu.roll(edge(r), LANES - 4 * f, 1) for f in range(1, FIELDS)]
+        beyond = flux_along(beyond, 3)
+        side = [[beyond, beyond]]
+        side.append([[pltpu.roll(g, shift, 1) for g in beyond] for shift in (LANES - 1, 1)])
 
         def piece(b):
             fields = [[load(f, q, r, at[b]) for f in range(FIELDS)] for q in range(PLANES)]
             base, left, right = [], [], []
             axial = []
             for q in range(PLANES):
-                vel_ax, vel_rad, vel_az, pressure = primitives(fields[q])
-                axial.append(flux(fields[q], vel_ax, pressure, 1))
-                radial = flux(fields[q], vel_rad, pressure, 2)
+                flow, (pressure, twist, swirl) = fluxes(fields[q], (1, 2, 3))
+                axial.append(flow[1])
                 for f in range(FIELDS):
-                    scratch[q, f, b, pl.ds(r + EIGHT, EIGHT), :] = radial[f] * radius
-                azimuthal = flux(fields[q], vel_az, pressure, 3)
-                left.append([pltpu.roll(g, 1, 1) for g in azimuthal])
-                right.append([pltpu.roll(g, LANES - 1, 1) for g in azimuthal])
-                source = (pressure + fields[q][3] * vel_az) * (2.0 * half_inv)
-                swirl = (fields[q][2] * vel_az) * (2.0 * half_inv)
-                base.append([None, None, source, -swirl, None])
+                    scratch[q, f, b, pl.ds(r + EIGHT, EIGHT), :] = flow[2][f] * radius
+                left.append([pltpu.roll(g, 1, 1) for g in flow[3]])
+                right.append([pltpu.roll(g, LANES - 1, 1) for g in flow[3]])
+                source = (pressure + twist) * inv_radius
+                base.append([None, None, source, swirl * -inv_radius, None])
             inner_flux = flux_along([inner(f, r, at[b]) for f in range(FIELDS)], 1)
             beside = [[x - y for x, y in zip(inner_flux, axial[1])], axial[0]]
             if outer is not None:
@@ -186,7 +190,7 @@
         load,
         above,
         below,
-        lambda c, r: edge[pl.ds(r, EIGHT), c : c + 1],
+        lambda r: edge[pl.ds(r, EIGHT), :],
         lambda f, r, at: inner[f, pl.ds(r, EIGHT), at],
         lambda f, r, at: outer[f, pl.ds(r, EIGHT), at],
         lambda f, q, r: out.at[f, plane_of(odd, q), pl.ds(r, EIGHT), :],
@@ -208,6 +212,7 @@
     edge,
     factor,
     table,
+    solve,
     token,
     hbm,
     rhs,
@@ -242,7 +247,7 @@
         lambda f, q, r, at: state[f, plane_of(odd, q), pl.ds(r, EIGHT), at],
         lambda f, q, at: low[f * PLANES + q : f * PLANES + q + 1, at],
         below,
-        lambda c, r: edge[pl.ds(r, EIGHT), c : c + 1],
+        lambda r: edge[pl.ds(r, EIGHT), :],
         lambda f, r, at: inner[f, pl.ds(r, EIGHT), at],
         lambda f, r, at: outer[f, pl.ds(r, EIGHT), at],
         lambda f, q, r: rhs.at[f * PLANES + q, pl.ds(r, EIGHT), :],
@@ -250,15 +255,8 @@
     )
 
     pieces = cells // LANES
-    steps = LANES.bit_length() - 1
     lane = lax.broadcasted_iota(jnp.int32, (R_NEAR, LANES), 1)
     width = factor[...]
-    ahead_coef = []
-    behind_coef = []
-    for k in range(steps):
-        coef = jnp.broadcast_to(table[:, k : k + 1], (R_NEAR, LANES))
-        ahead_coef.append(jnp.where(lane >= (1 << k), coef, 0.0))
-        behind_coef.append(jnp.where(lane < LANES - (1 << k), coef, 0.0))
     log_ratio = table[:, COL_LOG : COL_LOG + 1]
     block = jnp.floor((lane.astype(jnp.float32) + 0.5) / width)
     ahead_entry = jnp.exp(log_ratio * (block + 1.0))
@@ -266,38 +264,32 @@
     across = jnp.exp(log_ratio * (LANES / width))
 
     def line(k, ends):
-        ahead = []
-        behind = []
-        means = []
+        rows = jnp.concatenate([rhs[k, :, b * LANES : (b + 1) * LANES] for b in range(pieces)], axis=0)
+        solved = jnp.dot(
+            rows, solve[...], precision=lax.Precision.HIGHEST, preferred_element_type=jnp.float32
+        )
+        inside = []
         for b in range(pieces):
-            mean = rhs[k, :, b * LANES : (b + 1) * LANES]
-            for level in range(FMAX.bit_length() - 1):
-                size = 1 << level
-                partner = jnp.where(
-                    (lane & size) == 0, pltpu.roll(mean, LANES - size, 1), pltpu.roll(mean, size, 1)
-                )
-                mean = jnp.where(width > size, 0.5 * (mean + partner), mean)
-            up = mean
-            down = mean
-            for step in range(steps):
-                up = up + ahead_coef[step] * pltpu.roll(up, 1 << step, 1)
-                down = down + behind_coef[step] * pltpu.roll(down, LANES - (1 << step), 1)
-            means.append(mean)
-            ahead.append(up)
-            behind.append(down)
+            mine = solved[b * R_NEAR : (b + 1) * R_NEAR]
+            value = mine[:, :LANES]
+            for level in range(1, FMAX.bit_length()):
+                chosen = mine[:, level * LANES : (level + 1) * LANES]
+                value = jnp.where(width == (1 << level), chosen, value)
+            inside.append(value)
+        total = list(inside)
         enter = jnp.zeros((R_NEAR, LANES), jnp.float32)
         for b in range(pieces):
-            leave = jnp.broadcast_to(ahead[b][:, LANES - 1 : LANES], (R_NEAR, LANES))
-            ahead[b] = ahead[b] + ahead_entry * enter
+            leave = jnp.broadcast_to(inside[b][:, LANES - 1 : LANES], (R_NEAR, LANES))
+            total[b] = total[b] + ahead_entry * enter
             enter = leave + across * enter
         ends = jnp.where(lane == k, enter, ends)
         enter = jnp.zeros((R_NEAR, LANES), jnp.float32)
         for b in reversed(range(pieces)):
-            leave = jnp.broadcast_to(behind[b][:, 0:1], (R_NEAR, LANES))
-            behind[b] = behind[b] + behind_entry * enter
+            leave = jnp.broadcast_to(inside[b][:, 0:1], (R_NEAR, LANES))
+            total[b] = total[b] + behind_entry * enter
             enter = leave + across * enter
         for b in range(pieces):
-            local[k, :, b * LANES : (b + 1) * LANES] = ahead[b] + behind[b] - means[b]
+            local[k, :, b * LANES : (b + 1) * LANES] = total[b]
         return jnp.where(lane == k + LINES, enter, ends)
 
     carry[...] = lax.fori_loop(
@@ -365,15 +357,15 @@
     columns = jnp.ones((rows, LANES), jnp.float32)
     for f in range(FIELDS):
         for q in range(PLANES):
-            k = f * PLANES + q
             p = plane_of(odd, q)
-            columns = jnp.where(lane == k, left[f, p, :, LANES - 1 : LANES], columns)
-            columns = jnp.where(lane == k + LINES, right[f, p, :, 0:1], columns)
+            columns = jnp.where(lane == 4 * f + q, left[f, p, :, LANES - 1 : LANES], columns)
+            columns = jnp.where(lane == (4 * f - 1 - q) % LANES, right[f, p, :, 0:1], columns)
     edge[...] = columns
     copies[2].wait()
 
 
-def pack_rest_kernel(parts, state, token, *rest):
+def pack_rest_kernel(parts, tokens, state, *rest):
+    rest = rest[tokens:]
     odd = lax.axis_index("ax") % 2
     sems = rest[-1]
     copies = []
@@ -446,19 +438,19 @@
     )(in_hbm(state), token)
 
 
-def pack_rest(state, parts, token):
+def pack_rest(state, parts, *tokens):
     fields, _, _, cells = state.shape
     shapes = [jax.ShapeDtypeStruct((fields, last - first, cells), jnp.float32) for _, first, last in parts]
     return pl.pallas_call(
-        functools.partial(pack_rest_kernel, parts),
-        in_specs=[ANY, ANY],
+        functools.partial(pack_rest_kernel, parts, len(tokens)),
+        in_specs=[ANY] * (1 + len(tokens)),
         out_specs=[pl.BlockSpec(memory_space=pltpu.VMEM)] * len(shapes),
         out_shape=shapes,
         scratch_shapes=[pltpu.SemaphoreType.DMA((len(parts),))],
         compiler_params=PARAMS,
         cost_estimate=cost(0, sum(math.prod(x.shape) for x in shapes) * 8),
         name="pack_rest",
-    )(in_hbm(state), token)
+    )(in_hbm(state), *tokens)
 
 
 def flux_scratch(rows, cells):
@@ -505,7 +497,7 @@
     )(flags, *operands)
 
 
-def near(flags, state, low, high, inner, edge, dtheta, outer, factor, table, token, part=None):
+def near(flags, state, low, high, inner, edge, dtheta, outer, factor, table, solve, token, part=None):
     fields, planes, rows, cells = state.shape
     out = jax.ShapeDtypeStruct((LINES, R_NEAR, cells), jnp.float32)
     tail = min(R_NEAR // EIGHT, rows // EIGHT - 1)
@@ -532,6 +524,7 @@
                 whole(R_NEAR, LANES),
                 whole(R_NEAR, LANES),
                 whole(R_NEAR, LANES),
+                whole(*solve.shape),
                 ANY,
                 ANY,
             ],
@@ -542,7 +535,7 @@
         compiler_params=PARAMS,
         cost_estimate=cost(LINES * R_NEAR * cells * 200, LINES * R_NEAR * cells * 250),
         name="near",
-    )(flags, state, state, low, high, inner, outer, edge, factor, table, token, state)
+    )(flags, state, state, low, high, inner, outer, edge, factor, table, solve, token, state)
     return result if part is not None else (*result, None)
 
 
@@ -594,6 +587,17 @@
     table = jnp.where(column == COL_LOG, log_ratio, table)
     table = jnp.where(column == COL_GAIN, gain, table)
     return table, closing, across
+
+
+def piece_tables(dtheta):
+    tables = []
+    for level in range(FMAX.bit_length()):
+        width = 1 << level
+        half = 0.5 * (width * dtheta) ** 2 / KAPPA
+        ratio = 1.0 - (math.sqrt(half * (2.0 + half)) - half)
+        block = np.arange(LANES) // width
+        tables.append(ratio ** np.abs(block[:, None] - block[None, :]) / width)
+    return jnp.asarray(np.concatenate(tables, axis=1), jnp.float32)
 
 
 def ring(value, axis, shift):
@@ -640,7 +644,7 @@
     wanted = [(0, R_NEAR, spans[0][1])] + [(0, *span) for span in spans[1:]]
     if count > 1:
         wanted.insert(1, (1, *spans[1]))
-    parts = pack_rest(state, wanted, columns)
+    parts = pack_rest(state, wanted, columns, low, high)
     for k, value in enumerate(parts):
         if wanted[k][0]:
             outer.append(lax.ppermute(value, "ax", outer_pairs))
@@ -649,16 +653,17 @@
     if sec_count == 2:
         edge = ring(columns, "sec", 1)
     else:
-        from_left = jnp.arange(LANES)[None, :] < LINES
+        from_left = jnp.arange(LANES)[None, :] % 4 < 2
         edge = jnp.where(from_left, ring(columns, "sec", 1), ring(columns, "sec", -1))
 
     table, closing, across = smoothing_table(coarsen, cells, total_cells, dtheta)
     factor = jnp.broadcast_to(coarsen.astype(jnp.float32)[:, None], (R_NEAR, LANES))
 
+    solve = piece_tables(dtheta)
     given = (flags, state, low, high)
     part = spans[2] if count > 2 else None
     rhs, local, ends, part = near(
-        *given, inner[0], edge, dtheta, outer[0], factor, table, parts[0], part
+        *given, inner[0], edge, dtheta, outer[0], factor, table, solve, parts[0], part
     )
     if part is not None:
         outer.append(lax.ppermute(part, "ax", outer_pairs))

time: 85 us -> 72.8 us (0.86)
  Pallas kernels: 53.3 us -> 44.9 us
  waiting for transfers between devices: 9.12 us -> 6.23 us
  starting transfers between devices: 20.7 us -> 19.8 us
    pallas_call x1, Pallas kernels: 12.6 us -> 8.01 us  [near(): pl.pallas_call(functools.partial(near_kernel, dtheta, rows, part[0] if pa...]
    ppermute x1, waiting for transfers between devices: 4.25 us -> 0.01 us  [body(): high = lax.ppermute(high, 'rad', down)]
    pallas_call x3, Pallas kernels: 27.8 us -> 24 us  [bulk(): pl.pallas_call(functools.partial(bulk_kernel, dtheta, rows, first, total_...]
    ppermute x1, starting transfers between devices: 2.85 us -> 0.39 us  [body(): inner = [lax.ppermute(side, 'ax', inner_pairs)]]
    ppermute x2, waiting for transfers between devices: 2.41 us -> 3.88 us  [ring(): lax.ppermute(value, axis, [(i, (i + shift) % size) for i in range(size)])]
    ppermute x1, waiting for transfers between devices: 1.27 us -> 0.01 us  [body(): low = lax.ppermute(low, 'rad', up)]
    ppermute x1, waiting for transfers between devices: 0.01 us -> 1.17 us  [body(): outer = [lax.ppermute(part, 'ax', outer_pairs)]]
  transfers between devices with their start and end apart: 11 -> 11, of which waited for: 4 -> 3; matrix products, arithmetic and copies ran while one was open for 0% -> 1% of each run, Pallas kernels for 51% -> 49%
where the time goes in v4:
time: 72.8 us; the launch traced here: 72.5 us
  Pallas kernels  44.9 us (62%)
  starting transfers between devices  19.8 us (27%)
  waiting for transfers between devices  6.23 us (9%)
  local copies, waits for them, and re-layouts  1.15 us (2%)
    pallas_call x3, Pallas kernels, bulk(): pl.pallas_call(functools.partial(bulk_kernel, dtheta, rows, first, total_...  24 us
    pallas_call x1, Pallas kernels, near(): pl.pallas_call(functools.partial(near_kernel, dtheta, rows, part[0] if pa...  8.01 us
    pallas_call x1, Pallas kernels, pack_rest(): pl.pallas_call(functools.partial(pack_rest_kernel, parts, len(tokens)), i...  5.55 us
    ppermute x1, starting transfers between devices, body(): outer = [lax.ppermute(part, 'ax', outer_pairs)]  4.51 us
    ppermute x1, starting transfers between devices, body(): low = lax.ppermute(low, 'rad', up)  3.99 us
    ppermute x2, waiting for transfers between devices, ring(): lax.ppermute(value, axis, [(i, (i + shift) % size) for i in range(size)])  3.88 us
    ppermute x1, starting transfers between devices, body(): outer.append(lax.ppermute(part, 'ax', outer_pairs))  3.63 us
    pallas_call x1, Pallas kernels, pack_first(): pl.pallas_call(functools.partial(pack_first_kernel, count), in_specs=[ANY...  3.19 us
  transfers between devices with their start and end apart: 11, of which 3 were waited for; matrix products, arithmetic and copies ran while one was open for 1% of the time, Pallas kernels for 49%

profile of v4, /device:TPU:1, one launch (start us, length us, event | category | flops | bytes accessed | tf_op | source)
XLA Modules:
  0.0 72.5 jit_solution(17358479396647244019)
XLA Ops:
  0.0 3.2 %pack_first.1 = (f32[5,112,1024]{2,1,0:T(8,128)}, f32[10,1024]{1,0:T(8,128)S(1)}, f32[10,1024]{1,0:T(8,128)S(1)}) custom-call(f32[5,2,256,1024]{3,2,1,0:T(8,128)} %after.7), custom_call_target="tpu_custom_call" | custom-call | bytes 4587520 | tf_op jit(solution)/shard_map/pack_first/pallas_call | solution.py:410
  3.2 4.5 %collective-permute-start.5 = (f32[5,112,1024]{2,1,0:T(8,128)}, f32[5,112,1024]{2,1,0:T(8,128)S(1)}, u32[]{:S(2)}, u32[]{:S(2)}) collective-permute-start(f32[5,112,1024]{2,1,0:T(8,128)} %get-tuple-element.23), channel_id=1, source_target_pairs={{1,2},{2,1},{5,6},{6,5},{9,10},{10,9},{13,14},{14,13},{17,18},{18,... | collective-permute-start | bytes 6881288 | tf_op jit(solution)/shard_map/ppermute | solution.py:639
  7.7 1.3 %collective-permute-start.1 = (f32[10,1024]{1,0:T(8,128)S(1)}, f32[10,1024]{1,0:T(8,128)S(1)}, u32[]{:S(2)}, u32[]{:S(2)}) collective-permute-start(f32[10,1024]{1,0:T(8,128)S(1)} %get-tuple-element.19.token), channel_id=1, source_target_pairs={{4,0},{8,4},{12,8},{5,1},{9,5},{13,9},{6,2},{10,6},{14,10},{7,3},{... | collective-permute-start | bytes 122888 | tf_op jit(solution)/shard_map/ppermute | solution.py:642
  9.0 4.0 %collective-permute-start = (f32[10,1024]{1,0:T(8,128)S(1)}, f32[10,1024]{1,0:T(8,128)S(1)}, u32[]{:S(2)}, u32[]{:S(2)}) collective-permute-start(f32[10,1024]{1,0:T(8,128)S(1)} %get-tuple-element.18), channel_id=1, source_target_pairs={{0,4},{4,8},{8,12},{1,5},{5,9},{9,13},{2,6},{6,10},{10,14},{3,7},{... | collective-permute-start | bytes 122888 | tf_op jit(solution)/shard_map/ppermute | solution.py:641
  13.0 2.6 %pack_edges.1 = (f32[256,128]{1,0:T(8,128)S(1)}, f32[5,16,1024]{2,1,0:T(8,128)S(1)}) custom-call(f32[5,2,256,1024]{3,2,1,0:T(8,128)} %after.7, f32[10,1024]{1,0:T(8,128)S(1)} %get-tuple-element.19.token), custom_call_target="tpu_custom_call" | custom-call | bytes 5242880 | tf_op jit(solution)/shard_map/pack_edges/pallas_call | solution.py:426
  15.6 0.0 collective-permute-done.1.rest_2_.high
  15.6 0.0 collective-permute-done.rest_1_.low
  15.6 0.0 copy-start.2
  15.6 0.0 copy-start
  15.6 5.5 %pack_rest.1 = (f32[5,96,1024]{2,1,0:T(8,128)}, f32[5,96,1024]{2,1,0:T(8,128)}, f32[5,96,1024]{2,1,0:T(8,128)}, f32[5,48,1024]{2,1,0:T(8,128)S(1)}) custom-call(f32[5,2,256,1024]{3,2,1,0:T(8,128)} %after.7, f32[256,128]{1,0:T(8,128)S(1)} %get-tuple-element.20.rest_0_, f32[10,1024]{1,0:T(8,128)S(1)} %collective-permute-done.rest_1_.low, ...), custom_call_target="tpu_custom_call" | custom-call | bytes 13762560 | tf_op jit(solution)/shard_map/pack_rest/pallas_call | solution.py:444
  21.2 0.0 copy-start.1
  21.2 1.0 %copy-done.1 = f32[5,48,1024]{2,1,0:T(8,128)} copy-done((f32[5,48,1024]{2,1,0:T(8,128)}, f32[5,48,1024]{2,1,0:T(8,128)S(1)}, u32[]{:S(2)}) %copy-start.1) | copy-done | bytes 983064
  22.2 0.0 collective-permute-start.10
  22.2 0.5 collective-permute-start.8
  22.7 2.5 %collective-permute-start.9 = (f32[5,96,1024]{2,1,0:T(8,128)}, f32[5,96,1024]{2,1,0:T(8,128)}, u32[]{:S(2)}, u32[]{:S(2)}) collective-permute-start(f32[5,96,1024]{2,1,0:T(8,128)} %get-tuple-element.30), channel_id=1, source_target_pairs={{1,2},{2,1},{5,6},{6,5},{9,10},{10,9},{13,14},{14,13},{17,18},{18,... | collective-permute-start | bytes 5898248 | tf_op jit(solution)/shard_map/ppermute | solution.py:650
  25.1 1.3 %collective-permute-start.3 = (f32[256,128]{1,0:T(8,128)S(1)}, f32[256,128]{1,0:T(8,128)S(1)}, u32[]{:S(2)}, u32[]{:S(2)}) collective-permute-start(f32[256,128]{1,0:T(8,128)S(1)} %get-tuple-element.20.rest_0_), channel_id=1, source_target_pairs={{0,16},{16,0},{1,17},{17,1},{2,18},{18,2},{3,19},{19,3},{4,20},{20... | collective-permute-start | bytes 393224 | tf_op jit(solution)/shard_map/ppermute | solution.py:605
  26.5 0.0 copy-done.2
  26.6 0.1 stack.35.flags
  26.7 3.9 %collective-permute-done.3.edge = f32[256,128]{1,0:T(8,128)S(1)} collective-permute-done((f32[256,128]{1,0:T(8,128)S(1)}, f32[256,128]{1,0:T(8,128)S(1)}, u32[]{:S(2)}, u32[]{:S(2)}) %collective-permute-start.3) | collective-permute-done | bytes 131104 | tf_op jit(solution)/shard_map/ppermute | solution.py:605
  30.5 0.4 collective-permute-start.4
  30.9 0.1 fusion.3.table
  31.0 1.2 %collective-permute-done.4.inner = f32[5,16,1024]{2,1,0:T(8,128)S(1)} collective-permute-done((f32[5,16,1024]{2,1,0:T(8,128)S(1)}, f32[5,16,1024]{2,1,0:T(8,128)S(1)}, u32[]{:S(2)}, u32[]{:S(2)}) %collective-permute-start.4) | collective-permute-done | bytes 327712 | tf_op jit(solution)/shard_map/ppermute | solution.py:643
  32.2 0.4 collective-permute-start.2
  32.6 1.2 %collective-permute-done.5.outer = f32[5,112,1024]{2,1,0:T(8,128)S(1)} collective-permute-done((f32[5,112,1024]{2,1,0:T(8,128)}, f32[5,112,1024]{2,1,0:T(8,128)S(1)}, u32[]{:S(2)}, u32[]{:S(2)}) %collective-permute-start.5) | collective-permute-done | bytes 2293792 | tf_op jit(solution)/shard_map/ppermute | solution.py:639
  33.7 0.1 broadcast_in_dim.51.factor
  33.8 0.0 copy-done
  33.8 8.0 %near.1 = (f32[10,16,1024]{2,1,0:T(8,128)S(1)}, f32[10,16,1024]{2,1,0:T(8,128)S(1)}, f32[16,128]{1,0:T(8,128)S(1)}, f32[5,48,1024]{2,1,0:T(8,128)S(1)}) custom-call(s32[5]{0:T(128)S(1)} %stack.35.flags, f32[5,2,256,1024]{3,2,1,0:T(8,128)} %after.7, f32[5,2,256,1024]{3,2,1,0:T(8,128)} %after.7, f32[10,1024]{1,0:T(8,128)S(1)} %collective-permute-done.rest_1_.low, ...), custom_call_target="tpu_custom_call" | custom-call | flops 32768000 | bytes 40960000 | tf_op jit(solution)/shard_map/near/pallas_call | solution.py:512
  41.8 3.6 %collective-permute-start.6 = (f32[5,48,1024]{2,1,0:T(8,128)S(1)}, f32[5,48,1024]{2,1,0:T(8,128)S(1)}, u32[]{:S(2)}, u32[]{:S(2)}) collective-permute-start(f32[5,48,1024]{2,1,0:T(8,128)S(1)} %get-tuple-element.25), channel_id=1, source_target_pairs={{1,2},{2,1},{5,6},{6,5},{9,10},{10,9},{13,14},{14,13},{17,18},{18,... | collective-permute-start | bytes 2949128 | tf_op jit(solution)/shard_map/ppermute | solution.py:669
  45.5 0.0 collective-permute-done.10.inner
  45.5 1.3 %collective-permute-start.7 = (f32[16,128]{1,0:T(8,128)S(1)}, f32[16,128]{1,0:T(8,128)S(1)}, u32[]{:S(2)}, u32[]{:S(2)}) collective-permute-start(f32[16,128]{1,0:T(8,128)S(1)} %get-tuple-element.26.token), channel_id=1, source_target_pairs={{0,16},{16,0},{1,17},{17,1},{2,18},{18,2},{3,19},{19,3},{4,20},{20... | collective-permute-start | bytes 24584 | tf_op jit(solution)/shard_map/ppermute | solution.py:605
  46.8 8.9 %bulk.3.held = f32[5,2,256,1024]{3,2,1,0:T(8,128)} custom-call(s32[5]{0:T(128)S(1)} %stack.35.flags, f32[5,2,256,1024]{3,2,1,0:T(8,128)} %after.7, f32[5,2,256,1024]{3,2,1,0:T(8,128)} %after.7, f32[5,2,256,1024]{3,2,1,0:T(8,128)} %after.7, f32[10,1024]{1,0:T(8,128)S(1)} %collective-permute-done.rest_1_.low, ...), custom_call_target="tpu_custom_call" | custom-call | flops 58982400 | bytes 58982400 | tf_op jit(solution)/shard_map/bulk/pallas_call | solution.py:483
  55.7 0.0 collective-permute-done.8.inner
  55.7 0.0 collective-permute-done.9.outer
  55.7 9.2 %bulk.4.held = f32[5,2,256,1024]{3,2,1,0:T(8,128)} custom-call(s32[5]{0:T(128)S(1)} %stack.35.flags, f32[5,2,256,1024]{3,2,1,0:T(8,128)} %after.7, f32[5,2,256,1024]{3,2,1,0:T(8,128)} %after.7, f32[5,2,256,1024]{3,2,1,0:T(8,128)} %after.7, f32[10,1024]{1,0:T(8,128)S(1)} %collective-permute-done.rest_1_.low, ...), custom_call_target="tpu_custom_call", output_to_operand_aliasing={{}: (10, {})} | custom-call | flops 58982400 | bytes 58982400 | tf_op jit(solution)/shard_map/bulk/pallas_call | solution.py:483
  64.9 0.0 collective-permute-done.7
  64.9 0.1 add_multiply_fusion.carry
  65.0 1.6 %finish.1.held = f32[5,2,256,1024]{3,2,1,0:T(8,128)} custom-call(s32[5]{0:T(128)S(1)} %stack.35.flags, f32[16,128]{1,0:T(8,128)S(1)} %broadcast_in_dim.51.factor, f32[10,16,1024]{2,1,0:T(8,128)S(1)} %get-tuple-element.27.rhs, f32[10,16,1024]{2,1,0:T(8,128)S(1)} %get-tuple-element.28.local, ...), custom_call_target="tpu_custom_call", output_to_operand_aliasing={{}: (6, {})} | custom-call | flops 1638400 | bytes 3276800 | tf_op jit(solution)/shard_map/finish/pallas_call | solution.py:544
  66.6 0.0 collective-permute-done.2.inner
  66.6 0.0 collective-permute-done.6.outer
  66.6 5.9 %bulk.5 = f32[5,2,256,1024]{3,2,1,0:T(8,128)} custom-call(s32[5]{0:T(128)S(1)} %stack.35.flags, f32[5,2,256,1024]{3,2,1,0:T(8,128)} %after.7, f32[5,2,256,1024]{3,2,1,0:T(8,128)} %after.7, f32[5,2,256,1024]{3,2,1,0:T(8,128)} %after.7, f32[10,1024]{1,0:T(8,128)S(1)} %collective-permute-done.rest_1_.low, ...), custom_call_target="tpu_custom_call", output_to_operand_aliasing={{}: (10, {})} | custom-call | flops 29491200 | bytes 29491200 | tf_op jit(solution)/shard_map/bulk/pallas_call | solution.py:483
  (5 shorter events, 0.1 us)
Async XLA Ops:
  3.2 30.5 %collective-permute-start.5 = (f32[5,112,1024]{2,1,0:T(8,128)}, f32[5,112,1024]{2,1,0:T(8,128)S(1)}, u32[]{:S(2)}, u32[]{:S(2)}) collective-permute-start(f32[5,112,1024]{2,1,0:T(8,128)} %get-tuple-element.23), channel_id=1, source_target_pairs={{1,2},{2,1},{5,6},{6,5},{9,10},{10,9},{13,14},{14,13},{17,18},{18,... | collective-permute-start | bytes 6881288 | tf_op jit(solution)/shard_map/ppermute | solution.py:639
  7.7 7.9 %collective-permute-start.1 = (f32[10,1024]{1,0:T(8,128)S(1)}, f32[10,1024]{1,0:T(8,128)S(1)}, u32[]{:S(2)}, u32[]{:S(2)}) collective-permute-start(f32[10,1024]{1,0:T(8,128)S(1)} %get-tuple-element.19.token), channel_id=1, source_target_pairs={{4,0},{8,4},{12,8},{5,1},{9,5},{13,9},{6,2},{10,6},{14,10},{7,3},{... | collective-permute-start | bytes 122888 | tf_op jit(solution)/shard_map/ppermute | solution.py:642
  9.0 6.6 %collective-permute-start = (f32[10,1024]{1,0:T(8,128)S(1)}, f32[10,1024]{1,0:T(8,128)S(1)}, u32[]{:S(2)}, u32[]{:S(2)}) collective-permute-start(f32[10,1024]{1,0:T(8,128)S(1)} %get-tuple-element.18), channel_id=1, source_target_pairs={{0,4},{4,8},{8,12},{1,5},{5,9},{9,13},{2,6},{6,10},{10,14},{3,7},{... | collective-permute-start | bytes 122888 | tf_op jit(solution)/shard_map/ppermute | solution.py:641
  15.6 10.9 %copy-start.2 = (s32[16]{0:T(128)S(1)}, s32[16]{0:T(128)}, u32[]{:S(2)}) copy-start(s32[16]{0:T(128)} %param.4) | copy-start | bytes 196
  15.6 18.2 %copy-start = (f32[128,640]{1,0:T(8,128)S(1)}, f32[128,640]{1,0:T(8,128)}, u32[]{:S(2)}) copy-start(f32[128,640]{1,0:T(8,128)} %constant.54.clone.solve) | copy-start | bytes 983044
  21.2 1.0 %copy-start.1 = (f32[5,48,1024]{2,1,0:T(8,128)}, f32[5,48,1024]{2,1,0:T(8,128)S(1)}, u32[]{:S(2)}) copy-start(f32[5,48,1024]{2,1,0:T(8,128)S(1)} %get-tuple-element.21) | copy-start | bytes 2949124
  22.2 23.3 %collective-permute-start.10 = (f32[5,96,1024]{2,1,0:T(8,128)}, f32[5,96,1024]{2,1,0:T(8,128)}, u32[]{:S(2)}, u32[]{:S(2)}) collective-permute-start(f32[5,96,1024]{2,1,0:T(8,128)} %get-tuple-element.24.token), channel_id=1, source_target_pairs={{0,1},{1,0},{2,3},{3,2},{4,5},{5,4},{6,7},{7,6},{8,9},{9,8},{10,11... | collective-permute-start | bytes 5898248 | tf_op jit(solution)/shard_map/ppermute | solution.py:652
  22.2 33.5 %collective-permute-start.8 = (f32[5,96,1024]{2,1,0:T(8,128)}, f32[5,96,1024]{2,1,0:T(8,128)}, u32[]{:S(2)}, u32[]{:S(2)}) collective-permute-start(f32[5,96,1024]{2,1,0:T(8,128)} %get-tuple-element.29), channel_id=1, source_target_pairs={{0,1},{1,0},{2,3},{3,2},{4,5},{5,4},{6,7},{7,6},{8,9},{9,8},{10,11... | collective-permute-start | bytes 5898248 | tf_op jit(solution)/shard_map/ppermute | solution.py:652
  22.7 33.0 %collective-permute-start.9 = (f32[5,96,1024]{2,1,0:T(8,128)}, f32[5,96,1024]{2,1,0:T(8,128)}, u32[]{:S(2)}, u32[]{:S(2)}) collective-permute-start(f32[5,96,1024]{2,1,0:T(8,128)} %get-tuple-element.30), channel_id=1, source_target_pairs={{1,2},{2,1},{5,6},{6,5},{9,10},{10,9},{13,14},{14,13},{17,18},{18,... | collective-permute-start | bytes 5898248 | tf_op jit(solution)/shard_map/ppermute | solution.py:650
  25.1 5.4 %collective-permute-start.3 = (f32[256,128]{1,0:T(8,128)S(1)}, f32[256,128]{1,0:T(8,128)S(1)}, u32[]{:S(2)}, u32[]{:S(2)}) collective-permute-start(f32[256,128]{1,0:T(8,128)S(1)} %get-tuple-element.20.rest_0_), channel_id=1, source_target_pairs={{0,16},{16,0},{1,17},{17,1},{2,18},{18,2},{3,19},{19,3},{4,20},{20... | collective-permute-start | bytes 393224 | tf_op jit(solution)/shard_map/ppermute | solution.py:605
  30.5 1.7 %collective-permute-start.4 = (f32[5,16,1024]{2,1,0:T(8,128)S(1)}, f32[5,16,1024]{2,1,0:T(8,128)S(1)}, u32[]{:S(2)}, u32[]{:S(2)}) collective-permute-start(f32[5,16,1024]{2,1,0:T(8,128)S(1)} %get-tuple-element.22), channel_id=1, source_target_pairs={{0,1},{1,0},{2,3},{3,2},{4,5},{5,4},{6,7},{7,6},{8,9},{9,8},{10,11... | collective-permute-start | bytes 983048 | tf_op jit(solution)/shard_map/ppermute | solution.py:643
  32.2 34.4 %collective-permute-start.2 = (f32[5,48,1024]{2,1,0:T(8,128)}, f32[5,48,1024]{2,1,0:T(8,128)S(1)}, u32[]{:S(2)}, u32[]{:S(2)}) collective-permute-start(f32[5,48,1024]{2,1,0:T(8,128)} %copy-done.1), channel_id=1, source_target_pairs={{0,1},{1,0},{2,3},{3,2},{4,5},{5,4},{6,7},{7,6},{8,9},{9,8},{10,11... | collective-permute-start | bytes 2949128 | tf_op jit(solution)/shard_map/ppermute | solution.py:652
  41.8 24.7 %collective-permute-start.6 = (f32[5,48,1024]{2,1,0:T(8,128)S(1)}, f32[5,48,1024]{2,1,0:T(8,128)S(1)}, u32[]{:S(2)}, u32[]{:S(2)}) collective-permute-start(f32[5,48,1024]{2,1,0:T(8,128)S(1)} %get-tuple-element.25), channel_id=1, source_target_pairs={{1,2},{2,1},{5,6},{6,5},{9,10},{10,9},{13,14},{14,13},{17,18},{18,... | collective-permute-start | bytes 2949128 | tf_op jit(solution)/shard_map/ppermute | solution.py:669
  45.5 19.4 %collective-permute-start.7 = (f32[16,128]{1,0:T(8,128)S(1)}, f32[16,128]{1,0:T(8,128)S(1)}, u32[]{:S(2)}, u32[]{:S(2)}) collective-permute-start(f32[16,128]{1,0:T(8,128)S(1)} %get-tuple-element.26.token), channel_id=1, source_target_pairs={{0,16},{16,0},{1,17},{17,1},{2,18},{18,2},{3,19},{19,3},{4,20},{20... | collective-permute-start | bytes 24584 | tf_op jit(solution)/shard_map/ppermute | solution.py:605

commit v5 on v4

--- a/solution.py
+++ b/solution.py
@@ -159,9 +159,10 @@
     lax.fori_loop(0, strips, along, 0)
 
 
-def bulk_kernel(
-    dtheta, rows, first, total_rows, flags, state, before, after, low, high, inner, edge, outer, token, held, out, scratch
-):
+def bulk_kernel(dtheta, rows, first, total_rows, fused, flags, state, before, after, low, high, inner, edge, *rest):
+    rest = list(rest)
+    outer = rest.pop(0) if fused else None
+    _, _, out, scratch = rest
     odd = flags[ODD]
     step = pl.program_id(0)
     first_row = first + step * rows
@@ -192,16 +193,29 @@
         below,
         lambda r: edge[pl.ds(r, EIGHT), :],
         lambda f, r, at: inner[f, pl.ds(r, EIGHT), at],
-        lambda f, r, at: outer[f, pl.ds(r, EIGHT), at],
+        None if outer is None else lambda f, r, at: outer[f, pl.ds(r, EIGHT), at],
         lambda f, q, r: out.at[f, plane_of(odd, q), pl.ds(r, EIGHT), :],
         scratch,
     )
 
 
+def outer_kernel(flags, outer, held, out):
+    sign = jnp.where(flags[ODD] == 1, -0.5, 0.5)
+
+    def strip(t, carry):
+        r = pl.multiple_of(EIGHT * t, EIGHT)
+        at = pl.ds(r, EIGHT)
+        values = outer_flux(flags, [outer[f, at, :] for f in range(FIELDS)])
+        for f in range(FIELDS):
+            out[f, 0, at, :] = held[f, 0, at, :] + sign * values[f]
+        return carry
+
+    lax.fori_loop(0, outer.shape[1] // EIGHT, strip, 0)
+
+
 def near_kernel(
     dtheta,
     total_rows,
-    part_first,
     flags,
     state,
     after,
@@ -214,22 +228,15 @@
     table,
     solve,
     token,
-    hbm,
     rhs,
     local,
     carry,
-    *rest,
+    scratch,
 ):
     cells = state.shape[-1]
     odd = flags[ODD]
     at_end = total_rows == R_NEAR
     present = jnp.logical_not((flags[LAST] == 1) & at_end)
-    part = rest[0] if len(rest) > 1 else None
-    scratch = rest[-1 if part is None else -2]
-    if part is not None:
-        source = hbm.at[:, lax.axis_index("ax") % 2, part_first : part_first + part.shape[1], :]
-        copy = pltpu.make_async_copy(source, part, rest[-1])
-        copy.start()
 
     def below(q, at):
         values = []
@@ -295,8 +302,6 @@
     carry[...] = lax.fori_loop(
         0, LINES, line, jnp.zeros((R_NEAR, LANES), jnp.float32)
     )
-    if part is not None:
-        copy.wait()
 
 
 def finish_kernel(flags, factor, rhs, local, carry, table, held, out):
@@ -341,14 +346,17 @@
     copies[0].wait()
 
 
-def pack_edges_kernel(state, token, edge, side, left, right, sems):
+def pack_edges_kernel(spans, state, token, edge, *rest):
     _, _, rows, cells = state.shape
     odd = lax.axis_index("ax") % 2
+    left, right, sems = rest[-3:]
     copies = [
         pltpu.make_async_copy(state.at[:, :, :, cells - LANES : cells], left, sems.at[0]),
         pltpu.make_async_copy(state.at[:, :, :, 0:LANES], right, sems.at[1]),
-        pltpu.make_async_copy(state.at[:, 1 - odd, 0:R_NEAR, :], side, sems.at[2]),
     ]
+    for k, (first, last) in enumerate(spans):
+        source = state.at[:, odd, first:last, :]
+        copies.append(pltpu.make_async_copy(source, rest[k], sems.at[2 + k]))
     for copy in copies:
         copy.start()
     for copy in copies[:2]:
@@ -361,7 +369,8 @@
             columns = jnp.where(lane == 4 * f + q, left[f, p, :, LANES - 1 : LANES], columns)
             columns = jnp.where(lane == (4 * f - 1 - q) % LANES, right[f, p, :, 0:1], columns)
     edge[...] = columns
-    copies[2].wait()
+    for copy in copies[2:]:
+        copy.wait()
 
 
 def pack_rest_kernel(parts, tokens, state, *rest):
@@ -369,8 +378,8 @@
     odd = lax.axis_index("ax") % 2
     sems = rest[-1]
     copies = []
-    for k, (q, first, last) in enumerate(parts):
-        source = state.at[:, plane_of(odd, q), first:last, :]
+    for k, (first, last) in enumerate(parts):
+        source = state.at[:, 1 - odd, first:last, :]
         copies.append(pltpu.make_async_copy(source, rest[k], sems.at[k]))
     for copy in copies:
         copy.start()
@@ -410,7 +419,7 @@
     return pl.pallas_call(
         functools.partial(pack_first_kernel, count),
         in_specs=[ANY],
-        out_specs=[vmem, vmem, vmem],
+        out_specs=[vmem] * 3,
         out_shape=[jax.ShapeDtypeStruct((fields, count, cells), jnp.float32), row, row],
         scratch_shapes=[rows, rows, pltpu.SemaphoreType.DMA((3,))],
         compiler_params=PARAMS,
@@ -419,19 +428,17 @@
     )(in_hbm(state))
 
 
-def pack_edges(state, token):
+def pack_edges(state, spans, token):
     fields, planes, rows, cells = state.shape
-    vmem = pl.BlockSpec(memory_space=pltpu.VMEM)
     tiles = pltpu.VMEM((fields, planes, rows, LANES), jnp.float32)
+    shapes = [jax.ShapeDtypeStruct((rows, LANES), jnp.float32)]
+    shapes += [jax.ShapeDtypeStruct((fields, b - a, cells), jnp.float32) for a, b in spans]
     return pl.pallas_call(
-        pack_edges_kernel,
+        functools.partial(pack_edges_kernel, spans),
         in_specs=[ANY, ANY],
-        out_specs=[vmem, vmem],
-        out_shape=[
-            jax.ShapeDtypeStruct((rows, LANES), jnp.float32),
-            jax.ShapeDtypeStruct((fields, R_NEAR, cells), jnp.float32),
-        ],
-        scratch_shapes=[tiles, tiles, pltpu.SemaphoreType.DMA((3,))],
+        out_specs=[pl.BlockSpec(memory_space=pltpu.VMEM)] * len(shapes),
+        out_shape=shapes,
+        scratch_shapes=[tiles, tiles, pltpu.SemaphoreType.DMA((2 + len(spans),))],
         compiler_params=PARAMS,
         cost_estimate=cost(0, fields * planes * rows * LANES * 16),
         name="pack_edges",
@@ -440,7 +447,7 @@
 
 def pack_rest(state, parts, *tokens):
     fields, _, _, cells = state.shape
-    shapes = [jax.ShapeDtypeStruct((fields, last - first, cells), jnp.float32) for _, first, last in parts]
+    shapes = [jax.ShapeDtypeStruct((fields, b - a, cells), jnp.float32) for a, b in parts]
     return pl.pallas_call(
         functools.partial(pack_rest_kernel, parts, len(tokens)),
         in_specs=[ANY] * (1 + len(tokens)),
@@ -457,9 +464,9 @@
     return pltpu.VMEM((PLANES, FIELDS, cells // LANES, rows + 2 * EIGHT, LANES), jnp.float32)
 
 
-def bulk(flags, state, low, high, inner, edge, dtheta, outer, span, first, rows, token, held):
+def bulk(flags, state, low, high, inner, edge, dtheta, span, rows, token, held, outer=None, origin=0):
     fields, planes, total_rows, cells = state.shape
-    end = span[1]
+    first, end = span
     tail = total_rows // EIGHT - 1
     eights = rows // EIGHT
     at = first // EIGHT
@@ -472,16 +479,17 @@
         whole(LINES, cells),
         rows_from((fields, rows, cells), 1, 0, rows),
         rows_from((rows, LANES), 0, first, rows),
-        rows_from((fields, rows, cells), 1, first - span[0], rows),
-        ANY,
-        ANY,
     ]
     state = in_hbm(state)
-    operands = [state, state, state, low, high, inner, edge, outer]
+    operands = [state, state, state, low, high, inner, edge]
+    if outer is not None:
+        in_specs.append(rows_from((fields, rows, cells), 1, first - origin, rows))
+        operands.append(outer)
+    in_specs += [ANY, ANY]
     operands += [token, state if held is None else held]
     size = fields * planes * (end - first) * cells
     return pl.pallas_call(
-        functools.partial(bulk_kernel, dtheta, rows, first, total_rows),
+        functools.partial(bulk_kernel, dtheta, rows, first, total_rows, outer is not None),
         grid_spec=pltpu.PrefetchScalarGridSpec(
             num_scalar_prefetch=1,
             grid=((end - first) // rows,),
@@ -492,25 +500,41 @@
         out_shape=pltpu.HBM(state.shape, jnp.float32),
         input_output_aliases={} if held is None else {len(operands): 0},
         compiler_params=PARAMS,
-        cost_estimate=cost(size * 60, size * 60),
+        cost_estimate=cost(size * 60, size * 10),
         name="bulk",
     )(flags, *operands)
 
 
-def near(flags, state, low, high, inner, edge, dtheta, outer, factor, table, solve, token, part=None):
+def add_outer(flags, outer, span, rows, held):
+    fields, _, cells = outer.shape
+    first, end = span
+    place = pl.BlockSpec(
+        tuple(pl.Element(n) for n in (fields, 1, rows, cells)),
+        lambda i, s: (0, s[ODD], (first // EIGHT + i * (rows // EIGHT)) * EIGHT, 0),
+    )
+    return pl.pallas_call(
+        outer_kernel,
+        grid_spec=pltpu.PrefetchScalarGridSpec(
+            num_scalar_prefetch=1,
+            grid=((end - first) // rows,),
+            in_specs=[rows_from((fields, rows, cells), 1, 0, rows), place],
+            out_specs=place,
+        ),
+        out_shape=pltpu.HBM(held.shape, jnp.float32),
+        input_output_aliases={2: 0},
+        compiler_params=PARAMS,
+        cost_estimate=cost(outer.size * 6, outer.size * 16),
+        name="add_outer",
+    )(flags, outer, held)
+
+
+def near(flags, state, low, high, inner, edge, dtheta, outer, factor, table, solve, token):
     fields, planes, rows, cells = state.shape
     out = jax.ShapeDtypeStruct((LINES, R_NEAR, cells), jnp.float32)
     tail = min(R_NEAR // EIGHT, rows // EIGHT - 1)
     state = in_hbm(state)
-    out_specs = [whole(LINES, R_NEAR, cells), whole(LINES, R_NEAR, cells), whole(R_NEAR, LANES)]
-    out_shape = [out, out, jax.ShapeDtypeStruct((R_NEAR, LANES), jnp.float32)]
-    scratch = [flux_scratch(R_NEAR, cells)]
-    if part is not None:
-        out_specs.append(whole(fields, part[1] - part[0], cells))
-        out_shape.append(jax.ShapeDtypeStruct((fields, part[1] - part[0], cells), jnp.float32))
-        scratch.append(pltpu.SemaphoreType.DMA)
-    result = pl.pallas_call(
-        functools.partial(near_kernel, dtheta, rows, part[0] if part else 0),
+    return pl.pallas_call(
+        functools.partial(near_kernel, dtheta, rows),
         grid_spec=pltpu.PrefetchScalarGridSpec(
             num_scalar_prefetch=1,
             grid=(1,),
@@ -526,17 +550,19 @@
                 whole(R_NEAR, LANES),
                 whole(*solve.shape),
                 ANY,
-                ANY,
             ],
-            out_specs=out_specs,
-            scratch_shapes=scratch,
+            out_specs=[
+                whole(LINES, R_NEAR, cells),
+                whole(LINES, R_NEAR, cells),
+                whole(R_NEAR, LANES),
+            ],
+            scratch_shapes=[flux_scratch(R_NEAR, cells)],
         ),
-        out_shape=out_shape,
+        out_shape=[out, out, jax.ShapeDtypeStruct((R_NEAR, LANES), jnp.float32)],
         compiler_params=PARAMS,
-        cost_estimate=cost(LINES * R_NEAR * cells * 200, LINES * R_NEAR * cells * 250),
+        cost_estimate=cost(LINES * R_NEAR * cells * 200, LINES * R_NEAR * cells * 20),
         name="near",
-    )(flags, state, state, low, high, inner, outer, edge, factor, table, solve, token, state)
-    return result if part is not None else (*result, None)
+    )(flags, state, state, low, high, inner, outer, edge, factor, table, solve, token)
 
 
 def finish(flags, factor, rhs, local, carry, table, held):
@@ -565,11 +591,10 @@
 
 
 def chunks(rows):
-    size = 48 if (rows - R_NEAR) % 48 == 0 else EIGHT
-    blocks = (rows - R_NEAR) // size
-    cuts = sorted({-(-2 * blocks // 5), -(-4 * blocks // 5), blocks})
-    ends = [R_NEAR + c * size for c in cuts]
-    return size, list(zip([0] + ends[:-1], ends))
+    units = (rows - R_NEAR) // 16
+    cuts = [3, 3 + (units - 6) // 2, units - 3, units] if units > 7 else [units]
+    ends = [R_NEAR + 16 * c for c in cuts]
+    return list(zip([R_NEAR] + ends[:-1], ends))
 
 
 def smoothing_table(coarsen, cells, total_cells, dtheta):
@@ -632,41 +657,41 @@
             rad_index * rows,
         ]
     ).astype(jnp.int32)
-    size, spans = chunks(rows)
+    spans = chunks(rows)
     count = len(spans)
 
     part, low, high = pack_first(state, spans[0][1])
     outer = [lax.ppermute(part, "ax", outer_pairs)]
-    columns, side = pack_edges(state, high)
+    columns, *rest = pack_edges(state, spans[1:], high)
     low = lax.ppermute(low, "rad", up)
     high = lax.ppermute(high, "rad", down)
-    inner = [lax.ppermute(side, "ax", inner_pairs)]
-    wanted = [(0, R_NEAR, spans[0][1])] + [(0, *span) for span in spans[1:]]
-    if count > 1:
-        wanted.insert(1, (1, *spans[1]))
-    parts = pack_rest(state, wanted, columns, low, high)
-    for k, value in enumerate(parts):
-        if wanted[k][0]:
-            outer.append(lax.ppermute(value, "ax", outer_pairs))
-        else:
-            inner.append(lax.ppermute(value, "ax", inner_pairs))
+    outer += [lax.ppermute(part, "ax", outer_pairs) for part in rest]
     if sec_count == 2:
         edge = ring(columns, "sec", 1)
     else:
         from_left = jnp.arange(LANES)[None, :] % 4 < 2
         edge = jnp.where(from_left, ring(columns, "sec", 1), ring(columns, "sec", -1))
 
+    parts = pack_rest(state, [(0, R_NEAR)] + spans, low, high, edge)
+    near_inner, *inner = [lax.ppermute(value, "ax", inner_pairs) for value in parts]
+
     table, closing, across = smoothing_table(coarsen, cells, total_cells, dtheta)
     factor = jnp.broadcast_to(coarsen.astype(jnp.float32)[:, None], (R_NEAR, LANES))
-
     solve = piece_tables(dtheta)
-    given = (flags, state, low, high)
-    part = spans[2] if count > 2 else None
-    rhs, local, ends, part = near(
-        *given, inner[0], edge, dtheta, outer[0], factor, table, solve, parts[0], part
+    rhs, local, ends = near(
+        flags,
+        state,
+        low,
+        high,
+        near_inner,
+        edge,
+        dtheta,
+        outer[0],
+        factor,
+        table,
+        solve,
+        parts[0],
     )
-    if part is not None:
-        outer.append(lax.ppermute(part, "ax", outer_pairs))
     arrived = [ends] + [ring(ends, "sec", k) for k in range(1, sec_count)] + [ends]
     from_left = jnp.arange(LANES)[None, :] < LINES
     carry = jnp.zeros_like(ends)
@@ -674,13 +699,21 @@
         carry = carry * across + jnp.where(from_left, arrived[k], arrived[sec_count - k])
     carry = carry * closing
 
-    out = None
-    for k in range(count):
-        first = spans[k][0] if k else R_NEAR
-        if k == count - 1 and k:
+    def pass_over(k, held, **more):
+        span = spans[k]
+        block = (span[1] - span[0]) // 2
+        return bulk(flags, state, low, high, inner[k], edge, dtheta, span, block, ends, held, **more)
+
+    out = pass_over(0, None, outer=outer[0])
+    count = len(spans)
+    for k in range(1, count - 1):
+        if k == count - 2:
+            out = pass_over(-1, out)
             out = finish(flags, factor, rhs, local, carry, table, out)
-        out = bulk(*given, inner[k + 1], edge, dtheta, outer[k], spans[k], first, size, ends, out)
-    return out if count > 1 else finish(flags, factor, rhs, local, carry, table, out)
+        out = pass_over(k, out, outer=outer[k], origin=spans[k][0])
+    if count == 1:
+        return finish(flags, factor, rhs, local, carry, table, out)
+    return add_outer(flags, outer[-1], spans[-1], 24, out)
 
 
 def solution(mesh):

time: 72.8 us -> 78.9 us (1.084)
  starting transfers between devices: 19.8 us -> 23 us
  local copies, waits for them, and re-layouts: 1.15 us -> 4.34 us
  waiting for transfers between devices: 6.23 us -> 3.29 us
  Pallas kernels: 44.9 us -> 47.6 us
    pallas_call x2 -> x3, Pallas kernels: 10.6 us -> 15.4 us  [the longest x1 8.12 us: near(): pl.pallas_call(functools.partial(near_kernel, dtheta, rows), grid_spec=pl...]
    ppermute x6 -> x8, starting transfers between devices: 7.38 us -> 11.4 us  [the longest x3 10 us: body(): outer += [lax.ppermute(part, 'ax', outer_pairs) for part in rest]]
    unnamed x6 -> x16, local copies, waits for them, and re-layouts: 0.99 us -> 4.18 us
    ppermute x2, waiting for transfers between devices: 3.88 us -> 1.97 us  [ring(): lax.ppermute(value, axis, [(i, (i + shift) % size) for i in range(size)])]
    pallas_call x1, Pallas kernels: 5.55 us -> 3.68 us  [pack_rest(): pl.pallas_call(functools.partial(pack_rest_kernel, parts, len(tokens)), i...]
    ppermute x1, waiting for transfers between devices: 0.01 us -> 1.3 us  [body(): low = lax.ppermute(low, 'rad', up)]
    ppermute x1, waiting for transfers between devices: 1.17 us -> 0.01 us  [body(): outer = [lax.ppermute(part, 'ax', outer_pairs)]]
    ppermute x6 -> x8, waiting for transfers between devices: 1.18 us -> 0.02 us  [the longest x5 0.01 us: body(): lax.ppermute(value, 'ax', inner_pairs)]
  transfers between devices with their start and end apart: 11 -> 13, of which waited for: 3 -> 2; matrix products, arithmetic and copies ran while one was open for 1% -> 0% of each run, Pallas kernels for 49% -> 54%
where the time goes in v5:
time: 78.9 us; the launch traced here: 78.6 us
  Pallas kernels  47.6 us (60%)
  starting transfers between devices  23 us (29%)
  local copies, waits for them, and re-layouts  4.34 us (6%)
  waiting for transfers between devices  3.29 us (4%)
    pallas_call x4, Pallas kernels, bulk(): pl.pallas_call(functools.partial(bulk_kernel, dtheta, rows, first, total_...  24.3 us
    ppermute x3, starting transfers between devices, body(): outer += [lax.ppermute(part, 'ax', outer_pairs) for part in rest]  10 us
    pallas_call x1, Pallas kernels, near(): pl.pallas_call(functools.partial(near_kernel, dtheta, rows), grid_spec=pl...  8.12 us
    pallas_call x1, Pallas kernels, pack_edges(): pl.pallas_call(functools.partial(pack_edges_kernel, spans), in_specs=[ANY...  4.56 us
    ppermute x1, starting transfers between devices, body(): outer = [lax.ppermute(part, 'ax', outer_pairs)]  4.51 us
    unnamed x16, local copies, waits for them, and re-layouts  4.18 us
    ppermute x1, starting transfers between devices, body(): low = lax.ppermute(low, 'rad', up)  4.12 us
    pallas_call x1, Pallas kernels, pack_rest(): pl.pallas_call(functools.partial(pack_rest_kernel, parts, len(tokens)), i...  3.68 us
  transfers between devices with their start and end apart: 13, of which 2 were waited for; matrix products, arithmetic and copies ran while one was open for 0% of the time, Pallas kernels for 54%

profile of v5, /device:TPU:1, one launch (start us, length us, event | category | flops | bytes accessed | tf_op | source)
XLA Modules:
  0.0 78.6 jit_solution(5975999212208994057)
XLA Ops:
  0.0 2.6 %pack_first.1 = (f32[5,64,1024]{2,1,0:T(8,128)}, f32[10,1024]{1,0:T(8,128)S(1)}, f32[10,1024]{1,0:T(8,128)S(1)}) custom-call(f32[5,2,256,1024]{3,2,1,0:T(8,128)} %after.9), custom_call_target="tpu_custom_call" | custom-call | bytes 2621440 | tf_op jit(solution)/shard_map/pack_first/pallas_call | solution.py:419
  2.6 4.5 %collective-permute-start.7 = (f32[5,64,1024]{2,1,0:T(8,128)}, f32[5,64,1024]{2,1,0:T(8,128)S(1)}, u32[]{:S(2)}, u32[]{:S(2)}) collective-permute-start(f32[5,64,1024]{2,1,0:T(8,128)} %get-tuple-element.27), channel_id=1, source_target_pairs={{1,2},{2,1},{5,6},{6,5},{9,10},{10,9},{13,14},{14,13},{17,18},{18,... | collective-permute-start | bytes 3932168 | tf_op jit(solution)/shard_map/ppermute | solution.py:664
  7.1 4.6 %pack_edges.1 = (f32[256,128]{1,0:T(8,128)S(1)}, f32[5,64,1024]{2,1,0:T(8,128)}, f32[5,80,1024]{2,1,0:T(8,128)}, f32[5,48,1024]{2,1,0:T(8,128)S(1)}) custom-call(f32[5,2,256,1024]{3,2,1,0:T(8,128)} %after.9, f32[10,1024]{1,0:T(8,128)S(1)} %get-tuple-element.20.token), custom_call_target="tpu_custom_call" | custom-call | bytes 5242880 | tf_op jit(solution)/shard_map/pack_edges/pallas_call | solution.py:436
  11.7 0.0 copy-start.3
  11.7 1.0 %copy-done.3 = f32[5,48,1024]{2,1,0:T(8,128)} copy-done((f32[5,48,1024]{2,1,0:T(8,128)}, f32[5,48,1024]{2,1,0:T(8,128)S(1)}, u32[]{:S(2)}) %copy-start.3) | copy-done | bytes 983064
  12.7 1.9 %collective-permute-start.11 = (f32[5,64,1024]{2,1,0:T(8,128)}, f32[5,64,1024]{2,1,0:T(8,128)}, u32[]{:S(2)}, u32[]{:S(2)}) collective-permute-start(f32[5,64,1024]{2,1,0:T(8,128)} %get-tuple-element.33), channel_id=1, source_target_pairs={{1,2},{2,1},{5,6},{6,5},{9,10},{10,9},{13,14},{14,13},{17,18},{18,... | collective-permute-start | bytes 3932168 | tf_op jit(solution)/shard_map/ppermute | solution.py:668
  14.6 1.3 %collective-permute-start.3 = (f32[256,128]{1,0:T(8,128)S(1)}, f32[256,128]{1,0:T(8,128)S(1)}, u32[]{:S(2)}, u32[]{:S(2)}) collective-permute-start(f32[256,128]{1,0:T(8,128)S(1)} %get-tuple-element.23), channel_id=1, source_target_pairs={{0,16},{16,0},{1,17},{17,1},{2,18},{18,2},{3,19},{19,3},{4,20},{20... | collective-permute-start | bytes 393224 | tf_op jit(solution)/shard_map/ppermute | solution.py:630
  15.9 1.3 %collective-permute-start.2 = (f32[10,1024]{1,0:T(8,128)S(1)}, f32[10,1024]{1,0:T(8,128)S(1)}, u32[]{:S(2)}, u32[]{:S(2)}) collective-permute-start(f32[10,1024]{1,0:T(8,128)S(1)} %get-tuple-element.20.token), channel_id=1, source_target_pairs={{4,0},{8,4},{12,8},{5,1},{9,5},{13,9},{6,2},{10,6},{14,10},{7,3},{... | collective-permute-start | bytes 122888 | tf_op jit(solution)/shard_map/ppermute | solution.py:667
  17.2 0.0 copy-start.7
  17.2 0.0 copy-start
  17.2 4.1 %collective-permute-start.1 = (f32[10,1024]{1,0:T(8,128)S(1)}, f32[10,1024]{1,0:T(8,128)S(1)}, u32[]{:S(2)}, u32[]{:S(2)}) collective-permute-start(f32[10,1024]{1,0:T(8,128)S(1)} %get-tuple-element.22), channel_id=1, source_target_pairs={{0,4},{4,8},{8,12},{1,5},{5,9},{9,13},{2,6},{6,10},{10,14},{3,7},{... | collective-permute-start | bytes 122888 | tf_op jit(solution)/shard_map/ppermute | solution.py:666
  21.3 0.0 collective-permute-done.2.rest_1_.high
  21.3 1.3 %collective-permute-done.1.rest_0_.low = f32[10,1024]{1,0:T(8,128)S(1)} collective-permute-done((f32[10,1024]{1,0:T(8,128)S(1)}, f32[10,1024]{1,0:T(8,128)S(1)}, u32[]{:S(2)}, u32[]{:S(2)}) %collective-permute-start.1) | collective-permute-done | bytes 40992 | tf_op jit(solution)/shard_map/ppermute | solution.py:666
  22.6 0.0 collective-permute-done.3.rest_2_.edge
  22.6 3.7 %pack_rest.1 = (f32[5,16,1024]{2,1,0:T(8,128)}, f32[5,48,1024]{2,1,0:T(8,128)}, f32[5,64,1024]{2,1,0:T(8,128)S(1)}, f32[5,80,1024]{2,1,0:T(8,128)S(1)}, f32[5,48,1024]{2,1,0:T(8,128)S(1)}) custom-call(f32[5,2,256,1024]{3,2,1,0:T(8,128)} %after.9, f32[10,1024]{1,0:T(8,128)S(1)} %collective-permute-done.1.rest_0_.low, ...), custom_call_target="tpu_custom_call" | custom-call | bytes 10485760 | tf_op jit(solution)/shard_map/pack_rest/pallas_call | solution.py:451
  26.3 0.0 copy-start.1
  26.3 1.2 %copy-done.1 = f32[5,80,1024]{2,1,0:T(8,128)} copy-done((f32[5,80,1024]{2,1,0:T(8,128)}, f32[5,80,1024]{2,1,0:T(8,128)S(1)}, u32[]{:S(2)}) %copy-start.1) | copy-done | bytes 1638424
  27.5 0.0 copy-start.2
  27.5 1.1 %copy-done.2 = f32[5,64,1024]{2,1,0:T(8,128)} copy-done((f32[5,64,1024]{2,1,0:T(8,128)}, f32[5,64,1024]{2,1,0:T(8,128)S(1)}, u32[]{:S(2)}) %copy-start.2) | copy-done | bytes 1310744
  28.6 0.0 copy-start.5
  28.6 0.9 %copy-done.5 = f32[5,48,1024]{2,1,0:T(8,128)} copy-done((f32[5,48,1024]{2,1,0:T(8,128)}, f32[5,48,1024]{2,1,0:T(8,128)S(1)}, u32[]{:S(2)}) %copy-start.5) | copy-done | bytes 983064
  29.5 0.0 collective-permute-start.6
  29.5 0.5 collective-permute-start.12
  30.0 5.0 %collective-permute-start.5 = (f32[5,80,1024]{2,1,0:T(8,128)}, f32[5,80,1024]{2,1,0:T(8,128)S(1)}, u32[]{:S(2)}, u32[]{:S(2)}) collective-permute-start(f32[5,80,1024]{2,1,0:T(8,128)} %get-tuple-element.25), channel_id=1, source_target_pairs={{1,2},{2,1},{5,6},{6,5},{9,10},{10,9},{13,14},{14,13},{17,18},{18,... | collective-permute-start | bytes 4915208 | tf_op jit(solution)/shard_map/ppermute | solution.py:668
  35.1 0.0 copy-done.7
  35.1 0.1 stack.35.flags
  35.2 0.0 collective-permute-done.6.inner
  35.2 0.1 collective-permute-start.4
  35.4 0.0 collective-permute-done.7.outer.rest_0_
  35.4 0.6 collective-permute-start.10
  35.9 0.1 fusion.3.table
  36.0 0.1 broadcast_in_dim.51.factor
  36.1 0.0 copy-done
  36.1 0.0 copy-start.6
  36.1 0.0 copy-start.4
  36.1 8.1 %near.1 = (f32[10,16,1024]{2,1,0:T(8,128)S(1)}, f32[10,16,1024]{2,1,0:T(8,128)S(1)}, f32[16,128]{1,0:T(8,128)S(1)}) custom-call(s32[5]{0:T(128)S(1)} %stack.35.flags, f32[5,2,256,1024]{3,2,1,0:T(8,128)} %after.9, f32[5,2,256,1024]{3,2,1,0:T(8,128)} %after.9, f32[10,1024]{1,0:T(8,128)S(1)} %collective-permute-done.1.rest_0_.low, ...), custom_call_target="tpu_custom_call" | custom-call | flops 32768000 | bytes 3276800 | tf_op jit(solution)/shard_map/near/pallas_call | solution.py:536
  44.2 0.0 collective-permute-done.12.inner
  44.2 0.3 collective-permute-start.8
  44.5 0.0 collective-permute-done.11.rest_0_
  44.5 0.0 copy-done.6
  44.5 0.3 collective-permute-start.9
  44.8 2.0 %collective-permute-done.8 = f32[16,128]{1,0:T(8,128)S(1)} collective-permute-done((f32[16,128]{1,0:T(8,128)S(1)}, f32[16,128]{1,0:T(8,128)S(1)}, u32[]{:S(2)}, u32[]{:S(2)}) %collective-permute-start.8) | collective-permute-done | bytes 8224 | tf_op jit(solution)/shard_map/ppermute | solution.py:630
  46.8 0.0 copy-done.4
  46.8 3.1 %collective-permute-start = (f32[5,48,1024]{2,1,0:T(8,128)S(1)}, f32[5,48,1024]{2,1,0:T(8,128)S(1)}, u32[]{:S(2)}, u32[]{:S(2)}) collective-permute-start(f32[5,48,1024]{2,1,0:T(8,128)S(1)} %copy-done.4), channel_id=1, source_target_pairs={{1,2},{2,1},{5,6},{6,5},{9,10},{10,9},{13,14},{14,13},{17,18},{18,... | collective-permute-start | bytes 2949128 | tf_op jit(solution)/shard_map/ppermute | solution.py:668
  49.9 5.5 %bulk.4.rest_2_ = f32[5,2,256,1024]{3,2,1,0:T(8,128)} custom-call(s32[5]{0:T(128)S(1)} %stack.35.flags, f32[5,2,256,1024]{3,2,1,0:T(8,128)} %after.9, f32[5,2,256,1024]{3,2,1,0:T(8,128)} %after.9, f32[5,2,256,1024]{3,2,1,0:T(8,128)} %after.9, f32[10,1024]{1,0:T(8,128)S(1)} %collective-permute-done.1.rest_0_.low, ...), custom_call_target="tpu_custom_call" | custom-call | flops 29491200 | bytes 4915200 | tf_op jit(solution)/shard_map/bulk/pallas_call | solution.py:491
  55.4 0.1 add_multiply_fusion.carry
  55.4 0.0 collective-permute-done.10.inner
  55.4 6.5 %bulk.5.rest_1_ = f32[5,2,256,1024]{3,2,1,0:T(8,128)} custom-call(s32[5]{0:T(128)S(1)} %stack.35.flags, f32[5,2,256,1024]{3,2,1,0:T(8,128)} %after.9, f32[5,2,256,1024]{3,2,1,0:T(8,128)} %after.9, f32[5,2,256,1024]{3,2,1,0:T(8,128)} %after.9, f32[10,1024]{1,0:T(8,128)S(1)} %collective-permute-done.1.rest_0_.low, ...), custom_call_target="tpu_custom_call", output_to_operand_aliasing={{}: (10, {})} | custom-call | flops 39321600 | bytes 6553600 | tf_op jit(solution)/shard_map/bulk/pallas_call | solution.py:491
  61.9 0.0 collective-permute-done.9.inner
  61.9 5.2 %bulk.6.held = f32[5,2,256,1024]{3,2,1,0:T(8,128)} custom-call(s32[5]{0:T(128)S(1)} %stack.35.flags, f32[5,2,256,1024]{3,2,1,0:T(8,128)} %after.9, f32[5,2,256,1024]{3,2,1,0:T(8,128)} %after.9, f32[5,2,256,1024]{3,2,1,0:T(8,128)} %after.9, f32[10,1024]{1,0:T(8,128)S(1)} %collective-permute-done.1.rest_0_.low, ...), custom_call_target="tpu_custom_call", output_to_operand_aliasing={{}: (9, {})} | custom-call | flops 29491200 | bytes 4915200 | tf_op jit(solution)/shard_map/bulk/pallas_call | solution.py:491
  67.2 1.6 %finish.1.rest_2_ = f32[5,2,256,1024]{3,2,1,0:T(8,128)} custom-call(s32[5]{0:T(128)S(1)} %stack.35.flags, f32[16,128]{1,0:T(8,128)S(1)} %broadcast_in_dim.51.factor, f32[10,16,1024]{2,1,0:T(8,128)S(1)} %get-tuple-element.29.rhs, f32[10,16,1024]{2,1,0:T(8,128)S(1)} %get-tuple-element.30.local, ...), custom_call_target="tpu_custom_call", output_to_operand_aliasing={{}: (6, {})} | custom-call | flops 1638400 | bytes 3276800 | tf_op jit(solution)/shard_map/finish/pallas_call | solution.py:570
  68.8 0.0 collective-permute-done.5.rest_0_
  68.8 0.0 collective-permute-done.4.inner
  68.8 7.1 %bulk.7.held = f32[5,2,256,1024]{3,2,1,0:T(8,128)} custom-call(s32[5]{0:T(128)S(1)} %stack.35.flags, f32[5,2,256,1024]{3,2,1,0:T(8,128)} %after.9, f32[5,2,256,1024]{3,2,1,0:T(8,128)} %after.9, f32[5,2,256,1024]{3,2,1,0:T(8,128)} %after.9, f32[10,1024]{1,0:T(8,128)S(1)} %collective-permute-done.1.rest_0_.low, ...), custom_call_target="tpu_custom_call", output_to_operand_aliasing={{}: (10, {})} | custom-call | flops 49152000 | bytes 8192000 | tf_op jit(solution)/shard_map/bulk/pallas_call | solution.py:491
  75.9 0.0 collective-permute-done.outer
  75.9 2.8 %add_outer.1 = f32[5,2,256,1024]{3,2,1,0:T(8,128)} custom-call(s32[5]{0:T(128)S(1)} %stack.35.flags, f32[5,48,1024]{2,1,0:T(8,128)S(1)} %collective-permute-done.outer, f32[5,2,256,1024]{3,2,1,0:T(8,128)} %bulk.7.held), custom_call_target="tpu_custom_call", output_to_operand_aliasing={{}: (2, {})} | custom-call | flops 1474560 | bytes 3932160 | tf_op jit(solution)/shard_map/add_outer/pallas_call | solution.py:515
  (5 shorter events, 0.1 us)
Async XLA Ops:
  2.6 32.8 %collective-permute-start.7 = (f32[5,64,1024]{2,1,0:T(8,128)}, f32[5,64,1024]{2,1,0:T(8,128)S(1)}, u32[]{:S(2)}, u32[]{:S(2)}) collective-permute-start(f32[5,64,1024]{2,1,0:T(8,128)} %get-tuple-element.27), channel_id=1, source_target_pairs={{1,2},{2,1},{5,6},{6,5},{9,10},{10,9},{13,14},{14,13},{17,18},{18,... | collective-permute-start | bytes 3932168 | tf_op jit(solution)/shard_map/ppermute | solution.py:664
  11.7 1.0 %copy-start.3 = (f32[5,48,1024]{2,1,0:T(8,128)}, f32[5,48,1024]{2,1,0:T(8,128)S(1)}, u32[]{:S(2)}) copy-start(f32[5,48,1024]{2,1,0:T(8,128)S(1)} %get-tuple-element.21) | copy-start | bytes 2949124
  12.7 31.9 %collective-permute-start.11 = (f32[5,64,1024]{2,1,0:T(8,128)}, f32[5,64,1024]{2,1,0:T(8,128)}, u32[]{:S(2)}, u32[]{:S(2)}) collective-permute-start(f32[5,64,1024]{2,1,0:T(8,128)} %get-tuple-element.33), channel_id=1, source_target_pairs={{1,2},{2,1},{5,6},{6,5},{9,10},{10,9},{13,14},{14,13},{17,18},{18,... | collective-permute-start | bytes 3932168 | tf_op jit(solution)/shard_map/ppermute | solution.py:668
  14.6 8.1 %collective-permute-start.3 = (f32[256,128]{1,0:T(8,128)S(1)}, f32[256,128]{1,0:T(8,128)S(1)}, u32[]{:S(2)}, u32[]{:S(2)}) collective-permute-start(f32[256,128]{1,0:T(8,128)S(1)} %get-tuple-element.23), channel_id=1, source_target_pairs={{0,16},{16,0},{1,17},{17,1},{2,18},{18,2},{3,19},{19,3},{4,20},{20... | collective-permute-start | bytes 393224 | tf_op jit(solution)/shard_map/ppermute | solution.py:630
  15.9 5.4 %collective-permute-start.2 = (f32[10,1024]{1,0:T(8,128)S(1)}, f32[10,1024]{1,0:T(8,128)S(1)}, u32[]{:S(2)}, u32[]{:S(2)}) collective-permute-start(f32[10,1024]{1,0:T(8,128)S(1)} %get-tuple-element.20.token), channel_id=1, source_target_pairs={{4,0},{8,4},{12,8},{5,1},{9,5},{13,9},{6,2},{10,6},{14,10},{7,3},{... | collective-permute-start | bytes 122888 | tf_op jit(solution)/shard_map/ppermute | solution.py:667
  17.2 17.9 %copy-start.7 = (s32[16]{0:T(128)S(1)}, s32[16]{0:T(128)}, u32[]{:S(2)}) copy-start(s32[16]{0:T(128)} %param.4) | copy-start | bytes 196
  17.2 18.9 %copy-start = (f32[128,640]{1,0:T(8,128)S(1)}, f32[128,640]{1,0:T(8,128)}, u32[]{:S(2)}) copy-start(f32[128,640]{1,0:T(8,128)} %constant.54.clone.solve) | copy-start | bytes 983044
  17.2 5.4 %collective-permute-start.1 = (f32[10,1024]{1,0:T(8,128)S(1)}, f32[10,1024]{1,0:T(8,128)S(1)}, u32[]{:S(2)}, u32[]{:S(2)}) collective-permute-start(f32[10,1024]{1,0:T(8,128)S(1)} %get-tuple-element.22), channel_id=1, source_target_pairs={{0,4},{4,8},{8,12},{1,5},{5,9},{9,13},{2,6},{6,10},{10,14},{3,7},{... | collective-permute-start | bytes 122888 | tf_op jit(solution)/shard_map/ppermute | solution.py:666
  26.3 1.2 %copy-start.1 = (f32[5,80,1024]{2,1,0:T(8,128)}, f32[5,80,1024]{2,1,0:T(8,128)S(1)}, u32[]{:S(2)}) copy-start(f32[5,80,1024]{2,1,0:T(8,128)S(1)} %get-tuple-element.24) | copy-start | bytes 4915204
  27.5 1.1 %copy-start.2 = (f32[5,64,1024]{2,1,0:T(8,128)}, f32[5,64,1024]{2,1,0:T(8,128)S(1)}, u32[]{:S(2)}) copy-start(f32[5,64,1024]{2,1,0:T(8,128)S(1)} %get-tuple-element.32) | copy-start | bytes 3932164
  28.6 0.9 %copy-start.5 = (f32[5,48,1024]{2,1,0:T(8,128)}, f32[5,48,1024]{2,1,0:T(8,128)S(1)}, u32[]{:S(2)}) copy-start(f32[5,48,1024]{2,1,0:T(8,128)S(1)} %get-tuple-element.31) | copy-start | bytes 2949124
  29.5 5.7 %collective-permute-start.6 = (f32[5,16,1024]{2,1,0:T(8,128)}, f32[5,16,1024]{2,1,0:T(8,128)}, u32[]{:S(2)}, u32[]{:S(2)}) collective-permute-start(f32[5,16,1024]{2,1,0:T(8,128)} %get-tuple-element.26.token), channel_id=1, source_target_pairs={{0,1},{1,0},{2,3},{3,2},{4,5},{5,4},{6,7},{7,6},{8,9},{9,8},{10,11... | collective-permute-start | bytes 983048 | tf_op jit(solution)/shard_map/ppermute | solution.py:676
  29.5 14.7 %collective-permute-start.12 = (f32[5,48,1024]{2,1,0:T(8,128)}, f32[5,48,1024]{2,1,0:T(8,128)}, u32[]{:S(2)}, u32[]{:S(2)}) collective-permute-start(f32[5,48,1024]{2,1,0:T(8,128)} %get-tuple-element.34), channel_id=1, source_target_pairs={{0,1},{1,0},{2,3},{3,2},{4,5},{5,4},{6,7},{7,6},{8,9},{9,8},{10,11... | collective-permute-start | bytes 2949128 | tf_op jit(solution)/shard_map/ppermute | solution.py:676
  30.0 38.8 %collective-permute-start.5 = (f32[5,80,1024]{2,1,0:T(8,128)}, f32[5,80,1024]{2,1,0:T(8,128)S(1)}, u32[]{:S(2)}, u32[]{:S(2)}) collective-permute-start(f32[5,80,1024]{2,1,0:T(8,128)} %get-tuple-element.25), channel_id=1, source_target_pairs={{1,2},{2,1},{5,6},{6,5},{9,10},{10,9},{13,14},{14,13},{17,18},{18,... | collective-permute-start | bytes 4915208 | tf_op jit(solution)/shard_map/ppermute | solution.py:668
  35.2 33.6 %collective-permute-start.4 = (f32[5,80,1024]{2,1,0:T(8,128)}, f32[5,80,1024]{2,1,0:T(8,128)S(1)}, u32[]{:S(2)}, u32[]{:S(2)}) collective-permute-start(f32[5,80,1024]{2,1,0:T(8,128)} %copy-done.1), channel_id=1, source_target_pairs={{0,1},{1,0},{2,3},{3,2},{4,5},{5,4},{6,7},{7,6},{8,9},{9,8},{10,11... | collective-permute-start | bytes 4915208 | tf_op jit(solution)/shard_map/ppermute | solution.py:676
  35.4 20.1 %collective-permute-start.10 = (f32[5,64,1024]{2,1,0:T(8,128)}, f32[5,64,1024]{2,1,0:T(8,128)S(1)}, u32[]{:S(2)}, u32[]{:S(2)}) collective-permute-start(f32[5,64,1024]{2,1,0:T(8,128)} %copy-done.2), channel_id=1, source_target_pairs={{0,1},{1,0},{2,3},{3,2},{4,5},{5,4},{6,7},{7,6},{8,9},{9,8},{10,11... | collective-permute-start | bytes 3932168 | tf_op jit(solution)/shard_map/ppermute | solution.py:676
  36.1 8.4 %copy-start.6 = (f32[5,48,1024]{2,1,0:T(8,128)S(1)}, f32[5,48,1024]{2,1,0:T(8,128)}, u32[]{:S(2)}) copy-start(f32[5,48,1024]{2,1,0:T(8,128)} %copy-done.5) | copy-start | bytes 2949124
  36.1 10.7 %copy-start.4 = (f32[5,48,1024]{2,1,0:T(8,128)S(1)}, f32[5,48,1024]{2,1,0:T(8,128)}, u32[]{:S(2)}) copy-start(f32[5,48,1024]{2,1,0:T(8,128)} %copy-done.3) | copy-start | bytes 2949124
  44.2 2.6 %collective-permute-start.8 = (f32[16,128]{1,0:T(8,128)S(1)}, f32[16,128]{1,0:T(8,128)S(1)}, u32[]{:S(2)}, u32[]{:S(2)}) collective-permute-start(f32[16,128]{1,0:T(8,128)S(1)} %get-tuple-element.28.rest_1_.rest_0_), channel_id=1, source_target_pairs={{0,16},{16,0},{1,17},{17,1},{2,18},{18,2},{3,19},{19,3},{4,20},{20... | collective-permute-start | bytes 24584 | tf_op jit(solution)/shard_map/ppermute | solution.py:630
  44.5 17.4 %collective-permute-start.9 = (f32[5,48,1024]{2,1,0:T(8,128)S(1)}, f32[5,48,1024]{2,1,0:T(8,128)S(1)}, u32[]{:S(2)}, u32[]{:S(2)}) collective-permute-start(f32[5,48,1024]{2,1,0:T(8,128)S(1)} %copy-done.6), channel_id=1, source_target_pairs={{0,1},{1,0},{2,3},{3,2},{4,5},{5,4},{6,7},{7,6},{8,9},{9,8},{10,11... | collective-permute-start | bytes 2949128 | tf_op jit(solution)/shard_map/ppermute | solution.py:676
  46.8 29.1 %collective-permute-start = (f32[5,48,1024]{2,1,0:T(8,128)S(1)}, f32[5,48,1024]{2,1,0:T(8,128)S(1)}, u32[]{:S(2)}, u32[]{:S(2)}) collective-permute-start(f32[5,48,1024]{2,1,0:T(8,128)S(1)} %copy-done.4), channel_id=1, source_target_pairs={{1,2},{2,1},{5,6},{6,5},{9,10},{10,9},{13,14},{14,13},{17,18},{18,... | collective-permute-start | bytes 2949128 | tf_op jit(solution)/shard_map/ppermute | solution.py:668

commit v6 on v4

--- a/solution.py
+++ b/solution.py
@@ -68,133 +68,116 @@
     return flux_along(outer, 1)
 
 
-def stencil(flags, first_row, rows, dtheta, load, above, below, edge, inner, outer, place, scratch):
+def stencil(
+    flags, first_row, rows, total_rows, dtheta, load, next_rows, edge, inner, outer, place, radial, azimuthal
+):
     strips = rows // EIGHT
-    pieces = scratch.shape[2]
+    pieces = radial.shape[2]
     row = lax.broadcasted_iota(jnp.int32, (EIGHT, 1), 0)
     lane = lax.broadcasted_iota(jnp.int32, (EIGHT, LANES), 1)
     start = flags[BASE] + first_row
     axial_sign = jnp.where(flags[ODD] == 1, 0.5, -0.5)
-    no_above = (flags[FIRST] == 1) & (first_row == 0)
-    radius_above = jnp.where(no_above, 0.0, (start - 1).astype(jnp.float32) + 0.5)
-    radius_below = (start + rows).astype(jnp.float32) + 0.5
+    above = jnp.where((flags[FIRST] == 1) & (first_row == 0), 0.0, (start - 1).astype(jnp.float32) + 0.5)
+    end = first_row + rows == total_rows
+    below = jnp.where((flags[LAST] == 1) & end, 0.0, (start + rows).astype(jnp.float32) + 0.5)
+    scale = jnp.where(row >= EIGHT // 2, above, below)
     at = [slice(b * LANES, (b + 1) * LANES) for b in range(pieces)]
 
     for q in range(PLANES):
         for b in range(pieces):
-            values = [above(f, q, at[b]) for f in range(FIELDS)]
-            values[0] = jnp.where(no_above, 1.0, values[0])
-            flux_above = flux_along(values, 2)
-            values, present = below(q, at[b])
-            flux_below = flux_along(values, 2)
+            values = [next_rows(f, q, at[b]) for f in range(FIELDS)]
+            values[0] = jnp.where(scale > 0.0, values[0], 1.0)
+            flux_next = flux_along(values, 2)
             for f in range(FIELDS):
-                scratch[q, f, b, EIGHT - 1 : EIGHT, :] = flux_above[f] * radius_above
-                scratch[q, f, b, EIGHT + rows : EIGHT + rows + 1, :] = flux_below[f] * (
-                    radius_below * present
-                )
-
-    def across(t, carry):
+                radial[q, f, b, 0:EIGHT, :] = flux_next[f] * scale
+                radial[q, f, b, EIGHT + rows : 2 * EIGHT + rows, :] = flux_next[f] * scale
+
+    def inside(t, carry):
         r = pl.multiple_of(EIGHT * t, EIGHT)
         radius = (start + r + row).astype(jnp.float32) + 0.5
         inv_radius = 1.0 / radius
-        half_arc = inv_radius * (0.5 / dtheta)
-        beyond = [edge(r)] + [pltpu.roll(edge(r), LANES - 4 * f, 1) for f in range(1, FIELDS)]
-        beyond = flux_along(beyond, 3)
-        side = [[beyond, beyond]]
-        side.append([[pltpu.roll(g, shift, 1) for g in beyond] for shift in (LANES - 1, 1)])
-
-        def piece(b):
-            fields = [[load(f, q, r, at[b]) for f in range(FIELDS)] for q in range(PLANES)]
-            base, left, right = [], [], []
-            axial = []
+        for b in range(pieces):
+            beside = flux_along([inner(f, r, at[b]) for f in range(FIELDS)], 1)
+            axial, source = [], []
             for q in range(PLANES):
-                flow, (pressure, twist, swirl) = fluxes(fields[q], (1, 2, 3))
+                fields = [load(f, q, r, at[b]) for f in range(FIELDS)]
+                flow, (pressure, twist, swirl) = fluxes(fields, (1, 2, 3))
                 axial.append(flow[1])
                 for f in range(FIELDS):
-                    scratch[q, f, b, pl.ds(r + EIGHT, EIGHT), :] = flow[2][f] * radius
-                left.append([pltpu.roll(g, 1, 1) for g in flow[3]])
-                right.append([pltpu.roll(g, LANES - 1, 1) for g in flow[3]])
-                source = (pressure + twist) * inv_radius
-                base.append([None, None, source, swirl * -inv_radius, None])
-            inner_flux = flux_along([inner(f, r, at[b]) for f in range(FIELDS)], 1)
-            beside = [[x - y for x, y in zip(inner_flux, axial[1])], axial[0]]
-            if outer is not None:
+                    radial[q, f, b, pl.ds(r + EIGHT, EIGHT), :] = flow[2][f] * radius
+                    azimuthal[q, f, b, pl.ds(r, EIGHT), :] = flow[3][f]
+                source.append(((pressure + twist) * inv_radius, swirl * -inv_radius))
+            base = [[axial_sign * (x - y) for x, y in zip(beside, axial[1])]]
+            if outer is None:
+                base.append([axial_sign * x for x in axial[0]])
+            else:
                 far = outer_flux(flags, [outer(f, r, at[b]) for f in range(FIELDS)])
-                beside[1] = [x - y for x, y in zip(axial[0], far)]
+                base.append([axial_sign * (x - y) for x, y in zip(axial[0], far)])
             for q in range(PLANES):
+                base[q][2] = base[q][2] + source[q][0]
+                base[q][3] = base[q][3] + source[q][1]
                 for f in range(FIELDS):
-                    value = axial_sign * beside[q][f]
-                    base[q][f] = value if base[q][f] is None else base[q][f] + value
-            return base, left, right
-
-        before = [side[q][0] for q in range(PLANES)]
-        here = piece(0)
-        for b in range(pieces):
-            following = piece(b + 1) if b + 1 < pieces else None
-            base, left, right = here
-            for q in range(PLANES):
-                for f in range(FIELDS):
-                    after = side[q][1][f] if following is None else following[2][q][f]
-                    ahead = jnp.where(lane == LANES - 1, after, right[q][f])
-                    behind = jnp.where(lane == 0, before[q][f], left[q][f])
-                    place(f, q, r)[:, at[b]] = base[q][f] + (behind - ahead) * half_arc
-            before, here = left, following
+                    place(f, q, r)[:, at[b]] = base[q][f]
         return carry
 
-    lax.fori_loop(0, strips, across, 0)
-
-    def along(t, carry):
+    lax.fori_loop(0, strips, inside, 0)
+
+    def differences(t, carry):
         r = pl.multiple_of(EIGHT * t, EIGHT)
         radius = (start + r + row).astype(jnp.float32) + 0.5
         half_inv = 0.5 / radius
+        half_arc = half_inv * (1.0 / dtheta)
+        beyond = [edge(r)] + [pltpu.roll(edge(r), LANES - 4 * f, 1) for f in range(1, FIELDS)]
+        beyond = flux_along(beyond, 3)
         for q in range(PLANES):
             for f in range(FIELDS):
+                ends = [pltpu.roll(beyond[f], s, 1) if q else beyond[f] for s in (LANES - 1, 1)]
+                here = [azimuthal[q, f, b, pl.ds(r, EIGHT), :] for b in range(pieces)]
+                left = [ends[0]] + [pltpu.roll(x, 1, 1) for x in here]
+                right = [pltpu.roll(x, LANES - 1, 1) for x in here] + [ends[1]]
                 out = place(f, q, r)
                 for b in range(pieces):
-                    up = scratch[q, f, b, pl.ds(r + EIGHT - 1, EIGHT), :]
-                    down = scratch[q, f, b, pl.ds(r + EIGHT + 1, EIGHT), :]
-                    out[:, at[b]] = out[:, at[b]] + (up - down) * half_inv
+                    behind = jnp.where(lane == 0, left[b], left[b + 1])
+                    ahead = jnp.where(lane == LANES - 1, right[b + 1], right[b])
+                    up = radial[q, f, b, pl.ds(r + EIGHT - 1, EIGHT), :]
+                    down = radial[q, f, b, pl.ds(r + EIGHT + 1, EIGHT), :]
+                    change = (behind - ahead) * half_arc + (up - down) * half_inv
+                    out[:, at[b]] = out[:, at[b]] + change
         return carry
 
-    lax.fori_loop(0, strips, along, 0)
+    lax.fori_loop(0, strips, differences, 0)
 
 
 def bulk_kernel(
-    dtheta, rows, first, total_rows, flags, state, before, after, low, high, inner, edge, outer, token, held, out, scratch
+    dtheta, rows, first, total_rows, flags, state, before, after, low, high, inner, edge, outer, token, held, out, *scratch
 ):
     odd = flags[ODD]
     step = pl.program_id(0)
     first_row = first + step * rows
     at_end = first_row + rows == total_rows
-    present = jnp.logical_not((flags[LAST] == 1) & at_end)
+    sub = lax.broadcasted_iota(jnp.int32, (EIGHT, LANES), 0)
 
     def load(f, q, r, at):
         return state[f, plane_of(odd, q), pl.ds(r, EIGHT), at]
 
-    def above(f, q, at):
-        return before[f, plane_of(odd, q), EIGHT - 1 : EIGHT, at]
-
-    def below(q, at):
-        values = []
-        for f in range(FIELDS):
-            k = f * PLANES + q
-            value = jnp.where(at_end, high[k : k + 1, at], after[f, plane_of(odd, q), 0:1, at])
-            values.append(jnp.where(present, value, 1.0))
-        return values, jnp.where(present, 1.0, 0.0)
+    def next_rows(f, q, at):
+        p, k = plane_of(odd, q), f * PLANES + q
+        under = jnp.where(at_end, high[k : k + 1, at], after[f, p, :, at])
+        return jnp.where(sub >= EIGHT // 2, before[f, p, :, at], under)
 
     stencil(
         flags,
         first_row,
         rows,
+        total_rows,
         dtheta,
         load,
-        above,
-        below,
+        next_rows,
         lambda r: edge[pl.ds(r, EIGHT), :],
         lambda f, r, at: inner[f, pl.ds(r, EIGHT), at],
         lambda f, r, at: outer[f, pl.ds(r, EIGHT), at],
         lambda f, q, r: out.at[f, plane_of(odd, q), pl.ds(r, EIGHT), :],
-        scratch,
+        *scratch,
     )
 
 
@@ -222,36 +205,33 @@
 ):
     cells = state.shape[-1]
     odd = flags[ODD]
-    at_end = total_rows == R_NEAR
-    present = jnp.logical_not((flags[LAST] == 1) & at_end)
-    part = rest[0] if len(rest) > 1 else None
-    scratch = rest[-1 if part is None else -2]
+    part = rest[0] if len(rest) > 2 else None
+    scratch = rest[-2:] if part is None else rest[-3:-1]
     if part is not None:
         source = hbm.at[:, lax.axis_index("ax") % 2, part_first : part_first + part.shape[1], :]
         copy = pltpu.make_async_copy(source, part, rest[-1])
         copy.start()
 
-    def below(q, at):
-        values = []
-        for f in range(FIELDS):
-            k = f * PLANES + q
-            value = high[k : k + 1, at] if at_end else after[f, plane_of(odd, q), 0:1, at]
-            values.append(jnp.where(present, value, 1.0))
-        return values, jnp.where(present, 1.0, 0.0)
+    sub = lax.broadcasted_iota(jnp.int32, (EIGHT, LANES), 0)
+
+    def next_rows(f, q, at):
+        k = f * PLANES + q
+        under = high[k : k + 1, at] if total_rows == R_NEAR else after[f, plane_of(odd, q), :, at]
+        return jnp.where(sub >= EIGHT // 2, low[k : k + 1, at], under)
 
     stencil(
         flags,
         0,
         R_NEAR,
+        total_rows,
         dtheta,
         lambda f, q, r, at: state[f, plane_of(odd, q), pl.ds(r, EIGHT), at],
-        lambda f, q, at: low[f * PLANES + q : f * PLANES + q + 1, at],
-        below,
+        next_rows,
         lambda r: edge[pl.ds(r, EIGHT), :],
         lambda f, r, at: inner[f, pl.ds(r, EIGHT), at],
         lambda f, r, at: outer[f, pl.ds(r, EIGHT), at],
         lambda f, q, r: rhs.at[f * PLANES + q, pl.ds(r, EIGHT), :],
-        scratch,
+        *scratch,
     )
 
     pieces = cells // LANES
@@ -454,7 +434,8 @@
 
 
 def flux_scratch(rows, cells):
-    return pltpu.VMEM((PLANES, FIELDS, cells // LANES, rows + 2 * EIGHT, LANES), jnp.float32)
+    shape = (PLANES, FIELDS, cells // LANES)
+    return [pltpu.VMEM((*shape, n, LANES), jnp.float32) for n in (rows + 2 * EIGHT, rows)]
 
 
 def bulk(flags, state, low, high, inner, edge, dtheta, outer, span, first, rows, token, held):
@@ -487,7 +468,7 @@
             grid=((end - first) // rows,),
             in_specs=in_specs,
             out_specs=rows_from((fields, planes, rows, cells), 2, first, rows),
-            scratch_shapes=[flux_scratch(rows, cells)],
+            scratch_shapes=flux_scratch(rows, cells),
         ),
         out_shape=pltpu.HBM(state.shape, jnp.float32),
         input_output_aliases={} if held is None else {len(operands): 0},
@@ -504,7 +485,7 @@
     state = in_hbm(state)
     out_specs = [whole(LINES, R_NEAR, cells), whole(LINES, R_NEAR, cells), whole(R_NEAR, LANES)]
     out_shape = [out, out, jax.ShapeDtypeStruct((R_NEAR, LANES), jnp.float32)]
-    scratch = [flux_scratch(R_NEAR, cells)]
+    scratch = flux_scratch(R_NEAR, cells)
     if part is not None:
         out_specs.append(whole(fields, part[1] - part[0], cells))
         out_shape.append(jax.ShapeDtypeStruct((fields, part[1] - part[0], cells), jnp.float32))
@@ -565,10 +546,10 @@
 
 
 def chunks(rows):
-    size = 48 if (rows - R_NEAR) % 48 == 0 else EIGHT
-    blocks = (rows - R_NEAR) // size
-    cuts = sorted({-(-2 * blocks // 5), -(-4 * blocks // 5), blocks})
-    ends = [R_NEAR + c * size for c in cuts]
+    size = 24 if (rows - R_NEAR) % 48 == 0 else EIGHT
+    pairs = (rows - R_NEAR) // (2 * size)
+    cuts = sorted({-(-2 * pairs // 5), -(-4 * pairs // 5), pairs})
+    ends = [R_NEAR + 2 * size * c for c in cuts]
     return size, list(zip([0] + ends[:-1], ends))
 
 

time: 72.8 us -> 74.5 us (1.023)
  Pallas kernels: 44.9 us -> 46.4 us
    pallas_call x3, Pallas kernels: 24 us -> 25.5 us  [bulk(): pl.pallas_call(functools.partial(bulk_kernel, dtheta, rows, first, total_...]
  transfers between devices with their start and end apart: 11 -> 11, of which waited for: 3 -> 3; matrix products, arithmetic and copies ran while one was open for 1% -> 1% of each run, Pallas kernels for 49% -> 50%
where the time goes in v6:
time: 74.5 us; the launch traced here: 74 us
  Pallas kernels  46.4 us (62%)
  starting transfers between devices  19.8 us (27%)
  waiting for transfers between devices  6.23 us (8%)
  local copies, waits for them, and re-layouts  1.15 us (2%)
    pallas_call x3, Pallas kernels, bulk(): pl.pallas_call(functools.partial(bulk_kernel, dtheta, rows, first, total_...  25.5 us
    pallas_call x1, Pallas kernels, near(): pl.pallas_call(functools.partial(near_kernel, dtheta, rows, part[0] if pa...  8.03 us
    pallas_call x1, Pallas kernels, pack_rest(): pl.pallas_call(functools.partial(pack_rest_kernel, parts, len(tokens)), i...  5.55 us
    ppermute x1, starting transfers between devices, body(): outer = [lax.ppermute(part, 'ax', outer_pairs)]  4.51 us
    ppermute x1, starting transfers between devices, body(): low = lax.ppermute(low, 'rad', up)  3.99 us
    ppermute x2, waiting for transfers between devices, ring(): lax.ppermute(value, axis, [(i, (i + shift) % size) for i in range(size)])  3.88 us
    ppermute x1, starting transfers between devices, body(): outer.append(lax.ppermute(part, 'ax', outer_pairs))  3.64 us
    pallas_call x1, Pallas kernels, pack_first(): pl.pallas_call(functools.partial(pack_first_kernel, count), in_specs=[ANY...  3.19 us
  transfers between devices with their start and end apart: 11, of which 3 were waited for; matrix products, arithmetic and copies ran while one was open for 1% of the time, Pallas kernels for 50%

profile of v6, /device:TPU:1, one launch (start us, length us, event | category | flops | bytes accessed | tf_op | source)
XLA Modules:
  0.0 74.0 jit_solution(17577304917694584451)
XLA Ops:
  0.0 3.2 %pack_first.1 = (f32[5,112,1024]{2,1,0:T(8,128)}, f32[10,1024]{1,0:T(8,128)S(1)}, f32[10,1024]{1,0:T(8,128)S(1)}) custom-call(f32[5,2,256,1024]{3,2,1,0:T(8,128)} %after.7), custom_call_target="tpu_custom_call" | custom-call | bytes 4587520 | tf_op jit(solution)/shard_map/pack_first/pallas_call | solution.py:390
  3.2 4.5 %collective-permute-start.5 = (f32[5,112,1024]{2,1,0:T(8,128)}, f32[5,112,1024]{2,1,0:T(8,128)S(1)}, u32[]{:S(2)}, u32[]{:S(2)}) collective-permute-start(f32[5,112,1024]{2,1,0:T(8,128)} %get-tuple-element.23), channel_id=1, source_target_pairs={{1,2},{2,1},{5,6},{6,5},{9,10},{10,9},{13,14},{14,13},{17,18},{18,... | collective-permute-start | bytes 6881288 | tf_op jit(solution)/shard_map/ppermute | solution.py:620
  7.7 1.3 %collective-permute-start.1 = (f32[10,1024]{1,0:T(8,128)S(1)}, f32[10,1024]{1,0:T(8,128)S(1)}, u32[]{:S(2)}, u32[]{:S(2)}) collective-permute-start(f32[10,1024]{1,0:T(8,128)S(1)} %get-tuple-element.19.token), channel_id=1, source_target_pairs={{4,0},{8,4},{12,8},{5,1},{9,5},{13,9},{6,2},{10,6},{14,10},{7,3},{... | collective-permute-start | bytes 122888 | tf_op jit(solution)/shard_map/ppermute | solution.py:623
  9.0 4.0 %collective-permute-start = (f32[10,1024]{1,0:T(8,128)S(1)}, f32[10,1024]{1,0:T(8,128)S(1)}, u32[]{:S(2)}, u32[]{:S(2)}) collective-permute-start(f32[10,1024]{1,0:T(8,128)S(1)} %get-tuple-element.18), channel_id=1, source_target_pairs={{0,4},{4,8},{8,12},{1,5},{5,9},{9,13},{2,6},{6,10},{10,14},{3,7},{... | collective-permute-start | bytes 122888 | tf_op jit(solution)/shard_map/ppermute | solution.py:622
  13.0 2.6 %pack_edges.1 = (f32[256,128]{1,0:T(8,128)S(1)}, f32[5,16,1024]{2,1,0:T(8,128)S(1)}) custom-call(f32[5,2,256,1024]{3,2,1,0:T(8,128)} %after.7, f32[10,1024]{1,0:T(8,128)S(1)} %get-tuple-element.19.token), custom_call_target="tpu_custom_call" | custom-call | bytes 5242880 | tf_op jit(solution)/shard_map/pack_edges/pallas_call | solution.py:406
  15.6 0.0 collective-permute-done.1.rest_2_.high
  15.6 0.0 collective-permute-done.rest_1_.low
  15.6 0.0 copy-start.2
  15.6 0.0 copy-start
  15.6 5.5 %pack_rest.1 = (f32[5,96,1024]{2,1,0:T(8,128)}, f32[5,96,1024]{2,1,0:T(8,128)}, f32[5,96,1024]{2,1,0:T(8,128)}, f32[5,48,1024]{2,1,0:T(8,128)S(1)}) custom-call(f32[5,2,256,1024]{3,2,1,0:T(8,128)} %after.7, f32[256,128]{1,0:T(8,128)S(1)} %get-tuple-element.20.rest_0_, f32[10,1024]{1,0:T(8,128)S(1)} %collective-permute-done.rest_1_.low, ...), custom_call_target="tpu_custom_call" | custom-call | bytes 13762560 | tf_op jit(solution)/shard_map/pack_rest/pallas_call | solution.py:424
  21.2 0.0 copy-start.1
  21.2 1.0 %copy-done.1 = f32[5,48,1024]{2,1,0:T(8,128)} copy-done((f32[5,48,1024]{2,1,0:T(8,128)}, f32[5,48,1024]{2,1,0:T(8,128)S(1)}, u32[]{:S(2)}) %copy-start.1) | copy-done | bytes 983064
  22.2 0.0 collective-permute-start.10
  22.2 0.5 collective-permute-start.8
  22.7 2.5 %collective-permute-start.9 = (f32[5,96,1024]{2,1,0:T(8,128)}, f32[5,96,1024]{2,1,0:T(8,128)}, u32[]{:S(2)}, u32[]{:S(2)}) collective-permute-start(f32[5,96,1024]{2,1,0:T(8,128)} %get-tuple-element.30), channel_id=1, source_target_pairs={{1,2},{2,1},{5,6},{6,5},{9,10},{10,9},{13,14},{14,13},{17,18},{18,... | collective-permute-start | bytes 5898248 | tf_op jit(solution)/shard_map/ppermute | solution.py:631
  25.1 1.3 %collective-permute-start.3 = (f32[256,128]{1,0:T(8,128)S(1)}, f32[256,128]{1,0:T(8,128)S(1)}, u32[]{:S(2)}, u32[]{:S(2)}) collective-permute-start(f32[256,128]{1,0:T(8,128)S(1)} %get-tuple-element.20.rest_0_), channel_id=1, source_target_pairs={{0,16},{16,0},{1,17},{17,1},{2,18},{18,2},{3,19},{19,3},{4,20},{20... | collective-permute-start | bytes 393224 | tf_op jit(solution)/shard_map/ppermute | solution.py:586
  26.5 0.0 copy-done.2
  26.6 0.1 stack.35.flags
  26.7 3.9 %collective-permute-done.3.edge = f32[256,128]{1,0:T(8,128)S(1)} collective-permute-done((f32[256,128]{1,0:T(8,128)S(1)}, f32[256,128]{1,0:T(8,128)S(1)}, u32[]{:S(2)}, u32[]{:S(2)}) %collective-permute-start.3) | collective-permute-done | bytes 131104 | tf_op jit(solution)/shard_map/ppermute | solution.py:586
  30.5 0.4 collective-permute-start.4
  30.9 0.1 fusion.3.table
  31.0 1.2 %collective-permute-done.4.inner = f32[5,16,1024]{2,1,0:T(8,128)S(1)} collective-permute-done((f32[5,16,1024]{2,1,0:T(8,128)S(1)}, f32[5,16,1024]{2,1,0:T(8,128)S(1)}, u32[]{:S(2)}, u32[]{:S(2)}) %collective-permute-start.4) | collective-permute-done | bytes 327712 | tf_op jit(solution)/shard_map/ppermute | solution.py:624
  32.2 0.4 collective-permute-start.2
  32.6 1.2 %collective-permute-done.5.outer = f32[5,112,1024]{2,1,0:T(8,128)S(1)} collective-permute-done((f32[5,112,1024]{2,1,0:T(8,128)}, f32[5,112,1024]{2,1,0:T(8,128)S(1)}, u32[]{:S(2)}, u32[]{:S(2)}) %collective-permute-start.5) | collective-permute-done | bytes 2293792 | tf_op jit(solution)/shard_map/ppermute | solution.py:620
  33.7 0.1 broadcast_in_dim.51.factor
  33.8 0.0 copy-done
  33.8 8.0 %near.1 = (f32[10,16,1024]{2,1,0:T(8,128)S(1)}, f32[10,16,1024]{2,1,0:T(8,128)S(1)}, f32[16,128]{1,0:T(8,128)S(1)}, f32[5,48,1024]{2,1,0:T(8,128)S(1)}) custom-call(s32[5]{0:T(128)S(1)} %stack.35.flags, f32[5,2,256,1024]{3,2,1,0:T(8,128)} %after.7, f32[5,2,256,1024]{3,2,1,0:T(8,128)} %after.7, f32[10,1024]{1,0:T(8,128)S(1)} %collective-permute-done.rest_1_.low, ...), custom_call_target="tpu_custom_call" | custom-call | flops 32768000 | bytes 40960000 | tf_op jit(solution)/shard_map/near/pallas_call | solution.py:493
  41.9 3.6 %collective-permute-start.6 = (f32[5,48,1024]{2,1,0:T(8,128)S(1)}, f32[5,48,1024]{2,1,0:T(8,128)S(1)}, u32[]{:S(2)}, u32[]{:S(2)}) collective-permute-start(f32[5,48,1024]{2,1,0:T(8,128)S(1)} %get-tuple-element.25), channel_id=1, source_target_pairs={{1,2},{2,1},{5,6},{6,5},{9,10},{10,9},{13,14},{14,13},{17,18},{18,... | collective-permute-start | bytes 2949128 | tf_op jit(solution)/shard_map/ppermute | solution.py:650
  45.5 0.0 collective-permute-done.10.inner
  45.5 1.3 %collective-permute-start.7 = (f32[16,128]{1,0:T(8,128)S(1)}, f32[16,128]{1,0:T(8,128)S(1)}, u32[]{:S(2)}, u32[]{:S(2)}) collective-permute-start(f32[16,128]{1,0:T(8,128)S(1)} %get-tuple-element.26.token), channel_id=1, source_target_pairs={{0,16},{16,0},{1,17},{17,1},{2,18},{18,2},{3,19},{19,3},{4,20},{20... | collective-permute-start | bytes 24584 | tf_op jit(solution)/shard_map/ppermute | solution.py:586
  46.8 9.6 %bulk.3.held = f32[5,2,256,1024]{3,2,1,0:T(8,128)} custom-call(s32[5]{0:T(128)S(1)} %stack.35.flags, f32[5,2,256,1024]{3,2,1,0:T(8,128)} %after.7, f32[5,2,256,1024]{3,2,1,0:T(8,128)} %after.7, f32[5,2,256,1024]{3,2,1,0:T(8,128)} %after.7, f32[10,1024]{1,0:T(8,128)S(1)} %collective-permute-done.rest_1_.low, ...), custom_call_target="tpu_custom_call" | custom-call | flops 58982400 | bytes 58982400 | tf_op jit(solution)/shard_map/bulk/pallas_call | solution.py:464
  56.4 0.0 collective-permute-done.8.inner
  56.4 0.0 collective-permute-done.9.outer
  56.4 9.9 %bulk.4.held = f32[5,2,256,1024]{3,2,1,0:T(8,128)} custom-call(s32[5]{0:T(128)S(1)} %stack.35.flags, f32[5,2,256,1024]{3,2,1,0:T(8,128)} %after.7, f32[5,2,256,1024]{3,2,1,0:T(8,128)} %after.7, f32[5,2,256,1024]{3,2,1,0:T(8,128)} %after.7, f32[10,1024]{1,0:T(8,128)S(1)} %collective-permute-done.rest_1_.low, ...), custom_call_target="tpu_custom_call", output_to_operand_aliasing={{}: (10, {})} | custom-call | flops 58982400 | bytes 58982400 | tf_op jit(solution)/shard_map/bulk/pallas_call | solution.py:464
  66.4 0.0 collective-permute-done.7
  66.4 0.1 add_multiply_fusion.carry
  66.4 1.6 %finish.1.held = f32[5,2,256,1024]{3,2,1,0:T(8,128)} custom-call(s32[5]{0:T(128)S(1)} %stack.35.flags, f32[16,128]{1,0:T(8,128)S(1)} %broadcast_in_dim.51.factor, f32[10,16,1024]{2,1,0:T(8,128)S(1)} %get-tuple-element.27.rhs, f32[10,16,1024]{2,1,0:T(8,128)S(1)} %get-tuple-element.28.local, ...), custom_call_target="tpu_custom_call", output_to_operand_aliasing={{}: (6, {})} | custom-call | flops 1638400 | bytes 3276800 | tf_op jit(solution)/shard_map/finish/pallas_call | solution.py:525
  68.1 0.0 collective-permute-done.2.inner
  68.1 0.0 collective-permute-done.6.outer
  68.1 5.9 %bulk.5 = f32[5,2,256,1024]{3,2,1,0:T(8,128)} custom-call(s32[5]{0:T(128)S(1)} %stack.35.flags, f32[5,2,256,1024]{3,2,1,0:T(8,128)} %after.7, f32[5,2,256,1024]{3,2,1,0:T(8,128)} %after.7, f32[5,2,256,1024]{3,2,1,0:T(8,128)} %after.7, f32[10,1024]{1,0:T(8,128)S(1)} %collective-permute-done.rest_1_.low, ...), custom_call_target="tpu_custom_call", output_to_operand_aliasing={{}: (10, {})} | custom-call | flops 29491200 | bytes 29491200 | tf_op jit(solution)/shard_map/bulk/pallas_call | solution.py:464
  (5 shorter events, 0.1 us)
Async XLA Ops:
  3.2 30.5 %collective-permute-start.5 = (f32[5,112,1024]{2,1,0:T(8,128)}, f32[5,112,1024]{2,1,0:T(8,128)S(1)}, u32[]{:S(2)}, u32[]{:S(2)}) collective-permute-start(f32[5,112,1024]{2,1,0:T(8,128)} %get-tuple-element.23), channel_id=1, source_target_pairs={{1,2},{2,1},{5,6},{6,5},{9,10},{10,9},{13,14},{14,13},{17,18},{18,... | collective-permute-start | bytes 6881288 | tf_op jit(solution)/shard_map/ppermute | solution.py:620
  7.7 7.9 %collective-permute-start.1 = (f32[10,1024]{1,0:T(8,128)S(1)}, f32[10,1024]{1,0:T(8,128)S(1)}, u32[]{:S(2)}, u32[]{:S(2)}) collective-permute-start(f32[10,1024]{1,0:T(8,128)S(1)} %get-tuple-element.19.token), channel_id=1, source_target_pairs={{4,0},{8,4},{12,8},{5,1},{9,5},{13,9},{6,2},{10,6},{14,10},{7,3},{... | collective-permute-start | bytes 122888 | tf_op jit(solution)/shard_map/ppermute | solution.py:623
  9.0 6.6 %collective-permute-start = (f32[10,1024]{1,0:T(8,128)S(1)}, f32[10,1024]{1,0:T(8,128)S(1)}, u32[]{:S(2)}, u32[]{:S(2)}) collective-permute-start(f32[10,1024]{1,0:T(8,128)S(1)} %get-tuple-element.18), channel_id=1, source_target_pairs={{0,4},{4,8},{8,12},{1,5},{5,9},{9,13},{2,6},{6,10},{10,14},{3,7},{... | collective-permute-start | bytes 122888 | tf_op jit(solution)/shard_map/ppermute | solution.py:622
  15.6 10.9 %copy-start.2 = (s32[16]{0:T(128)S(1)}, s32[16]{0:T(128)}, u32[]{:S(2)}) copy-start(s32[16]{0:T(128)} %param.4) | copy-start | bytes 196
  15.6 18.2 %copy-start = (f32[128,640]{1,0:T(8,128)S(1)}, f32[128,640]{1,0:T(8,128)}, u32[]{:S(2)}) copy-start(f32[128,640]{1,0:T(8,128)} %constant.54.clone.solve) | copy-start | bytes 983044
  21.2 1.0 %copy-start.1 = (f32[5,48,1024]{2,1,0:T(8,128)}, f32[5,48,1024]{2,1,0:T(8,128)S(1)}, u32[]{:S(2)}) copy-start(f32[5,48,1024]{2,1,0:T(8,128)S(1)} %get-tuple-element.21) | copy-start | bytes 2949124
  22.2 23.3 %collective-permute-start.10 = (f32[5,96,1024]{2,1,0:T(8,128)}, f32[5,96,1024]{2,1,0:T(8,128)}, u32[]{:S(2)}, u32[]{:S(2)}) collective-permute-start(f32[5,96,1024]{2,1,0:T(8,128)} %get-tuple-element.24.token), channel_id=1, source_target_pairs={{0,1},{1,0},{2,3},{3,2},{4,5},{5,4},{6,7},{7,6},{8,9},{9,8},{10,11... | collective-permute-start | bytes 5898248 | tf_op jit(solution)/shard_map/ppermute | solution.py:633
  22.2 34.3 %collective-permute-start.8 = (f32[5,96,1024]{2,1,0:T(8,128)}, f32[5,96,1024]{2,1,0:T(8,128)}, u32[]{:S(2)}, u32[]{:S(2)}) collective-permute-start(f32[5,96,1024]{2,1,0:T(8,128)} %get-tuple-element.29), channel_id=1, source_target_pairs={{0,1},{1,0},{2,3},{3,2},{4,5},{5,4},{6,7},{7,6},{8,9},{9,8},{10,11... | collective-permute-start | bytes 5898248 | tf_op jit(solution)/shard_map/ppermute | solution.py:633
  22.7 33.8 %collective-permute-start.9 = (f32[5,96,1024]{2,1,0:T(8,128)}, f32[5,96,1024]{2,1,0:T(8,128)}, u32[]{:S(2)}, u32[]{:S(2)}) collective-permute-start(f32[5,96,1024]{2,1,0:T(8,128)} %get-tuple-element.30), channel_id=1, source_target_pairs={{1,2},{2,1},{5,6},{6,5},{9,10},{10,9},{13,14},{14,13},{17,18},{18,... | collective-permute-start | bytes 5898248 | tf_op jit(solution)/shard_map/ppermute | solution.py:631
  25.1 5.4 %collective-permute-start.3 = (f32[256,128]{1,0:T(8,128)S(1)}, f32[256,128]{1,0:T(8,128)S(1)}, u32[]{:S(2)}, u32[]{:S(2)}) collective-permute-start(f32[256,128]{1,0:T(8,128)S(1)} %get-tuple-element.20.rest_0_), channel_id=1, source_target_pairs={{0,16},{16,0},{1,17},{17,1},{2,18},{18,2},{3,19},{19,3},{4,20},{20... | collective-permute-start | bytes 393224 | tf_op jit(solution)/shard_map/ppermute | solution.py:586
  30.5 1.7 %collective-permute-start.4 = (f32[5,16,1024]{2,1,0:T(8,128)S(1)}, f32[5,16,1024]{2,1,0:T(8,128)S(1)}, u32[]{:S(2)}, u32[]{:S(2)}) collective-permute-start(f32[5,16,1024]{2,1,0:T(8,128)S(1)} %get-tuple-element.22), channel_id=1, source_target_pairs={{0,1},{1,0},{2,3},{3,2},{4,5},{5,4},{6,7},{7,6},{8,9},{9,8},{10,11... | collective-permute-start | bytes 983048 | tf_op jit(solution)/shard_map/ppermute | solution.py:624
  32.2 35.9 %collective-permute-start.2 = (f32[5,48,1024]{2,1,0:T(8,128)}, f32[5,48,1024]{2,1,0:T(8,128)S(1)}, u32[]{:S(2)}, u32[]{:S(2)}) collective-permute-start(f32[5,48,1024]{2,1,0:T(8,128)} %copy-done.1), channel_id=1, source_target_pairs={{0,1},{1,0},{2,3},{3,2},{4,5},{5,4},{6,7},{7,6},{8,9},{9,8},{10,11... | collective-permute-start | bytes 2949128 | tf_op jit(solution)/shard_map/ppermute | solution.py:633
  41.9 26.2 %collective-permute-start.6 = (f32[5,48,1024]{2,1,0:T(8,128)S(1)}, f32[5,48,1024]{2,1,0:T(8,128)S(1)}, u32[]{:S(2)}, u32[]{:S(2)}) collective-permute-start(f32[5,48,1024]{2,1,0:T(8,128)S(1)} %get-tuple-element.25), channel_id=1, source_target_pairs={{1,2},{2,1},{5,6},{6,5},{9,10},{10,9},{13,14},{14,13},{17,18},{18,... | collective-permute-start | bytes 2949128 | tf_op jit(solution)/shard_map/ppermute | solution.py:650
  45.5 20.8 %collective-permute-start.7 = (f32[16,128]{1,0:T(8,128)S(1)}, f32[16,128]{1,0:T(8,128)S(1)}, u32[]{:S(2)}, u32[]{:S(2)}) collective-permute-start(f32[16,128]{1,0:T(8,128)S(1)} %get-tuple-element.26.token), channel_id=1, source_target_pairs={{0,16},{16,0},{1,17},{17,1},{2,18},{18,2},{3,19},{19,3},{4,20},{20... | collective-permute-start | bytes 24584 | tf_op jit(solution)/shard_map/ppermute | solution.py:586

commit v7 on v6

--- a/solution.py
+++ b/solution.py
@@ -149,21 +149,53 @@
 
 
 def bulk_kernel(
-    dtheta, rows, first, total_rows, flags, state, before, after, low, high, inner, edge, outer, token, held, out, *scratch
+    dtheta, rows, span, origin, total_rows, flags, state, low, high, inner, edge, outer, token, held, out, *scratch
 ):
+    first, end = span
+    blocks = (end - first) // rows
+    state_rows, inner_rows, outer_rows, sems, *fluxes_scratch = scratch
     odd = flags[ODD]
     step = pl.program_id(0)
+
+    def copies(k):
+        a = first + k * rows + (EIGHT if k else -EIGHT)
+        b = min(first + (k + 1) * rows + EIGHT, total_rows)
+        at = a - first + EIGHT
+        rest = pl.ds(first - origin + k * rows, rows)
+        here = pl.ds(k * rows, rows)
+        return [
+            pltpu.make_async_copy(
+                state.at[:, :, a:b, :], state_rows.at[:, :, at : at + b - a, :], sems.at[3 * k]
+            ),
+            pltpu.make_async_copy(inner.at[:, here, :], inner_rows.at[:, here, :], sems.at[3 * k + 1]),
+            pltpu.make_async_copy(outer.at[:, rest, :], outer_rows.at[:, here, :], sems.at[3 * k + 2]),
+        ]
+
+    @pl.when(step == 0)
+    def _():
+        for k in range(blocks):
+            for copy in copies(k):
+                copy.start()
+
+    for k in range(blocks):
+
+        @pl.when(step == k)
+        def _():
+            for copy in copies(k):
+                copy.wait()
+
     first_row = first + step * rows
     at_end = first_row + rows == total_rows
+    base = pl.multiple_of(step * rows, EIGHT)
     sub = lax.broadcasted_iota(jnp.int32, (EIGHT, LANES), 0)
 
     def load(f, q, r, at):
-        return state[f, plane_of(odd, q), pl.ds(r, EIGHT), at]
+        return state_rows[f, plane_of(odd, q), pl.ds(base + EIGHT + r, EIGHT), at]
 
     def next_rows(f, q, at):
-        p, k = plane_of(odd, q), f * PLANES + q
-        under = jnp.where(at_end, high[k : k + 1, at], after[f, p, :, at])
-        return jnp.where(sub >= EIGHT // 2, before[f, p, :, at], under)
+        k = f * PLANES + q
+        under = jnp.where(at_end, high[k : k + 1, at], load(f, q, rows, at))
+        return jnp.where(sub >= EIGHT // 2, load(f, q, -EIGHT, at), under)
 
     stencil(
         flags,
@@ -174,10 +206,10 @@
         load,
         next_rows,
         lambda r: edge[pl.ds(r, EIGHT), :],
-        lambda f, r, at: inner[f, pl.ds(r, EIGHT), at],
-        lambda f, r, at: outer[f, pl.ds(r, EIGHT), at],
+        lambda f, r, at: inner_rows[f, pl.ds(base + r, EIGHT), at],
+        lambda f, r, at: outer_rows[f, pl.ds(base + r, EIGHT), at],
         lambda f, q, r: out.at[f, plane_of(odd, q), pl.ds(r, EIGHT), :],
-        *scratch,
+        *fluxes_scratch,
     )
 
 
@@ -440,40 +472,41 @@
 
 def bulk(flags, state, low, high, inner, edge, dtheta, outer, span, first, rows, token, held):
     fields, planes, total_rows, cells = state.shape
-    end = span[1]
-    tail = total_rows // EIGHT - 1
-    eights = rows // EIGHT
-    at = first // EIGHT
-    row_block = (fields, planes, EIGHT, cells)
-    in_specs = [
-        rows_from((fields, planes, rows, cells), 2, first, rows),
-        pl.BlockSpec(row_block, lambda i, s: (0, 0, at + i * eights - 1, 0)),
-        pl.BlockSpec(row_block, lambda i, s: (0, 0, jnp.minimum(at + (i + 1) * eights, tail), 0)),
-        whole(LINES, cells),
-        whole(LINES, cells),
-        rows_from((fields, rows, cells), 1, 0, rows),
-        rows_from((rows, LANES), 0, first, rows),
-        rows_from((fields, rows, cells), 1, first - span[0], rows),
-        ANY,
-        ANY,
-    ]
+    origin, end = span
+    count = end - first
+    blocks = count // rows
+    size = fields * planes * count * cells
+    aliases = {} if held is None else {8: 0}
     state = in_hbm(state)
-    operands = [state, state, state, low, high, inner, edge, outer]
-    operands += [token, state if held is None else held]
-    size = fields * planes * (end - first) * cells
+    operands = [state, low, high, inner, edge, outer, token, state if held is None else held]
     return pl.pallas_call(
-        functools.partial(bulk_kernel, dtheta, rows, first, total_rows),
+        functools.partial(bulk_kernel, dtheta, rows, (first, end), origin, total_rows),
         grid_spec=pltpu.PrefetchScalarGridSpec(
             num_scalar_prefetch=1,
-            grid=((end - first) // rows,),
-            in_specs=in_specs,
+            grid=(blocks,),
+            in_specs=[
+                ANY,
+                whole(LINES, cells),
+                whole(LINES, cells),
+                ANY,
+                rows_from((rows, LANES), 0, first, rows),
+                ANY,
+                ANY,
+                ANY,
+            ],
             out_specs=rows_from((fields, planes, rows, cells), 2, first, rows),
-            scratch_shapes=flux_scratch(rows, cells),
+            scratch_shapes=[
+                pltpu.VMEM((fields, planes, count + 2 * EIGHT, cells), jnp.float32),
+                pltpu.VMEM((fields, count, cells), jnp.float32),
+                pltpu.VMEM((fields, count, cells), jnp.float32),
+                pltpu.SemaphoreType.DMA((3 * blocks,)),
+                *flux_scratch(rows, cells),
+            ],
         ),
         out_shape=pltpu.HBM(state.shape, jnp.float32),
-        input_output_aliases={} if held is None else {len(operands): 0},
+        input_output_aliases=aliases,
         compiler_params=PARAMS,
-        cost_estimate=cost(size * 60, size * 60),
+        cost_estimate=cost(size * 60, size * 10),
         name="bulk",
     )(flags, *operands)
 

time: 74.5 us -> 73.5 us (0.987)
  Pallas kernels: 46.4 us -> 45.6 us
    pallas_call x3, Pallas kernels: 25.5 us -> 24.6 us  [bulk(): pl.pallas_call(functools.partial(bulk_kernel, dtheta, rows, (first, end),...]
where the time goes in v7:
time: 73.5 us; the launch traced here: 73.2 us
  Pallas kernels  45.6 us (62%)
  starting transfers between devices  19.8 us (27%)
  waiting for transfers between devices  6.23 us (8%)
  local copies, waits for them, and re-layouts  1.15 us (2%)
    pallas_call x3, Pallas kernels, bulk(): pl.pallas_call(functools.partial(bulk_kernel, dtheta, rows, (first, end),...  24.6 us
    pallas_call x1, Pallas kernels, near(): pl.pallas_call(functools.partial(near_kernel, dtheta, rows, part[0] if pa...  8.03 us
    pallas_call x1, Pallas kernels, pack_rest(): pl.pallas_call(functools.partial(pack_rest_kernel, parts, len(tokens)), i...  5.55 us
    ppermute x1, starting transfers between devices, body(): outer = [lax.ppermute(part, 'ax', outer_pairs)]  4.51 us
    ppermute x1, starting transfers between devices, body(): low = lax.ppermute(low, 'rad', up)  3.99 us
    ppermute x2, waiting for transfers between devices, ring(): lax.ppermute(value, axis, [(i, (i + shift) % size) for i in range(size)])  3.88 us
    ppermute x1, starting transfers between devices, body(): outer.append(lax.ppermute(part, 'ax', outer_pairs))  3.64 us
    pallas_call x1, Pallas kernels, pack_first(): pl.pallas_call(functools.partial(pack_first_kernel, count), in_specs=[ANY...  3.19 us
  transfers between devices with their start and end apart: 11, of which 3 were waited for; matrix products, arithmetic and copies ran while one was open for 1% of the time, Pallas kernels for 50%

profile of v7, /device:TPU:1, one launch (start us, length us, event | category | flops | bytes accessed | tf_op | source)
XLA Modules:
  0.0 73.2 jit_solution(5481474712919685581)
XLA Ops:
  0.0 3.2 %pack_first.1 = (f32[5,112,1024]{2,1,0:T(8,128)}, f32[10,1024]{1,0:T(8,128)S(1)}, f32[10,1024]{1,0:T(8,128)S(1)}) custom-call(f32[5,2,256,1024]{3,2,1,0:T(8,128)} %state.13), custom_call_target="tpu_custom_call" | custom-call | bytes 4587520 | tf_op jit(solution)/shard_map/pack_first/pallas_call | solution.py:422
  3.2 4.5 %collective-permute-start.5 = (f32[5,112,1024]{2,1,0:T(8,128)}, f32[5,112,1024]{2,1,0:T(8,128)S(1)}, u32[]{:S(2)}, u32[]{:S(2)}) collective-permute-start(f32[5,112,1024]{2,1,0:T(8,128)} %get-tuple-element.23), channel_id=1, source_target_pairs={{1,2},{2,1},{5,6},{6,5},{9,10},{10,9},{13,14},{14,13},{17,18},{18,... | collective-permute-start | bytes 6881288 | tf_op jit(solution)/shard_map/ppermute | solution.py:653
  7.7 1.3 %collective-permute-start.1 = (f32[10,1024]{1,0:T(8,128)S(1)}, f32[10,1024]{1,0:T(8,128)S(1)}, u32[]{:S(2)}, u32[]{:S(2)}) collective-permute-start(f32[10,1024]{1,0:T(8,128)S(1)} %get-tuple-element.19.token), channel_id=1, source_target_pairs={{4,0},{8,4},{12,8},{5,1},{9,5},{13,9},{6,2},{10,6},{14,10},{7,3},{... | collective-permute-start | bytes 122888 | tf_op jit(solution)/shard_map/ppermute | solution.py:656
  9.0 4.0 %collective-permute-start = (f32[10,1024]{1,0:T(8,128)S(1)}, f32[10,1024]{1,0:T(8,128)S(1)}, u32[]{:S(2)}, u32[]{:S(2)}) collective-permute-start(f32[10,1024]{1,0:T(8,128)S(1)} %get-tuple-element.18), channel_id=1, source_target_pairs={{0,4},{4,8},{8,12},{1,5},{5,9},{9,13},{2,6},{6,10},{10,14},{3,7},{... | collective-permute-start | bytes 122888 | tf_op jit(solution)/shard_map/ppermute | solution.py:655
  13.0 2.6 %pack_edges.1 = (f32[256,128]{1,0:T(8,128)S(1)}, f32[5,16,1024]{2,1,0:T(8,128)S(1)}) custom-call(f32[5,2,256,1024]{3,2,1,0:T(8,128)} %state.13, f32[10,1024]{1,0:T(8,128)S(1)} %get-tuple-element.19.token), custom_call_target="tpu_custom_call" | custom-call | bytes 5242880 | tf_op jit(solution)/shard_map/pack_edges/pallas_call | solution.py:438
  15.6 0.0 collective-permute-done.1.rest_2_.high
  15.6 0.0 collective-permute-done.rest_1_.low
  15.6 0.0 copy-start.2
  15.6 0.0 copy-start
  15.6 5.5 %pack_rest.1 = (f32[5,96,1024]{2,1,0:T(8,128)}, f32[5,96,1024]{2,1,0:T(8,128)}, f32[5,96,1024]{2,1,0:T(8,128)}, f32[5,48,1024]{2,1,0:T(8,128)S(1)}) custom-call(f32[5,2,256,1024]{3,2,1,0:T(8,128)} %state.13, f32[256,128]{1,0:T(8,128)S(1)} %get-tuple-element.20.rest_0_, f32[10,1024]{1,0:T(8,128)S(1)} %collective-permute-done.rest_1_.low, ...), custom_call_target="tpu_custom_call" | custom-call | bytes 13762560 | tf_op jit(solution)/shard_map/pack_rest/pallas_call | solution.py:456
  21.2 0.0 copy-start.1
  21.2 1.0 %copy-done.1 = f32[5,48,1024]{2,1,0:T(8,128)} copy-done((f32[5,48,1024]{2,1,0:T(8,128)}, f32[5,48,1024]{2,1,0:T(8,128)S(1)}, u32[]{:S(2)}) %copy-start.1) | copy-done | bytes 983064
  22.2 0.0 collective-permute-start.10
  22.2 0.5 collective-permute-start.8
  22.7 2.5 %collective-permute-start.9 = (f32[5,96,1024]{2,1,0:T(8,128)}, f32[5,96,1024]{2,1,0:T(8,128)}, u32[]{:S(2)}, u32[]{:S(2)}) collective-permute-start(f32[5,96,1024]{2,1,0:T(8,128)} %get-tuple-element.30), channel_id=1, source_target_pairs={{1,2},{2,1},{5,6},{6,5},{9,10},{10,9},{13,14},{14,13},{17,18},{18,... | collective-permute-start | bytes 5898248 | tf_op jit(solution)/shard_map/ppermute | solution.py:664
  25.1 1.3 %collective-permute-start.3 = (f32[256,128]{1,0:T(8,128)S(1)}, f32[256,128]{1,0:T(8,128)S(1)}, u32[]{:S(2)}, u32[]{:S(2)}) collective-permute-start(f32[256,128]{1,0:T(8,128)S(1)} %get-tuple-element.20.rest_0_), channel_id=1, source_target_pairs={{0,16},{16,0},{1,17},{17,1},{2,18},{18,2},{3,19},{19,3},{4,20},{20... | collective-permute-start | bytes 393224 | tf_op jit(solution)/shard_map/ppermute | solution.py:619
  26.5 0.0 copy-done.2
  26.6 0.1 stack.35.flags
  26.7 3.9 %collective-permute-done.3.edge = f32[256,128]{1,0:T(8,128)S(1)} collective-permute-done((f32[256,128]{1,0:T(8,128)S(1)}, f32[256,128]{1,0:T(8,128)S(1)}, u32[]{:S(2)}, u32[]{:S(2)}) %collective-permute-start.3) | collective-permute-done | bytes 131104 | tf_op jit(solution)/shard_map/ppermute | solution.py:619
  30.5 0.4 collective-permute-start.4
  30.9 0.1 fusion.3.table
  31.0 1.2 %collective-permute-done.4.inner = f32[5,16,1024]{2,1,0:T(8,128)S(1)} collective-permute-done((f32[5,16,1024]{2,1,0:T(8,128)S(1)}, f32[5,16,1024]{2,1,0:T(8,128)S(1)}, u32[]{:S(2)}, u32[]{:S(2)}) %collective-permute-start.4) | collective-permute-done | bytes 327712 | tf_op jit(solution)/shard_map/ppermute | solution.py:657
  32.2 0.4 collective-permute-start.2
  32.6 1.2 %collective-permute-done.5.outer = f32[5,112,1024]{2,1,0:T(8,128)S(1)} collective-permute-done((f32[5,112,1024]{2,1,0:T(8,128)}, f32[5,112,1024]{2,1,0:T(8,128)S(1)}, u32[]{:S(2)}, u32[]{:S(2)}) %collective-permute-start.5) | collective-permute-done | bytes 2293792 | tf_op jit(solution)/shard_map/ppermute | solution.py:653
  33.7 0.1 broadcast_in_dim.51.factor
  33.8 0.0 copy-done
  33.8 8.0 %near.1 = (f32[10,16,1024]{2,1,0:T(8,128)S(1)}, f32[10,16,1024]{2,1,0:T(8,128)S(1)}, f32[16,128]{1,0:T(8,128)S(1)}, f32[5,48,1024]{2,1,0:T(8,128)S(1)}) custom-call(s32[5]{0:T(128)S(1)} %stack.35.flags, f32[5,2,256,1024]{3,2,1,0:T(8,128)} %state.13, f32[5,2,256,1024]{3,2,1,0:T(8,128)} %state.13, f32[10,1024]{1,0:T(8,128)S(1)} %collective-permute-done.rest_1_.low, ...), custom_call_target="tpu_custom_call" | custom-call | flops 32768000 | bytes 40960000 | tf_op jit(solution)/shard_map/near/pallas_call | solution.py:526
  41.9 3.6 %collective-permute-start.6 = (f32[5,48,1024]{2,1,0:T(8,128)S(1)}, f32[5,48,1024]{2,1,0:T(8,128)S(1)}, u32[]{:S(2)}, u32[]{:S(2)}) collective-permute-start(f32[5,48,1024]{2,1,0:T(8,128)S(1)} %get-tuple-element.25), channel_id=1, source_target_pairs={{1,2},{2,1},{5,6},{6,5},{9,10},{10,9},{13,14},{14,13},{17,18},{18,... | collective-permute-start | bytes 2949128 | tf_op jit(solution)/shard_map/ppermute | solution.py:683
  45.5 0.0 collective-permute-done.10.inner
  45.5 1.3 %collective-permute-start.7 = (f32[16,128]{1,0:T(8,128)S(1)}, f32[16,128]{1,0:T(8,128)S(1)}, u32[]{:S(2)}, u32[]{:S(2)}) collective-permute-start(f32[16,128]{1,0:T(8,128)S(1)} %get-tuple-element.26.token), channel_id=1, source_target_pairs={{0,16},{16,0},{1,17},{17,1},{2,18},{18,2},{3,19},{19,3},{4,20},{20... | collective-permute-start | bytes 24584 | tf_op jit(solution)/shard_map/ppermute | solution.py:619
  46.8 9.2 %bulk.3.held = f32[5,2,256,1024]{3,2,1,0:T(8,128)} custom-call(s32[5]{0:T(128)S(1)} %stack.35.flags, f32[5,2,256,1024]{3,2,1,0:T(8,128)} %state.13, f32[10,1024]{1,0:T(8,128)S(1)} %collective-permute-done.rest_1_.low, f32[10,1024]{1,0:T(8,128)S(1)} %collective-permute-done.1.rest_2_.high, f32[5,96,1024]{2,1,0:T(8,128)} %collective-permute-done.10.inner, ...), custom_call_target="tpu_custom_call" | custom-call | flops 58982400 | bytes 9830400 | tf_op jit(solution)/shard_map/bulk/pallas_call | solution.py:482
  56.0 0.0 collective-permute-done.8.inner
  56.0 0.0 collective-permute-done.9.outer
  56.0 9.4 %bulk.4.held = f32[5,2,256,1024]{3,2,1,0:T(8,128)} custom-call(s32[5]{0:T(128)S(1)} %stack.35.flags, f32[5,2,256,1024]{3,2,1,0:T(8,128)} %state.13, f32[10,1024]{1,0:T(8,128)S(1)} %collective-permute-done.rest_1_.low, f32[10,1024]{1,0:T(8,128)S(1)} %collective-permute-done.1.rest_2_.high, ...), custom_call_target="tpu_custom_call", output_to_operand_aliasing={{}: (8, {})} | custom-call | flops 58982400 | bytes 9830400 | tf_op jit(solution)/shard_map/bulk/pallas_call | solution.py:482
  65.5 0.0 collective-permute-done.7
  65.5 0.1 add_multiply_fusion.carry
  65.5 1.6 %finish.1.held = f32[5,2,256,1024]{3,2,1,0:T(8,128)} custom-call(s32[5]{0:T(128)S(1)} %stack.35.flags, f32[16,128]{1,0:T(8,128)S(1)} %broadcast_in_dim.51.factor, f32[10,16,1024]{2,1,0:T(8,128)S(1)} %get-tuple-element.27.rhs, f32[10,16,1024]{2,1,0:T(8,128)S(1)} %get-tuple-element.28.local, ...), custom_call_target="tpu_custom_call", output_to_operand_aliasing={{}: (6, {})} | custom-call | flops 1638400 | bytes 3276800 | tf_op jit(solution)/shard_map/finish/pallas_call | solution.py:558
  67.2 0.0 collective-permute-done.2.inner
  67.2 0.0 collective-permute-done.6.outer
  67.2 6.0 %bulk.5 = f32[5,2,256,1024]{3,2,1,0:T(8,128)} custom-call(s32[5]{0:T(128)S(1)} %stack.35.flags, f32[5,2,256,1024]{3,2,1,0:T(8,128)} %state.13, f32[10,1024]{1,0:T(8,128)S(1)} %collective-permute-done.rest_1_.low, f32[10,1024]{1,0:T(8,128)S(1)} %collective-permute-done.1.rest_2_.high, ...), custom_call_target="tpu_custom_call", output_to_operand_aliasing={{}: (8, {})} | custom-call | flops 29491200 | bytes 4915200 | tf_op jit(solution)/shard_map/bulk/pallas_call | solution.py:482
  (5 shorter events, 0.1 us)
Async XLA Ops:
  3.2 30.5 %collective-permute-start.5 = (f32[5,112,1024]{2,1,0:T(8,128)}, f32[5,112,1024]{2,1,0:T(8,128)S(1)}, u32[]{:S(2)}, u32[]{:S(2)}) collective-permute-start(f32[5,112,1024]{2,1,0:T(8,128)} %get-tuple-element.23), channel_id=1, source_target_pairs={{1,2},{2,1},{5,6},{6,5},{9,10},{10,9},{13,14},{14,13},{17,18},{18,... | collective-permute-start | bytes 6881288 | tf_op jit(solution)/shard_map/ppermute | solution.py:653
  7.7 7.9 %collective-permute-start.1 = (f32[10,1024]{1,0:T(8,128)S(1)}, f32[10,1024]{1,0:T(8,128)S(1)}, u32[]{:S(2)}, u32[]{:S(2)}) collective-permute-start(f32[10,1024]{1,0:T(8,128)S(1)} %get-tuple-element.19.token), channel_id=1, source_target_pairs={{4,0},{8,4},{12,8},{5,1},{9,5},{13,9},{6,2},{10,6},{14,10},{7,3},{... | collective-permute-start | bytes 122888 | tf_op jit(solution)/shard_map/ppermute | solution.py:656
  9.0 6.6 %collective-permute-start = (f32[10,1024]{1,0:T(8,128)S(1)}, f32[10,1024]{1,0:T(8,128)S(1)}, u32[]{:S(2)}, u32[]{:S(2)}) collective-permute-start(f32[10,1024]{1,0:T(8,128)S(1)} %get-tuple-element.18), channel_id=1, source_target_pairs={{0,4},{4,8},{8,12},{1,5},{5,9},{9,13},{2,6},{6,10},{10,14},{3,7},{... | collective-permute-start | bytes 122888 | tf_op jit(solution)/shard_map/ppermute | solution.py:655
  15.6 10.9 %copy-start.2 = (s32[16]{0:T(128)S(1)}, s32[16]{0:T(128)}, u32[]{:S(2)}) copy-start(s32[16]{0:T(128)} %param.4) | copy-start | bytes 196
  15.6 18.2 %copy-start = (f32[128,640]{1,0:T(8,128)S(1)}, f32[128,640]{1,0:T(8,128)}, u32[]{:S(2)}) copy-start(f32[128,640]{1,0:T(8,128)} %constant.54.clone.solve) | copy-start | bytes 983044
  21.2 1.0 %copy-start.1 = (f32[5,48,1024]{2,1,0:T(8,128)}, f32[5,48,1024]{2,1,0:T(8,128)S(1)}, u32[]{:S(2)}) copy-start(f32[5,48,1024]{2,1,0:T(8,128)S(1)} %get-tuple-element.21) | copy-start | bytes 2949124
  22.2 23.3 %collective-permute-start.10 = (f32[5,96,1024]{2,1,0:T(8,128)}, f32[5,96,1024]{2,1,0:T(8,128)}, u32[]{:S(2)}, u32[]{:S(2)}) collective-permute-start(f32[5,96,1024]{2,1,0:T(8,128)} %get-tuple-element.24.token), channel_id=1, source_target_pairs={{0,1},{1,0},{2,3},{3,2},{4,5},{5,4},{6,7},{7,6},{8,9},{9,8},{10,11... | collective-permute-start | bytes 5898248 | tf_op jit(solution)/shard_map/ppermute | solution.py:666
  22.2 33.9 %collective-permute-start.8 = (f32[5,96,1024]{2,1,0:T(8,128)}, f32[5,96,1024]{2,1,0:T(8,128)}, u32[]{:S(2)}, u32[]{:S(2)}) collective-permute-start(f32[5,96,1024]{2,1,0:T(8,128)} %get-tuple-element.29), channel_id=1, source_target_pairs={{0,1},{1,0},{2,3},{3,2},{4,5},{5,4},{6,7},{7,6},{8,9},{9,8},{10,11... | collective-permute-start | bytes 5898248 | tf_op jit(solution)/shard_map/ppermute | solution.py:666
  22.7 33.4 %collective-permute-start.9 = (f32[5,96,1024]{2,1,0:T(8,128)}, f32[5,96,1024]{2,1,0:T(8,128)}, u32[]{:S(2)}, u32[]{:S(2)}) collective-permute-start(f32[5,96,1024]{2,1,0:T(8,128)} %get-tuple-element.30), channel_id=1, source_target_pairs={{1,2},{2,1},{5,6},{6,5},{9,10},{10,9},{13,14},{14,13},{17,18},{18,... | collective-permute-start | bytes 5898248 | tf_op jit(solution)/shard_map/ppermute | solution.py:664
  25.1 5.4 %collective-permute-start.3 = (f32[256,128]{1,0:T(8,128)S(1)}, f32[256,128]{1,0:T(8,128)S(1)}, u32[]{:S(2)}, u32[]{:S(2)}) collective-permute-start(f32[256,128]{1,0:T(8,128)S(1)} %get-tuple-element.20.rest_0_), channel_id=1, source_target_pairs={{0,16},{16,0},{1,17},{17,1},{2,18},{18,2},{3,19},{19,3},{4,20},{20... | collective-permute-start | bytes 393224 | tf_op jit(solution)/shard_map/ppermute | solution.py:619
  30.5 1.7 %collective-permute-start.4 = (f32[5,16,1024]{2,1,0:T(8,128)S(1)}, f32[5,16,1024]{2,1,0:T(8,128)S(1)}, u32[]{:S(2)}, u32[]{:S(2)}) collective-permute-start(f32[5,16,1024]{2,1,0:T(8,128)S(1)} %get-tuple-element.22), channel_id=1, source_target_pairs={{0,1},{1,0},{2,3},{3,2},{4,5},{5,4},{6,7},{7,6},{8,9},{9,8},{10,11... | collective-permute-start | bytes 983048 | tf_op jit(solution)/shard_map/ppermute | solution.py:657
  32.2 35.0 %collective-permute-start.2 = (f32[5,48,1024]{2,1,0:T(8,128)}, f32[5,48,1024]{2,1,0:T(8,128)S(1)}, u32[]{:S(2)}, u32[]{:S(2)}) collective-permute-start(f32[5,48,1024]{2,1,0:T(8,128)} %copy-done.1), channel_id=1, source_target_pairs={{0,1},{1,0},{2,3},{3,2},{4,5},{5,4},{6,7},{7,6},{8,9},{9,8},{10,11... | collective-permute-start | bytes 2949128 | tf_op jit(solution)/shard_map/ppermute | solution.py:666
  41.9 25.3 %collective-permute-start.6 = (f32[5,48,1024]{2,1,0:T(8,128)S(1)}, f32[5,48,1024]{2,1,0:T(8,128)S(1)}, u32[]{:S(2)}, u32[]{:S(2)}) collective-permute-start(f32[5,48,1024]{2,1,0:T(8,128)S(1)} %get-tuple-element.25), channel_id=1, source_target_pairs={{1,2},{2,1},{5,6},{6,5},{9,10},{10,9},{13,14},{14,13},{17,18},{18,... | collective-permute-start | bytes 2949128 | tf_op jit(solution)/shard_map/ppermute | solution.py:683
  45.5 20.0 %collective-permute-start.7 = (f32[16,128]{1,0:T(8,128)S(1)}, f32[16,128]{1,0:T(8,128)S(1)}, u32[]{:S(2)}, u32[]{:S(2)}) collective-permute-start(f32[16,128]{1,0:T(8,128)S(1)} %get-tuple-element.26.token), channel_id=1, source_target_pairs={{0,16},{16,0},{1,17},{17,1},{2,18},{18,2},{3,19},{19,3},{4,20},{20... | collective-permute-start | bytes 24584 | tf_op jit(solution)/shard_map/ppermute | solution.py:619

commit v8 on v7

--- a/solution.py
+++ b/solution.py
@@ -3,6 +3,7 @@
 
 import jax
 import jax.numpy as jnp
+import ml_dtypes
 import numpy as np
 from jax import lax
 from jax.experimental import pallas as pl
@@ -149,11 +150,12 @@
 
 
 def bulk_kernel(
-    dtheta, rows, span, origin, total_rows, flags, state, low, high, inner, edge, outer, token, held, out, *scratch
+    dtheta, rows, span, total_rows, fused, flags, state, low, high, inner, edge, outer, token, held, out, *scratch
 ):
     first, end = span
     blocks = (end - first) // rows
-    state_rows, inner_rows, outer_rows, sems, *fluxes_scratch = scratch
+    state_rows, inner_rows, sems, radial, azimuthal, *outer_rows = scratch
+    outer_rows = outer_rows[0] if fused else None
     odd = flags[ODD]
     step = pl.program_id(0)
 
@@ -161,15 +163,15 @@
         a = first + k * rows + (EIGHT if k else -EIGHT)
         b = min(first + (k + 1) * rows + EIGHT, total_rows)
         at = a - first + EIGHT
-        rest = pl.ds(first - origin + k * rows, rows)
+        rest = pl.ds(outer.shape[1] - (end - first) + k * rows, rows)
         here = pl.ds(k * rows, rows)
-        return [
-            pltpu.make_async_copy(
-                state.at[:, :, a:b, :], state_rows.at[:, :, at : at + b - a, :], sems.at[3 * k]
-            ),
-            pltpu.make_async_copy(inner.at[:, here, :], inner_rows.at[:, here, :], sems.at[3 * k + 1]),
-            pltpu.make_async_copy(outer.at[:, rest, :], outer_rows.at[:, here, :], sems.at[3 * k + 2]),
+        sets = [
+            (state.at[:, :, a:b, :], state_rows.at[:, :, at : at + b - a, :]),
+            (inner.at[:, here, :], inner_rows.at[:, here, :]),
         ]
+        if fused:
+            sets.append((outer.at[:, rest, :], outer_rows.at[:, here, :]))
+        return [pltpu.make_async_copy(x, y, sems.at[3 * k + i]) for i, (x, y) in enumerate(sets)]
 
     @pl.when(step == 0)
     def _():
@@ -207,10 +209,40 @@
         next_rows,
         lambda r: edge[pl.ds(r, EIGHT), :],
         lambda f, r, at: inner_rows[f, pl.ds(base + r, EIGHT), at],
-        lambda f, r, at: outer_rows[f, pl.ds(base + r, EIGHT), at],
+        (lambda f, r, at: outer_rows[f, pl.ds(base + r, EIGHT), at]) if fused else None,
         lambda f, q, r: out.at[f, plane_of(odd, q), pl.ds(r, EIGHT), :],
-        *fluxes_scratch,
+        radial,
+        azimuthal,
     )
+
+
+def outer_kernel(rows, span, flags, outer, held, out, outer_rows, held_rows, sems):
+    first, end = span
+    plane = lax.axis_index("ax") % 2
+    sign = jnp.where(flags[ODD] == 1, -0.5, 0.5)
+    steps = []
+    for k in range((end - first) // rows):
+        here = pl.ds(k * rows, rows)
+        there = pl.ds(first + k * rows, rows)
+        ways = [
+            (outer.at[:, here, :], outer_rows.at[:, here, :]),
+            (held.at[:, plane, there, :], held_rows.at[:, here, :]),
+            (held_rows.at[:, here, :], out.at[:, plane, there, :]),
+        ]
+        steps.append([pltpu.make_async_copy(x, y, sems.at[3 * k + i]) for i, (x, y) in enumerate(ways)])
+        steps[-1][0].start()
+        steps[-1][1].start()
+    for k, (come, have, leave) in enumerate(steps):
+        come.wait()
+        have.wait()
+        for t in range(rows // EIGHT):
+            at = pl.ds(k * rows + EIGHT * t, EIGHT)
+            values = outer_flux(flags, [outer_rows[f, at, :] for f in range(FIELDS)])
+            for f in range(FIELDS):
+                held_rows[f, at, :] = held_rows[f, at, :] + sign * values[f]
+        leave.start()
+    for _, _, leave in steps:
+        leave.wait()
 
 
 def near_kernel(
@@ -277,8 +309,10 @@
 
     def line(k, ends):
         rows = jnp.concatenate([rhs[k, :, b * LANES : (b + 1) * LANES] for b in range(pieces)], axis=0)
+        high = rows.astype(jnp.bfloat16)
+        low = (rows - high.astype(jnp.float32)).astype(jnp.bfloat16)
         solved = jnp.dot(
-            rows, solve[...], precision=lax.Precision.HIGHEST, preferred_element_type=jnp.float32
+            jnp.concatenate([high, low, high], axis=1), solve[...], preferred_element_type=jnp.float32
         )
         inside = []
         for b in range(pieces):
@@ -332,17 +366,39 @@
             out[f, plane_of(flags[ODD], q)] = jnp.where(near, smooth, rhs[k])
 
 
-def pack_first_kernel(count, state, part, low, high, top, bottom, sems):
+def stream(pieces, sems):
+    steps = []
+    for source, stage, target in pieces:
+        for f in range(FIELDS):
+            k = 2 * len(steps)
+            come = pltpu.make_async_copy(source.at[f], stage.at[f], sems.at[k])
+            leave = pltpu.make_async_copy(stage.at[f], target.at[f], sems.at[k + 1])
+            steps.append((come, leave))
+    for come, _ in steps:
+        come.start()
+
+    def finish():
+        for come, leave in steps:
+            come.wait()
+            leave.start()
+        for _, leave in steps:
+            leave.wait()
+
+    return finish
+
+
+def pack_first_kernel(count, state, part, low, high, stage, top, bottom, row_sems, sems):
     _, _, rows, _ = state.shape
     odd = lax.axis_index("ax") % 2
+    finish = stream([(state.at[:, odd, 0:count, :], stage, part)], sems)
     copies = [
-        pltpu.make_async_copy(state.at[:, odd, 0:count, :], part, sems.at[0]),
-        pltpu.make_async_copy(state.at[:, :, rows - EIGHT : rows, :], top, sems.at[1]),
-        pltpu.make_async_copy(state.at[:, :, 0:EIGHT, :], bottom, sems.at[2]),
+        pltpu.make_async_copy(state.at[:, :, rows - EIGHT : rows, :], top, row_sems.at[0]),
+        pltpu.make_async_copy(state.at[:, :, 0:EIGHT, :], bottom, row_sems.at[1]),
     ]
     for copy in copies:
         copy.start()
-    for copy in copies[1:]:
+    finish()
+    for copy in copies:
         copy.wait()
     for f in range(FIELDS):
         for q in range(PLANES):
@@ -350,7 +406,6 @@
             p = plane_of(odd, q)
             low[k : k + 1, :] = top[f, p, EIGHT - 1 : EIGHT, :]
             high[k : k + 1, :] = bottom[f, p, 0:1, :]
-    copies[0].wait()
 
 
 def pack_edges_kernel(state, token, edge, side, left, right, sems):
@@ -379,15 +434,11 @@
 def pack_rest_kernel(parts, tokens, state, *rest):
     rest = rest[tokens:]
     odd = lax.axis_index("ax") % 2
-    sems = rest[-1]
-    copies = []
+    count = len(parts)
+    pieces = []
     for k, (q, first, last) in enumerate(parts):
-        source = state.at[:, plane_of(odd, q), first:last, :]
-        copies.append(pltpu.make_async_copy(source, rest[k], sems.at[k]))
-    for copy in copies:
-        copy.start()
-    for copy in copies:
-        copy.wait()
+        pieces.append((state.at[:, plane_of(odd, q), first:last, :], rest[count + k], rest[k]))
+    stream(pieces, rest[-1])()
 
 
 ANY = pl.BlockSpec(memory_space=pl.ANY)
@@ -422,9 +473,15 @@
     return pl.pallas_call(
         functools.partial(pack_first_kernel, count),
         in_specs=[ANY],
-        out_specs=[vmem, vmem, vmem],
+        out_specs=[ANY, vmem, vmem],
         out_shape=[jax.ShapeDtypeStruct((fields, count, cells), jnp.float32), row, row],
-        scratch_shapes=[rows, rows, pltpu.SemaphoreType.DMA((3,))],
+        scratch_shapes=[
+            pltpu.VMEM((fields, count, cells), jnp.float32),
+            rows,
+            rows,
+            pltpu.SemaphoreType.DMA((2,)),
+            pltpu.SemaphoreType.DMA((2 * fields,)),
+        ],
         compiler_params=PARAMS,
         cost_estimate=cost(0, fields * count * cells * 8),
         name="pack_first",
@@ -456,9 +513,12 @@
     return pl.pallas_call(
         functools.partial(pack_rest_kernel, parts, len(tokens)),
         in_specs=[ANY] * (1 + len(tokens)),
-        out_specs=[pl.BlockSpec(memory_space=pltpu.VMEM)] * len(shapes),
+        out_specs=[ANY] * len(shapes),
         out_shape=shapes,
-        scratch_shapes=[pltpu.SemaphoreType.DMA((len(parts),))],
+        scratch_shapes=[
+            *[pltpu.VMEM(x.shape, jnp.float32) for x in shapes],
+            pltpu.SemaphoreType.DMA((2 * fields * len(parts),)),
+        ],
         compiler_params=PARAMS,
         cost_estimate=cost(0, sum(math.prod(x.shape) for x in shapes) * 8),
         name="pack_rest",
@@ -470,17 +530,19 @@
     return [pltpu.VMEM((*shape, n, LANES), jnp.float32) for n in (rows + 2 * EIGHT, rows)]
 
 
-def bulk(flags, state, low, high, inner, edge, dtheta, outer, span, first, rows, token, held):
+def bulk(flags, state, low, high, inner, edge, dtheta, outer, span, rows, token, held):
     fields, planes, total_rows, cells = state.shape
-    origin, end = span
+    first, end = span
     count = end - first
     blocks = count // rows
     size = fields * planes * count * cells
     aliases = {} if held is None else {8: 0}
     state = in_hbm(state)
-    operands = [state, low, high, inner, edge, outer, token, state if held is None else held]
+    operands = [state, low, high, inner, edge, inner if outer is None else outer, token]
+    operands.append(state if held is None else held)
+    chunk = pltpu.VMEM((fields, count, cells), jnp.float32)
     return pl.pallas_call(
-        functools.partial(bulk_kernel, dtheta, rows, (first, end), origin, total_rows),
+        functools.partial(bulk_kernel, dtheta, rows, span, total_rows, outer is not None),
         grid_spec=pltpu.PrefetchScalarGridSpec(
             num_scalar_prefetch=1,
             grid=(blocks,),
@@ -497,10 +559,10 @@
             out_specs=rows_from((fields, planes, rows, cells), 2, first, rows),
             scratch_shapes=[
                 pltpu.VMEM((fields, planes, count + 2 * EIGHT, cells), jnp.float32),
-                pltpu.VMEM((fields, count, cells), jnp.float32),
-                pltpu.VMEM((fields, count, cells), jnp.float32),
+                chunk,
                 pltpu.SemaphoreType.DMA((3 * blocks,)),
                 *flux_scratch(rows, cells),
+                *([] if outer is None else [chunk]),
             ],
         ),
         out_shape=pltpu.HBM(state.shape, jnp.float32),
@@ -509,6 +571,26 @@
         cost_estimate=cost(size * 60, size * 10),
         name="bulk",
     )(flags, *operands)
+
+
+def add_outer(flags, outer, span, rows, held):
+    fields, count, cells = outer.shape
+    chunk = pltpu.VMEM((fields, count, cells), jnp.float32)
+    return pl.pallas_call(
+        functools.partial(outer_kernel, rows, span),
+        grid_spec=pltpu.PrefetchScalarGridSpec(
+            num_scalar_prefetch=1,
+            grid=(1,),
+            in_specs=[ANY, ANY],
+            out_specs=ANY,
+            scratch_shapes=[chunk, chunk, pltpu.SemaphoreType.DMA((3 * (count // rows),))],
+        ),
+        out_shape=pltpu.HBM(held.shape, jnp.float32),
+        input_output_aliases={2: 0},
+        compiler_params=PARAMS,
+        cost_estimate=cost(outer.size * 6, outer.size * 16),
+        name="add_outer",
+    )(flags, outer, held)
 
 
 def near(flags, state, low, high, inner, edge, dtheta, outer, factor, table, solve, token, part=None):
@@ -579,10 +661,10 @@
 
 
 def chunks(rows):
-    size = 24 if (rows - R_NEAR) % 48 == 0 else EIGHT
-    pairs = (rows - R_NEAR) // (2 * size)
-    cuts = sorted({-(-2 * pairs // 5), -(-4 * pairs // 5), pairs})
-    ends = [R_NEAR + 2 * size * c for c in cuts]
+    size = 16
+    triples = (rows - R_NEAR) // (3 * size)
+    cuts = sorted({-(-2 * triples // 5), -(-4 * triples // 5), triples})
+    ends = [R_NEAR + 3 * size * c for c in cuts]
     return size, list(zip([0] + ends[:-1], ends))
 
 
@@ -611,7 +693,10 @@
         ratio = 1.0 - (math.sqrt(half * (2.0 + half)) - half)
         block = np.arange(LANES) // width
         tables.append(ratio ** np.abs(block[:, None] - block[None, :]) / width)
-    return jnp.asarray(np.concatenate(tables, axis=1), jnp.float32)
+    table = np.concatenate(tables, axis=1)
+    high = table.astype(ml_dtypes.bfloat16)
+    low = (table - high.astype(np.float64)).astype(ml_dtypes.bfloat16)
+    return jnp.asarray(np.concatenate([high, high, low], axis=0))
 
 
 def ring(value, axis, shift):
@@ -675,9 +760,15 @@
 
     solve = piece_tables(dtheta)
     given = (flags, state, low, high)
+    def pass_over(k, token, held, fused=True):
+        span = (spans[k][0] if k else R_NEAR, spans[k][1])
+        return bulk(*given, inner[k + 1], edge, dtheta, outer[k] if fused else None, span, size, token, held)
+
+    out = pass_over(2, parts[0], None, fused=False) if count > 2 else None
     part = spans[2] if count > 2 else None
+    token = parts[0] if out is None else out
     rhs, local, ends, part = near(
-        *given, inner[0], edge, dtheta, outer[0], factor, table, solve, parts[0], part
+        *given, inner[0], edge, dtheta, outer[0], factor, table, solve, token, part
     )
     if part is not None:
         outer.append(lax.ppermute(part, "ax", outer_pairs))
@@ -688,13 +779,10 @@
         carry = carry * across + jnp.where(from_left, arrived[k], arrived[sec_count - k])
     carry = carry * closing
 
-    out = None
-    for k in range(count):
-        first = spans[k][0] if k else R_NEAR
-        if k == count - 1 and k:
-            out = finish(flags, factor, rhs, local, carry, table, out)
-        out = bulk(*given, inner[k + 1], edge, dtheta, outer[k], spans[k], first, size, ends, out)
-    return out if count > 1 else finish(flags, factor, rhs, local, carry, table, out)
+    for k in range(min(count, 2)):
+        out = pass_over(k, ends, out)
+    out = finish(flags, factor, rhs, local, carry, table, out)
+    return add_outer(flags, outer[2], spans[2], size, out) if count > 2 else out
 
 
 def solution(mesh):

time: 73.5 us -> 72.3 us (0.984)
  waiting for transfers between devices: 6.23 us -> 1.95 us
  local copies, waits for them, and re-layouts: 1.15 us -> 4.86 us
  starting transfers between devices: 19.8 us -> 18.5 us
    ppermute x2, waiting for transfers between devices: 3.88 us -> 0.01 us  [ring(): lax.ppermute(value, axis, [(i, (i + shift) % size) for i in range(size)])]
    unnamed x6 -> x8, local copies, waits for them, and re-layouts: 0.99 us -> 4.7 us
    pallas_call x3 -> x4, Pallas kernels: 24.6 us -> 27.5 us  [the longest x3 24.8 us: bulk(): pl.pallas_call(functools.partial(bulk_kernel, dtheta, rows, span, total_r...]
    pallas_call x1, Pallas kernels: 8.03 us -> 6.28 us  [near(): pl.pallas_call(functools.partial(near_kernel, dtheta, rows, part[0] if pa...]
    ppermute x1, waiting for transfers between devices: 1.16 us -> 0.01 us  [body(): inner = [lax.ppermute(side, 'ax', inner_pairs)]]
    ppermute x1, starting transfers between devices: 3.99 us -> 3.2 us  [body(): low = lax.ppermute(low, 'rad', up)]
  transfers between devices with their start and end apart: 11 -> 11, of which waited for: 3 -> 2; matrix products, arithmetic and copies ran while one was open for 1% -> 1% of each run, Pallas kernels for 50% -> 57%
where the time goes in v8:
time: 72.3 us; the launch traced here: 72 us
  Pallas kernels  46.2 us (64%)
  starting transfers between devices  18.5 us (26%)
  local copies, waits for them, and re-layouts  4.86 us (7%)
  waiting for transfers between devices  1.95 us (3%)
    pallas_call x3, Pallas kernels, bulk(): pl.pallas_call(functools.partial(bulk_kernel, dtheta, rows, span, total_r...  24.8 us
    pallas_call x1, Pallas kernels, near(): pl.pallas_call(functools.partial(near_kernel, dtheta, rows, part[0] if pa...  6.28 us
    pallas_call x1, Pallas kernels, pack_rest(): pl.pallas_call(functools.partial(pack_rest_kernel, parts, len(tokens)), i...  5.64 us
    unnamed x8, local copies, waits for them, and re-layouts  4.7 us
    ppermute x1, starting transfers between devices, body(): outer = [lax.ppermute(part, 'ax', outer_pairs)]  4.51 us
    ppermute x1, starting transfers between devices, body(): outer.append(lax.ppermute(part, 'ax', outer_pairs))  3.64 us
    ppermute x1, starting transfers between devices, body(): low = lax.ppermute(low, 'rad', up)  3.2 us
    pallas_call x1, Pallas kernels, pack_first(): pl.pallas_call(functools.partial(pack_first_kernel, count), in_specs=[ANY...  2.66 us
  transfers between devices with their start and end apart: 11, of which 2 were waited for; matrix products, arithmetic and copies ran while one was open for 1% of the time, Pallas kernels for 57%

profile of v8, /device:TPU:1, one launch (start us, length us, event | category | flops | bytes accessed | tf_op | source)
XLA Modules:
  0.0 72.0 jit_solution(14563147859681636309)
XLA Ops:
  0.0 2.7 %pack_first.1 = (f32[5,112,1024]{2,1,0:T(8,128)}, f32[10,1024]{1,0:T(8,128)S(1)}, f32[10,1024]{1,0:T(8,128)S(1)}) custom-call(f32[5,2,256,1024]{3,2,1,0:T(8,128)} %state.13), custom_call_target="tpu_custom_call" | custom-call | bytes 4587520 | tf_op jit(solution)/shard_map/pack_first/pallas_call | solution.py:473
  2.7 4.5 %collective-permute-start.3 = (f32[5,112,1024]{2,1,0:T(8,128)}, f32[5,112,1024]{2,1,0:T(8,128)S(1)}, u32[]{:S(2)}, u32[]{:S(2)}) collective-permute-start(f32[5,112,1024]{2,1,0:T(8,128)} %get-tuple-element.21), channel_id=1, source_target_pairs={{1,2},{2,1},{5,6},{6,5},{9,10},{10,9},{13,14},{14,13},{17,18},{18,... | collective-permute-start | bytes 6881288 | tf_op jit(solution)/shard_map/ppermute | solution.py:738
  7.2 3.2 %collective-permute-start = (f32[10,1024]{1,0:T(8,128)S(1)}, f32[10,1024]{1,0:T(8,128)S(1)}, u32[]{:S(2)}, u32[]{:S(2)}) collective-permute-start(f32[10,1024]{1,0:T(8,128)S(1)} %get-tuple-element.18), channel_id=1, source_target_pairs={{0,4},{4,8},{8,12},{1,5},{5,9},{9,13},{2,6},{6,10},{10,14},{3,7},{... | collective-permute-start | bytes 122888 | tf_op jit(solution)/shard_map/ppermute | solution.py:740
  10.4 1.3 %collective-permute-start.1 = (f32[10,1024]{1,0:T(8,128)S(1)}, f32[10,1024]{1,0:T(8,128)S(1)}, u32[]{:S(2)}, u32[]{:S(2)}) collective-permute-start(f32[10,1024]{1,0:T(8,128)S(1)} %get-tuple-element.19.token), channel_id=1, source_target_pairs={{4,0},{8,4},{12,8},{5,1},{9,5},{13,9},{6,2},{10,6},{14,10},{7,3},{... | collective-permute-start | bytes 122888 | tf_op jit(solution)/shard_map/ppermute | solution.py:741
  11.7 2.6 %pack_edges.1 = (f32[256,128]{1,0:T(8,128)S(1)}, f32[5,16,1024]{2,1,0:T(8,128)S(1)}) custom-call(f32[5,2,256,1024]{3,2,1,0:T(8,128)} %state.13, f32[10,1024]{1,0:T(8,128)S(1)} %get-tuple-element.19.token), custom_call_target="tpu_custom_call" | custom-call | bytes 5242880 | tf_op jit(solution)/shard_map/pack_edges/pallas_call | solution.py:495
  14.3 0.0 copy-start.2
  14.3 0.7 copy-done.2
  15.0 0.0 copy-start.3
  15.0 1.2 %collective-permute-start.4 = (f32[256,128]{1,0:T(8,128)S(1)}, f32[256,128]{1,0:T(8,128)S(1)}, u32[]{:S(2)}, u32[]{:S(2)}) collective-permute-start(f32[256,128]{1,0:T(8,128)S(1)} %get-tuple-element.22.rest_0_), channel_id=1, source_target_pairs={{0,16},{16,0},{1,17},{17,1},{2,18},{18,2},{3,19},{19,3},{4,20},{20... | collective-permute-start | bytes 393224 | tf_op jit(solution)/shard_map/ppermute | solution.py:704
  16.2 0.0 collective-permute-done.rest_1_.low
  16.2 0.0 collective-permute-done.1.rest_2_.high
  16.2 5.6 %pack_rest.1 = (f32[5,96,1024]{2,1,0:T(8,128)}, f32[5,96,1024]{2,1,0:T(8,128)}, f32[5,96,1024]{2,1,0:T(8,128)}, f32[5,48,1024]{2,1,0:T(8,128)}) custom-call(f32[5,2,256,1024]{3,2,1,0:T(8,128)} %state.13, f32[256,128]{1,0:T(8,128)S(1)} %get-tuple-element.22.rest_0_, f32[10,1024]{1,0:T(8,128)S(1)} %collective-permute-done.rest_1_.low, ...), custom_call_target="tpu_custom_call" | custom-call | bytes 13762560 | tf_op jit(solution)/shard_map/pack_rest/pallas_call | solution.py:513
  21.9 0.1 collective-permute-start.5
  22.0 0.5 collective-permute-start.10
  22.5 0.1 collective-permute-start.8
  22.5 0.0 collective-permute-done.4.edge
  22.5 2.5 %collective-permute-start.9 = (f32[5,96,1024]{2,1,0:T(8,128)}, f32[5,96,1024]{2,1,0:T(8,128)}, u32[]{:S(2)}, u32[]{:S(2)}) collective-permute-start(f32[5,96,1024]{2,1,0:T(8,128)} %get-tuple-element.30), channel_id=1, source_target_pairs={{1,2},{2,1},{5,6},{6,5},{9,10},{10,9},{13,14},{14,13},{17,18},{18,... | collective-permute-start | bytes 5898248 | tf_op jit(solution)/shard_map/ppermute | solution.py:749
  25.1 0.0 copy-done.3
  25.1 0.1 stack.35.flags
  25.3 0.1 collective-permute-done.5.inner.outer
  25.3 0.1 collective-permute-start.2
  25.5 0.1 fusion.3.table
  25.6 0.0 copy-start.1
  25.6 5.8 %bulk.3.token.held = f32[5,2,256,1024]{3,2,1,0:T(8,128)} custom-call(s32[5]{0:T(128)S(1)} %stack.35.flags, f32[5,2,256,1024]{3,2,1,0:T(8,128)} %state.13, f32[10,1024]{1,0:T(8,128)S(1)} %collective-permute-done.rest_1_.low, f32[10,1024]{1,0:T(8,128)S(1)} %collective-permute-done.1.rest_2_.high, f32[5,48,1024]{2,1,0:T(8,128)S(1)} %collective-permute-done.5.inner.outer, ...), custom_call_target="tpu_custom_call" | custom-call | flops 29491200 | bytes 4915200 | tf_op jit(solution)/shard_map/bulk/pallas_call | solution.py:544
  31.4 0.0 collective-permute-done.2.inner
  31.4 1.8 %collective-permute-done.3.outer = f32[5,112,1024]{2,1,0:T(8,128)S(1)} collective-permute-done((f32[5,112,1024]{2,1,0:T(8,128)}, f32[5,112,1024]{2,1,0:T(8,128)S(1)}, u32[]{:S(2)}, u32[]{:S(2)}) %collective-permute-start.3) | collective-permute-done | bytes 2293792 | tf_op jit(solution)/shard_map/ppermute | solution.py:738
  33.2 0.1 broadcast_in_dim.51.factor
  33.3 0.0 copy-done.1
  33.3 0.0 copy-start
  33.3 4.0 %copy-done = f32[5,2,256,1024]{3,2,1,0:T(8,128)S(1)} copy-done((f32[5,2,256,1024]{3,2,1,0:T(8,128)S(1)}, f32[5,2,256,1024]{3,2,1,0:T(8,128)}, u32[]{:S(2)}) %copy-start) | copy-done | bytes 10485784
  37.3 6.3 %near.1 = (f32[10,16,1024]{2,1,0:T(8,128)S(1)}, f32[10,16,1024]{2,1,0:T(8,128)S(1)}, f32[16,128]{1,0:T(8,128)S(1)}, f32[5,48,1024]{2,1,0:T(8,128)S(1)}) custom-call(s32[5]{0:T(128)S(1)} %stack.35.flags, f32[5,2,256,1024]{3,2,1,0:T(8,128)} %state.13, f32[5,2,256,1024]{3,2,1,0:T(8,128)} %state.13, f32[10,1024]{1,0:T(8,128)S(1)} %collective-permute-done.rest_1_.low, ...), custom_call_target="tpu_custom_call" | custom-call | flops 32768000 | bytes 40960000 | tf_op jit(solution)/shard_map/near/pallas_call | solution.py:608
  43.5 3.6 %collective-permute-start.6 = (f32[5,48,1024]{2,1,0:T(8,128)S(1)}, f32[5,48,1024]{2,1,0:T(8,128)S(1)}, u32[]{:S(2)}, u32[]{:S(2)}) collective-permute-start(f32[5,48,1024]{2,1,0:T(8,128)S(1)} %get-tuple-element.25), channel_id=1, source_target_pairs={{1,2},{2,1},{5,6},{6,5},{9,10},{10,9},{13,14},{14,13},{17,18},{18,... | collective-permute-start | bytes 2949128 | tf_op jit(solution)/shard_map/ppermute | solution.py:774
  47.2 1.3 %collective-permute-start.7 = (f32[16,128]{1,0:T(8,128)S(1)}, f32[16,128]{1,0:T(8,128)S(1)}, u32[]{:S(2)}, u32[]{:S(2)}) collective-permute-start(f32[16,128]{1,0:T(8,128)S(1)} %get-tuple-element.28.token), channel_id=1, source_target_pairs={{0,16},{16,0},{1,17},{17,1},{2,18},{18,2},{3,19},{19,3},{4,20},{20... | collective-permute-start | bytes 24584 | tf_op jit(solution)/shard_map/ppermute | solution.py:704
  48.5 0.0 collective-permute-done.10.inner
  48.5 9.4 %bulk.4.held = f32[5,2,256,1024]{3,2,1,0:T(8,128)} custom-call(s32[5]{0:T(128)S(1)} %stack.35.flags, f32[5,2,256,1024]{3,2,1,0:T(8,128)} %state.13, f32[10,1024]{1,0:T(8,128)S(1)} %collective-permute-done.rest_1_.low, f32[10,1024]{1,0:T(8,128)S(1)} %collective-permute-done.1.rest_2_.high, ...), custom_call_target="tpu_custom_call", output_to_operand_aliasing={{}: (8, {})} | custom-call | flops 58982400 | bytes 9830400 | tf_op jit(solution)/shard_map/bulk/pallas_call | solution.py:544
  57.9 0.0 collective-permute-done.8.inner
  57.9 0.0 collective-permute-done.9.outer
  58.0 9.6 %bulk.5.held = f32[5,2,256,1024]{3,2,1,0:T(8,128)} custom-call(s32[5]{0:T(128)S(1)} %stack.35.flags, f32[5,2,256,1024]{3,2,1,0:T(8,128)} %state.13, f32[10,1024]{1,0:T(8,128)S(1)} %collective-permute-done.rest_1_.low, f32[10,1024]{1,0:T(8,128)S(1)} %collective-permute-done.1.rest_2_.high, ...), custom_call_target="tpu_custom_call", output_to_operand_aliasing={{}: (8, {})} | custom-call | flops 58982400 | bytes 9830400 | tf_op jit(solution)/shard_map/bulk/pallas_call | solution.py:544
  67.6 0.0 collective-permute-done.7
  67.6 0.1 add_multiply_fusion.carry
  67.7 1.6 %finish.1.held = f32[5,2,256,1024]{3,2,1,0:T(8,128)} custom-call(s32[5]{0:T(128)S(1)} %stack.35.flags, f32[16,128]{1,0:T(8,128)S(1)} %broadcast_in_dim.51.factor, f32[10,16,1024]{2,1,0:T(8,128)S(1)} %get-tuple-element.26.rhs, f32[10,16,1024]{2,1,0:T(8,128)S(1)} %get-tuple-element.27.local, ...), custom_call_target="tpu_custom_call", output_to_operand_aliasing={{}: (6, {})} | custom-call | flops 1638400 | bytes 3276800 | tf_op jit(solution)/shard_map/finish/pallas_call | solution.py:640
  69.3 0.0 collective-permute-done.6.outer
  69.3 2.7 %add_outer.1 = f32[5,2,256,1024]{3,2,1,0:T(8,128)} custom-call(s32[5]{0:T(128)S(1)} %stack.35.flags, f32[5,48,1024]{2,1,0:T(8,128)S(1)} %collective-permute-done.6.outer, f32[5,2,256,1024]{3,2,1,0:T(8,128)} %finish.1.held), custom_call_target="tpu_custom_call", output_to_operand_aliasing={{}: (2, {})} | custom-call | flops 1474560 | bytes 3932160 | tf_op jit(solution)/shard_map/add_outer/pallas_call | solution.py:579
  (5 shorter events, 0.1 us)
Async XLA Ops:
  2.7 30.5 %collective-permute-start.3 = (f32[5,112,1024]{2,1,0:T(8,128)}, f32[5,112,1024]{2,1,0:T(8,128)S(1)}, u32[]{:S(2)}, u32[]{:S(2)}) collective-permute-start(f32[5,112,1024]{2,1,0:T(8,128)} %get-tuple-element.21), channel_id=1, source_target_pairs={{1,2},{2,1},{5,6},{6,5},{9,10},{10,9},{13,14},{14,13},{17,18},{18,... | collective-permute-start | bytes 6881288 | tf_op jit(solution)/shard_map/ppermute | solution.py:738
  7.2 9.0 %collective-permute-start = (f32[10,1024]{1,0:T(8,128)S(1)}, f32[10,1024]{1,0:T(8,128)S(1)}, u32[]{:S(2)}, u32[]{:S(2)}) collective-permute-start(f32[10,1024]{1,0:T(8,128)S(1)} %get-tuple-element.18), channel_id=1, source_target_pairs={{0,4},{4,8},{8,12},{1,5},{5,9},{9,13},{2,6},{6,10},{10,14},{3,7},{... | collective-permute-start | bytes 122888 | tf_op jit(solution)/shard_map/ppermute | solution.py:740
  10.4 5.8 %collective-permute-start.1 = (f32[10,1024]{1,0:T(8,128)S(1)}, f32[10,1024]{1,0:T(8,128)S(1)}, u32[]{:S(2)}, u32[]{:S(2)}) collective-permute-start(f32[10,1024]{1,0:T(8,128)S(1)} %get-tuple-element.19.token), channel_id=1, source_target_pairs={{4,0},{8,4},{12,8},{5,1},{9,5},{13,9},{6,2},{10,6},{14,10},{7,3},{... | collective-permute-start | bytes 122888 | tf_op jit(solution)/shard_map/ppermute | solution.py:741
  14.3 0.7 %copy-start.2 = (f32[5,16,1024]{2,1,0:T(8,128)}, f32[5,16,1024]{2,1,0:T(8,128)S(1)}, u32[]{:S(2)}) copy-start(f32[5,16,1024]{2,1,0:T(8,128)S(1)} %get-tuple-element.20) | copy-start | bytes 983044
  15.0 10.1 %copy-start.3 = (s32[16]{0:T(128)S(1)}, s32[16]{0:T(128)}, u32[]{:S(2)}) copy-start(s32[16]{0:T(128)} %param.4) | copy-start | bytes 196
  15.0 7.6 %collective-permute-start.4 = (f32[256,128]{1,0:T(8,128)S(1)}, f32[256,128]{1,0:T(8,128)S(1)}, u32[]{:S(2)}, u32[]{:S(2)}) collective-permute-start(f32[256,128]{1,0:T(8,128)S(1)} %get-tuple-element.22.rest_0_), channel_id=1, source_target_pairs={{0,16},{16,0},{1,17},{17,1},{2,18},{18,2},{3,19},{19,3},{4,20},{20... | collective-permute-start | bytes 393224 | tf_op jit(solution)/shard_map/ppermute | solution.py:704
  21.9 3.5 %collective-permute-start.5 = (f32[5,48,1024]{2,1,0:T(8,128)}, f32[5,48,1024]{2,1,0:T(8,128)S(1)}, u32[]{:S(2)}, u32[]{:S(2)}) collective-permute-start(f32[5,48,1024]{2,1,0:T(8,128)} %get-tuple-element.23), channel_id=1, source_target_pairs={{0,1},{1,0},{2,3},{3,2},{4,5},{5,4},{6,7},{7,6},{8,9},{9,8},{10,11... | collective-permute-start | bytes 2949128 | tf_op jit(solution)/shard_map/ppermute | solution.py:751
  22.0 26.5 %collective-permute-start.10 = (f32[5,96,1024]{2,1,0:T(8,128)}, f32[5,96,1024]{2,1,0:T(8,128)}, u32[]{:S(2)}, u32[]{:S(2)}) collective-permute-start(f32[5,96,1024]{2,1,0:T(8,128)} %get-tuple-element.24.token), channel_id=1, source_target_pairs={{0,1},{1,0},{2,3},{3,2},{4,5},{5,4},{6,7},{7,6},{8,9},{9,8},{10,11... | collective-permute-start | bytes 5898248 | tf_op jit(solution)/shard_map/ppermute | solution.py:751
  22.5 35.5 %collective-permute-start.8 = (f32[5,96,1024]{2,1,0:T(8,128)}, f32[5,96,1024]{2,1,0:T(8,128)}, u32[]{:S(2)}, u32[]{:S(2)}) collective-permute-start(f32[5,96,1024]{2,1,0:T(8,128)} %get-tuple-element.29), channel_id=1, source_target_pairs={{0,1},{1,0},{2,3},{3,2},{4,5},{5,4},{6,7},{7,6},{8,9},{9,8},{10,11... | collective-permute-start | bytes 5898248 | tf_op jit(solution)/shard_map/ppermute | solution.py:751
  22.5 35.4 %collective-permute-start.9 = (f32[5,96,1024]{2,1,0:T(8,128)}, f32[5,96,1024]{2,1,0:T(8,128)}, u32[]{:S(2)}, u32[]{:S(2)}) collective-permute-start(f32[5,96,1024]{2,1,0:T(8,128)} %get-tuple-element.30), channel_id=1, source_target_pairs={{1,2},{2,1},{5,6},{6,5},{9,10},{10,9},{13,14},{14,13},{17,18},{18,... | collective-permute-start | bytes 5898248 | tf_op jit(solution)/shard_map/ppermute | solution.py:749
  25.3 6.0 %collective-permute-start.2 = (f32[5,16,1024]{2,1,0:T(8,128)}, f32[5,16,1024]{2,1,0:T(8,128)S(1)}, u32[]{:S(2)}, u32[]{:S(2)}) collective-permute-start(f32[5,16,1024]{2,1,0:T(8,128)} %copy-done.2), channel_id=1, source_target_pairs={{0,1},{1,0},{2,3},{3,2},{4,5},{5,4},{6,7},{7,6},{8,9},{9,8},{10,11... | collective-permute-start | bytes 983048 | tf_op jit(solution)/shard_map/ppermute | solution.py:742
  25.6 7.7 %copy-start.1 = (bf16[384,640]{1,0:T(8,128)(2,1)S(1)}, bf16[384,640]{1,0:T(8,128)(2,1)}, u32[]{:S(2)}) copy-start(bf16[384,640]{1,0:T(8,128)(2,1)} %constant.54.clone.solve) | copy-start | bytes 1474564
  33.3 4.0 %copy-start = (f32[5,2,256,1024]{3,2,1,0:T(8,128)S(1)}, f32[5,2,256,1024]{3,2,1,0:T(8,128)}, u32[]{:S(2)}) copy-start(f32[5,2,256,1024]{3,2,1,0:T(8,128)} %bulk.3.token.held) | copy-start | bytes 31457284
  43.5 25.8 %collective-permute-start.6 = (f32[5,48,1024]{2,1,0:T(8,128)S(1)}, f32[5,48,1024]{2,1,0:T(8,128)S(1)}, u32[]{:S(2)}, u32[]{:S(2)}) collective-permute-start(f32[5,48,1024]{2,1,0:T(8,128)S(1)} %get-tuple-element.25), channel_id=1, source_target_pairs={{1,2},{2,1},{5,6},{6,5},{9,10},{10,9},{13,14},{14,13},{17,18},{18,... | collective-permute-start | bytes 2949128 | tf_op jit(solution)/shard_map/ppermute | solution.py:774
  47.2 20.4 %collective-permute-start.7 = (f32[16,128]{1,0:T(8,128)S(1)}, f32[16,128]{1,0:T(8,128)S(1)}, u32[]{:S(2)}, u32[]{:S(2)}) collective-permute-start(f32[16,128]{1,0:T(8,128)S(1)} %get-tuple-element.28.token), channel_id=1, source_target_pairs={{0,16},{16,0},{1,17},{17,1},{2,18},{18,2},{3,19},{19,3},{4,20},{20... | collective-permute-start | bytes 24584 | tf_op jit(solution)/shard_map/ppermute | solution.py:704

commit v9 on v8

--- a/solution.py
+++ b/solution.py
@@ -538,7 +538,7 @@
     size = fields * planes * count * cells
     aliases = {} if held is None else {8: 0}
     state = in_hbm(state)
-    operands = [state, low, high, inner, edge, inner if outer is None else outer, token]
+    operands = [state, low, high, inner, edge, inner if outer is None else outer, in_hbm(token)]
     operands.append(state if held is None else held)
     chunk = pltpu.VMEM((fields, count, cells), jnp.float32)
     return pl.pallas_call(
@@ -631,7 +631,7 @@
         compiler_params=PARAMS,
         cost_estimate=cost(LINES * R_NEAR * cells * 200, LINES * R_NEAR * cells * 250),
         name="near",
-    )(flags, state, state, low, high, inner, outer, edge, factor, table, solve, token, state)
+    )(flags, state, state, low, high, inner, outer, edge, factor, table, solve, in_hbm(token), state)
     return result if part is not None else (*result, None)
 
 

time: 72.3 us -> 69.7 us (0.964)
  local copies, waits for them, and re-layouts: 4.86 us -> 0.88 us
    unnamed x8 -> x6, local copies, waits for them, and re-layouts: 4.7 us -> 0.72 us
  transfers between devices with their start and end apart: 11 -> 11, of which waited for: 2 -> 2; matrix products, arithmetic and copies ran while one was open for 1% -> 2% of each run, Pallas kernels for 57% -> 60%
where the time goes in v9:
time: 69.7 us; the launch traced here: 69.3 us
  Pallas kernels  46.8 us (67%)
  starting transfers between devices  18.5 us (27%)
  waiting for transfers between devices  1.95 us (3%)
  other arithmetic  0.92 us (1%)
  local copies, waits for them, and re-layouts  0.88 us (1%)
    pallas_call x3, Pallas kernels, bulk(): pl.pallas_call(functools.partial(bulk_kernel, dtheta, rows, span, total_r...  24.8 us
    pallas_call x1, Pallas kernels, near(): pl.pallas_call(functools.partial(near_kernel, dtheta, rows, part[0] if pa...  6.87 us
    pallas_call x1, Pallas kernels, pack_rest(): pl.pallas_call(functools.partial(pack_rest_kernel, parts, len(tokens)), i...  5.64 us
    ppermute x1, starting transfers between devices, body(): outer = [lax.ppermute(part, 'ax', outer_pairs)]  4.51 us
    ppermute x1, starting transfers between devices, body(): outer.append(lax.ppermute(part, 'ax', outer_pairs))  3.64 us
    ppermute x1, starting transfers between devices, body(): low = lax.ppermute(low, 'rad', up)  3.2 us
    pallas_call x1, Pallas kernels, pack_first(): pl.pallas_call(functools.partial(pack_first_kernel, count), in_specs=[ANY...  2.67 us
    pallas_call x1, Pallas kernels, add_outer(): pl.pallas_call(functools.partial(outer_kernel, rows, span), grid_spec=plt...  2.65 us
  transfers between devices with their start and end apart: 11, of which 2 were waited for; matrix products, arithmetic and copies ran while one was open for 2% of the time, Pallas kernels for 60%

profile of v9, /device:TPU:1, one launch (start us, length us, event | category | flops | bytes accessed | tf_op | source)
XLA Modules:
  0.0 69.3 jit_solution(7238029191311987617)
XLA Ops:
  0.0 2.7 %pack_first.1 = (f32[5,112,1024]{2,1,0:T(8,128)}, f32[10,1024]{1,0:T(8,128)S(1)}, f32[10,1024]{1,0:T(8,128)S(1)}) custom-call(f32[5,2,256,1024]{3,2,1,0:T(8,128)} %state.13), custom_call_target="tpu_custom_call" | custom-call | bytes 4587520 | tf_op jit(solution)/shard_map/pack_first/pallas_call | solution.py:473
  2.7 4.5 %collective-permute-start.3 = (f32[5,112,1024]{2,1,0:T(8,128)}, f32[5,112,1024]{2,1,0:T(8,128)S(1)}, u32[]{:S(2)}, u32[]{:S(2)}) collective-permute-start(f32[5,112,1024]{2,1,0:T(8,128)} %get-tuple-element.21), channel_id=1, source_target_pairs={{1,2},{2,1},{5,6},{6,5},{9,10},{10,9},{13,14},{14,13},{17,18},{18,... | collective-permute-start | bytes 6881288 | tf_op jit(solution)/shard_map/ppermute | solution.py:738
  7.2 3.2 %collective-permute-start = (f32[10,1024]{1,0:T(8,128)S(1)}, f32[10,1024]{1,0:T(8,128)S(1)}, u32[]{:S(2)}, u32[]{:S(2)}) collective-permute-start(f32[10,1024]{1,0:T(8,128)S(1)} %get-tuple-element.18), channel_id=1, source_target_pairs={{0,4},{4,8},{8,12},{1,5},{5,9},{9,13},{2,6},{6,10},{10,14},{3,7},{... | collective-permute-start | bytes 122888 | tf_op jit(solution)/shard_map/ppermute | solution.py:740
  10.4 1.3 %collective-permute-start.1 = (f32[10,1024]{1,0:T(8,128)S(1)}, f32[10,1024]{1,0:T(8,128)S(1)}, u32[]{:S(2)}, u32[]{:S(2)}) collective-permute-start(f32[10,1024]{1,0:T(8,128)S(1)} %get-tuple-element.19.token), channel_id=1, source_target_pairs={{4,0},{8,4},{12,8},{5,1},{9,5},{13,9},{6,2},{10,6},{14,10},{7,3},{... | collective-permute-start | bytes 122888 | tf_op jit(solution)/shard_map/ppermute | solution.py:741
  11.7 2.6 %pack_edges.1 = (f32[256,128]{1,0:T(8,128)S(1)}, f32[5,16,1024]{2,1,0:T(8,128)S(1)}) custom-call(f32[5,2,256,1024]{3,2,1,0:T(8,128)} %state.13, f32[10,1024]{1,0:T(8,128)S(1)} %get-tuple-element.19.token), custom_call_target="tpu_custom_call" | custom-call | bytes 5242880 | tf_op jit(solution)/shard_map/pack_edges/pallas_call | solution.py:495
  14.3 0.0 copy-start.1
  14.3 0.7 %copy-done.1 = f32[5,16,1024]{2,1,0:T(8,128)} copy-done((f32[5,16,1024]{2,1,0:T(8,128)}, f32[5,16,1024]{2,1,0:T(8,128)S(1)}, u32[]{:S(2)}) %copy-start.1) | copy-done | bytes 327704
  15.0 0.0 copy-start.2
  15.0 1.2 %collective-permute-start.4 = (f32[256,128]{1,0:T(8,128)S(1)}, f32[256,128]{1,0:T(8,128)S(1)}, u32[]{:S(2)}, u32[]{:S(2)}) collective-permute-start(f32[256,128]{1,0:T(8,128)S(1)} %get-tuple-element.22.rest_0_), channel_id=1, source_target_pairs={{0,16},{16,0},{1,17},{17,1},{2,18},{18,2},{3,19},{19,3},{4,20},{20... | collective-permute-start | bytes 393224 | tf_op jit(solution)/shard_map/ppermute | solution.py:704
  16.2 0.0 collective-permute-done.rest_1_.low
  16.2 0.0 collective-permute-done.1.rest_2_.high
  16.2 5.6 %pack_rest.1 = (f32[5,96,1024]{2,1,0:T(8,128)}, f32[5,96,1024]{2,1,0:T(8,128)}, f32[5,96,1024]{2,1,0:T(8,128)}, f32[5,48,1024]{2,1,0:T(8,128)}) custom-call(f32[5,2,256,1024]{3,2,1,0:T(8,128)} %state.13, f32[256,128]{1,0:T(8,128)S(1)} %get-tuple-element.22.rest_0_, f32[10,1024]{1,0:T(8,128)S(1)} %collective-permute-done.rest_1_.low, ...), custom_call_target="tpu_custom_call" | custom-call | bytes 13762560 | tf_op jit(solution)/shard_map/pack_rest/pallas_call | solution.py:513
  21.9 0.1 collective-permute-start.5
  22.0 0.5 collective-permute-start.10
  22.5 0.1 collective-permute-start.8
  22.5 0.0 collective-permute-done.4.edge
  22.5 2.5 %collective-permute-start.9 = (f32[5,96,1024]{2,1,0:T(8,128)}, f32[5,96,1024]{2,1,0:T(8,128)}, u32[]{:S(2)}, u32[]{:S(2)}) collective-permute-start(f32[5,96,1024]{2,1,0:T(8,128)} %get-tuple-element.30), channel_id=1, source_target_pairs={{1,2},{2,1},{5,6},{6,5},{9,10},{10,9},{13,14},{14,13},{17,18},{18,... | collective-permute-start | bytes 5898248 | tf_op jit(solution)/shard_map/ppermute | solution.py:749
  25.1 0.0 copy-done.2
  25.1 0.1 stack.35.flags
  25.3 0.1 collective-permute-done.5.inner.outer
  25.4 0.1 collective-permute-start.2
  25.5 0.1 fusion.3.table
  25.6 0.0 copy-start
  25.6 5.8 %bulk.3.token.held = f32[5,2,256,1024]{3,2,1,0:T(8,128)} custom-call(s32[5]{0:T(128)S(1)} %stack.35.flags, f32[5,2,256,1024]{3,2,1,0:T(8,128)} %state.13, f32[10,1024]{1,0:T(8,128)S(1)} %collective-permute-done.rest_1_.low, f32[10,1024]{1,0:T(8,128)S(1)} %collective-permute-done.1.rest_2_.high, f32[5,48,1024]{2,1,0:T(8,128)S(1)} %collective-permute-done.5.inner.outer, ...), custom_call_target="tpu_custom_call" | custom-call | flops 29491200 | bytes 4915200 | tf_op jit(solution)/shard_map/bulk/pallas_call | solution.py:544
  31.4 0.0 collective-permute-done.2.inner
  31.4 1.8 %collective-permute-done.3.outer = f32[5,112,1024]{2,1,0:T(8,128)S(1)} collective-permute-done((f32[5,112,1024]{2,1,0:T(8,128)}, f32[5,112,1024]{2,1,0:T(8,128)S(1)}, u32[]{:S(2)}, u32[]{:S(2)}) %collective-permute-start.3) | collective-permute-done | bytes 2293792 | tf_op jit(solution)/shard_map/ppermute | solution.py:738
  33.2 0.1 broadcast_in_dim.51.factor
  33.3 0.0 copy-done
  33.3 6.9 %near.1 = (f32[10,16,1024]{2,1,0:T(8,128)S(1)}, f32[10,16,1024]{2,1,0:T(8,128)S(1)}, f32[16,128]{1,0:T(8,128)}, f32[5,48,1024]{2,1,0:T(8,128)S(1)}) custom-call(s32[5]{0:T(128)S(1)} %stack.35.flags, f32[5,2,256,1024]{3,2,1,0:T(8,128)} %state.13, f32[5,2,256,1024]{3,2,1,0:T(8,128)} %state.13, f32[10,1024]{1,0:T(8,128)S(1)} %collective-permute-done.rest_1_.low, ...), custom_call_target="tpu_custom_call" | custom-call | flops 32768000 | bytes 40960000 | tf_op jit(solution)/shard_map/near/pallas_call | solution.py:608
  40.2 3.6 %collective-permute-start.6 = (f32[5,48,1024]{2,1,0:T(8,128)S(1)}, f32[5,48,1024]{2,1,0:T(8,128)S(1)}, u32[]{:S(2)}, u32[]{:S(2)}) collective-permute-start(f32[5,48,1024]{2,1,0:T(8,128)S(1)} %get-tuple-element.25), channel_id=1, source_target_pairs={{1,2},{2,1},{5,6},{6,5},{9,10},{10,9},{13,14},{14,13},{17,18},{18,... | collective-permute-start | bytes 2949128 | tf_op jit(solution)/shard_map/ppermute | solution.py:774
  43.8 1.3 %collective-permute-start.7 = (f32[16,128]{1,0:T(8,128)}, f32[16,128]{1,0:T(8,128)S(1)}, u32[]{:S(2)}, u32[]{:S(2)}) collective-permute-start(f32[16,128]{1,0:T(8,128)} %get-tuple-element.28.token), channel_id=1, source_target_pairs={{0,16},{16,0},{1,17},{17,1},{2,18},{18,2},{3,19},{19,3},{4,20},{20... | collective-permute-start | bytes 24584 | tf_op jit(solution)/shard_map/ppermute | solution.py:704
  45.1 0.0 collective-permute-done.10.inner
  45.1 9.4 %bulk.4.held = f32[5,2,256,1024]{3,2,1,0:T(8,128)} custom-call(s32[5]{0:T(128)S(1)} %stack.35.flags, f32[5,2,256,1024]{3,2,1,0:T(8,128)} %state.13, f32[10,1024]{1,0:T(8,128)S(1)} %collective-permute-done.rest_1_.low, f32[10,1024]{1,0:T(8,128)S(1)} %collective-permute-done.1.rest_2_.high, ...), custom_call_target="tpu_custom_call", output_to_operand_aliasing={{}: (8, {})} | custom-call | flops 58982400 | bytes 9830400 | tf_op jit(solution)/shard_map/bulk/pallas_call | solution.py:544
  54.6 0.0 collective-permute-done.8.inner
  54.6 0.0 collective-permute-done.9.outer
  54.6 9.6 %bulk.5.held = f32[5,2,256,1024]{3,2,1,0:T(8,128)} custom-call(s32[5]{0:T(128)S(1)} %stack.35.flags, f32[5,2,256,1024]{3,2,1,0:T(8,128)} %state.13, f32[10,1024]{1,0:T(8,128)S(1)} %collective-permute-done.rest_1_.low, f32[10,1024]{1,0:T(8,128)S(1)} %collective-permute-done.1.rest_2_.high, ...), custom_call_target="tpu_custom_call", output_to_operand_aliasing={{}: (8, {})} | custom-call | flops 58982400 | bytes 9830400 | tf_op jit(solution)/shard_map/bulk/pallas_call | solution.py:544
  64.2 0.0 collective-permute-done.7
  64.2 0.8 %add_multiply_fusion.carry = f32[16,128]{1,0:T(8,128)S(1)} fusion(f32[16,128]{1,0:T(8,128)S(1)} %collective-permute-done.7, f32[16,128]{1,0:T(8,128)} %get-tuple-element.28.token, f32[16]{0:T(128)S(1)} %get-tuple-element.34, f32[16]{0:T(128)S(1)} %get-tuple-element.32, f32[16]{0:T(128)S(1)} %get-tuple-element.31), kind=kLoop, calls=%fused_computation.5 | loop fusion | flops 8192 | bytes 24768 | tf_op jit(solution)/shard_map/mul | solution.py:780
  65.0 1.6 %finish.1.held = f32[5,2,256,1024]{3,2,1,0:T(8,128)} custom-call(s32[5]{0:T(128)S(1)} %stack.35.flags, f32[16,128]{1,0:T(8,128)S(1)} %broadcast_in_dim.51.factor, f32[10,16,1024]{2,1,0:T(8,128)S(1)} %get-tuple-element.26.rhs, f32[10,16,1024]{2,1,0:T(8,128)S(1)} %get-tuple-element.27.local, ...), custom_call_target="tpu_custom_call", output_to_operand_aliasing={{}: (6, {})} | custom-call | flops 1638400 | bytes 3276800 | tf_op jit(solution)/shard_map/finish/pallas_call | solution.py:640
  66.6 0.0 collective-permute-done.6.outer
  66.6 2.7 %add_outer.1 = f32[5,2,256,1024]{3,2,1,0:T(8,128)} custom-call(s32[5]{0:T(128)S(1)} %stack.35.flags, f32[5,48,1024]{2,1,0:T(8,128)S(1)} %collective-permute-done.6.outer, f32[5,2,256,1024]{3,2,1,0:T(8,128)} %finish.1.held), custom_call_target="tpu_custom_call", output_to_operand_aliasing={{}: (2, {})} | custom-call | flops 1474560 | bytes 3932160 | tf_op jit(solution)/shard_map/add_outer/pallas_call | solution.py:579
  (5 shorter events, 0.1 us)
Async XLA Ops:
  2.7 30.5 %collective-permute-start.3 = (f32[5,112,1024]{2,1,0:T(8,128)}, f32[5,112,1024]{2,1,0:T(8,128)S(1)}, u32[]{:S(2)}, u32[]{:S(2)}) collective-permute-start(f32[5,112,1024]{2,1,0:T(8,128)} %get-tuple-element.21), channel_id=1, source_target_pairs={{1,2},{2,1},{5,6},{6,5},{9,10},{10,9},{13,14},{14,13},{17,18},{18,... | collective-permute-start | bytes 6881288 | tf_op jit(solution)/shard_map/ppermute | solution.py:738
  7.2 9.0 %collective-permute-start = (f32[10,1024]{1,0:T(8,128)S(1)}, f32[10,1024]{1,0:T(8,128)S(1)}, u32[]{:S(2)}, u32[]{:S(2)}) collective-permute-start(f32[10,1024]{1,0:T(8,128)S(1)} %get-tuple-element.18), channel_id=1, source_target_pairs={{0,4},{4,8},{8,12},{1,5},{5,9},{9,13},{2,6},{6,10},{10,14},{3,7},{... | collective-permute-start | bytes 122888 | tf_op jit(solution)/shard_map/ppermute | solution.py:740
  10.4 5.8 %collective-permute-start.1 = (f32[10,1024]{1,0:T(8,128)S(1)}, f32[10,1024]{1,0:T(8,128)S(1)}, u32[]{:S(2)}, u32[]{:S(2)}) collective-permute-start(f32[10,1024]{1,0:T(8,128)S(1)} %get-tuple-element.19.token), channel_id=1, source_target_pairs={{4,0},{8,4},{12,8},{5,1},{9,5},{13,9},{6,2},{10,6},{14,10},{7,3},{... | collective-permute-start | bytes 122888 | tf_op jit(solution)/shard_map/ppermute | solution.py:741
  14.3 0.7 %copy-start.1 = (f32[5,16,1024]{2,1,0:T(8,128)}, f32[5,16,1024]{2,1,0:T(8,128)S(1)}, u32[]{:S(2)}) copy-start(f32[5,16,1024]{2,1,0:T(8,128)S(1)} %get-tuple-element.20) | copy-start | bytes 983044
  15.0 10.1 %copy-start.2 = (s32[16]{0:T(128)S(1)}, s32[16]{0:T(128)}, u32[]{:S(2)}) copy-start(s32[16]{0:T(128)} %param.4) | copy-start | bytes 196
  15.0 7.6 %collective-permute-start.4 = (f32[256,128]{1,0:T(8,128)S(1)}, f32[256,128]{1,0:T(8,128)S(1)}, u32[]{:S(2)}, u32[]{:S(2)}) collective-permute-start(f32[256,128]{1,0:T(8,128)S(1)} %get-tuple-element.22.rest_0_), channel_id=1, source_target_pairs={{0,16},{16,0},{1,17},{17,1},{2,18},{18,2},{3,19},{19,3},{4,20},{20... | collective-permute-start | bytes 393224 | tf_op jit(solution)/shard_map/ppermute | solution.py:704
  21.9 3.5 %collective-permute-start.5 = (f32[5,48,1024]{2,1,0:T(8,128)}, f32[5,48,1024]{2,1,0:T(8,128)S(1)}, u32[]{:S(2)}, u32[]{:S(2)}) collective-permute-start(f32[5,48,1024]{2,1,0:T(8,128)} %get-tuple-element.23), channel_id=1, source_target_pairs={{0,1},{1,0},{2,3},{3,2},{4,5},{5,4},{6,7},{7,6},{8,9},{9,8},{10,11... | collective-permute-start | bytes 2949128 | tf_op jit(solution)/shard_map/ppermute | solution.py:751
  22.0 23.2 %collective-permute-start.10 = (f32[5,96,1024]{2,1,0:T(8,128)}, f32[5,96,1024]{2,1,0:T(8,128)}, u32[]{:S(2)}, u32[]{:S(2)}) collective-permute-start(f32[5,96,1024]{2,1,0:T(8,128)} %get-tuple-element.24.token), channel_id=1, source_target_pairs={{0,1},{1,0},{2,3},{3,2},{4,5},{5,4},{6,7},{7,6},{8,9},{9,8},{10,11... | collective-permute-start | bytes 5898248 | tf_op jit(solution)/shard_map/ppermute | solution.py:751
  22.5 32.1 %collective-permute-start.8 = (f32[5,96,1024]{2,1,0:T(8,128)}, f32[5,96,1024]{2,1,0:T(8,128)}, u32[]{:S(2)}, u32[]{:S(2)}) collective-permute-start(f32[5,96,1024]{2,1,0:T(8,128)} %get-tuple-element.29), channel_id=1, source_target_pairs={{0,1},{1,0},{2,3},{3,2},{4,5},{5,4},{6,7},{7,6},{8,9},{9,8},{10,11... | collective-permute-start | bytes 5898248 | tf_op jit(solution)/shard_map/ppermute | solution.py:751
  22.5 32.0 %collective-permute-start.9 = (f32[5,96,1024]{2,1,0:T(8,128)}, f32[5,96,1024]{2,1,0:T(8,128)}, u32[]{:S(2)}, u32[]{:S(2)}) collective-permute-start(f32[5,96,1024]{2,1,0:T(8,128)} %get-tuple-element.30), channel_id=1, source_target_pairs={{1,2},{2,1},{5,6},{6,5},{9,10},{10,9},{13,14},{14,13},{17,18},{18,... | collective-permute-start | bytes 5898248 | tf_op jit(solution)/shard_map/ppermute | solution.py:749
  25.4 6.0 %collective-permute-start.2 = (f32[5,16,1024]{2,1,0:T(8,128)}, f32[5,16,1024]{2,1,0:T(8,128)S(1)}, u32[]{:S(2)}, u32[]{:S(2)}) collective-permute-start(f32[5,16,1024]{2,1,0:T(8,128)} %copy-done.1), channel_id=1, source_target_pairs={{0,1},{1,0},{2,3},{3,2},{4,5},{5,4},{6,7},{7,6},{8,9},{9,8},{10,11... | collective-permute-start | bytes 983048 | tf_op jit(solution)/shard_map/ppermute | solution.py:742
  25.6 7.7 %copy-start = (bf16[384,640]{1,0:T(8,128)(2,1)S(1)}, bf16[384,640]{1,0:T(8,128)(2,1)}, u32[]{:S(2)}) copy-start(bf16[384,640]{1,0:T(8,128)(2,1)} %constant.54.clone.solve) | copy-start | bytes 1474564
  40.2 26.5 %collective-permute-start.6 = (f32[5,48,1024]{2,1,0:T(8,128)S(1)}, f32[5,48,1024]{2,1,0:T(8,128)S(1)}, u32[]{:S(2)}, u32[]{:S(2)}) collective-permute-start(f32[5,48,1024]{2,1,0:T(8,128)S(1)} %get-tuple-element.25), channel_id=1, source_target_pairs={{1,2},{2,1},{5,6},{6,5},{9,10},{10,9},{13,14},{14,13},{17,18},{18,... | collective-permute-start | bytes 2949128 | tf_op jit(solution)/shard_map/ppermute | solution.py:774
  43.8 20.4 %collective-permute-start.7 = (f32[16,128]{1,0:T(8,128)}, f32[16,128]{1,0:T(8,128)S(1)}, u32[]{:S(2)}, u32[]{:S(2)}) collective-permute-start(f32[16,128]{1,0:T(8,128)} %get-tuple-element.28.token), channel_id=1, source_target_pairs={{0,16},{16,0},{1,17},{17,1},{2,18},{18,2},{3,19},{19,3},{4,20},{20... | collective-permute-start | bytes 24584 | tf_op jit(solution)/shard_map/ppermute | solution.py:704

commit v10 on v9

--- a/solution.py
+++ b/solution.py
@@ -74,7 +74,7 @@
 ):
     strips = rows // EIGHT
     pieces = radial.shape[2]
-    row = lax.broadcasted_iota(jnp.int32, (EIGHT, 1), 0)
+    row = lax.broadcasted_iota(jnp.int32, (EIGHT, LANES), 0)
     lane = lax.broadcasted_iota(jnp.int32, (EIGHT, LANES), 1)
     start = flags[BASE] + first_row
     axial_sign = jnp.where(flags[ODD] == 1, 0.5, -0.5)
@@ -352,7 +352,7 @@
     block = jnp.floor((lane + 0.5) / width)
     count = cells / width
     log_ratio = table[:, COL_LOG : COL_LOG + 1]
-    gain = table[:, COL_GAIN : COL_GAIN + 1]
+    gain = jnp.broadcast_to(table[:, COL_GAIN : COL_GAIN + 1], (R_NEAR, cells))
     from_left = jnp.exp(log_ratio * (block + 1.0))
     from_right = jnp.exp(log_ratio * (count - block))
     near = flags[FIRST] == 1
@@ -662,9 +662,9 @@
 
 def chunks(rows):
     size = 16
-    triples = (rows - R_NEAR) // (3 * size)
-    cuts = sorted({-(-2 * triples // 5), -(-4 * triples // 5), triples})
-    ends = [R_NEAR + 3 * size * c for c in cuts]
+    blocks = (rows - R_NEAR) // size
+    cuts = sorted({-(-2 * blocks // 5), -(-4 * blocks // 5), blocks})
+    ends = [R_NEAR + size * c for c in cuts]
     return size, list(zip([0] + ends[:-1], ends))
 
 

time: 69.7 us -> 69.7 us (level)
  no operation moved by 1% of the time
where the time goes in v10:
time: 69.7 us; the launch traced here: 69.3 us
  Pallas kernels  46.8 us (67%)
  starting transfers between devices  18.5 us (27%)
  waiting for transfers between devices  1.95 us (3%)
  other arithmetic  0.92 us (1%)
  local copies, waits for them, and re-layouts  0.88 us (1%)
    pallas_call x3, Pallas kernels, bulk(): pl.pallas_call(functools.partial(bulk_kernel, dtheta, rows, span, total_r...  24.8 us
    pallas_call x1, Pallas kernels, near(): pl.pallas_call(functools.partial(near_kernel, dtheta, rows, part[0] if pa...  6.87 us
    pallas_call x1, Pallas kernels, pack_rest(): pl.pallas_call(functools.partial(pack_rest_kernel, parts, len(tokens)), i...  5.64 us
    ppermute x1, starting transfers between devices, body(): outer = [lax.ppermute(part, 'ax', outer_pairs)]  4.51 us
    ppermute x1, starting transfers between devices, body(): outer.append(lax.ppermute(part, 'ax', outer_pairs))  3.64 us
    ppermute x1, starting transfers between devices, body(): low = lax.ppermute(low, 'rad', up)  3.2 us
    pallas_call x1, Pallas kernels, pack_first(): pl.pallas_call(functools.partial(pack_first_kernel, count), in_specs=[ANY...  2.67 us
    pallas_call x1, Pallas kernels, add_outer(): pl.pallas_call(functools.partial(outer_kernel, rows, span), grid_spec=plt...  2.65 us
  transfers between devices with their start and end apart: 11, of which 2 were waited for; matrix products, arithmetic and copies ran while one was open for 2% of the time, Pallas kernels for 60%

profile of v10, /device:TPU:1, one launch (start us, length us, event | category | flops | bytes accessed | tf_op | source)
XLA Modules:
  0.0 69.3 jit_solution(13936070939676028252)
XLA Ops:
  0.0 2.7 %pack_first.1 = (f32[5,112,1024]{2,1,0:T(8,128)}, f32[10,1024]{1,0:T(8,128)S(1)}, f32[10,1024]{1,0:T(8,128)S(1)}) custom-call(f32[5,2,256,1024]{3,2,1,0:T(8,128)} %state.13), custom_call_target="tpu_custom_call" | custom-call | bytes 4587520 | tf_op jit(solution)/shard_map/pack_first/pallas_call | solution.py:473
  2.7 4.5 %collective-permute-start.3 = (f32[5,112,1024]{2,1,0:T(8,128)}, f32[5,112,1024]{2,1,0:T(8,128)S(1)}, u32[]{:S(2)}, u32[]{:S(2)}) collective-permute-start(f32[5,112,1024]{2,1,0:T(8,128)} %get-tuple-element.21), channel_id=1, source_target_pairs={{1,2},{2,1},{5,6},{6,5},{9,10},{10,9},{13,14},{14,13},{17,18},{18,... | collective-permute-start | bytes 6881288 | tf_op jit(solution)/shard_map/ppermute | solution.py:738
  7.2 3.2 %collective-permute-start = (f32[10,1024]{1,0:T(8,128)S(1)}, f32[10,1024]{1,0:T(8,128)S(1)}, u32[]{:S(2)}, u32[]{:S(2)}) collective-permute-start(f32[10,1024]{1,0:T(8,128)S(1)} %get-tuple-element.18), channel_id=1, source_target_pairs={{0,4},{4,8},{8,12},{1,5},{5,9},{9,13},{2,6},{6,10},{10,14},{3,7},{... | collective-permute-start | bytes 122888 | tf_op jit(solution)/shard_map/ppermute | solution.py:740
  10.4 1.3 %collective-permute-start.1 = (f32[10,1024]{1,0:T(8,128)S(1)}, f32[10,1024]{1,0:T(8,128)S(1)}, u32[]{:S(2)}, u32[]{:S(2)}) collective-permute-start(f32[10,1024]{1,0:T(8,128)S(1)} %get-tuple-element.19.token), channel_id=1, source_target_pairs={{4,0},{8,4},{12,8},{5,1},{9,5},{13,9},{6,2},{10,6},{14,10},{7,3},{... | collective-permute-start | bytes 122888 | tf_op jit(solution)/shard_map/ppermute | solution.py:741
  11.7 2.6 %pack_edges.1 = (f32[256,128]{1,0:T(8,128)S(1)}, f32[5,16,1024]{2,1,0:T(8,128)S(1)}) custom-call(f32[5,2,256,1024]{3,2,1,0:T(8,128)} %state.13, f32[10,1024]{1,0:T(8,128)S(1)} %get-tuple-element.19.token), custom_call_target="tpu_custom_call" | custom-call | bytes 5242880 | tf_op jit(solution)/shard_map/pack_edges/pallas_call | solution.py:495
  14.3 0.0 copy-start.1
  14.3 0.7 %copy-done.1 = f32[5,16,1024]{2,1,0:T(8,128)} copy-done((f32[5,16,1024]{2,1,0:T(8,128)}, f32[5,16,1024]{2,1,0:T(8,128)S(1)}, u32[]{:S(2)}) %copy-start.1) | copy-done | bytes 327704
  15.0 0.0 copy-start.2
  15.0 1.2 %collective-permute-start.4 = (f32[256,128]{1,0:T(8,128)S(1)}, f32[256,128]{1,0:T(8,128)S(1)}, u32[]{:S(2)}, u32[]{:S(2)}) collective-permute-start(f32[256,128]{1,0:T(8,128)S(1)} %get-tuple-element.22.rest_0_), channel_id=1, source_target_pairs={{0,16},{16,0},{1,17},{17,1},{2,18},{18,2},{3,19},{19,3},{4,20},{20... | collective-permute-start | bytes 393224 | tf_op jit(solution)/shard_map/ppermute | solution.py:704
  16.2 0.0 collective-permute-done.rest_1_.low
  16.2 0.0 collective-permute-done.1.rest_2_.high
  16.2 5.6 %pack_rest.1 = (f32[5,96,1024]{2,1,0:T(8,128)}, f32[5,96,1024]{2,1,0:T(8,128)}, f32[5,96,1024]{2,1,0:T(8,128)}, f32[5,48,1024]{2,1,0:T(8,128)}) custom-call(f32[5,2,256,1024]{3,2,1,0:T(8,128)} %state.13, f32[256,128]{1,0:T(8,128)S(1)} %get-tuple-element.22.rest_0_, f32[10,1024]{1,0:T(8,128)S(1)} %collective-permute-done.rest_1_.low, ...), custom_call_target="tpu_custom_call" | custom-call | bytes 13762560 | tf_op jit(solution)/shard_map/pack_rest/pallas_call | solution.py:513
  21.9 0.1 collective-permute-start.5
  22.0 0.5 collective-permute-start.10
  22.5 0.1 collective-permute-start.8
  22.5 0.0 collective-permute-done.4.edge
  22.5 2.5 %collective-permute-start.9 = (f32[5,96,1024]{2,1,0:T(8,128)}, f32[5,96,1024]{2,1,0:T(8,128)}, u32[]{:S(2)}, u32[]{:S(2)}) collective-permute-start(f32[5,96,1024]{2,1,0:T(8,128)} %get-tuple-element.30), channel_id=1, source_target_pairs={{1,2},{2,1},{5,6},{6,5},{9,10},{10,9},{13,14},{14,13},{17,18},{18,... | collective-permute-start | bytes 5898248 | tf_op jit(solution)/shard_map/ppermute | solution.py:749
  25.1 0.0 copy-done.2
  25.1 0.1 stack.35.flags
  25.3 0.1 collective-permute-done.5.inner.outer
  25.4 0.1 collective-permute-start.2
  25.5 0.1 fusion.3.table
  25.6 0.0 copy-start
  25.6 5.8 %bulk.3.token.held = f32[5,2,256,1024]{3,2,1,0:T(8,128)} custom-call(s32[5]{0:T(128)S(1)} %stack.35.flags, f32[5,2,256,1024]{3,2,1,0:T(8,128)} %state.13, f32[10,1024]{1,0:T(8,128)S(1)} %collective-permute-done.rest_1_.low, f32[10,1024]{1,0:T(8,128)S(1)} %collective-permute-done.1.rest_2_.high, f32[5,48,1024]{2,1,0:T(8,128)S(1)} %collective-permute-done.5.inner.outer, ...), custom_call_target="tpu_custom_call" | custom-call | flops 29491200 | bytes 4915200 | tf_op jit(solution)/shard_map/bulk/pallas_call | solution.py:544
  31.4 0.0 collective-permute-done.2.inner
  31.4 1.8 %collective-permute-done.3.outer = f32[5,112,1024]{2,1,0:T(8,128)S(1)} collective-permute-done((f32[5,112,1024]{2,1,0:T(8,128)}, f32[5,112,1024]{2,1,0:T(8,128)S(1)}, u32[]{:S(2)}, u32[]{:S(2)}) %collective-permute-start.3) | collective-permute-done | bytes 2293792 | tf_op jit(solution)/shard_map/ppermute | solution.py:738
  33.2 0.1 broadcast_in_dim.51.factor
  33.3 0.0 copy-done
  33.3 6.9 %near.1 = (f32[10,16,1024]{2,1,0:T(8,128)S(1)}, f32[10,16,1024]{2,1,0:T(8,128)S(1)}, f32[16,128]{1,0:T(8,128)}, f32[5,48,1024]{2,1,0:T(8,128)S(1)}) custom-call(s32[5]{0:T(128)S(1)} %stack.35.flags, f32[5,2,256,1024]{3,2,1,0:T(8,128)} %state.13, f32[5,2,256,1024]{3,2,1,0:T(8,128)} %state.13, f32[10,1024]{1,0:T(8,128)S(1)} %collective-permute-done.rest_1_.low, ...), custom_call_target="tpu_custom_call" | custom-call | flops 32768000 | bytes 40960000 | tf_op jit(solution)/shard_map/near/pallas_call | solution.py:608
  40.2 3.6 %collective-permute-start.6 = (f32[5,48,1024]{2,1,0:T(8,128)S(1)}, f32[5,48,1024]{2,1,0:T(8,128)S(1)}, u32[]{:S(2)}, u32[]{:S(2)}) collective-permute-start(f32[5,48,1024]{2,1,0:T(8,128)S(1)} %get-tuple-element.25), channel_id=1, source_target_pairs={{1,2},{2,1},{5,6},{6,5},{9,10},{10,9},{13,14},{14,13},{17,18},{18,... | collective-permute-start | bytes 2949128 | tf_op jit(solution)/shard_map/ppermute | solution.py:774
  43.8 1.3 %collective-permute-start.7 = (f32[16,128]{1,0:T(8,128)}, f32[16,128]{1,0:T(8,128)S(1)}, u32[]{:S(2)}, u32[]{:S(2)}) collective-permute-start(f32[16,128]{1,0:T(8,128)} %get-tuple-element.28.token), channel_id=1, source_target_pairs={{0,16},{16,0},{1,17},{17,1},{2,18},{18,2},{3,19},{19,3},{4,20},{20... | collective-permute-start | bytes 24584 | tf_op jit(solution)/shard_map/ppermute | solution.py:704
  45.1 0.0 collective-permute-done.10.inner
  45.1 9.4 %bulk.4.held = f32[5,2,256,1024]{3,2,1,0:T(8,128)} custom-call(s32[5]{0:T(128)S(1)} %stack.35.flags, f32[5,2,256,1024]{3,2,1,0:T(8,128)} %state.13, f32[10,1024]{1,0:T(8,128)S(1)} %collective-permute-done.rest_1_.low, f32[10,1024]{1,0:T(8,128)S(1)} %collective-permute-done.1.rest_2_.high, ...), custom_call_target="tpu_custom_call", output_to_operand_aliasing={{}: (8, {})} | custom-call | flops 58982400 | bytes 9830400 | tf_op jit(solution)/shard_map/bulk/pallas_call | solution.py:544
  54.6 0.0 collective-permute-done.8.inner
  54.6 0.0 collective-permute-done.9.outer
  54.6 9.6 %bulk.5.held = f32[5,2,256,1024]{3,2,1,0:T(8,128)} custom-call(s32[5]{0:T(128)S(1)} %stack.35.flags, f32[5,2,256,1024]{3,2,1,0:T(8,128)} %state.13, f32[10,1024]{1,0:T(8,128)S(1)} %collective-permute-done.rest_1_.low, f32[10,1024]{1,0:T(8,128)S(1)} %collective-permute-done.1.rest_2_.high, ...), custom_call_target="tpu_custom_call", output_to_operand_aliasing={{}: (8, {})} | custom-call | flops 58982400 | bytes 9830400 | tf_op jit(solution)/shard_map/bulk/pallas_call | solution.py:544
  64.2 0.0 collective-permute-done.7
  64.2 0.8 %add_multiply_fusion.carry = f32[16,128]{1,0:T(8,128)S(1)} fusion(f32[16,128]{1,0:T(8,128)S(1)} %collective-permute-done.7, f32[16,128]{1,0:T(8,128)} %get-tuple-element.28.token, f32[16]{0:T(128)S(1)} %get-tuple-element.34, f32[16]{0:T(128)S(1)} %get-tuple-element.32, f32[16]{0:T(128)S(1)} %get-tuple-element.31), kind=kLoop, calls=%fused_computation.5 | loop fusion | flops 8192 | bytes 24768 | tf_op jit(solution)/shard_map/mul | solution.py:780
  65.0 1.6 %finish.1.held = f32[5,2,256,1024]{3,2,1,0:T(8,128)} custom-call(s32[5]{0:T(128)S(1)} %stack.35.flags, f32[16,128]{1,0:T(8,128)S(1)} %broadcast_in_dim.51.factor, f32[10,16,1024]{2,1,0:T(8,128)S(1)} %get-tuple-element.26.rhs, f32[10,16,1024]{2,1,0:T(8,128)S(1)} %get-tuple-element.27.local, ...), custom_call_target="tpu_custom_call", output_to_operand_aliasing={{}: (6, {})} | custom-call | flops 1638400 | bytes 3276800 | tf_op jit(solution)/shard_map/finish/pallas_call | solution.py:640
  66.6 0.0 collective-permute-done.6.outer
  66.6 2.7 %add_outer.1 = f32[5,2,256,1024]{3,2,1,0:T(8,128)} custom-call(s32[5]{0:T(128)S(1)} %stack.35.flags, f32[5,48,1024]{2,1,0:T(8,128)S(1)} %collective-permute-done.6.outer, f32[5,2,256,1024]{3,2,1,0:T(8,128)} %finish.1.held), custom_call_target="tpu_custom_call", output_to_operand_aliasing={{}: (2, {})} | custom-call | flops 1474560 | bytes 3932160 | tf_op jit(solution)/shard_map/add_outer/pallas_call | solution.py:579
  (5 shorter events, 0.1 us)
Async XLA Ops:
  2.7 30.5 %collective-permute-start.3 = (f32[5,112,1024]{2,1,0:T(8,128)}, f32[5,112,1024]{2,1,0:T(8,128)S(1)}, u32[]{:S(2)}, u32[]{:S(2)}) collective-permute-start(f32[5,112,1024]{2,1,0:T(8,128)} %get-tuple-element.21), channel_id=1, source_target_pairs={{1,2},{2,1},{5,6},{6,5},{9,10},{10,9},{13,14},{14,13},{17,18},{18,... | collective-permute-start | bytes 6881288 | tf_op jit(solution)/shard_map/ppermute | solution.py:738
  7.2 9.0 %collective-permute-start = (f32[10,1024]{1,0:T(8,128)S(1)}, f32[10,1024]{1,0:T(8,128)S(1)}, u32[]{:S(2)}, u32[]{:S(2)}) collective-permute-start(f32[10,1024]{1,0:T(8,128)S(1)} %get-tuple-element.18), channel_id=1, source_target_pairs={{0,4},{4,8},{8,12},{1,5},{5,9},{9,13},{2,6},{6,10},{10,14},{3,7},{... | collective-permute-start | bytes 122888 | tf_op jit(solution)/shard_map/ppermute | solution.py:740
  10.4 5.8 %collective-permute-start.1 = (f32[10,1024]{1,0:T(8,128)S(1)}, f32[10,1024]{1,0:T(8,128)S(1)}, u32[]{:S(2)}, u32[]{:S(2)}) collective-permute-start(f32[10,1024]{1,0:T(8,128)S(1)} %get-tuple-element.19.token), channel_id=1, source_target_pairs={{4,0},{8,4},{12,8},{5,1},{9,5},{13,9},{6,2},{10,6},{14,10},{7,3},{... | collective-permute-start | bytes 122888 | tf_op jit(solution)/shard_map/ppermute | solution.py:741
  14.3 0.7 %copy-start.1 = (f32[5,16,1024]{2,1,0:T(8,128)}, f32[5,16,1024]{2,1,0:T(8,128)S(1)}, u32[]{:S(2)}) copy-start(f32[5,16,1024]{2,1,0:T(8,128)S(1)} %get-tuple-element.20) | copy-start | bytes 983044
  15.0 10.1 %copy-start.2 = (s32[16]{0:T(128)S(1)}, s32[16]{0:T(128)}, u32[]{:S(2)}) copy-start(s32[16]{0:T(128)} %param.4) | copy-start | bytes 196
  15.0 7.6 %collective-permute-start.4 = (f32[256,128]{1,0:T(8,128)S(1)}, f32[256,128]{1,0:T(8,128)S(1)}, u32[]{:S(2)}, u32[]{:S(2)}) collective-permute-start(f32[256,128]{1,0:T(8,128)S(1)} %get-tuple-element.22.rest_0_), channel_id=1, source_target_pairs={{0,16},{16,0},{1,17},{17,1},{2,18},{18,2},{3,19},{19,3},{4,20},{20... | collective-permute-start | bytes 393224 | tf_op jit(solution)/shard_map/ppermute | solution.py:704
  21.9 3.5 %collective-permute-start.5 = (f32[5,48,1024]{2,1,0:T(8,128)}, f32[5,48,1024]{2,1,0:T(8,128)S(1)}, u32[]{:S(2)}, u32[]{:S(2)}) collective-permute-start(f32[5,48,1024]{2,1,0:T(8,128)} %get-tuple-element.23), channel_id=1, source_target_pairs={{0,1},{1,0},{2,3},{3,2},{4,5},{5,4},{6,7},{7,6},{8,9},{9,8},{10,11... | collective-permute-start | bytes 2949128 | tf_op jit(solution)/shard_map/ppermute | solution.py:751
  22.0 23.2 %collective-permute-start.10 = (f32[5,96,1024]{2,1,0:T(8,128)}, f32[5,96,1024]{2,1,0:T(8,128)}, u32[]{:S(2)}, u32[]{:S(2)}) collective-permute-start(f32[5,96,1024]{2,1,0:T(8,128)} %get-tuple-element.24.token), channel_id=1, source_target_pairs={{0,1},{1,0},{2,3},{3,2},{4,5},{5,4},{6,7},{7,6},{8,9},{9,8},{10,11... | collective-permute-start | bytes 5898248 | tf_op jit(solution)/shard_map/ppermute | solution.py:751
  22.5 32.1 %collective-permute-start.8 = (f32[5,96,1024]{2,1,0:T(8,128)}, f32[5,96,1024]{2,1,0:T(8,128)}, u32[]{:S(2)}, u32[]{:S(2)}) collective-permute-start(f32[5,96,1024]{2,1,0:T(8,128)} %get-tuple-element.29), channel_id=1, source_target_pairs={{0,1},{1,0},{2,3},{3,2},{4,5},{5,4},{6,7},{7,6},{8,9},{9,8},{10,11... | collective-permute-start | bytes 5898248 | tf_op jit(solution)/shard_map/ppermute | solution.py:751
  22.5 32.0 %collective-permute-start.9 = (f32[5,96,1024]{2,1,0:T(8,128)}, f32[5,96,1024]{2,1,0:T(8,128)}, u32[]{:S(2)}, u32[]{:S(2)}) collective-permute-start(f32[5,96,1024]{2,1,0:T(8,128)} %get-tuple-element.30), channel_id=1, source_target_pairs={{1,2},{2,1},{5,6},{6,5},{9,10},{10,9},{13,14},{14,13},{17,18},{18,... | collective-permute-start | bytes 5898248 | tf_op jit(solution)/shard_map/ppermute | solution.py:749
  25.4 6.0 %collective-permute-start.2 = (f32[5,16,1024]{2,1,0:T(8,128)}, f32[5,16,1024]{2,1,0:T(8,128)S(1)}, u32[]{:S(2)}, u32[]{:S(2)}) collective-permute-start(f32[5,16,1024]{2,1,0:T(8,128)} %copy-done.1), channel_id=1, source_target_pairs={{0,1},{1,0},{2,3},{3,2},{4,5},{5,4},{6,7},{7,6},{8,9},{9,8},{10,11... | collective-permute-start | bytes 983048 | tf_op jit(solution)/shard_map/ppermute | solution.py:742
  25.6 7.7 %copy-start = (bf16[384,640]{1,0:T(8,128)(2,1)S(1)}, bf16[384,640]{1,0:T(8,128)(2,1)}, u32[]{:S(2)}) copy-start(bf16[384,640]{1,0:T(8,128)(2,1)} %constant.54.clone.solve) | copy-start | bytes 1474564
  40.2 26.5 %collective-permute-start.6 = (f32[5,48,1024]{2,1,0:T(8,128)S(1)}, f32[5,48,1024]{2,1,0:T(8,128)S(1)}, u32[]{:S(2)}, u32[]{:S(2)}) collective-permute-start(f32[5,48,1024]{2,1,0:T(8,128)S(1)} %get-tuple-element.25), channel_id=1, source_target_pairs={{1,2},{2,1},{5,6},{6,5},{9,10},{10,9},{13,14},{14,13},{17,18},{18,... | collective-permute-start | bytes 2949128 | tf_op jit(solution)/shard_map/ppermute | solution.py:774
  43.8 20.4 %collective-permute-start.7 = (f32[16,128]{1,0:T(8,128)}, f32[16,128]{1,0:T(8,128)S(1)}, u32[]{:S(2)}, u32[]{:S(2)}) collective-permute-start(f32[16,128]{1,0:T(8,128)} %get-tuple-element.28.token), channel_id=1, source_target_pairs={{0,16},{16,0},{1,17},{17,1},{2,18},{18,2},{3,19},{19,3},{4,20},{20... | collective-permute-start | bytes 24584 | tf_op jit(solution)/shard_map/ppermute | solution.py:704

commit v11 on v10

--- a/solution.py
+++ b/solution.py
@@ -25,6 +25,8 @@
 
 COL_LOG = 32
 COL_GAIN = 33
+COL_CLOSING = 34
+COL_ACROSS = 35
 
 ODD, OUTER, FIRST, LAST, BASE = range(5)
 
@@ -150,8 +152,10 @@
 
 
 def bulk_kernel(
-    dtheta, rows, span, total_rows, fused, flags, state, low, high, inner, edge, outer, token, held, out, *scratch
+    dtheta, rows, span, total_rows, fused, pieces, flags, state, low, high, edge, outer, token, held, *rest
 ):
+    inner, out, scratch = rest[:pieces], rest[pieces], rest[pieces + 1 :]
+    inner_blocks = [(x, pl.ds(r, rows)) for x in inner for r in range(0, x.shape[1], rows)]
     first, end = span
     blocks = (end - first) // rows
     state_rows, inner_rows, sems, radial, azimuthal, *outer_rows = scratch
@@ -167,7 +171,7 @@
         here = pl.ds(k * rows, rows)
         sets = [
             (state.at[:, :, a:b, :], state_rows.at[:, :, at : at + b - a, :]),
-            (inner.at[:, here, :], inner_rows.at[:, here, :]),
+            (inner_blocks[k][0].at[:, inner_blocks[k][1], :], inner_rows.at[:, here, :]),
         ]
         if fused:
             sets.append((outer.at[:, rest, :], outer_rows.at[:, here, :]))
@@ -345,8 +349,17 @@
         copy.wait()
 
 
-def finish_kernel(flags, factor, rhs, local, carry, table, held, out):
+def finish_kernel(flags, factor, rhs, local, table, *rest):
+    *ends, held, out = rest
     cells = out.shape[-1]
+    column = lax.broadcasted_iota(jnp.int32, (R_NEAR, LANES), 1)
+    ends = [x[...] for x in ends]
+    ends.append(ends[0])
+    carry = jnp.zeros((R_NEAR, LANES), jnp.float32)
+    for k in range(len(ends) - 1, 0, -1):
+        arrived = jnp.where(column < LINES, ends[k], ends[len(ends) - 1 - k])
+        carry = carry * table[:, COL_ACROSS : COL_ACROSS + 1] + arrived
+    carry = carry * table[:, COL_CLOSING : COL_CLOSING + 1]
     lane = lax.broadcasted_iota(jnp.int32, (R_NEAR, cells), 1).astype(jnp.float32)
     width = factor[:, 0:1]
     block = jnp.floor((lane + 0.5) / width)
@@ -387,38 +400,46 @@
     return finish
 
 
-def pack_first_kernel(count, state, part, low, high, stage, top, bottom, row_sems, sems):
+def pack_first_kernel(count, state, part, low, high, stage, top, bottom, low_row, high_row, row_sems, sems):
     _, _, rows, _ = state.shape
     odd = lax.axis_index("ax") % 2
-    finish = stream([(state.at[:, odd, 0:count, :], stage, part)], sems)
     copies = [
         pltpu.make_async_copy(state.at[:, :, rows - EIGHT : rows, :], top, row_sems.at[0]),
         pltpu.make_async_copy(state.at[:, :, 0:EIGHT, :], bottom, row_sems.at[1]),
     ]
+    leave = [
+        pltpu.make_async_copy(low_row, low, row_sems.at[2]),
+        pltpu.make_async_copy(high_row, high, row_sems.at[3]),
+    ]
     for copy in copies:
         copy.start()
-    finish()
+    finish = stream([(state.at[:, odd, 0:count, :], stage, part)], sems)
     for copy in copies:
         copy.wait()
     for f in range(FIELDS):
         for q in range(PLANES):
             k = f * PLANES + q
             p = plane_of(odd, q)
-            low[k : k + 1, :] = top[f, p, EIGHT - 1 : EIGHT, :]
-            high[k : k + 1, :] = bottom[f, p, 0:1, :]
-
-
-def pack_edges_kernel(state, token, edge, side, left, right, sems):
+            low_row[k : k + 1, :] = top[f, p, EIGHT - 1 : EIGHT, :]
+            high_row[k : k + 1, :] = bottom[f, p, 0:1, :]
+    for copy in leave:
+        copy.start()
+    finish()
+    for copy in leave:
+        copy.wait()
+
+
+def pack_edges_kernel(state, token, edge, side, left, right, columns_row, stage, col_sems, sems):
     _, _, rows, cells = state.shape
     odd = lax.axis_index("ax") % 2
     copies = [
-        pltpu.make_async_copy(state.at[:, :, :, cells - LANES : cells], left, sems.at[0]),
-        pltpu.make_async_copy(state.at[:, :, :, 0:LANES], right, sems.at[1]),
-        pltpu.make_async_copy(state.at[:, 1 - odd, 0:R_NEAR, :], side, sems.at[2]),
+        pltpu.make_async_copy(state.at[:, :, :, cells - LANES : cells], left, col_sems.at[0]),
+        pltpu.make_async_copy(state.at[:, :, :, 0:LANES], right, col_sems.at[1]),
     ]
     for copy in copies:
         copy.start()
-    for copy in copies[:2]:
+    finish = stream([(state.at[:, 1 - odd, 0:R_NEAR, :], stage, side)], sems)
+    for copy in copies:
         copy.wait()
     lane = lax.broadcasted_iota(jnp.int32, (rows, LANES), 1)
     columns = jnp.ones((rows, LANES), jnp.float32)
@@ -427,8 +448,11 @@
             p = plane_of(odd, q)
             columns = jnp.where(lane == 4 * f + q, left[f, p, :, LANES - 1 : LANES], columns)
             columns = jnp.where(lane == (4 * f - 1 - q) % LANES, right[f, p, :, 0:1], columns)
-    edge[...] = columns
-    copies[2].wait()
+    columns_row[...] = columns
+    leave = pltpu.make_async_copy(columns_row, edge, col_sems.at[2])
+    leave.start()
+    finish()
+    leave.wait()
 
 
 def pack_rest_kernel(parts, tokens, state, *rest):
@@ -467,19 +491,24 @@
 
 def pack_first(state, count):
     fields, planes, _, cells = state.shape
-    vmem = pl.BlockSpec(memory_space=pltpu.VMEM)
-    row = jax.ShapeDtypeStruct((LINES, cells), jnp.float32)
     rows = pltpu.VMEM((fields, planes, EIGHT, cells), jnp.float32)
+    row = pltpu.VMEM((LINES, cells), jnp.float32)
     return pl.pallas_call(
         functools.partial(pack_first_kernel, count),
         in_specs=[ANY],
-        out_specs=[ANY, vmem, vmem],
-        out_shape=[jax.ShapeDtypeStruct((fields, count, cells), jnp.float32), row, row],
+        out_specs=[ANY] * 3,
+        out_shape=[
+            jax.ShapeDtypeStruct((fields, count, cells), jnp.float32),
+            jax.ShapeDtypeStruct((LINES, cells), jnp.float32),
+            jax.ShapeDtypeStruct((LINES, cells), jnp.float32),
+        ],
         scratch_shapes=[
             pltpu.VMEM((fields, count, cells), jnp.float32),
             rows,
             rows,
-            pltpu.SemaphoreType.DMA((2,)),
+            row,
+            row,
+            pltpu.SemaphoreType.DMA((4,)),
             pltpu.SemaphoreType.DMA((2 * fields,)),
         ],
         compiler_params=PARAMS,
@@ -490,17 +519,23 @@
 
 def pack_edges(state, token):
     fields, planes, rows, cells = state.shape
-    vmem = pl.BlockSpec(memory_space=pltpu.VMEM)
     tiles = pltpu.VMEM((fields, planes, rows, LANES), jnp.float32)
     return pl.pallas_call(
         pack_edges_kernel,
         in_specs=[ANY, ANY],
-        out_specs=[vmem, vmem],
+        out_specs=[ANY, ANY],
         out_shape=[
             jax.ShapeDtypeStruct((rows, LANES), jnp.float32),
-            jax.ShapeDtypeStruct((fields, R_NEAR, cells), jnp.float32),
+            pltpu.HBM((fields, R_NEAR, cells), jnp.float32),
         ],
-        scratch_shapes=[tiles, tiles, pltpu.SemaphoreType.DMA((3,))],
+        scratch_shapes=[
+            tiles,
+            tiles,
+            pltpu.VMEM((rows, LANES), jnp.float32),
+            pltpu.VMEM((fields, R_NEAR, cells), jnp.float32),
+            pltpu.SemaphoreType.DMA((3,)),
+            pltpu.SemaphoreType.DMA((2 * fields,)),
+        ],
         compiler_params=PARAMS,
         cost_estimate=cost(0, fields * planes * rows * LANES * 16),
         name="pack_edges",
@@ -536,13 +571,13 @@
     count = end - first
     blocks = count // rows
     size = fields * planes * count * cells
-    aliases = {} if held is None else {8: 0}
+    aliases = {} if held is None else {7: 0}
     state = in_hbm(state)
-    operands = [state, low, high, inner, edge, inner if outer is None else outer, in_hbm(token)]
-    operands.append(state if held is None else held)
+    operands = [state, low, high, edge, inner[0] if outer is None else outer, in_hbm(token)]
+    operands += [state if held is None else held, *inner]
     chunk = pltpu.VMEM((fields, count, cells), jnp.float32)
     return pl.pallas_call(
-        functools.partial(bulk_kernel, dtheta, rows, span, total_rows, outer is not None),
+        functools.partial(bulk_kernel, dtheta, rows, span, total_rows, outer is not None, len(inner)),
         grid_spec=pltpu.PrefetchScalarGridSpec(
             num_scalar_prefetch=1,
             grid=(blocks,),
@@ -550,11 +585,8 @@
                 ANY,
                 whole(LINES, cells),
                 whole(LINES, cells),
-                ANY,
                 rows_from((rows, LANES), 0, first, rows),
-                ANY,
-                ANY,
-                ANY,
+                *[ANY] * (3 + len(inner)),
             ],
             out_specs=rows_from((fields, planes, rows, cells), 2, first, rows),
             scratch_shapes=[
@@ -635,7 +667,7 @@
     return result if part is not None else (*result, None)
 
 
-def finish(flags, factor, rhs, local, carry, table, held):
+def finish(flags, factor, rhs, local, table, ends, held):
     _, _, cells = rhs.shape
     return pl.pallas_call(
         finish_kernel,
@@ -647,23 +679,23 @@
                 whole(LINES, R_NEAR, cells),
                 whole(LINES, R_NEAR, cells),
                 whole(R_NEAR, LANES),
-                whole(R_NEAR, LANES),
+                *[whole(R_NEAR, LANES)] * len(ends),
                 ANY,
             ],
             out_specs=whole(FIELDS, PLANES, R_NEAR, cells),
         ),
         out_shape=pltpu.HBM(held.shape, jnp.float32),
-        input_output_aliases={6: 0},
+        input_output_aliases={5 + len(ends): 0},
         compiler_params=PARAMS,
         cost_estimate=cost(LINES * R_NEAR * cells * 10, LINES * R_NEAR * cells * 20),
         name="finish",
-    )(flags, factor, rhs, local, carry, table, held)
+    )(flags, factor, rhs, local, table, *ends, held)
 
 
 def chunks(rows):
     size = 16
     blocks = (rows - R_NEAR) // size
-    cuts = sorted({-(-2 * blocks // 5), -(-4 * blocks // 5), blocks})
+    cuts = sorted({-(-2 * blocks // 5), -(-11 * blocks // 15), blocks})
     ends = [R_NEAR + size * c for c in cuts]
     return size, list(zip([0] + ends[:-1], ends))
 
@@ -682,7 +714,8 @@
     table = jnp.where(width >= factor, jnp.exp(log_ratio * (width / factor)), 0.0)
     table = jnp.where(column == COL_LOG, log_ratio, table)
     table = jnp.where(column == COL_GAIN, gain, table)
-    return table, closing, across
+    table = jnp.where(column == COL_CLOSING, closing, table)
+    return jnp.where(column == COL_ACROSS, across, table)
 
 
 def piece_tables(dtheta):
@@ -739,49 +772,50 @@
     columns, side = pack_edges(state, high)
     low = lax.ppermute(low, "rad", up)
     high = lax.ppermute(high, "rad", down)
-    inner = [lax.ppermute(side, "ax", inner_pairs)]
-    wanted = [(0, R_NEAR, spans[0][1])] + [(0, *span) for span in spans[1:]]
+    near_inner = lax.ppermute(side, "ax", inner_pairs)
+    wanted = [(0, R_NEAR, spans[0][1], 0)]
+    for k in range(1, count):
+        first, last = spans[k]
+        cut = min(first + 2 * size, last) if k == count - 1 else last
+        wanted += [(0, a, b, k) for a, b in ((first, cut), (cut, last)) if a < b]
     if count > 1:
-        wanted.insert(1, (1, *spans[1]))
-    parts = pack_rest(state, wanted, columns, low, high)
-    for k, value in enumerate(parts):
-        if wanted[k][0]:
+        wanted.insert(1, (1, *spans[1], 1))
+    parts = pack_rest(state, [piece[:3] for piece in wanted], columns, low, high)
+    inner = [[] for _ in spans]
+    for (q, _, _, k), value in zip(wanted, parts):
+        if q:
             outer.append(lax.ppermute(value, "ax", outer_pairs))
         else:
-            inner.append(lax.ppermute(value, "ax", inner_pairs))
+            inner[k].append(lax.ppermute(value, "ax", inner_pairs))
     if sec_count == 2:
         edge = ring(columns, "sec", 1)
     else:
         from_left = jnp.arange(LANES)[None, :] % 4 < 2
         edge = jnp.where(from_left, ring(columns, "sec", 1), ring(columns, "sec", -1))
 
-    table, closing, across = smoothing_table(coarsen, cells, total_cells, dtheta)
+    table = smoothing_table(coarsen, cells, total_cells, dtheta)
     factor = jnp.broadcast_to(coarsen.astype(jnp.float32)[:, None], (R_NEAR, LANES))
 
     solve = piece_tables(dtheta)
     given = (flags, state, low, high)
     def pass_over(k, token, held, fused=True):
         span = (spans[k][0] if k else R_NEAR, spans[k][1])
-        return bulk(*given, inner[k + 1], edge, dtheta, outer[k] if fused else None, span, size, token, held)
+        far = outer[k] if fused else None
+        return bulk(*given, inner[k], edge, dtheta, far, span, size, token, held)
 
     out = pass_over(2, parts[0], None, fused=False) if count > 2 else None
     part = spans[2] if count > 2 else None
     token = parts[0] if out is None else out
     rhs, local, ends, part = near(
-        *given, inner[0], edge, dtheta, outer[0], factor, table, solve, token, part
+        *given, near_inner, edge, dtheta, outer[0], factor, table, solve, token, part
     )
     if part is not None:
         outer.append(lax.ppermute(part, "ax", outer_pairs))
-    arrived = [ends] + [ring(ends, "sec", k) for k in range(1, sec_count)] + [ends]
-    from_left = jnp.arange(LANES)[None, :] < LINES
-    carry = jnp.zeros_like(ends)
-    for k in range(sec_count, 0, -1):
-        carry = carry * across + jnp.where(from_left, arrived[k], arrived[sec_count - k])
-    carry = carry * closing
+    all_ends = [ends] + [ring(ends, "sec", k) for k in range(1, sec_count)]
 
     for k in range(min(count, 2)):
         out = pass_over(k, ends, out)
-    out = finish(flags, factor, rhs, local, carry, table, out)
+    out = finish(flags, factor, rhs, local, table, all_ends, out)
     return add_outer(flags, outer[2], spans[2], size, out) if count > 2 else out
 
 

time: 69.7 us -> 71 us (1.019)
  local copies, waits for them, and re-layouts: 0.88 us -> 2.61 us
  Pallas kernels: 46.8 us -> 48.4 us
  starting transfers between devices: 18.5 us -> 17.3 us
  other arithmetic: 0.92 us -> 0.15 us
    ppermute x1, waiting for transfers between devices: 1.85 us -> 0.01 us  [body(): outer = [lax.ppermute(part, 'ax', outer_pairs)]]
    ppermute x4 -> x5, waiting for transfers between devices: 0.09 us -> 1.87 us  [the longest x4 1.86 us: body(): inner[k].append(lax.ppermute(value, 'ax', inner_pairs))]
    unnamed x6 -> x8, local copies, waits for them, and re-layouts: 0.72 us -> 2.46 us
    pallas_call x1, Pallas kernels: 2.55 us -> 3.63 us  [pack_edges(): pl.pallas_call(pack_edges_kernel, in_specs=[ANY, ANY], out_specs=[ANY, AN...]
    ppermute x2, starting transfers between devices: 2.54 us -> 1.59 us  [ring(): lax.ppermute(value, axis, [(i, (i + shift) % size) for i in range(size)])]
    pallas_call x1, Pallas kernels: 5.64 us -> 4.74 us  [pack_rest(): pl.pallas_call(functools.partial(pack_rest_kernel, parts, len(tokens)), i...]
    mul x1 -> x0, other arithmetic: 0.77 us -> none  [body(): carry = carry * closing]
    pallas_call x1, Pallas kernels: 1.62 us -> 2.37 us  [finish(): pl.pallas_call(finish_kernel, grid_spec=pltpu.PrefetchScalarGridSpec(num_...]
  transfers between devices with their start and end apart: 11 -> 12, of which waited for: 2 -> 1; matrix products, arithmetic and copies ran while one was open for 2% -> 0% of each run, Pallas kernels for 60% -> 60%
where the time goes in v11:
time: 71 us; the launch traced here: 70.6 us
  Pallas kernels  48.4 us (68%)
  starting transfers between devices  17.3 us (24%)
  local copies, waits for them, and re-layouts  2.61 us (4%)
  waiting for transfers between devices  1.88 us (3%)
    pallas_call x3, Pallas kernels, bulk(): pl.pallas_call(functools.partial(bulk_kernel, dtheta, rows, span, total_r...  24.6 us
    pallas_call x1, Pallas kernels, near(): pl.pallas_call(functools.partial(near_kernel, dtheta, rows, part[0] if pa...  6.92 us
    pallas_call x1, Pallas kernels, pack_rest(): pl.pallas_call(functools.partial(pack_rest_kernel, parts, len(tokens)), i...  4.74 us
    ppermute x1, starting transfers between devices, body(): outer = [lax.ppermute(part, 'ax', outer_pairs)]  4.51 us
    pallas_call x1, Pallas kernels, pack_edges(): pl.pallas_call(pack_edges_kernel, in_specs=[ANY, ANY], out_specs=[ANY, AN...  3.63 us
    pallas_call x1, Pallas kernels, pack_first(): pl.pallas_call(functools.partial(pack_first_kernel, count), in_specs=[ANY...  3.34 us
    ppermute x1, starting transfers between devices, body(): low = lax.ppermute(low, 'rad', up)  3.2 us
    ppermute x1, starting transfers between devices, body(): outer.append(lax.ppermute(part, 'ax', outer_pairs))  3.05 us
  transfers between devices with their start and end apart: 12, of which 1 were waited for; matrix products, arithmetic and copies ran while one was open for 0% of the time, Pallas kernels for 60%

profile of v11, /device:TPU:1, one launch (start us, length us, event | category | flops | bytes accessed | tf_op | source)
XLA Modules:
  0.0 70.6 jit_solution(1831380050957860855)
XLA Ops:
  0.0 3.3 %pack_first.1 = (f32[5,112,1024]{2,1,0:T(8,128)}, f32[10,1024]{1,0:T(8,128)S(1)}, f32[10,1024]{1,0:T(8,128)S(1)}) custom-call(f32[5,2,256,1024]{3,2,1,0:T(8,128)} %state.13), custom_call_target="tpu_custom_call" | custom-call | bytes 4587520 | tf_op jit(solution)/shard_map/pack_first/pallas_call | solution.py:496
  3.3 4.5 %collective-permute-start.3 = (f32[5,112,1024]{2,1,0:T(8,128)}, f32[5,112,1024]{2,1,0:T(8,128)S(1)}, u32[]{:S(2)}, u32[]{:S(2)}) collective-permute-start(f32[5,112,1024]{2,1,0:T(8,128)} %get-tuple-element.22), channel_id=1, source_target_pairs={{1,2},{2,1},{5,6},{6,5},{9,10},{10,9},{13,14},{14,13},{17,18},{18,... | collective-permute-start | bytes 6881288 | tf_op jit(solution)/shard_map/ppermute | solution.py:771
  7.9 3.2 %collective-permute-start = (f32[10,1024]{1,0:T(8,128)S(1)}, f32[10,1024]{1,0:T(8,128)S(1)}, u32[]{:S(2)}, u32[]{:S(2)}) collective-permute-start(f32[10,1024]{1,0:T(8,128)S(1)} %get-tuple-element.19), channel_id=1, source_target_pairs={{0,4},{4,8},{8,12},{1,5},{5,9},{9,13},{2,6},{6,10},{10,14},{3,7},{... | collective-permute-start | bytes 122888 | tf_op jit(solution)/shard_map/ppermute | solution.py:773
  11.1 1.3 %collective-permute-start.1 = (f32[10,1024]{1,0:T(8,128)S(1)}, f32[10,1024]{1,0:T(8,128)S(1)}, u32[]{:S(2)}, u32[]{:S(2)}) collective-permute-start(f32[10,1024]{1,0:T(8,128)S(1)} %get-tuple-element.20.token), channel_id=1, source_target_pairs={{4,0},{8,4},{12,8},{5,1},{9,5},{13,9},{6,2},{10,6},{14,10},{7,3},{... | collective-permute-start | bytes 122888 | tf_op jit(solution)/shard_map/ppermute | solution.py:774
  12.4 3.6 %pack_edges.1 = (f32[256,128]{1,0:T(8,128)S(1)}, f32[5,16,1024]{2,1,0:T(8,128)}) custom-call(f32[5,2,256,1024]{3,2,1,0:T(8,128)} %state.13, f32[10,1024]{1,0:T(8,128)S(1)} %get-tuple-element.20.token), custom_call_target="tpu_custom_call" | custom-call | bytes 5242880 | tf_op jit(solution)/shard_map/pack_edges/pallas_call | solution.py:523
  16.0 0.0 copy-start.3
  16.0 1.3 %collective-permute-start.4 = (f32[256,128]{1,0:T(8,128)S(1)}, f32[256,128]{1,0:T(8,128)S(1)}, u32[]{:S(2)}, u32[]{:S(2)}) collective-permute-start(f32[256,128]{1,0:T(8,128)S(1)} %get-tuple-element.23.rest_0_), channel_id=1, source_target_pairs={{0,16},{16,0},{1,17},{17,1},{2,18},{18,2},{3,19},{19,3},{4,20},{20... | collective-permute-start | bytes 393224 | tf_op jit(solution)/shard_map/ppermute | solution.py:737
  17.3 0.0 collective-permute-done.rest_1_.low
  17.3 0.0 collective-permute-done.1.rest_2_.high
  17.3 4.7 %pack_rest.1 = (f32[5,96,1024]{2,1,0:T(8,128)}, f32[5,80,1024]{2,1,0:T(8,128)S(1)}, f32[5,80,1024]{2,1,0:T(8,128)S(1)}, f32[5,32,1024]{2,1,0:T(8,128)}, f32[5,32,1024]{2,1,0:T(8,128)}) custom-call(f32[5,2,256,1024]{3,2,1,0:T(8,128)} %state.13, f32[256,128]{1,0:T(8,128)S(1)} %get-tuple-element.23.rest_0_, f32[10,1024]{1,0:T(8,128)S(1)} %collective-permute-done.rest_1_.low, ...), custom_call_target="tpu_custom_call" | custom-call | bytes 13107200 | tf_op jit(solution)/shard_map/pack_rest/pallas_call | solution.py:548
  22.1 0.0 copy-start.1
  22.1 1.2 %copy-done.1 = f32[5,80,1024]{2,1,0:T(8,128)} copy-done((f32[5,80,1024]{2,1,0:T(8,128)}, f32[5,80,1024]{2,1,0:T(8,128)S(1)}, u32[]{:S(2)}) %copy-start.1) | copy-done | bytes 1638424
  23.3 0.0 copy-start.2
  23.3 1.3 %copy-done.2 = f32[5,80,1024]{2,1,0:T(8,128)} copy-done((f32[5,80,1024]{2,1,0:T(8,128)}, f32[5,80,1024]{2,1,0:T(8,128)S(1)}, u32[]{:S(2)}) %copy-start.2) | copy-done | bytes 1638424
  24.5 0.0 collective-permute-start.5
  24.5 0.5 collective-permute-start.6
  25.1 0.0 copy-done.3
  25.1 0.1 collective-permute-start.10
  25.3 0.1 stack.35.flags
  25.3 0.0 collective-permute-done.4.edge
  25.3 0.6 collective-permute-start.2
  25.9 1.9 %collective-permute-done.5.outer.rest_0_ = f32[5,32,1024]{2,1,0:T(8,128)S(1)} collective-permute-done((f32[5,32,1024]{2,1,0:T(8,128)}, f32[5,32,1024]{2,1,0:T(8,128)S(1)}, u32[]{:S(2)}, u32[]{:S(2)}) %collective-permute-start.5) | collective-permute-done | bytes 655392 | tf_op jit(solution)/shard_map/ppermute | solution.py:789
  27.8 2.5 %collective-permute-start.9 = (f32[5,80,1024]{2,1,0:T(8,128)}, f32[5,80,1024]{2,1,0:T(8,128)S(1)}, u32[]{:S(2)}, u32[]{:S(2)}) collective-permute-start(f32[5,80,1024]{2,1,0:T(8,128)} %copy-done.2), channel_id=1, source_target_pairs={{1,2},{2,1},{5,6},{6,5},{9,10},{10,9},{13,14},{14,13},{17,18},{18,... | collective-permute-start | bytes 4915208 | tf_op jit(solution)/shard_map/ppermute | solution.py:787
  30.2 0.0 collective-permute-done.6.rest_1_
  30.2 0.1 collective-permute-start.11
  30.3 0.1 fusion.5.table
  30.4 0.0 copy-start
  30.4 6.8 %bulk.3.token.held = f32[5,2,256,1024]{3,2,1,0:T(8,128)} custom-call(s32[5]{0:T(128)S(1)} %stack.35.flags, f32[5,2,256,1024]{3,2,1,0:T(8,128)} %state.13, f32[10,1024]{1,0:T(8,128)S(1)} %collective-permute-done.rest_1_.low, f32[10,1024]{1,0:T(8,128)S(1)} %collective-permute-done.1.rest_2_.high, f32[256,128]{1,0:T(8,128)S(1)} %collective-permute-done.4.edge, ...), custom_call_target="tpu_custom_call" | custom-call | flops 39321600 | bytes 6553600 | tf_op jit(solution)/shard_map/bulk/pallas_call | solution.py:579
  37.3 0.0 collective-permute-done.2.inner
  37.3 0.0 collective-permute-done.3.outer
  37.3 0.1 broadcast_in_dim.58.factor
  37.4 0.0 copy-done
  37.4 6.9 %near.1 = (f32[10,16,1024]{2,1,0:T(8,128)S(1)}, f32[10,16,1024]{2,1,0:T(8,128)S(1)}, f32[16,128]{1,0:T(8,128)}, f32[5,64,1024]{2,1,0:T(8,128)S(1)}) custom-call(s32[5]{0:T(128)S(1)} %stack.35.flags, f32[5,2,256,1024]{3,2,1,0:T(8,128)} %state.13, f32[5,2,256,1024]{3,2,1,0:T(8,128)} %state.13, f32[10,1024]{1,0:T(8,128)S(1)} %collective-permute-done.rest_1_.low, ...), custom_call_target="tpu_custom_call" | custom-call | flops 32768000 | bytes 40960000 | tf_op jit(solution)/shard_map/near/pallas_call | solution.py:640
  44.3 3.1 %collective-permute-start.7 = (f32[5,64,1024]{2,1,0:T(8,128)S(1)}, f32[5,64,1024]{2,1,0:T(8,128)S(1)}, u32[]{:S(2)}, u32[]{:S(2)}) collective-permute-start(f32[5,64,1024]{2,1,0:T(8,128)S(1)} %get-tuple-element.27), channel_id=1, source_target_pairs={{1,2},{2,1},{5,6},{6,5},{9,10},{10,9},{13,14},{14,13},{17,18},{18,... | collective-permute-start | bytes 3932168 | tf_op jit(solution)/shard_map/ppermute | solution.py:813
  47.4 0.3 collective-permute-start.8
  47.6 0.0 collective-permute-done.10.rest_0_
  47.6 9.5 %bulk.4.held = f32[5,2,256,1024]{3,2,1,0:T(8,128)} custom-call(s32[5]{0:T(128)S(1)} %stack.35.flags, f32[5,2,256,1024]{3,2,1,0:T(8,128)} %state.13, f32[10,1024]{1,0:T(8,128)S(1)} %collective-permute-done.rest_1_.low, f32[10,1024]{1,0:T(8,128)S(1)} %collective-permute-done.1.rest_2_.high, ...), custom_call_target="tpu_custom_call", output_to_operand_aliasing={{}: (7, {})} | custom-call | flops 58982400 | bytes 9830400 | tf_op jit(solution)/shard_map/bulk/pallas_call | solution.py:579
  57.1 0.0 collective-permute-done.9.outer
  57.1 0.0 collective-permute-done.11.rest_0_
  57.1 8.3 %bulk.5.rest_2_ = f32[5,2,256,1024]{3,2,1,0:T(8,128)} custom-call(s32[5]{0:T(128)S(1)} %stack.35.flags, f32[5,2,256,1024]{3,2,1,0:T(8,128)} %state.13, f32[10,1024]{1,0:T(8,128)S(1)} %collective-permute-done.rest_1_.low, f32[10,1024]{1,0:T(8,128)S(1)} %collective-permute-done.1.rest_2_.high, ...), custom_call_target="tpu_custom_call", output_to_operand_aliasing={{}: (7, {})} | custom-call | flops 49152000 | bytes 8192000 | tf_op jit(solution)/shard_map/bulk/pallas_call | solution.py:579
  65.4 0.0 collective-permute-done.8.rest_1_
  65.4 2.4 %finish.1.held = f32[5,2,256,1024]{3,2,1,0:T(8,128)} custom-call(s32[5]{0:T(128)S(1)} %stack.35.flags, f32[16,128]{1,0:T(8,128)S(1)} %broadcast_in_dim.58.factor, f32[10,16,1024]{2,1,0:T(8,128)S(1)} %get-tuple-element.28.rhs, f32[10,16,1024]{2,1,0:T(8,128)S(1)} %get-tuple-element.29.local, ...), custom_call_target="tpu_custom_call", output_to_operand_aliasing={{}: (7, {})} | custom-call | flops 1638400 | bytes 3276800 | tf_op jit(solution)/shard_map/finish/pallas_call | solution.py:672
  67.8 0.0 collective-permute-done.7.outer
  67.8 2.8 %add_outer.1 = f32[5,2,256,1024]{3,2,1,0:T(8,128)} custom-call(s32[5]{0:T(128)S(1)} %stack.35.flags, f32[5,64,1024]{2,1,0:T(8,128)S(1)} %collective-permute-done.7.outer, f32[5,2,256,1024]{3,2,1,0:T(8,128)} %finish.1.held), custom_call_target="tpu_custom_call", output_to_operand_aliasing={{}: (2, {})} | custom-call | flops 1966080 | bytes 5242880 | tf_op jit(solution)/shard_map/add_outer/pallas_call | solution.py:611
  (6 shorter events, 0.1 us)
Async XLA Ops:
  3.3 33.9 %collective-permute-start.3 = (f32[5,112,1024]{2,1,0:T(8,128)}, f32[5,112,1024]{2,1,0:T(8,128)S(1)}, u32[]{:S(2)}, u32[]{:S(2)}) collective-permute-start(f32[5,112,1024]{2,1,0:T(8,128)} %get-tuple-element.22), channel_id=1, source_target_pairs={{1,2},{2,1},{5,6},{6,5},{9,10},{10,9},{13,14},{14,13},{17,18},{18,... | collective-permute-start | bytes 6881288 | tf_op jit(solution)/shard_map/ppermute | solution.py:771
  7.9 9.5 %collective-permute-start = (f32[10,1024]{1,0:T(8,128)S(1)}, f32[10,1024]{1,0:T(8,128)S(1)}, u32[]{:S(2)}, u32[]{:S(2)}) collective-permute-start(f32[10,1024]{1,0:T(8,128)S(1)} %get-tuple-element.19), channel_id=1, source_target_pairs={{0,4},{4,8},{8,12},{1,5},{5,9},{9,13},{2,6},{6,10},{10,14},{3,7},{... | collective-permute-start | bytes 122888 | tf_op jit(solution)/shard_map/ppermute | solution.py:773
  11.1 6.3 %collective-permute-start.1 = (f32[10,1024]{1,0:T(8,128)S(1)}, f32[10,1024]{1,0:T(8,128)S(1)}, u32[]{:S(2)}, u32[]{:S(2)}) collective-permute-start(f32[10,1024]{1,0:T(8,128)S(1)} %get-tuple-element.20.token), channel_id=1, source_target_pairs={{4,0},{8,4},{12,8},{5,1},{9,5},{13,9},{6,2},{10,6},{14,10},{7,3},{... | collective-permute-start | bytes 122888 | tf_op jit(solution)/shard_map/ppermute | solution.py:774
  16.0 9.0 %copy-start.3 = (s32[16]{0:T(128)S(1)}, s32[16]{0:T(128)}, u32[]{:S(2)}) copy-start(s32[16]{0:T(128)} %param.4) | copy-start | bytes 196
  16.0 9.3 %collective-permute-start.4 = (f32[256,128]{1,0:T(8,128)S(1)}, f32[256,128]{1,0:T(8,128)S(1)}, u32[]{:S(2)}, u32[]{:S(2)}) collective-permute-start(f32[256,128]{1,0:T(8,128)S(1)} %get-tuple-element.23.rest_0_), channel_id=1, source_target_pairs={{0,16},{16,0},{1,17},{17,1},{2,18},{18,2},{3,19},{19,3},{4,20},{20... | collective-permute-start | bytes 393224 | tf_op jit(solution)/shard_map/ppermute | solution.py:737
  22.1 1.2 %copy-start.1 = (f32[5,80,1024]{2,1,0:T(8,128)}, f32[5,80,1024]{2,1,0:T(8,128)S(1)}, u32[]{:S(2)}) copy-start(f32[5,80,1024]{2,1,0:T(8,128)S(1)} %get-tuple-element.32) | copy-start | bytes 4915204
  23.3 1.3 %copy-start.2 = (f32[5,80,1024]{2,1,0:T(8,128)}, f32[5,80,1024]{2,1,0:T(8,128)S(1)}, u32[]{:S(2)}) copy-start(f32[5,80,1024]{2,1,0:T(8,128)S(1)} %get-tuple-element.31) | copy-start | bytes 4915204
  24.5 3.2 %collective-permute-start.5 = (f32[5,32,1024]{2,1,0:T(8,128)}, f32[5,32,1024]{2,1,0:T(8,128)S(1)}, u32[]{:S(2)}, u32[]{:S(2)}) collective-permute-start(f32[5,32,1024]{2,1,0:T(8,128)} %get-tuple-element.24), channel_id=1, source_target_pairs={{0,1},{1,0},{2,3},{3,2},{4,5},{5,4},{6,7},{7,6},{8,9},{9,8},{10,11... | collective-permute-start | bytes 1966088 | tf_op jit(solution)/shard_map/ppermute | solution.py:789
  24.5 5.7 %collective-permute-start.6 = (f32[5,32,1024]{2,1,0:T(8,128)}, f32[5,32,1024]{2,1,0:T(8,128)}, u32[]{:S(2)}, u32[]{:S(2)}) collective-permute-start(f32[5,32,1024]{2,1,0:T(8,128)} %get-tuple-element.26), channel_id=1, source_target_pairs={{0,1},{1,0},{2,3},{3,2},{4,5},{5,4},{6,7},{7,6},{8,9},{9,8},{10,11... | collective-permute-start | bytes 1966088 | tf_op jit(solution)/shard_map/ppermute | solution.py:789
  25.1 22.6 %collective-permute-start.10 = (f32[5,96,1024]{2,1,0:T(8,128)}, f32[5,96,1024]{2,1,0:T(8,128)}, u32[]{:S(2)}, u32[]{:S(2)}) collective-permute-start(f32[5,96,1024]{2,1,0:T(8,128)} %get-tuple-element.25.token), channel_id=1, source_target_pairs={{0,1},{1,0},{2,3},{3,2},{4,5},{5,4},{6,7},{7,6},{8,9},{9,8},{10,11... | collective-permute-start | bytes 5898248 | tf_op jit(solution)/shard_map/ppermute | solution.py:789
  25.3 11.9 %collective-permute-start.2 = (f32[5,16,1024]{2,1,0:T(8,128)}, f32[5,16,1024]{2,1,0:T(8,128)S(1)}, u32[]{:S(2)}, u32[]{:S(2)}) collective-permute-start(f32[5,16,1024]{2,1,0:T(8,128)} %get-tuple-element.21), channel_id=1, source_target_pairs={{0,1},{1,0},{2,3},{3,2},{4,5},{5,4},{6,7},{7,6},{8,9},{9,8},{10,11... | collective-permute-start | bytes 983048 | tf_op jit(solution)/shard_map/ppermute | solution.py:775
  27.8 29.4 %collective-permute-start.9 = (f32[5,80,1024]{2,1,0:T(8,128)}, f32[5,80,1024]{2,1,0:T(8,128)S(1)}, u32[]{:S(2)}, u32[]{:S(2)}) collective-permute-start(f32[5,80,1024]{2,1,0:T(8,128)} %copy-done.2), channel_id=1, source_target_pairs={{1,2},{2,1},{5,6},{6,5},{9,10},{10,9},{13,14},{14,13},{17,18},{18,... | collective-permute-start | bytes 4915208 | tf_op jit(solution)/shard_map/ppermute | solution.py:787
  30.2 26.9 %collective-permute-start.11 = (f32[5,80,1024]{2,1,0:T(8,128)}, f32[5,80,1024]{2,1,0:T(8,128)S(1)}, u32[]{:S(2)}, u32[]{:S(2)}) collective-permute-start(f32[5,80,1024]{2,1,0:T(8,128)} %copy-done.1), channel_id=1, source_target_pairs={{0,1},{1,0},{2,3},{3,2},{4,5},{5,4},{6,7},{7,6},{8,9},{9,8},{10,11... | collective-permute-start | bytes 4915208 | tf_op jit(solution)/shard_map/ppermute | solution.py:789
  30.4 6.9 %copy-start = (bf16[384,640]{1,0:T(8,128)(2,1)S(1)}, bf16[384,640]{1,0:T(8,128)(2,1)}, u32[]{:S(2)}) copy-start(bf16[384,640]{1,0:T(8,128)(2,1)} %constant.56.clone.solve) | copy-start | bytes 1474564
  44.3 23.5 %collective-permute-start.7 = (f32[5,64,1024]{2,1,0:T(8,128)S(1)}, f32[5,64,1024]{2,1,0:T(8,128)S(1)}, u32[]{:S(2)}, u32[]{:S(2)}) collective-permute-start(f32[5,64,1024]{2,1,0:T(8,128)S(1)} %get-tuple-element.27), channel_id=1, source_target_pairs={{1,2},{2,1},{5,6},{6,5},{9,10},{10,9},{13,14},{14,13},{17,18},{18,... | collective-permute-start | bytes 3932168 | tf_op jit(solution)/shard_map/ppermute | solution.py:813
  47.4 18.1 %collective-permute-start.8 = (f32[16,128]{1,0:T(8,128)}, f32[16,128]{1,0:T(8,128)S(1)}, u32[]{:S(2)}, u32[]{:S(2)}) collective-permute-start(f32[16,128]{1,0:T(8,128)} %get-tuple-element.30.token.rest_0_), channel_id=1, source_target_pairs={{0,16},{16,0},{1,17},{17,1},{2,18},{18,2},{3,19},{19,3},{4,20},{20... | collective-permute-start | bytes 24584 | tf_op jit(solution)/shard_map/ppermute | solution.py:737

commit v12 on v10

--- a/solution.py
+++ b/solution.py
@@ -150,11 +150,13 @@
 
 
 def bulk_kernel(
-    dtheta, rows, span, total_rows, fused, flags, state, low, high, inner, edge, outer, token, held, out, *scratch
+    dtheta, rows, span, total_rows, fused, near, flags, state, low, high, inner, edge, outer, token, held, *rest
 ):
+    near_parts, out, scratch = rest[:near], rest[near], rest[near + 1 :]
     first, end = span
     blocks = (end - first) // rows
     state_rows, inner_rows, sems, radial, azimuthal, *outer_rows = scratch
+    *outer_rows, near_rows, near_sem = [*outer_rows, None, None] if not near else outer_rows
     outer_rows = outer_rows[0] if fused else None
     odd = flags[ODD]
     step = pl.program_id(0)
@@ -178,6 +180,9 @@
         for k in range(blocks):
             for copy in copies(k):
                 copy.start()
+        if near:
+            close_circle(flags, *near_parts, near_rows)
+            pltpu.make_async_copy(near_rows, held.at[:, :, 0:R_NEAR, :], near_sem).start()
 
     for k in range(blocks):
 
@@ -214,6 +219,11 @@
         radial,
         azimuthal,
     )
+    if near:
+
+        @pl.when(step == blocks - 1)
+        def _():
+            pltpu.make_async_copy(near_rows, held.at[:, :, 0:R_NEAR, :], near_sem).wait()
 
 
 def outer_kernel(rows, span, flags, outer, held, out, outer_rows, held_rows, sems):
@@ -345,7 +355,7 @@
         copy.wait()
 
 
-def finish_kernel(flags, factor, rhs, local, carry, table, held, out):
+def close_circle(flags, factor, rhs, local, carry, table, out):
     cells = out.shape[-1]
     lane = lax.broadcasted_iota(jnp.int32, (R_NEAR, cells), 1).astype(jnp.float32)
     width = factor[:, 0:1]
@@ -530,19 +540,21 @@
     return [pltpu.VMEM((*shape, n, LANES), jnp.float32) for n in (rows + 2 * EIGHT, rows)]
 
 
-def bulk(flags, state, low, high, inner, edge, dtheta, outer, span, rows, token, held):
+def bulk(flags, state, low, high, inner, edge, dtheta, outer, span, token, held, near_parts=()):
     fields, planes, total_rows, cells = state.shape
     first, end = span
     count = end - first
+    rows = 32 if count % 32 == 0 else 24 if count % 24 == 0 else 16
     blocks = count // rows
     size = fields * planes * count * cells
     aliases = {} if held is None else {8: 0}
     state = in_hbm(state)
-    operands = [state, low, high, inner, edge, inner if outer is None else outer, in_hbm(token)]
-    operands.append(state if held is None else held)
+    operands = [state, low, high, inner, edge, inner if outer is None else outer, token]
+    operands += [state if held is None else held, *near_parts]
     chunk = pltpu.VMEM((fields, count, cells), jnp.float32)
+    near_scratch = [pltpu.VMEM((fields, planes, R_NEAR, cells), jnp.float32), pltpu.SemaphoreType.DMA]
     return pl.pallas_call(
-        functools.partial(bulk_kernel, dtheta, rows, span, total_rows, outer is not None),
+        functools.partial(bulk_kernel, dtheta, rows, span, total_rows, outer is not None, len(near_parts)),
         grid_spec=pltpu.PrefetchScalarGridSpec(
             num_scalar_prefetch=1,
             grid=(blocks,),
@@ -555,6 +567,7 @@
                 ANY,
                 ANY,
                 ANY,
+                *[whole(*x.shape) for x in near_parts],
             ],
             out_specs=rows_from((fields, planes, rows, cells), 2, first, rows),
             scratch_shapes=[
@@ -563,6 +576,7 @@
                 pltpu.SemaphoreType.DMA((3 * blocks,)),
                 *flux_scratch(rows, cells),
                 *([] if outer is None else [chunk]),
+                *(near_scratch if near_parts else []),
             ],
         ),
         out_shape=pltpu.HBM(state.shape, jnp.float32),
@@ -635,31 +649,6 @@
     return result if part is not None else (*result, None)
 
 
-def finish(flags, factor, rhs, local, carry, table, held):
-    _, _, cells = rhs.shape
-    return pl.pallas_call(
-        finish_kernel,
-        grid_spec=pltpu.PrefetchScalarGridSpec(
-            num_scalar_prefetch=1,
-            grid=(1,),
-            in_specs=[
-                whole(R_NEAR, LANES),
-                whole(LINES, R_NEAR, cells),
-                whole(LINES, R_NEAR, cells),
-                whole(R_NEAR, LANES),
-                whole(R_NEAR, LANES),
-                ANY,
-            ],
-            out_specs=whole(FIELDS, PLANES, R_NEAR, cells),
-        ),
-        out_shape=pltpu.HBM(held.shape, jnp.float32),
-        input_output_aliases={6: 0},
-        compiler_params=PARAMS,
-        cost_estimate=cost(LINES * R_NEAR * cells * 10, LINES * R_NEAR * cells * 20),
-        name="finish",
-    )(flags, factor, rhs, local, carry, table, held)
-
-
 def chunks(rows):
     size = 16
     blocks = (rows - R_NEAR) // size
@@ -760,11 +749,13 @@
 
     solve = piece_tables(dtheta)
     given = (flags, state, low, high)
-    def pass_over(k, token, held, fused=True):
+
+    def pass_over(k, token, held, fused=True, near_parts=()):
         span = (spans[k][0] if k else R_NEAR, spans[k][1])
-        return bulk(*given, inner[k + 1], edge, dtheta, outer[k] if fused else None, span, size, token, held)
-
-    out = pass_over(2, parts[0], None, fused=False) if count > 2 else None
+        far = outer[k] if fused else None
+        return bulk(*given, inner[k + 1], edge, dtheta, far, span, token, held, near_parts)
+
+    out = pass_over(2, in_hbm(parts[0]), None, fused=False) if count > 2 else None
     part = spans[2] if count > 2 else None
     token = parts[0] if out is None else out
     rhs, local, ends, part = near(
@@ -778,10 +769,10 @@
     for k in range(sec_count, 0, -1):
         carry = carry * across + jnp.where(from_left, arrived[k], arrived[sec_count - k])
     carry = carry * closing
-
-    for k in range(min(count, 2)):
-        out = pass_over(k, ends, out)
-    out = finish(flags, factor, rhs, local, carry, table, out)
+    passes = min(count, 2)
+    for k in range(passes):
+        near_parts = (factor, rhs, local, carry, table) if k == passes - 1 else ()
+        out = pass_over(k, ends, out, near_parts=near_parts)
     return add_outer(flags, outer[2], spans[2], size, out) if count > 2 else out
 
 

time: 69.7 us -> 68.6 us (0.984)
  Pallas kernels: 46.8 us -> 44.7 us
  waiting for transfers between devices: 1.95 us -> 3.93 us
  other arithmetic: 0.92 us -> 0.22 us
    ppermute x2, waiting for transfers between devices: 0.01 us -> 3.48 us  [ring(): lax.ppermute(value, axis, [(i, (i + shift) % size) for i in range(size)])]
    ppermute x1, waiting for transfers between devices: 1.85 us -> 0.01 us  [body(): outer = [lax.ppermute(part, 'ax', outer_pairs)]]
    ppermute x1, starting transfers between devices: 3.64 us -> 1.92 us  [body(): outer.append(lax.ppermute(part, 'ax', outer_pairs))]
    pallas_call x1 -> x0, Pallas kernels: 1.62 us -> none  [finish(): pl.pallas_call(finish_kernel, grid_spec=pltpu.PrefetchScalarGridSpec(num_...]
    ppermute x1, starting transfers between devices: 2.52 us -> 3.74 us  [body(): outer.append(lax.ppermute(value, 'ax', outer_pairs))]
  transfers between devices with their start and end apart: 11 -> 11, of which waited for: 2 -> 2; matrix products, arithmetic and copies ran while one was open for 2% -> 1% of each run, Pallas kernels for 60% -> 58%
where the time goes in v12:
time: 68.6 us; the launch traced here: 68.2 us
  Pallas kernels  44.7 us (65%)
  starting transfers between devices  18.2 us (27%)
  waiting for transfers between devices  3.93 us (6%)
  local copies, waits for them, and re-layouts  0.88 us (1%)
    pallas_call x3, Pallas kernels, bulk(): pl.pallas_call(functools.partial(bulk_kernel, dtheta, rows, span, total_r...  24.9 us
    pallas_call x1, Pallas kernels, near(): pl.pallas_call(functools.partial(near_kernel, dtheta, rows, part[0] if pa...  6.28 us
    pallas_call x1, Pallas kernels, pack_rest(): pl.pallas_call(functools.partial(pack_rest_kernel, parts, len(tokens)), i...  5.66 us
    ppermute x1, starting transfers between devices, body(): outer = [lax.ppermute(part, 'ax', outer_pairs)]  4.51 us
    ppermute x1, starting transfers between devices, body(): outer.append(lax.ppermute(value, 'ax', outer_pairs))  3.74 us
    ppermute x2, waiting for transfers between devices, ring(): lax.ppermute(value, axis, [(i, (i + shift) % size) for i in range(size)])  3.48 us
    ppermute x1, starting transfers between devices, body(): low = lax.ppermute(low, 'rad', up)  3.2 us
    pallas_call x1, Pallas kernels, pack_first(): pl.pallas_call(functools.partial(pack_first_kernel, count), in_specs=[ANY...  2.67 us
  transfers between devices with their start and end apart: 11, of which 2 were waited for; matrix products, arithmetic and copies ran while one was open for 1% of the time, Pallas kernels for 58%

profile of v12, /device:TPU:1, one launch (start us, length us, event | category | flops | bytes accessed | tf_op | source)
XLA Modules:
  0.0 68.2 jit_solution(162296228455333107)
XLA Ops:
  0.0 2.7 %pack_first.1 = (f32[5,112,1024]{2,1,0:T(8,128)}, f32[10,1024]{1,0:T(8,128)S(1)}, f32[10,1024]{1,0:T(8,128)S(1)}) custom-call(f32[5,2,256,1024]{3,2,1,0:T(8,128)} %state.13), custom_call_target="tpu_custom_call" | custom-call | bytes 4587520 | tf_op jit(solution)/shard_map/pack_first/pallas_call | solution.py:483
  2.7 4.5 %collective-permute-start.3 = (f32[5,112,1024]{2,1,0:T(8,128)}, f32[5,112,1024]{2,1,0:T(8,128)S(1)}, u32[]{:S(2)}, u32[]{:S(2)}) collective-permute-start(f32[5,112,1024]{2,1,0:T(8,128)} %get-tuple-element.21), channel_id=1, source_target_pairs={{1,2},{2,1},{5,6},{6,5},{9,10},{10,9},{13,14},{14,13},{17,18},{18,... | collective-permute-start | bytes 6881288 | tf_op jit(solution)/shard_map/ppermute | solution.py:727
  7.2 3.2 %collective-permute-start = (f32[10,1024]{1,0:T(8,128)S(1)}, f32[10,1024]{1,0:T(8,128)S(1)}, u32[]{:S(2)}, u32[]{:S(2)}) collective-permute-start(f32[10,1024]{1,0:T(8,128)S(1)} %get-tuple-element.18), channel_id=1, source_target_pairs={{0,4},{4,8},{8,12},{1,5},{5,9},{9,13},{2,6},{6,10},{10,14},{3,7},{... | collective-permute-start | bytes 122888 | tf_op jit(solution)/shard_map/ppermute | solution.py:729
  10.4 1.3 %collective-permute-start.1 = (f32[10,1024]{1,0:T(8,128)S(1)}, f32[10,1024]{1,0:T(8,128)S(1)}, u32[]{:S(2)}, u32[]{:S(2)}) collective-permute-start(f32[10,1024]{1,0:T(8,128)S(1)} %get-tuple-element.19.token), channel_id=1, source_target_pairs={{4,0},{8,4},{12,8},{5,1},{9,5},{13,9},{6,2},{10,6},{14,10},{7,3},{... | collective-permute-start | bytes 122888 | tf_op jit(solution)/shard_map/ppermute | solution.py:730
  11.7 2.6 %pack_edges.1 = (f32[256,128]{1,0:T(8,128)S(1)}, f32[5,16,1024]{2,1,0:T(8,128)S(1)}) custom-call(f32[5,2,256,1024]{3,2,1,0:T(8,128)} %state.13, f32[10,1024]{1,0:T(8,128)S(1)} %get-tuple-element.19.token), custom_call_target="tpu_custom_call" | custom-call | bytes 5242880 | tf_op jit(solution)/shard_map/pack_edges/pallas_call | solution.py:505
  14.3 0.0 copy-start.1
  14.3 0.7 %copy-done.1 = f32[5,16,1024]{2,1,0:T(8,128)} copy-done((f32[5,16,1024]{2,1,0:T(8,128)}, f32[5,16,1024]{2,1,0:T(8,128)S(1)}, u32[]{:S(2)}) %copy-start.1) | copy-done | bytes 327704
  15.0 0.0 collective-permute-done.rest_1_.low
  15.0 0.4 collective-permute-done.1.rest_2_.high
  15.4 0.0 copy-start.2
  15.4 5.7 %pack_rest.1 = (f32[5,96,1024]{2,1,0:T(8,128)}, f32[5,96,1024]{2,1,0:T(8,128)}, f32[5,96,1024]{2,1,0:T(8,128)}, f32[5,48,1024]{2,1,0:T(8,128)}) custom-call(f32[5,2,256,1024]{3,2,1,0:T(8,128)} %state.13, f32[256,128]{1,0:T(8,128)S(1)} %get-tuple-element.22.rest_0_, f32[10,1024]{1,0:T(8,128)S(1)} %collective-permute-done.rest_1_.low, ...), custom_call_target="tpu_custom_call" | custom-call | bytes 13762560 | tf_op jit(solution)/shard_map/pack_rest/pallas_call | solution.py:523
  21.1 0.1 collective-permute-start.5
  21.2 0.5 collective-permute-start.9
  21.7 1.3 %collective-permute-start.4 = (f32[256,128]{1,0:T(8,128)S(1)}, f32[256,128]{1,0:T(8,128)S(1)}, u32[]{:S(2)}, u32[]{:S(2)}) collective-permute-start(f32[256,128]{1,0:T(8,128)S(1)} %get-tuple-element.22.rest_0_), channel_id=1, source_target_pairs={{0,16},{16,0},{1,17},{17,1},{2,18},{18,2},{3,19},{19,3},{4,20},{20... | collective-permute-start | bytes 393224 | tf_op jit(solution)/shard_map/ppermute | solution.py:693
  22.9 0.3 collective-permute-start.7
  23.3 3.5 %collective-permute-done.4.edge = f32[256,128]{1,0:T(8,128)S(1)} collective-permute-done((f32[256,128]{1,0:T(8,128)S(1)}, f32[256,128]{1,0:T(8,128)S(1)}, u32[]{:S(2)}, u32[]{:S(2)}) %collective-permute-start.4) | collective-permute-done | bytes 131104 | tf_op jit(solution)/shard_map/ppermute | solution.py:693
  26.7 3.7 %collective-permute-start.8 = (f32[5,96,1024]{2,1,0:T(8,128)}, f32[5,96,1024]{2,1,0:T(8,128)}, u32[]{:S(2)}, u32[]{:S(2)}) collective-permute-start(f32[5,96,1024]{2,1,0:T(8,128)} %get-tuple-element.27), channel_id=1, source_target_pairs={{1,2},{2,1},{5,6},{6,5},{9,10},{10,9},{13,14},{14,13},{17,18},{18,... | collective-permute-start | bytes 5898248 | tf_op jit(solution)/shard_map/ppermute | solution.py:738
  30.5 0.0 copy-done.2
  30.5 0.1 stack.35.flags
  30.7 0.0 collective-permute-done.5.inner.outer
  30.7 0.1 collective-permute-start.2
  30.8 0.1 fusion.3.table.rest_4_
  30.9 0.0 copy-start
  30.9 5.8 %bulk.3.token.held = f32[5,2,256,1024]{3,2,1,0:T(8,128)} custom-call(s32[5]{0:T(128)S(1)} %stack.35.flags, f32[5,2,256,1024]{3,2,1,0:T(8,128)} %state.13, f32[10,1024]{1,0:T(8,128)S(1)} %collective-permute-done.rest_1_.low, f32[10,1024]{1,0:T(8,128)S(1)} %collective-permute-done.1.rest_2_.high, f32[5,48,1024]{2,1,0:T(8,128)S(1)} %collective-permute-done.5.inner.outer, ...), custom_call_target="tpu_custom_call" | custom-call | flops 29491200 | bytes 4915200 | tf_op jit(solution)/shard_map/bulk/pallas_call | solution.py:556
  36.7 0.0 collective-permute-done.2.inner
  36.7 0.0 collective-permute-done.3.outer
  36.7 0.1 broadcast_in_dim.51.factor.rest_0_
  36.8 0.0 copy-done
  36.8 6.3 %near.1 = (f32[10,16,1024]{2,1,0:T(8,128)S(1)}, f32[10,16,1024]{2,1,0:T(8,128)S(1)}, f32[16,128]{1,0:T(8,128)S(1)}, f32[5,48,1024]{2,1,0:T(8,128)S(1)}) custom-call(s32[5]{0:T(128)S(1)} %stack.35.flags, f32[5,2,256,1024]{3,2,1,0:T(8,128)} %state.13, f32[5,2,256,1024]{3,2,1,0:T(8,128)} %state.13, f32[10,1024]{1,0:T(8,128)S(1)} %collective-permute-done.rest_1_.low, ...), custom_call_target="tpu_custom_call" | custom-call | flops 32768000 | bytes 40960000 | tf_op jit(solution)/shard_map/near/pallas_call | solution.py:622
  43.1 1.9 %collective-permute-start.6 = (f32[5,48,1024]{2,1,0:T(8,128)S(1)}, f32[5,48,1024]{2,1,0:T(8,128)S(1)}, u32[]{:S(2)}, u32[]{:S(2)}) collective-permute-start(f32[5,48,1024]{2,1,0:T(8,128)S(1)} %get-tuple-element.25), channel_id=1, source_target_pairs={{1,2},{2,1},{5,6},{6,5},{9,10},{10,9},{13,14},{14,13},{17,18},{18,... | collective-permute-start | bytes 2949128 | tf_op jit(solution)/shard_map/ppermute | solution.py:765
  45.0 1.3 %collective-permute-start.10 = (f32[16,128]{1,0:T(8,128)S(1)}, f32[16,128]{1,0:T(8,128)S(1)}, u32[]{:S(2)}, u32[]{:S(2)}) collective-permute-start(f32[16,128]{1,0:T(8,128)S(1)} %get-tuple-element.28.token), channel_id=1, source_target_pairs={{0,16},{16,0},{1,17},{17,1},{2,18},{18,2},{3,19},{19,3},{4,20},{20... | collective-permute-start | bytes 24584 | tf_op jit(solution)/shard_map/ppermute | solution.py:693
  46.3 0.0 collective-permute-done.9.inner
  46.3 9.3 %bulk.4.held = f32[5,2,256,1024]{3,2,1,0:T(8,128)} custom-call(s32[5]{0:T(128)S(1)} %stack.35.flags, f32[5,2,256,1024]{3,2,1,0:T(8,128)} %state.13, f32[10,1024]{1,0:T(8,128)S(1)} %collective-permute-done.rest_1_.low, f32[10,1024]{1,0:T(8,128)S(1)} %collective-permute-done.1.rest_2_.high, ...), custom_call_target="tpu_custom_call", output_to_operand_aliasing={{}: (8, {})} | custom-call | flops 58982400 | bytes 9830400 | tf_op jit(solution)/shard_map/bulk/pallas_call | solution.py:556
  55.6 0.0 collective-permute-done.10
  55.6 0.1 add_multiply_fusion.rest_3_
  55.7 0.0 collective-permute-done.7.inner
  55.7 0.0 collective-permute-done.8.outer
  55.7 9.9 %bulk.5.held = f32[5,2,256,1024]{3,2,1,0:T(8,128)} custom-call(s32[5]{0:T(128)S(1)} %stack.35.flags, f32[5,2,256,1024]{3,2,1,0:T(8,128)} %state.13, f32[10,1024]{1,0:T(8,128)S(1)} %collective-permute-done.rest_1_.low, f32[10,1024]{1,0:T(8,128)S(1)} %collective-permute-done.1.rest_2_.high, ...), custom_call_target="tpu_custom_call", output_to_operand_aliasing={{}: (8, {})} | custom-call | flops 58982400 | bytes 9830400 | tf_op jit(solution)/shard_map/bulk/pallas_call | solution.py:556
  65.6 0.0 collective-permute-done.6.outer
  65.6 2.7 %add_outer.1 = f32[5,2,256,1024]{3,2,1,0:T(8,128)} custom-call(s32[5]{0:T(128)S(1)} %stack.35.flags, f32[5,48,1024]{2,1,0:T(8,128)S(1)} %collective-permute-done.6.outer, f32[5,2,256,1024]{3,2,1,0:T(8,128)} %bulk.5.held), custom_call_target="tpu_custom_call", output_to_operand_aliasing={{}: (2, {})} | custom-call | flops 1474560 | bytes 3932160 | tf_op jit(solution)/shard_map/add_outer/pallas_call | solution.py:593
  (5 shorter events, 0.1 us)
Async XLA Ops:
  2.7 34.0 %collective-permute-start.3 = (f32[5,112,1024]{2,1,0:T(8,128)}, f32[5,112,1024]{2,1,0:T(8,128)S(1)}, u32[]{:S(2)}, u32[]{:S(2)}) collective-permute-start(f32[5,112,1024]{2,1,0:T(8,128)} %get-tuple-element.21), channel_id=1, source_target_pairs={{1,2},{2,1},{5,6},{6,5},{9,10},{10,9},{13,14},{14,13},{17,18},{18,... | collective-permute-start | bytes 6881288 | tf_op jit(solution)/shard_map/ppermute | solution.py:727
  7.2 7.8 %collective-permute-start = (f32[10,1024]{1,0:T(8,128)S(1)}, f32[10,1024]{1,0:T(8,128)S(1)}, u32[]{:S(2)}, u32[]{:S(2)}) collective-permute-start(f32[10,1024]{1,0:T(8,128)S(1)} %get-tuple-element.18), channel_id=1, source_target_pairs={{0,4},{4,8},{8,12},{1,5},{5,9},{9,13},{2,6},{6,10},{10,14},{3,7},{... | collective-permute-start | bytes 122888 | tf_op jit(solution)/shard_map/ppermute | solution.py:729
  10.4 5.0 %collective-permute-start.1 = (f32[10,1024]{1,0:T(8,128)S(1)}, f32[10,1024]{1,0:T(8,128)S(1)}, u32[]{:S(2)}, u32[]{:S(2)}) collective-permute-start(f32[10,1024]{1,0:T(8,128)S(1)} %get-tuple-element.19.token), channel_id=1, source_target_pairs={{4,0},{8,4},{12,8},{5,1},{9,5},{13,9},{6,2},{10,6},{14,10},{7,3},{... | collective-permute-start | bytes 122888 | tf_op jit(solution)/shard_map/ppermute | solution.py:730
  14.3 0.7 %copy-start.1 = (f32[5,16,1024]{2,1,0:T(8,128)}, f32[5,16,1024]{2,1,0:T(8,128)S(1)}, u32[]{:S(2)}) copy-start(f32[5,16,1024]{2,1,0:T(8,128)S(1)} %get-tuple-element.20) | copy-start | bytes 983044
  15.4 15.1 %copy-start.2 = (s32[16]{0:T(128)S(1)}, s32[16]{0:T(128)}, u32[]{:S(2)}) copy-start(s32[16]{0:T(128)} %param.4) | copy-start | bytes 196
  21.1 9.6 %collective-permute-start.5 = (f32[5,48,1024]{2,1,0:T(8,128)}, f32[5,48,1024]{2,1,0:T(8,128)S(1)}, u32[]{:S(2)}, u32[]{:S(2)}) collective-permute-start(f32[5,48,1024]{2,1,0:T(8,128)} %get-tuple-element.23), channel_id=1, source_target_pairs={{0,1},{1,0},{2,3},{3,2},{4,5},{5,4},{6,7},{7,6},{8,9},{9,8},{10,11... | collective-permute-start | bytes 2949128 | tf_op jit(solution)/shard_map/ppermute | solution.py:740
  21.2 25.1 %collective-permute-start.9 = (f32[5,96,1024]{2,1,0:T(8,128)}, f32[5,96,1024]{2,1,0:T(8,128)}, u32[]{:S(2)}, u32[]{:S(2)}) collective-permute-start(f32[5,96,1024]{2,1,0:T(8,128)} %get-tuple-element.24.token), channel_id=1, source_target_pairs={{0,1},{1,0},{2,3},{3,2},{4,5},{5,4},{6,7},{7,6},{8,9},{9,8},{10,11... | collective-permute-start | bytes 5898248 | tf_op jit(solution)/shard_map/ppermute | solution.py:740
  21.7 5.1 %collective-permute-start.4 = (f32[256,128]{1,0:T(8,128)S(1)}, f32[256,128]{1,0:T(8,128)S(1)}, u32[]{:S(2)}, u32[]{:S(2)}) collective-permute-start(f32[256,128]{1,0:T(8,128)S(1)} %get-tuple-element.22.rest_0_), channel_id=1, source_target_pairs={{0,16},{16,0},{1,17},{17,1},{2,18},{18,2},{3,19},{19,3},{4,20},{20... | collective-permute-start | bytes 393224 | tf_op jit(solution)/shard_map/ppermute | solution.py:693
  22.9 32.8 %collective-permute-start.7 = (f32[5,96,1024]{2,1,0:T(8,128)}, f32[5,96,1024]{2,1,0:T(8,128)}, u32[]{:S(2)}, u32[]{:S(2)}) collective-permute-start(f32[5,96,1024]{2,1,0:T(8,128)} %get-tuple-element.26), channel_id=1, source_target_pairs={{0,1},{1,0},{2,3},{3,2},{4,5},{5,4},{6,7},{7,6},{8,9},{9,8},{10,11... | collective-permute-start | bytes 5898248 | tf_op jit(solution)/shard_map/ppermute | solution.py:740
  26.7 28.9 %collective-permute-start.8 = (f32[5,96,1024]{2,1,0:T(8,128)}, f32[5,96,1024]{2,1,0:T(8,128)}, u32[]{:S(2)}, u32[]{:S(2)}) collective-permute-start(f32[5,96,1024]{2,1,0:T(8,128)} %get-tuple-element.27), channel_id=1, source_target_pairs={{1,2},{2,1},{5,6},{6,5},{9,10},{10,9},{13,14},{14,13},{17,18},{18,... | collective-permute-start | bytes 5898248 | tf_op jit(solution)/shard_map/ppermute | solution.py:738
  30.7 6.0 %collective-permute-start.2 = (f32[5,16,1024]{2,1,0:T(8,128)}, f32[5,16,1024]{2,1,0:T(8,128)S(1)}, u32[]{:S(2)}, u32[]{:S(2)}) collective-permute-start(f32[5,16,1024]{2,1,0:T(8,128)} %copy-done.1), channel_id=1, source_target_pairs={{0,1},{1,0},{2,3},{3,2},{4,5},{5,4},{6,7},{7,6},{8,9},{9,8},{10,11... | collective-permute-start | bytes 983048 | tf_op jit(solution)/shard_map/ppermute | solution.py:731
  30.9 5.9 %copy-start = (bf16[384,640]{1,0:T(8,128)(2,1)S(1)}, bf16[384,640]{1,0:T(8,128)(2,1)}, u32[]{:S(2)}) copy-start(bf16[384,640]{1,0:T(8,128)(2,1)} %constant.54.clone.solve) | copy-start | bytes 1474564
  43.1 22.5 %collective-permute-start.6 = (f32[5,48,1024]{2,1,0:T(8,128)S(1)}, f32[5,48,1024]{2,1,0:T(8,128)S(1)}, u32[]{:S(2)}, u32[]{:S(2)}) collective-permute-start(f32[5,48,1024]{2,1,0:T(8,128)S(1)} %get-tuple-element.25), channel_id=1, source_target_pairs={{1,2},{2,1},{5,6},{6,5},{9,10},{10,9},{13,14},{14,13},{17,18},{18,... | collective-permute-start | bytes 2949128 | tf_op jit(solution)/shard_map/ppermute | solution.py:765
  45.0 10.6 %collective-permute-start.10 = (f32[16,128]{1,0:T(8,128)S(1)}, f32[16,128]{1,0:T(8,128)S(1)}, u32[]{:S(2)}, u32[]{:S(2)}) collective-permute-start(f32[16,128]{1,0:T(8,128)S(1)} %get-tuple-element.28.token), channel_id=1, source_target_pairs={{0,16},{16,0},{1,17},{17,1},{2,18},{18,2},{3,19},{19,3},{4,20},{20... | collective-permute-start | bytes 24584 | tf_op jit(solution)/shard_map/ppermute | solution.py:693

commit v13 on v12

--- a/solution.py
+++ b/solution.py
@@ -728,21 +728,24 @@
     columns, side = pack_edges(state, high)
     low = lax.ppermute(low, "rad", up)
     high = lax.ppermute(high, "rad", down)
-    inner = [lax.ppermute(side, "ax", inner_pairs)]
-    wanted = [(0, R_NEAR, spans[0][1])] + [(0, *span) for span in spans[1:]]
-    if count > 1:
-        wanted.insert(1, (1, *spans[1]))
-    parts = pack_rest(state, wanted, columns, low, high)
-    for k, value in enumerate(parts):
-        if wanted[k][0]:
-            outer.append(lax.ppermute(value, "ax", outer_pairs))
-        else:
-            inner.append(lax.ppermute(value, "ax", inner_pairs))
+    near_inner = lax.ppermute(side, "ax", inner_pairs)
     if sec_count == 2:
         edge = ring(columns, "sec", 1)
     else:
         from_left = jnp.arange(LANES)[None, :] % 4 < 2
         edge = jnp.where(from_left, ring(columns, "sec", 1), ring(columns, "sec", -1))
+    early = [(0, *span) for span in spans[2:]] + [(1, *span) for span in spans[1:2]]
+    late = [(0, R_NEAR, spans[0][1])] + [(0, *span) for span in spans[1:2]]
+    parts = pack_rest(state, early, columns, low, high) if early else []
+    order = in_hbm(parts[0]) if early else columns
+    parts = list(parts) + list(pack_rest(state, late, order, edge))
+    inner = {}
+    for (q, first, last), value in zip(early + late, parts):
+        if q:
+            outer.append(lax.ppermute(value, "ax", outer_pairs))
+        else:
+            inner[first, last] = lax.ppermute(value, "ax", inner_pairs)
+    order = in_hbm(parts[-1])
 
     table, closing, across = smoothing_table(coarsen, cells, total_cells, dtheta)
     factor = jnp.broadcast_to(coarsen.astype(jnp.float32)[:, None], (R_NEAR, LANES))
@@ -753,13 +756,13 @@
     def pass_over(k, token, held, fused=True, near_parts=()):
         span = (spans[k][0] if k else R_NEAR, spans[k][1])
         far = outer[k] if fused else None
-        return bulk(*given, inner[k + 1], edge, dtheta, far, span, token, held, near_parts)
-
-    out = pass_over(2, in_hbm(parts[0]), None, fused=False) if count > 2 else None
+        return bulk(*given, inner[span], edge, dtheta, far, span, token, held, near_parts)
+
+    out = pass_over(2, order, None, fused=False) if count > 2 else None
     part = spans[2] if count > 2 else None
-    token = parts[0] if out is None else out
+    token = order if out is None else out
     rhs, local, ends, part = near(
-        *given, inner[0], edge, dtheta, outer[0], factor, table, solve, token, part
+        *given, near_inner, edge, dtheta, outer[0], factor, table, solve, token, part
     )
     if part is not None:
         outer.append(lax.ppermute(part, "ax", outer_pairs))

time: 68.6 us -> 67.9 us (0.990)
  waiting for transfers between devices: 3.93 us -> 1.8 us
  starting transfers between devices: 18.2 us -> 18.9 us
  Pallas kernels: 44.7 us -> 45.4 us
    ppermute x2, waiting for transfers between devices: 3.48 us -> 0.01 us  [ring(): lax.ppermute(value, axis, [(i, (i + shift) % size) for i in range(size)])]
    ppermute x1, starting transfers between devices: 1.92 us -> 3.64 us  [body(): outer.append(lax.ppermute(part, 'ax', outer_pairs))]
    ppermute x1, starting transfers between devices: 3.74 us -> 2.52 us  [body(): outer.append(lax.ppermute(value, 'ax', outer_pairs))]
    ppermute x1, waiting for transfers between devices: 0.01 us -> 0.73 us  [body(): outer = [lax.ppermute(part, 'ax', outer_pairs)]]
    pallas_call x1 -> x2, Pallas kernels: 5.66 us -> 6.35 us  [pack_rest(): pl.pallas_call(functools.partial(pack_rest_kernel, parts, len(tokens)), i...]
  transfers between devices with their start and end apart: 11 -> 11, of which waited for: 2 -> 3; matrix products, arithmetic and copies ran while one was open for 1% -> 1% of each run, Pallas kernels for 58% -> 59%
where the time goes in v13:
time: 67.9 us; the launch traced here: 67.5 us
  Pallas kernels  45.4 us (67%)
  starting transfers between devices  18.9 us (28%)
  waiting for transfers between devices  1.8 us (3%)
  local copies, waits for them, and re-layouts  0.88 us (1%)
    pallas_call x3, Pallas kernels, bulk(): pl.pallas_call(functools.partial(bulk_kernel, dtheta, rows, span, total_r...  24.9 us
    pallas_call x2, Pallas kernels, pack_rest(): pl.pallas_call(functools.partial(pack_rest_kernel, parts, len(tokens)), i...  6.35 us
    pallas_call x1, Pallas kernels, near(): pl.pallas_call(functools.partial(near_kernel, dtheta, rows, part[0] if pa...  6.29 us
    ppermute x1, starting transfers between devices, body(): outer = [lax.ppermute(part, 'ax', outer_pairs)]  4.51 us
    ppermute x1, starting transfers between devices, body(): outer.append(lax.ppermute(part, 'ax', outer_pairs))  3.64 us
    ppermute x1, starting transfers between devices, body(): low = lax.ppermute(low, 'rad', up)  3.2 us
    pallas_call x1, Pallas kernels, pack_first(): pl.pallas_call(functools.partial(pack_first_kernel, count), in_specs=[ANY...  2.66 us
    pallas_call x1, Pallas kernels, add_outer(): pl.pallas_call(functools.partial(outer_kernel, rows, span), grid_spec=plt...  2.65 us
  transfers between devices with their start and end apart: 11, of which 3 were waited for; matrix products, arithmetic and copies ran while one was open for 1% of the time, Pallas kernels for 59%

profile of v13, /device:TPU:1, one launch (start us, length us, event | category | flops | bytes accessed | tf_op | source)
XLA Modules:
  0.0 67.5 jit_solution(1123646495775358380)
XLA Ops:
  0.0 2.7 %pack_first.1 = (f32[5,112,1024]{2,1,0:T(8,128)}, f32[10,1024]{1,0:T(8,128)S(1)}, f32[10,1024]{1,0:T(8,128)S(1)}) custom-call(f32[5,2,256,1024]{3,2,1,0:T(8,128)} %state.15), custom_call_target="tpu_custom_call" | custom-call | bytes 4587520 | tf_op jit(solution)/shard_map/pack_first/pallas_call | solution.py:483
  2.7 4.5 %collective-permute-start.3 = (f32[5,112,1024]{2,1,0:T(8,128)}, f32[5,112,1024]{2,1,0:T(8,128)S(1)}, u32[]{:S(2)}, u32[]{:S(2)}) collective-permute-start(f32[5,112,1024]{2,1,0:T(8,128)} %get-tuple-element.21), channel_id=1, source_target_pairs={{1,2},{2,1},{5,6},{6,5},{9,10},{10,9},{13,14},{14,13},{17,18},{18,... | collective-permute-start | bytes 6881288 | tf_op jit(solution)/shard_map/ppermute | solution.py:727
  7.2 3.2 %collective-permute-start = (f32[10,1024]{1,0:T(8,128)S(1)}, f32[10,1024]{1,0:T(8,128)S(1)}, u32[]{:S(2)}, u32[]{:S(2)}) collective-permute-start(f32[10,1024]{1,0:T(8,128)S(1)} %get-tuple-element.18), channel_id=1, source_target_pairs={{0,4},{4,8},{8,12},{1,5},{5,9},{9,13},{2,6},{6,10},{10,14},{3,7},{... | collective-permute-start | bytes 122888 | tf_op jit(solution)/shard_map/ppermute | solution.py:729
  10.4 1.3 %collective-permute-start.1 = (f32[10,1024]{1,0:T(8,128)S(1)}, f32[10,1024]{1,0:T(8,128)S(1)}, u32[]{:S(2)}, u32[]{:S(2)}) collective-permute-start(f32[10,1024]{1,0:T(8,128)S(1)} %get-tuple-element.19.token), channel_id=1, source_target_pairs={{4,0},{8,4},{12,8},{5,1},{9,5},{13,9},{6,2},{10,6},{14,10},{7,3},{... | collective-permute-start | bytes 122888 | tf_op jit(solution)/shard_map/ppermute | solution.py:730
  11.7 2.6 %pack_edges.1 = (f32[256,128]{1,0:T(8,128)S(1)}, f32[5,16,1024]{2,1,0:T(8,128)S(1)}) custom-call(f32[5,2,256,1024]{3,2,1,0:T(8,128)} %state.15, f32[10,1024]{1,0:T(8,128)S(1)} %get-tuple-element.19.token), custom_call_target="tpu_custom_call" | custom-call | bytes 5242880 | tf_op jit(solution)/shard_map/pack_edges/pallas_call | solution.py:505
  14.3 0.0 copy-start.1
  14.3 0.7 %copy-done.1 = f32[5,16,1024]{2,1,0:T(8,128)} copy-done((f32[5,16,1024]{2,1,0:T(8,128)}, f32[5,16,1024]{2,1,0:T(8,128)S(1)}, u32[]{:S(2)}) %copy-start.1) | copy-done | bytes 327704
  15.0 1.2 %collective-permute-start.4 = (f32[256,128]{1,0:T(8,128)S(1)}, f32[256,128]{1,0:T(8,128)S(1)}, u32[]{:S(2)}, u32[]{:S(2)}) collective-permute-start(f32[256,128]{1,0:T(8,128)S(1)} %get-tuple-element.22.rest_0_), channel_id=1, source_target_pairs={{0,16},{16,0},{1,17},{17,1},{2,18},{18,2},{3,19},{19,3},{4,20},{20... | collective-permute-start | bytes 393224 | tf_op jit(solution)/shard_map/ppermute | solution.py:693
  16.2 0.0 collective-permute-done.rest_1_.low
  16.2 0.0 collective-permute-done.1.rest_2_.high
  16.2 2.9 %pack_rest.2 = (f32[5,48,1024]{2,1,0:T(8,128)}, f32[5,96,1024]{2,1,0:T(8,128)}) custom-call(f32[5,2,256,1024]{3,2,1,0:T(8,128)} %state.15, f32[256,128]{1,0:T(8,128)S(1)} %get-tuple-element.22.rest_0_, f32[10,1024]{1,0:T(8,128)S(1)} %collective-permute-done.rest_1_.low, f32[10,1024]{1,0:T(8,128)S(1)} %collective-permute-done.1.rest_2_.high), custom_call_target="tpu_custom_call" | custom-call | bytes 5898240 | tf_op jit(solution)/shard_map/pack_rest/pallas_call | solution.py:523
  19.1 0.0 copy-start.2
  19.2 0.1 collective-permute-start.5
  19.2 0.0 collective-permute-done.4.rest_1_.edge
  19.3 3.4 %pack_rest.3 = (f32[5,96,1024]{2,1,0:T(8,128)}, f32[5,96,1024]{2,1,0:T(8,128)}) custom-call(f32[5,2,256,1024]{3,2,1,0:T(8,128)} %state.15, f32[5,48,1024]{2,1,0:T(8,128)} %get-tuple-element.23.rest_0_, f32[256,128]{1,0:T(8,128)S(1)} %collective-permute-done.4.rest_1_.edge), custom_call_target="tpu_custom_call" | custom-call | bytes 7864320 | tf_op jit(solution)/shard_map/pack_rest/pallas_call | solution.py:523
  22.7 0.5 collective-permute-start.9
  23.2 2.5 %collective-permute-start.8 = (f32[5,96,1024]{2,1,0:T(8,128)}, f32[5,96,1024]{2,1,0:T(8,128)}, u32[]{:S(2)}, u32[]{:S(2)}) collective-permute-start(f32[5,96,1024]{2,1,0:T(8,128)} %get-tuple-element.26), channel_id=1, source_target_pairs={{1,2},{2,1},{5,6},{6,5},{9,10},{10,9},{13,14},{14,13},{17,18},{18,... | collective-permute-start | bytes 5898248 | tf_op jit(solution)/shard_map/ppermute | solution.py:745
  25.8 0.1 collective-permute-start.7
  25.9 0.0 copy-done.2
  25.9 0.1 stack.35.flags
  26.0 0.0 collective-permute-done.5.inner.outer
  26.1 0.5 collective-permute-start.2
  26.6 0.1 fusion.3.table.rest_4_
  26.7 0.0 copy-start
  26.7 5.8 %bulk.3.token.held = f32[5,2,256,1024]{3,2,1,0:T(8,128)} custom-call(s32[5]{0:T(128)S(1)} %stack.35.flags, f32[5,2,256,1024]{3,2,1,0:T(8,128)} %state.15, f32[10,1024]{1,0:T(8,128)S(1)} %collective-permute-done.rest_1_.low, f32[10,1024]{1,0:T(8,128)S(1)} %collective-permute-done.1.rest_2_.high, f32[5,48,1024]{2,1,0:T(8,128)S(1)} %collective-permute-done.5.inner.outer, ...), custom_call_target="tpu_custom_call" | custom-call | flops 29491200 | bytes 4915200 | tf_op jit(solution)/shard_map/bulk/pallas_call | solution.py:556
  32.5 0.0 collective-permute-done.2.inner
  32.5 0.7 %collective-permute-done.3.outer = f32[5,112,1024]{2,1,0:T(8,128)S(1)} collective-permute-done((f32[5,112,1024]{2,1,0:T(8,128)}, f32[5,112,1024]{2,1,0:T(8,128)S(1)}, u32[]{:S(2)}, u32[]{:S(2)}) %collective-permute-start.3) | collective-permute-done | bytes 2293792 | tf_op jit(solution)/shard_map/ppermute | solution.py:727
  33.2 0.1 broadcast_in_dim.51.factor.rest_0_
  33.3 0.0 copy-done
  33.3 6.3 %near.1 = (f32[10,16,1024]{2,1,0:T(8,128)S(1)}, f32[10,16,1024]{2,1,0:T(8,128)S(1)}, f32[16,128]{1,0:T(8,128)S(1)}, f32[5,48,1024]{2,1,0:T(8,128)S(1)}) custom-call(s32[5]{0:T(128)S(1)} %stack.35.flags, f32[5,2,256,1024]{3,2,1,0:T(8,128)} %state.15, f32[5,2,256,1024]{3,2,1,0:T(8,128)} %state.15, f32[10,1024]{1,0:T(8,128)S(1)} %collective-permute-done.rest_1_.low, ...), custom_call_target="tpu_custom_call" | custom-call | flops 32768000 | bytes 40960000 | tf_op jit(solution)/shard_map/near/pallas_call | solution.py:622
  39.6 3.6 %collective-permute-start.6 = (f32[5,48,1024]{2,1,0:T(8,128)S(1)}, f32[5,48,1024]{2,1,0:T(8,128)S(1)}, u32[]{:S(2)}, u32[]{:S(2)}) collective-permute-start(f32[5,48,1024]{2,1,0:T(8,128)S(1)} %get-tuple-element.25), channel_id=1, source_target_pairs={{1,2},{2,1},{5,6},{6,5},{9,10},{10,9},{13,14},{14,13},{17,18},{18,... | collective-permute-start | bytes 2949128 | tf_op jit(solution)/shard_map/ppermute | solution.py:768
  43.2 1.3 %collective-permute-start.10 = (f32[16,128]{1,0:T(8,128)S(1)}, f32[16,128]{1,0:T(8,128)S(1)}, u32[]{:S(2)}, u32[]{:S(2)}) collective-permute-start(f32[16,128]{1,0:T(8,128)S(1)} %get-tuple-element.27.token), channel_id=1, source_target_pairs={{0,16},{16,0},{1,17},{17,1},{2,18},{18,2},{3,19},{19,3},{4,20},{20... | collective-permute-start | bytes 24584 | tf_op jit(solution)/shard_map/ppermute | solution.py:693
  44.5 0.0 collective-permute-done.9.inner
  44.5 9.3 %bulk.4.held = f32[5,2,256,1024]{3,2,1,0:T(8,128)} custom-call(s32[5]{0:T(128)S(1)} %stack.35.flags, f32[5,2,256,1024]{3,2,1,0:T(8,128)} %state.15, f32[10,1024]{1,0:T(8,128)S(1)} %collective-permute-done.rest_1_.low, f32[10,1024]{1,0:T(8,128)S(1)} %collective-permute-done.1.rest_2_.high, ...), custom_call_target="tpu_custom_call", output_to_operand_aliasing={{}: (8, {})} | custom-call | flops 58982400 | bytes 9830400 | tf_op jit(solution)/shard_map/bulk/pallas_call | solution.py:556
  53.8 0.0 collective-permute-done.10
  53.8 0.1 add_multiply_fusion.rest_3_
  53.9 0.5 collective-permute-done.8.outer
  54.4 0.0 collective-permute-done.7.inner
  54.4 9.9 %bulk.5.held = f32[5,2,256,1024]{3,2,1,0:T(8,128)} custom-call(s32[5]{0:T(128)S(1)} %stack.35.flags, f32[5,2,256,1024]{3,2,1,0:T(8,128)} %state.15, f32[10,1024]{1,0:T(8,128)S(1)} %collective-permute-done.rest_1_.low, f32[10,1024]{1,0:T(8,128)S(1)} %collective-permute-done.1.rest_2_.high, ...), custom_call_target="tpu_custom_call", output_to_operand_aliasing={{}: (8, {})} | custom-call | flops 58982400 | bytes 9830400 | tf_op jit(solution)/shard_map/bulk/pallas_call | solution.py:556
  64.2 0.6 collective-permute-done.6.outer
  64.8 2.7 %add_outer.1 = f32[5,2,256,1024]{3,2,1,0:T(8,128)} custom-call(s32[5]{0:T(128)S(1)} %stack.35.flags, f32[5,48,1024]{2,1,0:T(8,128)S(1)} %collective-permute-done.6.outer, f32[5,2,256,1024]{3,2,1,0:T(8,128)} %bulk.5.held), custom_call_target="tpu_custom_call", output_to_operand_aliasing={{}: (2, {})} | custom-call | flops 1474560 | bytes 3932160 | tf_op jit(solution)/shard_map/add_outer/pallas_call | solution.py:593
  (5 shorter events, 0.1 us)
Async XLA Ops:
  2.7 30.5 %collective-permute-start.3 = (f32[5,112,1024]{2,1,0:T(8,128)}, f32[5,112,1024]{2,1,0:T(8,128)S(1)}, u32[]{:S(2)}, u32[]{:S(2)}) collective-permute-start(f32[5,112,1024]{2,1,0:T(8,128)} %get-tuple-element.21), channel_id=1, source_target_pairs={{1,2},{2,1},{5,6},{6,5},{9,10},{10,9},{13,14},{14,13},{17,18},{18,... | collective-permute-start | bytes 6881288 | tf_op jit(solution)/shard_map/ppermute | solution.py:727
  7.2 9.0 %collective-permute-start = (f32[10,1024]{1,0:T(8,128)S(1)}, f32[10,1024]{1,0:T(8,128)S(1)}, u32[]{:S(2)}, u32[]{:S(2)}) collective-permute-start(f32[10,1024]{1,0:T(8,128)S(1)} %get-tuple-element.18), channel_id=1, source_target_pairs={{0,4},{4,8},{8,12},{1,5},{5,9},{9,13},{2,6},{6,10},{10,14},{3,7},{... | collective-permute-start | bytes 122888 | tf_op jit(solution)/shard_map/ppermute | solution.py:729
  10.4 5.8 %collective-permute-start.1 = (f32[10,1024]{1,0:T(8,128)S(1)}, f32[10,1024]{1,0:T(8,128)S(1)}, u32[]{:S(2)}, u32[]{:S(2)}) collective-permute-start(f32[10,1024]{1,0:T(8,128)S(1)} %get-tuple-element.19.token), channel_id=1, source_target_pairs={{4,0},{8,4},{12,8},{5,1},{9,5},{13,9},{6,2},{10,6},{14,10},{7,3},{... | collective-permute-start | bytes 122888 | tf_op jit(solution)/shard_map/ppermute | solution.py:730
  14.3 0.7 %copy-start.1 = (f32[5,16,1024]{2,1,0:T(8,128)}, f32[5,16,1024]{2,1,0:T(8,128)S(1)}, u32[]{:S(2)}) copy-start(f32[5,16,1024]{2,1,0:T(8,128)S(1)} %get-tuple-element.20) | copy-start | bytes 983044
  15.0 4.3 %collective-permute-start.4 = (f32[256,128]{1,0:T(8,128)S(1)}, f32[256,128]{1,0:T(8,128)S(1)}, u32[]{:S(2)}, u32[]{:S(2)}) collective-permute-start(f32[256,128]{1,0:T(8,128)S(1)} %get-tuple-element.22.rest_0_), channel_id=1, source_target_pairs={{0,16},{16,0},{1,17},{17,1},{2,18},{18,2},{3,19},{19,3},{4,20},{20... | collective-permute-start | bytes 393224 | tf_op jit(solution)/shard_map/ppermute | solution.py:693
  19.1 6.7 %copy-start.2 = (s32[16]{0:T(128)S(1)}, s32[16]{0:T(128)}, u32[]{:S(2)}) copy-start(s32[16]{0:T(128)} %param.4) | copy-start | bytes 196
  19.2 6.9 %collective-permute-start.5 = (f32[5,48,1024]{2,1,0:T(8,128)}, f32[5,48,1024]{2,1,0:T(8,128)S(1)}, u32[]{:S(2)}, u32[]{:S(2)}) collective-permute-start(f32[5,48,1024]{2,1,0:T(8,128)} %get-tuple-element.23.rest_0_), channel_id=1, source_target_pairs={{0,1},{1,0},{2,3},{3,2},{4,5},{5,4},{6,7},{7,6},{8,9},{9,8},{10,11... | collective-permute-start | bytes 2949128 | tf_op jit(solution)/shard_map/ppermute | solution.py:747
  22.7 21.8 %collective-permute-start.9 = (f32[5,96,1024]{2,1,0:T(8,128)}, f32[5,96,1024]{2,1,0:T(8,128)}, u32[]{:S(2)}, u32[]{:S(2)}) collective-permute-start(f32[5,96,1024]{2,1,0:T(8,128)} %get-tuple-element.28), channel_id=1, source_target_pairs={{0,1},{1,0},{2,3},{3,2},{4,5},{5,4},{6,7},{7,6},{8,9},{9,8},{10,11... | collective-permute-start | bytes 5898248 | tf_op jit(solution)/shard_map/ppermute | solution.py:747
  23.2 31.2 %collective-permute-start.8 = (f32[5,96,1024]{2,1,0:T(8,128)}, f32[5,96,1024]{2,1,0:T(8,128)}, u32[]{:S(2)}, u32[]{:S(2)}) collective-permute-start(f32[5,96,1024]{2,1,0:T(8,128)} %get-tuple-element.26), channel_id=1, source_target_pairs={{1,2},{2,1},{5,6},{6,5},{9,10},{10,9},{13,14},{14,13},{17,18},{18,... | collective-permute-start | bytes 5898248 | tf_op jit(solution)/shard_map/ppermute | solution.py:745
  25.8 28.6 %collective-permute-start.7 = (f32[5,96,1024]{2,1,0:T(8,128)}, f32[5,96,1024]{2,1,0:T(8,128)}, u32[]{:S(2)}, u32[]{:S(2)}) collective-permute-start(f32[5,96,1024]{2,1,0:T(8,128)} %get-tuple-element.24.token), channel_id=1, source_target_pairs={{0,1},{1,0},{2,3},{3,2},{4,5},{5,4},{6,7},{7,6},{8,9},{9,8},{10,11... | collective-permute-start | bytes 5898248 | tf_op jit(solution)/shard_map/ppermute | solution.py:747
  26.1 6.4 %collective-permute-start.2 = (f32[5,16,1024]{2,1,0:T(8,128)}, f32[5,16,1024]{2,1,0:T(8,128)S(1)}, u32[]{:S(2)}, u32[]{:S(2)}) collective-permute-start(f32[5,16,1024]{2,1,0:T(8,128)} %copy-done.1), channel_id=1, source_target_pairs={{0,1},{1,0},{2,3},{3,2},{4,5},{5,4},{6,7},{7,6},{8,9},{9,8},{10,11... | collective-permute-start | bytes 983048 | tf_op jit(solution)/shard_map/ppermute | solution.py:731
  26.7 6.6 %copy-start = (bf16[384,640]{1,0:T(8,128)(2,1)S(1)}, bf16[384,640]{1,0:T(8,128)(2,1)}, u32[]{:S(2)}) copy-start(bf16[384,640]{1,0:T(8,128)(2,1)} %constant.54.clone.solve) | copy-start | bytes 1474564
  39.6 25.2 %collective-permute-start.6 = (f32[5,48,1024]{2,1,0:T(8,128)S(1)}, f32[5,48,1024]{2,1,0:T(8,128)S(1)}, u32[]{:S(2)}, u32[]{:S(2)}) collective-permute-start(f32[5,48,1024]{2,1,0:T(8,128)S(1)} %get-tuple-element.25), channel_id=1, source_target_pairs={{1,2},{2,1},{5,6},{6,5},{9,10},{10,9},{13,14},{14,13},{17,18},{18,... | collective-permute-start | bytes 2949128 | tf_op jit(solution)/shard_map/ppermute | solution.py:768
  43.2 10.6 %collective-permute-start.10 = (f32[16,128]{1,0:T(8,128)S(1)}, f32[16,128]{1,0:T(8,128)S(1)}, u32[]{:S(2)}, u32[]{:S(2)}) collective-permute-start(f32[16,128]{1,0:T(8,128)S(1)} %get-tuple-element.27.token), channel_id=1, source_target_pairs={{0,16},{16,0},{1,17},{17,1},{2,18},{18,2},{3,19},{19,3},{4,20},{20... | collective-permute-start | bytes 24584 | tf_op jit(solution)/shard_map/ppermute | solution.py:693

commit v14 on v13

--- a/solution.py
+++ b/solution.py
@@ -27,6 +27,15 @@
 COL_GAIN = 33
 
 ODD, OUTER, FIRST, LAST, BASE = range(5)
+
+
+def place_flags(counts, rows):
+    ax_count, rad_count = counts
+    ax = lax.axis_index("ax")
+    rad = lax.axis_index("rad")
+    beside = (ax > 0) & (ax < ax_count - 1)
+    flags = [ax % 2, beside, rad == 0, rad == rad_count - 1, rad * rows]
+    return [x.astype(jnp.int32) for x in flags]
 
 
 def plane_of(odd, q):
@@ -150,8 +159,9 @@
 
 
 def bulk_kernel(
-    dtheta, rows, span, total_rows, fused, near, flags, state, low, high, inner, edge, outer, token, held, *rest
+    dtheta, rows, span, total_rows, fused, near, counts, state, low, high, inner, edge, outer, token, held, *rest
 ):
+    flags = place_flags(counts, total_rows)
     near_parts, out, scratch = rest[:near], rest[near], rest[near + 1 :]
     first, end = span
     blocks = (end - first) // rows
@@ -226,7 +236,8 @@
             pltpu.make_async_copy(near_rows, held.at[:, :, 0:R_NEAR, :], near_sem).wait()
 
 
-def outer_kernel(rows, span, flags, outer, held, out, outer_rows, held_rows, sems):
+def outer_kernel(rows, span, counts, outer, held, out, outer_rows, held_rows, sems):
+    flags = place_flags(counts, 0)
     first, end = span
     plane = lax.axis_index("ax") % 2
     sign = jnp.where(flags[ODD] == 1, -0.5, 0.5)
@@ -259,7 +270,7 @@
     dtheta,
     total_rows,
     part_first,
-    flags,
+    counts,
     state,
     after,
     low,
@@ -277,6 +288,7 @@
     carry,
     *rest,
 ):
+    flags = place_flags(counts, total_rows)
     cells = state.shape[-1]
     odd = flags[ODD]
     part = rest[0] if len(rest) > 2 else None
@@ -387,27 +399,29 @@
     for come, _ in steps:
         come.start()
 
-    def finish():
+    def forward():
         for come, leave in steps:
             come.wait()
             leave.start()
+
+    def finish():
         for _, leave in steps:
             leave.wait()
 
-    return finish
+    return forward, finish
 
 
 def pack_first_kernel(count, state, part, low, high, stage, top, bottom, row_sems, sems):
     _, _, rows, _ = state.shape
     odd = lax.axis_index("ax") % 2
-    finish = stream([(state.at[:, odd, 0:count, :], stage, part)], sems)
+    forward, finish = stream([(state.at[:, odd, 0:count, :], stage, part)], sems)
     copies = [
         pltpu.make_async_copy(state.at[:, :, rows - EIGHT : rows, :], top, row_sems.at[0]),
         pltpu.make_async_copy(state.at[:, :, 0:EIGHT, :], bottom, row_sems.at[1]),
     ]
     for copy in copies:
         copy.start()
-    finish()
+    forward()
     for copy in copies:
         copy.wait()
     for f in range(FIELDS):
@@ -416,6 +430,7 @@
             p = plane_of(odd, q)
             low[k : k + 1, :] = top[f, p, EIGHT - 1 : EIGHT, :]
             high[k : k + 1, :] = bottom[f, p, 0:1, :]
+    finish()
 
 
 def pack_edges_kernel(state, token, edge, side, left, right, sems):
@@ -448,7 +463,8 @@
     pieces = []
     for k, (q, first, last) in enumerate(parts):
         pieces.append((state.at[:, plane_of(odd, q), first:last, :], rest[count + k], rest[k]))
-    stream(pieces, rest[-1])()
+    for step in stream(pieces, rest[-1]):
+        step()
 
 
 ANY = pl.BlockSpec(memory_space=pl.ANY)
@@ -456,11 +472,11 @@
 
 
 def whole(*shape):
-    return pl.BlockSpec(shape, lambda i, s: (0,) * len(shape))
+    return pl.BlockSpec(shape, lambda i: (0,) * len(shape))
 
 
 def rows_from(shape, axis, first, step):
-    def place(i, s):
+    def place(i):
         row = (first // EIGHT + i * (step // EIGHT)) * EIGHT
         return tuple(row if d == axis else 0 for d in range(len(shape)))
 
@@ -540,23 +556,23 @@
     return [pltpu.VMEM((*shape, n, LANES), jnp.float32) for n in (rows + 2 * EIGHT, rows)]
 
 
-def bulk(flags, state, low, high, inner, edge, dtheta, outer, span, token, held, near_parts=()):
+def bulk(counts, state, low, high, inner, edge, dtheta, outer, span, token, held, near_parts=()):
     fields, planes, total_rows, cells = state.shape
     first, end = span
     count = end - first
     rows = 32 if count % 32 == 0 else 24 if count % 24 == 0 else 16
     blocks = count // rows
     size = fields * planes * count * cells
-    aliases = {} if held is None else {8: 0}
+    aliases = {} if held is None else {7: 0}
     state = in_hbm(state)
     operands = [state, low, high, inner, edge, inner if outer is None else outer, token]
     operands += [state if held is None else held, *near_parts]
     chunk = pltpu.VMEM((fields, count, cells), jnp.float32)
     near_scratch = [pltpu.VMEM((fields, planes, R_NEAR, cells), jnp.float32), pltpu.SemaphoreType.DMA]
     return pl.pallas_call(
-        functools.partial(bulk_kernel, dtheta, rows, span, total_rows, outer is not None, len(near_parts)),
+        functools.partial(bulk_kernel, dtheta, rows, span, total_rows, outer is not None, len(near_parts), counts),
         grid_spec=pltpu.PrefetchScalarGridSpec(
-            num_scalar_prefetch=1,
+            num_scalar_prefetch=0,
             grid=(blocks,),
             in_specs=[
                 ANY,
@@ -584,30 +600,30 @@
         compiler_params=PARAMS,
         cost_estimate=cost(size * 60, size * 10),
         name="bulk",
-    )(flags, *operands)
-
-
-def add_outer(flags, outer, span, rows, held):
+    )(*operands)
+
+
+def add_outer(counts, outer, span, rows, held):
     fields, count, cells = outer.shape
     chunk = pltpu.VMEM((fields, count, cells), jnp.float32)
     return pl.pallas_call(
-        functools.partial(outer_kernel, rows, span),
+        functools.partial(outer_kernel, rows, span, counts),
         grid_spec=pltpu.PrefetchScalarGridSpec(
-            num_scalar_prefetch=1,
+            num_scalar_prefetch=0,
             grid=(1,),
             in_specs=[ANY, ANY],
             out_specs=ANY,
             scratch_shapes=[chunk, chunk, pltpu.SemaphoreType.DMA((3 * (count // rows),))],
         ),
         out_shape=pltpu.HBM(held.shape, jnp.float32),
-        input_output_aliases={2: 0},
+        input_output_aliases={1: 0},
         compiler_params=PARAMS,
         cost_estimate=cost(outer.size * 6, outer.size * 16),
         name="add_outer",
-    )(flags, outer, held)
-
-
-def near(flags, state, low, high, inner, edge, dtheta, outer, factor, table, solve, token, part=None):
+    )(outer, held)
+
+
+def near(counts, state, low, high, inner, edge, dtheta, outer, factor, table, solve, token, part=None):
     fields, planes, rows, cells = state.shape
     out = jax.ShapeDtypeStruct((LINES, R_NEAR, cells), jnp.float32)
     tail = min(R_NEAR // EIGHT, rows // EIGHT - 1)
@@ -620,13 +636,13 @@
         out_shape.append(jax.ShapeDtypeStruct((fields, part[1] - part[0], cells), jnp.float32))
         scratch.append(pltpu.SemaphoreType.DMA)
     result = pl.pallas_call(
-        functools.partial(near_kernel, dtheta, rows, part[0] if part else 0),
+        functools.partial(near_kernel, dtheta, rows, part[0] if part else 0, counts),
         grid_spec=pltpu.PrefetchScalarGridSpec(
-            num_scalar_prefetch=1,
+            num_scalar_prefetch=0,
             grid=(1,),
             in_specs=[
                 whole(fields, planes, R_NEAR, cells),
-                pl.BlockSpec((fields, planes, EIGHT, cells), lambda i, s: (0, 0, tail, 0)),
+                pl.BlockSpec((fields, planes, EIGHT, cells), lambda i: (0, 0, tail, 0)),
                 whole(LINES, cells),
                 whole(LINES, cells),
                 whole(fields, R_NEAR, cells),
@@ -645,7 +661,7 @@
         compiler_params=PARAMS,
         cost_estimate=cost(LINES * R_NEAR * cells * 200, LINES * R_NEAR * cells * 250),
         name="near",
-    )(flags, state, state, low, high, inner, outer, edge, factor, table, solve, in_hbm(token), state)
+    )(state, state, low, high, inner, outer, edge, factor, table, solve, in_hbm(token), state)
     return result if part is not None else (*result, None)
 
 
@@ -699,8 +715,6 @@
     rad_count = lax.axis_size("rad")
     ax_count = lax.axis_size("ax")
     assert fields == FIELDS and planes == PLANES and ax_count % 2 == 0
-    rad_index = lax.axis_index("rad")
-    ax_index = lax.axis_index("ax")
     total_cells = cells * sec_count
     dtheta = 2.0 * math.pi / total_cells
     outer_pairs = []
@@ -711,15 +725,7 @@
         inner_pairs += [(i, i + 1), (i + 1, i)]
     up = [(i, i + 1) for i in range(rad_count - 1)]
     down = [(i + 1, i) for i in range(rad_count - 1)]
-    flags = jnp.stack(
-        [
-            ax_index % 2,
-            ((ax_index > 0) & (ax_index < ax_count - 1)).astype(jnp.int32),
-            (rad_index == 0).astype(jnp.int32),
-            (rad_index == rad_count - 1).astype(jnp.int32),
-            rad_index * rows,
-        ]
-    ).astype(jnp.int32)
+    counts = (ax_count, rad_count)
     size, spans = chunks(rows)
     count = len(spans)
 
@@ -751,7 +757,7 @@
     factor = jnp.broadcast_to(coarsen.astype(jnp.float32)[:, None], (R_NEAR, LANES))
 
     solve = piece_tables(dtheta)
-    given = (flags, state, low, high)
+    given = (counts, state, low, high)
 
     def pass_over(k, token, held, fused=True, near_parts=()):
         span = (spans[k][0] if k else R_NEAR, spans[k][1])
@@ -776,7 +782,7 @@
     for k in range(passes):
         near_parts = (factor, rhs, local, carry, table) if k == passes - 1 else ()
         out = pass_over(k, ends, out, near_parts=near_parts)
-    return add_outer(flags, outer[2], spans[2], size, out) if count > 2 else out
+    return add_outer(counts, outer[2], spans[2], size, out) if count > 2 else out
 
 
 def solution(mesh):

time: 67.9 us -> 67 us (0.987)
  Pallas kernels: 45.4 us -> 42 us
  waiting for transfers between devices: 1.8 us -> 4.2 us
    pallas_call x3, Pallas kernels: 24.9 us -> 22.6 us  [bulk(): pl.pallas_call(functools.partial(bulk_kernel, dtheta, rows, span, total_r...]
    ppermute x1, waiting for transfers between devices: 0.56 us -> 1.78 us  [body(): outer.append(lax.ppermute(part, 'ax', outer_pairs))]
    ppermute x1, waiting for transfers between devices: 0.48 us -> 1.61 us  [body(): outer.append(lax.ppermute(value, 'ax', outer_pairs))]
  transfers between devices with their start and end apart: 11 -> 11, of which waited for: 3 -> 4; matrix products, arithmetic and copies ran while one was open for 1% -> 0% of each run, Pallas kernels for 59% -> 56%
where the time goes in v14:
time: 67 us; the launch traced here: 66.6 us
  Pallas kernels  42 us (63%)
  starting transfers between devices  19.1 us (29%)
  waiting for transfers between devices  4.2 us (6%)
  local copies, waits for them, and re-layouts  0.92 us (1%)
    pallas_call x3, Pallas kernels, bulk(): pl.pallas_call(functools.partial(bulk_kernel, dtheta, rows, span, total_r...  22.6 us
    pallas_call x2, Pallas kernels, pack_rest(): pl.pallas_call(functools.partial(pack_rest_kernel, parts, len(tokens)), i...  6.34 us
    pallas_call x1, Pallas kernels, near(): pl.pallas_call(functools.partial(near_kernel, dtheta, rows, part[0] if pa...  5.77 us
    ppermute x1, starting transfers between devices, body(): outer = [lax.ppermute(part, 'ax', outer_pairs)]  4.51 us
    ppermute x1, starting transfers between devices, body(): outer.append(lax.ppermute(part, 'ax', outer_pairs))  3.67 us
    ppermute x1, starting transfers between devices, body(): low = lax.ppermute(low, 'rad', up)  3.2 us
    ppermute x1, starting transfers between devices, body(): outer.append(lax.ppermute(value, 'ax', outer_pairs))  3.06 us
    pallas_call x1, Pallas kernels, pack_first(): pl.pallas_call(functools.partial(pack_first_kernel, count), in_specs=[ANY...  2.61 us
  transfers between devices with their start and end apart: 11, of which 4 were waited for; matrix products, arithmetic and copies ran while one was open for 0% of the time, Pallas kernels for 56%

profile of v14, /device:TPU:1, one launch (start us, length us, event | category | flops | bytes accessed | tf_op | source)
XLA Modules:
  0.0 66.6 jit_solution(11856894849473113507)
XLA Ops:
  0.0 2.6 %pack_first.1 = (f32[5,112,1024]{2,1,0:T(8,128)S(1)}, f32[10,1024]{1,0:T(8,128)S(1)}, f32[10,1024]{1,0:T(8,128)S(1)}) custom-call(f32[5,2,256,1024]{3,2,1,0:T(8,128)} %state.15), custom_call_target="tpu_custom_call" | custom-call | bytes 4587520 | tf_op jit(solution)/shard_map/pack_first/pallas_call | solution.py:499
  2.6 4.5 %collective-permute-start.3 = (f32[5,112,1024]{2,1,0:T(8,128)S(1)}, f32[5,112,1024]{2,1,0:T(8,128)S(1)}, u32[]{:S(2)}, u32[]{:S(2)}) collective-permute-start(f32[5,112,1024]{2,1,0:T(8,128)S(1)} %get-tuple-element.21), channel_id=1, source_target_pairs={{1,2},{2,1},{5,6},{6,5},{9,10},{10,9},{13,14},{14,13},{17,18},{18,... | collective-permute-start | bytes 6881288 | tf_op jit(solution)/shard_map/ppermute | solution.py:733
  7.1 3.2 %collective-permute-start = (f32[10,1024]{1,0:T(8,128)S(1)}, f32[10,1024]{1,0:T(8,128)S(1)}, u32[]{:S(2)}, u32[]{:S(2)}) collective-permute-start(f32[10,1024]{1,0:T(8,128)S(1)} %get-tuple-element.18), channel_id=1, source_target_pairs={{0,4},{4,8},{8,12},{1,5},{5,9},{9,13},{2,6},{6,10},{10,14},{3,7},{... | collective-permute-start | bytes 122888 | tf_op jit(solution)/shard_map/ppermute | solution.py:735
  10.3 1.3 %collective-permute-start.1 = (f32[10,1024]{1,0:T(8,128)S(1)}, f32[10,1024]{1,0:T(8,128)S(1)}, u32[]{:S(2)}, u32[]{:S(2)}) collective-permute-start(f32[10,1024]{1,0:T(8,128)S(1)} %get-tuple-element.19.token), channel_id=1, source_target_pairs={{4,0},{8,4},{12,8},{5,1},{9,5},{13,9},{6,2},{10,6},{14,10},{7,3},{... | collective-permute-start | bytes 122888 | tf_op jit(solution)/shard_map/ppermute | solution.py:736
  11.6 2.6 %pack_edges.1 = (f32[256,128]{1,0:T(8,128)S(1)}, f32[5,16,1024]{2,1,0:T(8,128)S(1)}) custom-call(f32[5,2,256,1024]{3,2,1,0:T(8,128)} %state.15, f32[10,1024]{1,0:T(8,128)S(1)} %get-tuple-element.19.token), custom_call_target="tpu_custom_call" | custom-call | bytes 5242880 | tf_op jit(solution)/shard_map/pack_edges/pallas_call | solution.py:521
  14.2 1.3 %collective-permute-start.4 = (f32[256,128]{1,0:T(8,128)S(1)}, f32[256,128]{1,0:T(8,128)S(1)}, u32[]{:S(2)}, u32[]{:S(2)}) collective-permute-start(f32[256,128]{1,0:T(8,128)S(1)} %get-tuple-element.22.rest_0_), channel_id=1, source_target_pairs={{0,16},{16,0},{1,17},{17,1},{2,18},{18,2},{3,19},{19,3},{4,20},{20... | collective-permute-start | bytes 393224 | tf_op jit(solution)/shard_map/ppermute | solution.py:709
  15.5 0.0 collective-permute-done.rest_1_.low
  15.5 0.1 collective-permute-done.1.rest_2_.high
  15.7 3.3 %pack_rest.2 = (f32[5,48,1024]{2,1,0:T(8,128)S(1)}, f32[5,96,1024]{2,1,0:T(8,128)S(1)}) custom-call(f32[5,2,256,1024]{3,2,1,0:T(8,128)} %state.15, f32[256,128]{1,0:T(8,128)S(1)} %get-tuple-element.22.rest_0_, f32[10,1024]{1,0:T(8,128)S(1)} %collective-permute-done.rest_1_.low, f32[10,1024]{1,0:T(8,128)S(1)} %collective-permute-done.1.rest_2_.high), custom_call_target="tpu_custom_call" | custom-call | bytes 5898240 | tf_op jit(solution)/shard_map/pack_rest/pallas_call | solution.py:539
  18.9 0.0 copy-start.1
  19.0 0.0 copy-start.3
  19.0 0.1 collective-permute-start.5
  19.1 0.0 collective-permute-done.4.rest_1_.edge
  19.1 0.8 %copy-done.1 = f32[5,48,1024]{2,1,0:T(8,128)} copy-done((f32[5,48,1024]{2,1,0:T(8,128)}, f32[5,48,1024]{2,1,0:T(8,128)S(1)}, u32[]{:S(2)}) %copy-start.1) | copy-done | bytes 983064
  19.9 3.1 %pack_rest.3 = (f32[5,96,1024]{2,1,0:T(8,128)S(1)}, f32[5,96,1024]{2,1,0:T(8,128)S(1)}) custom-call(f32[5,2,256,1024]{3,2,1,0:T(8,128)} %state.15, f32[5,48,1024]{2,1,0:T(8,128)} %copy-done.1, f32[256,128]{1,0:T(8,128)S(1)} %collective-permute-done.4.rest_1_.edge), custom_call_target="tpu_custom_call" | custom-call | bytes 7864320 | tf_op jit(solution)/shard_map/pack_rest/pallas_call | solution.py:539
  23.0 0.0 copy-start
  23.0 0.1 collective-permute-start.9
  23.0 3.1 %collective-permute-start.8 = (f32[5,96,1024]{2,1,0:T(8,128)S(1)}, f32[5,96,1024]{2,1,0:T(8,128)S(1)}, u32[]{:S(2)}, u32[]{:S(2)}) collective-permute-start(f32[5,96,1024]{2,1,0:T(8,128)S(1)} %get-tuple-element.26), channel_id=1, source_target_pairs={{1,2},{2,1},{5,6},{6,5},{9,10},{10,9},{13,14},{14,13},{17,18},{18,... | collective-permute-start | bytes 5898248 | tf_op jit(solution)/shard_map/ppermute | solution.py:751
  26.1 0.1 collective-permute-start.7
  26.2 0.0 copy-done.3
  26.3 0.0 collective-permute-done.5.inner.outer
  26.3 0.5 collective-permute-start.2
  26.8 0.1 fusion.3.table.rest_4_
  26.9 0.0 copy-done
  26.9 0.0 copy-start.2
  27.0 5.3 %bulk.3.token.held = f32[5,2,256,1024]{3,2,1,0:T(8,128)} custom-call(f32[5,2,256,1024]{3,2,1,0:T(8,128)} %state.15, f32[10,1024]{1,0:T(8,128)S(1)} %collective-permute-done.rest_1_.low, f32[10,1024]{1,0:T(8,128)S(1)} %collective-permute-done.1.rest_2_.high, f32[5,48,1024]{2,1,0:T(8,128)S(1)} %collective-permute-done.5.inner.outer, ...), custom_call_target="tpu_custom_call" | custom-call | flops 29491200 | bytes 4915200 | tf_op jit(solution)/shard_map/bulk/pallas_call | solution.py:572
  32.3 0.0 collective-permute-done.2.inner
  32.3 0.7 collective-permute-done.3.outer
  32.9 0.1 broadcast_in_dim.51.factor.rest_0_
  33.0 0.0 copy-done.2
  33.0 5.8 %near.1 = (f32[10,16,1024]{2,1,0:T(8,128)S(1)}, f32[10,16,1024]{2,1,0:T(8,128)S(1)}, f32[16,128]{1,0:T(8,128)S(1)}, f32[5,48,1024]{2,1,0:T(8,128)S(1)}) custom-call(f32[5,2,256,1024]{3,2,1,0:T(8,128)} %state.15, f32[5,2,256,1024]{3,2,1,0:T(8,128)} %state.15, f32[10,1024]{1,0:T(8,128)S(1)} %collective-permute-done.rest_1_.low, ...), custom_call_target="tpu_custom_call" | custom-call | flops 32768000 | bytes 40960000 | tf_op jit(solution)/shard_map/near/pallas_call | solution.py:638
  38.8 3.7 %collective-permute-start.6 = (f32[5,48,1024]{2,1,0:T(8,128)S(1)}, f32[5,48,1024]{2,1,0:T(8,128)S(1)}, u32[]{:S(2)}, u32[]{:S(2)}) collective-permute-start(f32[5,48,1024]{2,1,0:T(8,128)S(1)} %get-tuple-element.25), channel_id=1, source_target_pairs={{1,2},{2,1},{5,6},{6,5},{9,10},{10,9},{13,14},{14,13},{17,18},{18,... | collective-permute-start | bytes 2949128 | tf_op jit(solution)/shard_map/ppermute | solution.py:774
  42.5 1.3 %collective-permute-start.10 = (f32[16,128]{1,0:T(8,128)S(1)}, f32[16,128]{1,0:T(8,128)S(1)}, u32[]{:S(2)}, u32[]{:S(2)}) collective-permute-start(f32[16,128]{1,0:T(8,128)S(1)} %get-tuple-element.27.token), channel_id=1, source_target_pairs={{0,16},{16,0},{1,17},{17,1},{2,18},{18,2},{3,19},{19,3},{4,20},{20... | collective-permute-start | bytes 24584 | tf_op jit(solution)/shard_map/ppermute | solution.py:709
  43.7 0.0 collective-permute-done.9.inner
  43.7 8.6 %bulk.4.held = f32[5,2,256,1024]{3,2,1,0:T(8,128)} custom-call(f32[5,2,256,1024]{3,2,1,0:T(8,128)} %state.15, f32[10,1024]{1,0:T(8,128)S(1)} %collective-permute-done.rest_1_.low, f32[10,1024]{1,0:T(8,128)S(1)} %collective-permute-done.1.rest_2_.high, f32[5,96,1024]{2,1,0:T(8,128)S(1)} %collective-permute-done.9.inner, ...), custom_call_target="tpu_custom_call", output_to_operand_aliasing={{}: (7, {})} | custom-call | flops 58982400 | bytes 9830400 | tf_op jit(solution)/shard_map/bulk/pallas_call | solution.py:572
  52.3 0.0 collective-permute-done.10
  52.3 0.1 add_multiply_fusion.rest_3_
  52.4 1.6 %collective-permute-done.8.outer = f32[5,96,1024]{2,1,0:T(8,128)S(1)} collective-permute-done((f32[5,96,1024]{2,1,0:T(8,128)S(1)}, f32[5,96,1024]{2,1,0:T(8,128)S(1)}, u32[]{:S(2)}, u32[]{:S(2)}) %collective-permute-start.8) | collective-permute-done | bytes 1966112 | tf_op jit(solution)/shard_map/ppermute | solution.py:751
  54.0 0.0 collective-permute-done.7.inner
  54.0 8.7 %bulk.5.held = f32[5,2,256,1024]{3,2,1,0:T(8,128)} custom-call(f32[5,2,256,1024]{3,2,1,0:T(8,128)} %state.15, f32[10,1024]{1,0:T(8,128)S(1)} %collective-permute-done.rest_1_.low, f32[10,1024]{1,0:T(8,128)S(1)} %collective-permute-done.1.rest_2_.high, f32[5,96,1024]{2,1,0:T(8,128)S(1)} %collective-permute-done.7.inner, ...), custom_call_target="tpu_custom_call", output_to_operand_aliasing={{}: (7, {})} | custom-call | flops 58982400 | bytes 9830400 | tf_op jit(solution)/shard_map/bulk/pallas_call | solution.py:572
  62.8 1.8 %collective-permute-done.6.outer = f32[5,48,1024]{2,1,0:T(8,128)S(1)} collective-permute-done((f32[5,48,1024]{2,1,0:T(8,128)S(1)}, f32[5,48,1024]{2,1,0:T(8,128)S(1)}, u32[]{:S(2)}, u32[]{:S(2)}) %collective-permute-start.6) | collective-permute-done | bytes 983072 | tf_op jit(solution)/shard_map/ppermute | solution.py:774
  64.5 2.1 %add_outer.1 = f32[5,2,256,1024]{3,2,1,0:T(8,128)} custom-call(f32[5,48,1024]{2,1,0:T(8,128)S(1)} %collective-permute-done.6.outer, f32[5,2,256,1024]{3,2,1,0:T(8,128)} %bulk.5.held), custom_call_target="tpu_custom_call", output_to_operand_aliasing={{}: (1, {})} | custom-call | flops 1474560 | bytes 3932160 | tf_op jit(solution)/shard_map/add_outer/pallas_call | solution.py:609
  (5 shorter events, 0.1 us)
Async XLA Ops:
  2.6 30.3 %collective-permute-start.3 = (f32[5,112,1024]{2,1,0:T(8,128)S(1)}, f32[5,112,1024]{2,1,0:T(8,128)S(1)}, u32[]{:S(2)}, u32[]{:S(2)}) collective-permute-start(f32[5,112,1024]{2,1,0:T(8,128)S(1)} %get-tuple-element.21), channel_id=1, source_target_pairs={{1,2},{2,1},{5,6},{6,5},{9,10},{10,9},{13,14},{14,13},{17,18},{18,... | collective-permute-start | bytes 6881288 | tf_op jit(solution)/shard_map/ppermute | solution.py:733
  7.1 8.4 %collective-permute-start = (f32[10,1024]{1,0:T(8,128)S(1)}, f32[10,1024]{1,0:T(8,128)S(1)}, u32[]{:S(2)}, u32[]{:S(2)}) collective-permute-start(f32[10,1024]{1,0:T(8,128)S(1)} %get-tuple-element.18), channel_id=1, source_target_pairs={{0,4},{4,8},{8,12},{1,5},{5,9},{9,13},{2,6},{6,10},{10,14},{3,7},{... | collective-permute-start | bytes 122888 | tf_op jit(solution)/shard_map/ppermute | solution.py:735
  10.3 5.3 %collective-permute-start.1 = (f32[10,1024]{1,0:T(8,128)S(1)}, f32[10,1024]{1,0:T(8,128)S(1)}, u32[]{:S(2)}, u32[]{:S(2)}) collective-permute-start(f32[10,1024]{1,0:T(8,128)S(1)} %get-tuple-element.19.token), channel_id=1, source_target_pairs={{4,0},{8,4},{12,8},{5,1},{9,5},{13,9},{6,2},{10,6},{14,10},{7,3},{... | collective-permute-start | bytes 122888 | tf_op jit(solution)/shard_map/ppermute | solution.py:736
  14.2 4.8 %collective-permute-start.4 = (f32[256,128]{1,0:T(8,128)S(1)}, f32[256,128]{1,0:T(8,128)S(1)}, u32[]{:S(2)}, u32[]{:S(2)}) collective-permute-start(f32[256,128]{1,0:T(8,128)S(1)} %get-tuple-element.22.rest_0_), channel_id=1, source_target_pairs={{0,16},{16,0},{1,17},{17,1},{2,18},{18,2},{3,19},{19,3},{4,20},{20... | collective-permute-start | bytes 393224 | tf_op jit(solution)/shard_map/ppermute | solution.py:709
  18.9 0.9 %copy-start.1 = (f32[5,48,1024]{2,1,0:T(8,128)}, f32[5,48,1024]{2,1,0:T(8,128)S(1)}, u32[]{:S(2)}) copy-start(f32[5,48,1024]{2,1,0:T(8,128)S(1)} %get-tuple-element.23.rest_0_) | copy-start | bytes 2949124
  19.0 7.2 %copy-start.3 = (s32[16]{0:T(128)S(1)}, s32[16]{0:T(128)}, u32[]{:S(2)}) copy-start(s32[16]{0:T(128)} %param.4) | copy-start | bytes 196
  19.0 7.3 %collective-permute-start.5 = (f32[5,48,1024]{2,1,0:T(8,128)S(1)}, f32[5,48,1024]{2,1,0:T(8,128)S(1)}, u32[]{:S(2)}, u32[]{:S(2)}) collective-permute-start(f32[5,48,1024]{2,1,0:T(8,128)S(1)} %get-tuple-element.23.rest_0_), channel_id=1, source_target_pairs={{0,1},{1,0},{2,3},{3,2},{4,5},{5,4},{6,7},{7,6},{8,9},{9,8},{10,11... | collective-permute-start | bytes 2949128 | tf_op jit(solution)/shard_map/ppermute | solution.py:753
  23.0 4.0 %copy-start = (f32[5,96,1024]{2,1,0:T(8,128)}, f32[5,96,1024]{2,1,0:T(8,128)S(1)}, u32[]{:S(2)}) copy-start(f32[5,96,1024]{2,1,0:T(8,128)S(1)} %get-tuple-element.24.token) | copy-start | bytes 5898244
  23.0 20.8 %collective-permute-start.9 = (f32[5,96,1024]{2,1,0:T(8,128)S(1)}, f32[5,96,1024]{2,1,0:T(8,128)S(1)}, u32[]{:S(2)}, u32[]{:S(2)}) collective-permute-start(f32[5,96,1024]{2,1,0:T(8,128)S(1)} %get-tuple-element.28), channel_id=1, source_target_pairs={{0,1},{1,0},{2,3},{3,2},{4,5},{5,4},{6,7},{7,6},{8,9},{9,8},{10,11... | collective-permute-start | bytes 5898248 | tf_op jit(solution)/shard_map/ppermute | solution.py:753
  23.0 31.0 %collective-permute-start.8 = (f32[5,96,1024]{2,1,0:T(8,128)S(1)}, f32[5,96,1024]{2,1,0:T(8,128)S(1)}, u32[]{:S(2)}, u32[]{:S(2)}) collective-permute-start(f32[5,96,1024]{2,1,0:T(8,128)S(1)} %get-tuple-element.26), channel_id=1, source_target_pairs={{1,2},{2,1},{5,6},{6,5},{9,10},{10,9},{13,14},{14,13},{17,18},{18,... | collective-permute-start | bytes 5898248 | tf_op jit(solution)/shard_map/ppermute | solution.py:751
  26.1 27.9 %collective-permute-start.7 = (f32[5,96,1024]{2,1,0:T(8,128)S(1)}, f32[5,96,1024]{2,1,0:T(8,128)S(1)}, u32[]{:S(2)}, u32[]{:S(2)}) collective-permute-start(f32[5,96,1024]{2,1,0:T(8,128)S(1)} %get-tuple-element.24.token), channel_id=1, source_target_pairs={{0,1},{1,0},{2,3},{3,2},{4,5},{5,4},{6,7},{7,6},{8,9},{9,8},{10,11... | collective-permute-start | bytes 5898248 | tf_op jit(solution)/shard_map/ppermute | solution.py:753
  26.3 6.0 %collective-permute-start.2 = (f32[5,16,1024]{2,1,0:T(8,128)S(1)}, f32[5,16,1024]{2,1,0:T(8,128)S(1)}, u32[]{:S(2)}, u32[]{:S(2)}) collective-permute-start(f32[5,16,1024]{2,1,0:T(8,128)S(1)} %get-tuple-element.20), channel_id=1, source_target_pairs={{0,1},{1,0},{2,3},{3,2},{4,5},{5,4},{6,7},{7,6},{8,9},{9,8},{10,11... | collective-permute-start | bytes 983048 | tf_op jit(solution)/shard_map/ppermute | solution.py:737
  26.9 6.1 %copy-start.2 = (bf16[384,640]{1,0:T(8,128)(2,1)S(1)}, bf16[384,640]{1,0:T(8,128)(2,1)}, u32[]{:S(2)}) copy-start(bf16[384,640]{1,0:T(8,128)(2,1)} %constant.30.clone.solve) | copy-start | bytes 1474564
  38.8 25.7 %collective-permute-start.6 = (f32[5,48,1024]{2,1,0:T(8,128)S(1)}, f32[5,48,1024]{2,1,0:T(8,128)S(1)}, u32[]{:S(2)}, u32[]{:S(2)}) collective-permute-start(f32[5,48,1024]{2,1,0:T(8,128)S(1)} %get-tuple-element.25), channel_id=1, source_target_pairs={{1,2},{2,1},{5,6},{6,5},{9,10},{10,9},{13,14},{14,13},{17,18},{18,... | collective-permute-start | bytes 2949128 | tf_op jit(solution)/shard_map/ppermute | solution.py:774
  42.5 9.8 %collective-permute-start.10 = (f32[16,128]{1,0:T(8,128)S(1)}, f32[16,128]{1,0:T(8,128)S(1)}, u32[]{:S(2)}, u32[]{:S(2)}) collective-permute-start(f32[16,128]{1,0:T(8,128)S(1)} %get-tuple-element.27.token), channel_id=1, source_target_pairs={{0,16},{16,0},{1,17},{17,1},{2,18},{18,2},{3,19},{19,3},{4,20},{20... | collective-permute-start | bytes 24584 | tf_op jit(solution)/shard_map/ppermute | solution.py:709

commit v15 on v14

--- a/solution.py
+++ b/solution.py
@@ -414,7 +414,10 @@
 def pack_first_kernel(count, state, part, low, high, stage, top, bottom, row_sems, sems):
     _, _, rows, _ = state.shape
     odd = lax.axis_index("ax") % 2
-    forward, finish = stream([(state.at[:, odd, 0:count, :], stage, part)], sems)
+    pieces = []
+    for a, b in ((0, count // 16 * EIGHT), (count // 16 * EIGHT, count)):
+        pieces.append((state.at[:, odd, a:b, :], stage.at[:, a:b, :], part.at[:, a:b, :]))
+    forward, finish = stream(pieces, sems)
     copies = [
         pltpu.make_async_copy(state.at[:, :, rows - EIGHT : rows, :], top, row_sems.at[0]),
         pltpu.make_async_copy(state.at[:, :, 0:EIGHT, :], bottom, row_sems.at[1]),
@@ -506,7 +509,7 @@
             rows,
             rows,
             pltpu.SemaphoreType.DMA((2,)),
-            pltpu.SemaphoreType.DMA((2 * fields,)),
+            pltpu.SemaphoreType.DMA((4 * fields,)),
         ],
         compiler_params=PARAMS,
         cost_estimate=cost(0, fields * count * cells * 8),

time: 67 us -> 68.5 us (1.022)
  Pallas kernels: 42 us -> 43.5 us
    pallas_call x1, Pallas kernels: 2.61 us -> 4.1 us  [pack_first(): pl.pallas_call(functools.partial(pack_first_kernel, count), in_specs=[ANY...]
  transfers between devices with their start and end apart: 11 -> 11, of which waited for: 4 -> 4; matrix products, arithmetic and copies ran while one was open for 0% -> 0% of each run, Pallas kernels for 56% -> 55%
where the time goes in v15:
time: 68.5 us; the launch traced here: 68.1 us
  Pallas kernels  43.5 us (64%)
  starting transfers between devices  19 us (28%)
  waiting for transfers between devices  4.2 us (6%)
  local copies, waits for them, and re-layouts  0.92 us (1%)
    pallas_call x3, Pallas kernels, bulk(): pl.pallas_call(functools.partial(bulk_kernel, dtheta, rows, span, total_r...  22.6 us
    pallas_call x2, Pallas kernels, pack_rest(): pl.pallas_call(functools.partial(pack_rest_kernel, parts, len(tokens)), i...  6.34 us
    pallas_call x1, Pallas kernels, near(): pl.pallas_call(functools.partial(near_kernel, dtheta, rows, part[0] if pa...  5.8 us
    ppermute x1, starting transfers between devices, body(): outer = [lax.ppermute(part, 'ax', outer_pairs)]  4.51 us
    pallas_call x1, Pallas kernels, pack_first(): pl.pallas_call(functools.partial(pack_first_kernel, count), in_specs=[ANY...  4.1 us
    ppermute x1, starting transfers between devices, body(): outer.append(lax.ppermute(part, 'ax', outer_pairs))  3.64 us
    ppermute x1, starting transfers between devices, body(): low = lax.ppermute(low, 'rad', up)  3.2 us
    ppermute x1, starting transfers between devices, body(): outer.append(lax.ppermute(value, 'ax', outer_pairs))  3.06 us
  transfers between devices with their start and end apart: 11, of which 4 were waited for; matrix products, arithmetic and copies ran while one was open for 0% of the time, Pallas kernels for 55%

profile of v15, /device:TPU:1, one launch (start us, length us, event | category | flops | bytes accessed | tf_op | source)
XLA Modules:
  0.0 68.1 jit_solution(11671199219654351151)
XLA Ops:
  0.0 4.1 %pack_first.1 = (f32[5,112,1024]{2,1,0:T(8,128)S(1)}, f32[10,1024]{1,0:T(8,128)S(1)}, f32[10,1024]{1,0:T(8,128)S(1)}) custom-call(f32[5,2,256,1024]{3,2,1,0:T(8,128)} %state.15), custom_call_target="tpu_custom_call" | custom-call | bytes 4587520 | tf_op jit(solution)/shard_map/pack_first/pallas_call | solution.py:502
  4.1 4.5 %collective-permute-start.3 = (f32[5,112,1024]{2,1,0:T(8,128)S(1)}, f32[5,112,1024]{2,1,0:T(8,128)S(1)}, u32[]{:S(2)}, u32[]{:S(2)}) collective-permute-start(f32[5,112,1024]{2,1,0:T(8,128)S(1)} %get-tuple-element.21), channel_id=1, source_target_pairs={{1,2},{2,1},{5,6},{6,5},{9,10},{10,9},{13,14},{14,13},{17,18},{18,... | collective-permute-start | bytes 6881288 | tf_op jit(solution)/shard_map/ppermute | solution.py:736
  8.6 3.2 %collective-permute-start = (f32[10,1024]{1,0:T(8,128)S(1)}, f32[10,1024]{1,0:T(8,128)S(1)}, u32[]{:S(2)}, u32[]{:S(2)}) collective-permute-start(f32[10,1024]{1,0:T(8,128)S(1)} %get-tuple-element.18), channel_id=1, source_target_pairs={{0,4},{4,8},{8,12},{1,5},{5,9},{9,13},{2,6},{6,10},{10,14},{3,7},{... | collective-permute-start | bytes 122888 | tf_op jit(solution)/shard_map/ppermute | solution.py:738
  11.8 1.3 %collective-permute-start.1 = (f32[10,1024]{1,0:T(8,128)S(1)}, f32[10,1024]{1,0:T(8,128)S(1)}, u32[]{:S(2)}, u32[]{:S(2)}) collective-permute-start(f32[10,1024]{1,0:T(8,128)S(1)} %get-tuple-element.19.token), channel_id=1, source_target_pairs={{4,0},{8,4},{12,8},{5,1},{9,5},{13,9},{6,2},{10,6},{14,10},{7,3},{... | collective-permute-start | bytes 122888 | tf_op jit(solution)/shard_map/ppermute | solution.py:739
  13.1 2.6 %pack_edges.1 = (f32[256,128]{1,0:T(8,128)S(1)}, f32[5,16,1024]{2,1,0:T(8,128)S(1)}) custom-call(f32[5,2,256,1024]{3,2,1,0:T(8,128)} %state.15, f32[10,1024]{1,0:T(8,128)S(1)} %get-tuple-element.19.token), custom_call_target="tpu_custom_call" | custom-call | bytes 5242880 | tf_op jit(solution)/shard_map/pack_edges/pallas_call | solution.py:524
  15.7 1.3 %collective-permute-start.4 = (f32[256,128]{1,0:T(8,128)S(1)}, f32[256,128]{1,0:T(8,128)S(1)}, u32[]{:S(2)}, u32[]{:S(2)}) collective-permute-start(f32[256,128]{1,0:T(8,128)S(1)} %get-tuple-element.22.rest_0_), channel_id=1, source_target_pairs={{0,16},{16,0},{1,17},{17,1},{2,18},{18,2},{3,19},{19,3},{4,20},{20... | collective-permute-start | bytes 393224 | tf_op jit(solution)/shard_map/ppermute | solution.py:712
  17.0 0.0 collective-permute-done.rest_1_.low
  17.0 0.1 collective-permute-done.1.rest_2_.high
  17.1 3.3 %pack_rest.2 = (f32[5,48,1024]{2,1,0:T(8,128)S(1)}, f32[5,96,1024]{2,1,0:T(8,128)S(1)}) custom-call(f32[5,2,256,1024]{3,2,1,0:T(8,128)} %state.15, f32[256,128]{1,0:T(8,128)S(1)} %get-tuple-element.22.rest_0_, f32[10,1024]{1,0:T(8,128)S(1)} %collective-permute-done.rest_1_.low, f32[10,1024]{1,0:T(8,128)S(1)} %collective-permute-done.1.rest_2_.high), custom_call_target="tpu_custom_call" | custom-call | bytes 5898240 | tf_op jit(solution)/shard_map/pack_rest/pallas_call | solution.py:542
  20.4 0.0 copy-start.1
  20.4 0.0 copy-start.3
  20.5 0.1 collective-permute-start.5
  20.5 0.0 collective-permute-done.4.rest_1_.edge
  20.5 0.8 %copy-done.1 = f32[5,48,1024]{2,1,0:T(8,128)} copy-done((f32[5,48,1024]{2,1,0:T(8,128)}, f32[5,48,1024]{2,1,0:T(8,128)S(1)}, u32[]{:S(2)}) %copy-start.1) | copy-done | bytes 983064
  21.4 3.1 %pack_rest.3 = (f32[5,96,1024]{2,1,0:T(8,128)S(1)}, f32[5,96,1024]{2,1,0:T(8,128)S(1)}) custom-call(f32[5,2,256,1024]{3,2,1,0:T(8,128)} %state.15, f32[5,48,1024]{2,1,0:T(8,128)} %copy-done.1, f32[256,128]{1,0:T(8,128)S(1)} %collective-permute-done.4.rest_1_.edge), custom_call_target="tpu_custom_call" | custom-call | bytes 7864320 | tf_op jit(solution)/shard_map/pack_rest/pallas_call | solution.py:542
  24.4 0.0 copy-start
  24.5 0.1 collective-permute-start.9
  24.5 3.1 %collective-permute-start.8 = (f32[5,96,1024]{2,1,0:T(8,128)S(1)}, f32[5,96,1024]{2,1,0:T(8,128)S(1)}, u32[]{:S(2)}, u32[]{:S(2)}) collective-permute-start(f32[5,96,1024]{2,1,0:T(8,128)S(1)} %get-tuple-element.26), channel_id=1, source_target_pairs={{1,2},{2,1},{5,6},{6,5},{9,10},{10,9},{13,14},{14,13},{17,18},{18,... | collective-permute-start | bytes 5898248 | tf_op jit(solution)/shard_map/ppermute | solution.py:754
  27.6 0.1 collective-permute-start.7
  27.7 0.0 copy-done.3
  27.8 0.0 collective-permute-done.5.inner.outer
  27.8 0.5 collective-permute-start.2
  28.3 0.1 fusion.3.table.rest_4_
  28.4 0.0 copy-done
  28.4 0.0 copy-start.2
  28.4 5.3 %bulk.3.token.held = f32[5,2,256,1024]{3,2,1,0:T(8,128)} custom-call(f32[5,2,256,1024]{3,2,1,0:T(8,128)} %state.15, f32[10,1024]{1,0:T(8,128)S(1)} %collective-permute-done.rest_1_.low, f32[10,1024]{1,0:T(8,128)S(1)} %collective-permute-done.1.rest_2_.high, f32[5,48,1024]{2,1,0:T(8,128)S(1)} %collective-permute-done.5.inner.outer, ...), custom_call_target="tpu_custom_call" | custom-call | flops 29491200 | bytes 4915200 | tf_op jit(solution)/shard_map/bulk/pallas_call | solution.py:575
  33.8 0.0 collective-permute-done.2.inner
  33.8 0.7 collective-permute-done.3.outer
  34.4 0.1 broadcast_in_dim.51.factor.rest_0_
  34.5 0.0 copy-done.2
  34.5 5.8 %near.1 = (f32[10,16,1024]{2,1,0:T(8,128)S(1)}, f32[10,16,1024]{2,1,0:T(8,128)S(1)}, f32[16,128]{1,0:T(8,128)S(1)}, f32[5,48,1024]{2,1,0:T(8,128)S(1)}) custom-call(f32[5,2,256,1024]{3,2,1,0:T(8,128)} %state.15, f32[5,2,256,1024]{3,2,1,0:T(8,128)} %state.15, f32[10,1024]{1,0:T(8,128)S(1)} %collective-permute-done.rest_1_.low, ...), custom_call_target="tpu_custom_call" | custom-call | flops 32768000 | bytes 40960000 | tf_op jit(solution)/shard_map/near/pallas_call | solution.py:641
  40.3 3.6 %collective-permute-start.6 = (f32[5,48,1024]{2,1,0:T(8,128)S(1)}, f32[5,48,1024]{2,1,0:T(8,128)S(1)}, u32[]{:S(2)}, u32[]{:S(2)}) collective-permute-start(f32[5,48,1024]{2,1,0:T(8,128)S(1)} %get-tuple-element.25), channel_id=1, source_target_pairs={{1,2},{2,1},{5,6},{6,5},{9,10},{10,9},{13,14},{14,13},{17,18},{18,... | collective-permute-start | bytes 2949128 | tf_op jit(solution)/shard_map/ppermute | solution.py:777
  44.0 1.3 %collective-permute-start.10 = (f32[16,128]{1,0:T(8,128)S(1)}, f32[16,128]{1,0:T(8,128)S(1)}, u32[]{:S(2)}, u32[]{:S(2)}) collective-permute-start(f32[16,128]{1,0:T(8,128)S(1)} %get-tuple-element.27.token), channel_id=1, source_target_pairs={{0,16},{16,0},{1,17},{17,1},{2,18},{18,2},{3,19},{19,3},{4,20},{20... | collective-permute-start | bytes 24584 | tf_op jit(solution)/shard_map/ppermute | solution.py:712
  45.2 0.0 collective-permute-done.9.inner
  45.2 8.6 %bulk.4.held = f32[5,2,256,1024]{3,2,1,0:T(8,128)} custom-call(f32[5,2,256,1024]{3,2,1,0:T(8,128)} %state.15, f32[10,1024]{1,0:T(8,128)S(1)} %collective-permute-done.rest_1_.low, f32[10,1024]{1,0:T(8,128)S(1)} %collective-permute-done.1.rest_2_.high, f32[5,96,1024]{2,1,0:T(8,128)S(1)} %collective-permute-done.9.inner, ...), custom_call_target="tpu_custom_call", output_to_operand_aliasing={{}: (7, {})} | custom-call | flops 58982400 | bytes 9830400 | tf_op jit(solution)/shard_map/bulk/pallas_call | solution.py:575
  53.8 0.0 collective-permute-done.10
  53.8 0.1 add_multiply_fusion.rest_3_
  53.9 1.6 %collective-permute-done.8.outer = f32[5,96,1024]{2,1,0:T(8,128)S(1)} collective-permute-done((f32[5,96,1024]{2,1,0:T(8,128)S(1)}, f32[5,96,1024]{2,1,0:T(8,128)S(1)}, u32[]{:S(2)}, u32[]{:S(2)}) %collective-permute-start.8) | collective-permute-done | bytes 1966112 | tf_op jit(solution)/shard_map/ppermute | solution.py:754
  55.5 0.0 collective-permute-done.7.inner
  55.5 8.7 %bulk.5.held = f32[5,2,256,1024]{3,2,1,0:T(8,128)} custom-call(f32[5,2,256,1024]{3,2,1,0:T(8,128)} %state.15, f32[10,1024]{1,0:T(8,128)S(1)} %collective-permute-done.rest_1_.low, f32[10,1024]{1,0:T(8,128)S(1)} %collective-permute-done.1.rest_2_.high, f32[5,96,1024]{2,1,0:T(8,128)S(1)} %collective-permute-done.7.inner, ...), custom_call_target="tpu_custom_call", output_to_operand_aliasing={{}: (7, {})} | custom-call | flops 58982400 | bytes 9830400 | tf_op jit(solution)/shard_map/bulk/pallas_call | solution.py:575
  64.3 1.8 %collective-permute-done.6.outer = f32[5,48,1024]{2,1,0:T(8,128)S(1)} collective-permute-done((f32[5,48,1024]{2,1,0:T(8,128)S(1)}, f32[5,48,1024]{2,1,0:T(8,128)S(1)}, u32[]{:S(2)}, u32[]{:S(2)}) %collective-permute-start.6) | collective-permute-done | bytes 983072 | tf_op jit(solution)/shard_map/ppermute | solution.py:777
  66.0 2.1 %add_outer.1 = f32[5,2,256,1024]{3,2,1,0:T(8,128)} custom-call(f32[5,48,1024]{2,1,0:T(8,128)S(1)} %collective-permute-done.6.outer, f32[5,2,256,1024]{3,2,1,0:T(8,128)} %bulk.5.held), custom_call_target="tpu_custom_call", output_to_operand_aliasing={{}: (1, {})} | custom-call | flops 1474560 | bytes 3932160 | tf_op jit(solution)/shard_map/add_outer/pallas_call | solution.py:612
  (5 shorter events, 0.1 us)
Async XLA Ops:
  4.1 30.3 %collective-permute-start.3 = (f32[5,112,1024]{2,1,0:T(8,128)S(1)}, f32[5,112,1024]{2,1,0:T(8,128)S(1)}, u32[]{:S(2)}, u32[]{:S(2)}) collective-permute-start(f32[5,112,1024]{2,1,0:T(8,128)S(1)} %get-tuple-element.21), channel_id=1, source_target_pairs={{1,2},{2,1},{5,6},{6,5},{9,10},{10,9},{13,14},{14,13},{17,18},{18,... | collective-permute-start | bytes 6881288 | tf_op jit(solution)/shard_map/ppermute | solution.py:736
  8.6 8.4 %collective-permute-start = (f32[10,1024]{1,0:T(8,128)S(1)}, f32[10,1024]{1,0:T(8,128)S(1)}, u32[]{:S(2)}, u32[]{:S(2)}) collective-permute-start(f32[10,1024]{1,0:T(8,128)S(1)} %get-tuple-element.18), channel_id=1, source_target_pairs={{0,4},{4,8},{8,12},{1,5},{5,9},{9,13},{2,6},{6,10},{10,14},{3,7},{... | collective-permute-start | bytes 122888 | tf_op jit(solution)/shard_map/ppermute | solution.py:738
  11.8 5.3 %collective-permute-start.1 = (f32[10,1024]{1,0:T(8,128)S(1)}, f32[10,1024]{1,0:T(8,128)S(1)}, u32[]{:S(2)}, u32[]{:S(2)}) collective-permute-start(f32[10,1024]{1,0:T(8,128)S(1)} %get-tuple-element.19.token), channel_id=1, source_target_pairs={{4,0},{8,4},{12,8},{5,1},{9,5},{13,9},{6,2},{10,6},{14,10},{7,3},{... | collective-permute-start | bytes 122888 | tf_op jit(solution)/shard_map/ppermute | solution.py:739
  15.7 4.8 %collective-permute-start.4 = (f32[256,128]{1,0:T(8,128)S(1)}, f32[256,128]{1,0:T(8,128)S(1)}, u32[]{:S(2)}, u32[]{:S(2)}) collective-permute-start(f32[256,128]{1,0:T(8,128)S(1)} %get-tuple-element.22.rest_0_), channel_id=1, source_target_pairs={{0,16},{16,0},{1,17},{17,1},{2,18},{18,2},{3,19},{19,3},{4,20},{20... | collective-permute-start | bytes 393224 | tf_op jit(solution)/shard_map/ppermute | solution.py:712
  20.4 0.9 %copy-start.1 = (f32[5,48,1024]{2,1,0:T(8,128)}, f32[5,48,1024]{2,1,0:T(8,128)S(1)}, u32[]{:S(2)}) copy-start(f32[5,48,1024]{2,1,0:T(8,128)S(1)} %get-tuple-element.23.rest_0_) | copy-start | bytes 2949124
  20.4 7.2 %copy-start.3 = (s32[16]{0:T(128)S(1)}, s32[16]{0:T(128)}, u32[]{:S(2)}) copy-start(s32[16]{0:T(128)} %param.4) | copy-start | bytes 196
  20.5 7.3 %collective-permute-start.5 = (f32[5,48,1024]{2,1,0:T(8,128)S(1)}, f32[5,48,1024]{2,1,0:T(8,128)S(1)}, u32[]{:S(2)}, u32[]{:S(2)}) collective-permute-start(f32[5,48,1024]{2,1,0:T(8,128)S(1)} %get-tuple-element.23.rest_0_), channel_id=1, source_target_pairs={{0,1},{1,0},{2,3},{3,2},{4,5},{5,4},{6,7},{7,6},{8,9},{9,8},{10,11... | collective-permute-start | bytes 2949128 | tf_op jit(solution)/shard_map/ppermute | solution.py:756
  24.4 4.0 %copy-start = (f32[5,96,1024]{2,1,0:T(8,128)}, f32[5,96,1024]{2,1,0:T(8,128)S(1)}, u32[]{:S(2)}) copy-start(f32[5,96,1024]{2,1,0:T(8,128)S(1)} %get-tuple-element.24.token) | copy-start | bytes 5898244
  24.5 20.8 %collective-permute-start.9 = (f32[5,96,1024]{2,1,0:T(8,128)S(1)}, f32[5,96,1024]{2,1,0:T(8,128)S(1)}, u32[]{:S(2)}, u32[]{:S(2)}) collective-permute-start(f32[5,96,1024]{2,1,0:T(8,128)S(1)} %get-tuple-element.28), channel_id=1, source_target_pairs={{0,1},{1,0},{2,3},{3,2},{4,5},{5,4},{6,7},{7,6},{8,9},{9,8},{10,11... | collective-permute-start | bytes 5898248 | tf_op jit(solution)/shard_map/ppermute | solution.py:756
  24.5 31.0 %collective-permute-start.8 = (f32[5,96,1024]{2,1,0:T(8,128)S(1)}, f32[5,96,1024]{2,1,0:T(8,128)S(1)}, u32[]{:S(2)}, u32[]{:S(2)}) collective-permute-start(f32[5,96,1024]{2,1,0:T(8,128)S(1)} %get-tuple-element.26), channel_id=1, source_target_pairs={{1,2},{2,1},{5,6},{6,5},{9,10},{10,9},{13,14},{14,13},{17,18},{18,... | collective-permute-start | bytes 5898248 | tf_op jit(solution)/shard_map/ppermute | solution.py:754
  27.6 27.9 %collective-permute-start.7 = (f32[5,96,1024]{2,1,0:T(8,128)S(1)}, f32[5,96,1024]{2,1,0:T(8,128)S(1)}, u32[]{:S(2)}, u32[]{:S(2)}) collective-permute-start(f32[5,96,1024]{2,1,0:T(8,128)S(1)} %get-tuple-element.24.token), channel_id=1, source_target_pairs={{0,1},{1,0},{2,3},{3,2},{4,5},{5,4},{6,7},{7,6},{8,9},{9,8},{10,11... | collective-permute-start | bytes 5898248 | tf_op jit(solution)/shard_map/ppermute | solution.py:756
  27.8 6.0 %collective-permute-start.2 = (f32[5,16,1024]{2,1,0:T(8,128)S(1)}, f32[5,16,1024]{2,1,0:T(8,128)S(1)}, u32[]{:S(2)}, u32[]{:S(2)}) collective-permute-start(f32[5,16,1024]{2,1,0:T(8,128)S(1)} %get-tuple-element.20), channel_id=1, source_target_pairs={{0,1},{1,0},{2,3},{3,2},{4,5},{5,4},{6,7},{7,6},{8,9},{9,8},{10,11... | collective-permute-start | bytes 983048 | tf_op jit(solution)/shard_map/ppermute | solution.py:740
  28.4 6.1 %copy-start.2 = (bf16[384,640]{1,0:T(8,128)(2,1)S(1)}, bf16[384,640]{1,0:T(8,128)(2,1)}, u32[]{:S(2)}) copy-start(bf16[384,640]{1,0:T(8,128)(2,1)} %constant.30.clone.solve) | copy-start | bytes 1474564
  40.3 25.7 %collective-permute-start.6 = (f32[5,48,1024]{2,1,0:T(8,128)S(1)}, f32[5,48,1024]{2,1,0:T(8,128)S(1)}, u32[]{:S(2)}, u32[]{:S(2)}) collective-permute-start(f32[5,48,1024]{2,1,0:T(8,128)S(1)} %get-tuple-element.25), channel_id=1, source_target_pairs={{1,2},{2,1},{5,6},{6,5},{9,10},{10,9},{13,14},{14,13},{17,18},{18,... | collective-permute-start | bytes 2949128 | tf_op jit(solution)/shard_map/ppermute | solution.py:777
  44.0 9.8 %collective-permute-start.10 = (f32[16,128]{1,0:T(8,128)S(1)}, f32[16,128]{1,0:T(8,128)S(1)}, u32[]{:S(2)}, u32[]{:S(2)}) collective-permute-start(f32[16,128]{1,0:T(8,128)S(1)} %get-tuple-element.27.token), channel_id=1, source_target_pairs={{0,16},{16,0},{1,17},{17,1},{2,18},{18,2},{3,19},{19,3},{4,20},{20... | collective-permute-start | bytes 24584 | tf_op jit(solution)/shard_map/ppermute | solution.py:712

commit v16 on v14

--- a/solution.py
+++ b/solution.py
@@ -19,6 +19,7 @@
 FIELDS = 5
 PLANES = 2
 LINES = FIELDS * PLANES
+GROUPS = (slice(0, 3), slice(3, FIELDS))
 EIGHT = 8
 LANES = 128
 VMEM_LIMIT = 28 * 1024 * 1024
@@ -391,7 +392,7 @@
 def stream(pieces, sems):
     steps = []
     for source, stage, target in pieces:
-        for f in range(FIELDS):
+        for f in GROUPS:
             k = 2 * len(steps)
             come = pltpu.make_async_copy(source.at[f], stage.at[f], sems.at[k])
             leave = pltpu.make_async_copy(stage.at[f], target.at[f], sems.at[k + 1])
@@ -506,7 +507,7 @@
             rows,
             rows,
             pltpu.SemaphoreType.DMA((2,)),
-            pltpu.SemaphoreType.DMA((2 * fields,)),
+            pltpu.SemaphoreType.DMA((2 * len(GROUPS),)),
         ],
         compiler_params=PARAMS,
         cost_estimate=cost(0, fields * count * cells * 8),
@@ -543,7 +544,7 @@
         out_shape=shapes,
         scratch_shapes=[
             *[pltpu.VMEM(x.shape, jnp.float32) for x in shapes],
-            pltpu.SemaphoreType.DMA((2 * fields * len(parts),)),
+            pltpu.SemaphoreType.DMA((2 * len(GROUPS) * len(parts),)),
         ],
         compiler_params=PARAMS,
         cost_estimate=cost(0, sum(math.prod(x.shape) for x in shapes) * 8),
@@ -556,11 +557,16 @@
     return [pltpu.VMEM((*shape, n, LANES), jnp.float32) for n in (rows + 2 * EIGHT, rows)]
 
 
+def block_rows(span):
+    count = span[1] - span[0]
+    return 32 if count % 32 == 0 else 24 if count % 24 == 0 else 16
+
+
 def bulk(counts, state, low, high, inner, edge, dtheta, outer, span, token, held, near_parts=()):
     fields, planes, total_rows, cells = state.shape
     first, end = span
     count = end - first
-    rows = 32 if count % 32 == 0 else 24 if count % 24 == 0 else 16
+    rows = block_rows(span)
     blocks = count // rows
     size = fields * planes * count * cells
     aliases = {} if held is None else {7: 0}
@@ -782,7 +788,7 @@
     for k in range(passes):
         near_parts = (factor, rhs, local, carry, table) if k == passes - 1 else ()
         out = pass_over(k, ends, out, near_parts=near_parts)
-    return add_outer(counts, outer[2], spans[2], size, out) if count > 2 else out
+    return add_outer(counts, outer[2], spans[2], block_rows(spans[2]), out) if count > 2 else out
 
 
 def solution(mesh):

time: 67 us -> 66.6 us (level)
  Pallas kernels: 42 us -> 39.4 us
  waiting for transfers between devices: 4.2 us -> 6.76 us
    ppermute x1, waiting for transfers between devices: 0.66 us -> 2.84 us  [body(): outer = [lax.ppermute(part, 'ax', outer_pairs)]]
    pallas_call x2, Pallas kernels: 6.34 us -> 4.17 us  [pack_rest(): pl.pallas_call(functools.partial(pack_rest_kernel, parts, len(tokens)), i...]
  transfers between devices with their start and end apart: 11 -> 11, of which waited for: 4 -> 5; matrix products, arithmetic and copies ran while one was open for 0% -> 0% of each run, Pallas kernels for 56% -> 53%
where the time goes in v16:
time: 66.6 us; the launch traced here: 66.2 us
  Pallas kernels  39.4 us (59%)
  starting transfers between devices  19.1 us (29%)
  waiting for transfers between devices  6.76 us (10%)
    pallas_call x3, Pallas kernels, bulk(): pl.pallas_call(functools.partial(bulk_kernel, dtheta, rows, span, total_r...  22.6 us
    pallas_call x1, Pallas kernels, near(): pl.pallas_call(functools.partial(near_kernel, dtheta, rows, part[0] if pa...  5.77 us
    ppermute x1, starting transfers between devices, body(): outer = [lax.ppermute(part, 'ax', outer_pairs)]  4.51 us
    pallas_call x2, Pallas kernels, pack_rest(): pl.pallas_call(functools.partial(pack_rest_kernel, parts, len(tokens)), i...  4.17 us
    ppermute x1, starting transfers between devices, body(): outer.append(lax.ppermute(part, 'ax', outer_pairs))  3.67 us
    ppermute x1, starting transfers between devices, body(): low = lax.ppermute(low, 'rad', up)  3.2 us
    ppermute x1, starting transfers between devices, body(): outer.append(lax.ppermute(value, 'ax', outer_pairs))  3.06 us
    ppermute x1, waiting for transfers between devices, body(): outer = [lax.ppermute(part, 'ax', outer_pairs)]  2.84 us
  transfers between devices with their start and end apart: 11, of which 5 were waited for; matrix products, arithmetic and copies ran while one was open for 0% of the time, Pallas kernels for 53%

profile of v16, /device:TPU:1, one launch (start us, length us, event | category | flops | bytes accessed | tf_op | source)
XLA Modules:
  0.0 66.2 jit_solution(14111890619950734112)
XLA Ops:
  0.0 2.1 %pack_first.1 = (f32[5,112,1024]{2,1,0:T(8,128)S(1)}, f32[10,1024]{1,0:T(8,128)S(1)}, f32[10,1024]{1,0:T(8,128)S(1)}) custom-call(f32[5,2,256,1024]{3,2,1,0:T(8,128)} %state.15), custom_call_target="tpu_custom_call" | custom-call | bytes 4587520 | tf_op jit(solution)/shard_map/pack_first/pallas_call | solution.py:500
  2.1 4.5 %collective-permute-start.3 = (f32[5,112,1024]{2,1,0:T(8,128)S(1)}, f32[5,112,1024]{2,1,0:T(8,128)S(1)}, u32[]{:S(2)}, u32[]{:S(2)}) collective-permute-start(f32[5,112,1024]{2,1,0:T(8,128)S(1)} %get-tuple-element.21), channel_id=1, source_target_pairs={{1,2},{2,1},{5,6},{6,5},{9,10},{10,9},{13,14},{14,13},{17,18},{18,... | collective-permute-start | bytes 6881288 | tf_op jit(solution)/shard_map/ppermute | solution.py:739
  6.6 3.2 %collective-permute-start = (f32[10,1024]{1,0:T(8,128)S(1)}, f32[10,1024]{1,0:T(8,128)S(1)}, u32[]{:S(2)}, u32[]{:S(2)}) collective-permute-start(f32[10,1024]{1,0:T(8,128)S(1)} %get-tuple-element.18), channel_id=1, source_target_pairs={{0,4},{4,8},{8,12},{1,5},{5,9},{9,13},{2,6},{6,10},{10,14},{3,7},{... | collective-permute-start | bytes 122888 | tf_op jit(solution)/shard_map/ppermute | solution.py:741
  9.8 1.3 %collective-permute-start.1 = (f32[10,1024]{1,0:T(8,128)S(1)}, f32[10,1024]{1,0:T(8,128)S(1)}, u32[]{:S(2)}, u32[]{:S(2)}) collective-permute-start(f32[10,1024]{1,0:T(8,128)S(1)} %get-tuple-element.19.token), channel_id=1, source_target_pairs={{4,0},{8,4},{12,8},{5,1},{9,5},{13,9},{6,2},{10,6},{14,10},{7,3},{... | collective-permute-start | bytes 122888 | tf_op jit(solution)/shard_map/ppermute | solution.py:742
  11.1 2.6 %pack_edges.1 = (f32[256,128]{1,0:T(8,128)S(1)}, f32[5,16,1024]{2,1,0:T(8,128)S(1)}) custom-call(f32[5,2,256,1024]{3,2,1,0:T(8,128)} %state.15, f32[10,1024]{1,0:T(8,128)S(1)} %get-tuple-element.19.token), custom_call_target="tpu_custom_call" | custom-call | bytes 5242880 | tf_op jit(solution)/shard_map/pack_edges/pallas_call | solution.py:522
  13.7 1.3 %collective-permute-start.4 = (f32[256,128]{1,0:T(8,128)S(1)}, f32[256,128]{1,0:T(8,128)S(1)}, u32[]{:S(2)}, u32[]{:S(2)}) collective-permute-start(f32[256,128]{1,0:T(8,128)S(1)} %get-tuple-element.22.rest_0_), channel_id=1, source_target_pairs={{0,16},{16,0},{1,17},{17,1},{2,18},{18,2},{3,19},{19,3},{4,20},{20... | collective-permute-start | bytes 393224 | tf_op jit(solution)/shard_map/ppermute | solution.py:715
  15.0 0.0 collective-permute-done.rest_1_.low
  15.0 0.1 collective-permute-done.1.rest_2_.high
  15.1 1.9 %pack_rest.2 = (f32[5,48,1024]{2,1,0:T(8,128)S(1)}, f32[5,96,1024]{2,1,0:T(8,128)S(1)}) custom-call(f32[5,2,256,1024]{3,2,1,0:T(8,128)} %state.15, f32[256,128]{1,0:T(8,128)S(1)} %get-tuple-element.22.rest_0_, f32[10,1024]{1,0:T(8,128)S(1)} %collective-permute-done.rest_1_.low, f32[10,1024]{1,0:T(8,128)S(1)} %collective-permute-done.1.rest_2_.high), custom_call_target="tpu_custom_call" | custom-call | bytes 5898240 | tf_op jit(solution)/shard_map/pack_rest/pallas_call | solution.py:540
  17.1 0.0 copy-start.1
  17.1 0.0 copy-start.3
  17.1 0.1 collective-permute-start.5
  17.2 0.4 collective-permute-done.4.rest_1_.edge
  17.6 0.5 copy-done.1
  18.0 2.2 %pack_rest.3 = (f32[5,96,1024]{2,1,0:T(8,128)S(1)}, f32[5,96,1024]{2,1,0:T(8,128)S(1)}) custom-call(f32[5,2,256,1024]{3,2,1,0:T(8,128)} %state.15, f32[5,48,1024]{2,1,0:T(8,128)} %copy-done.1, f32[256,128]{1,0:T(8,128)S(1)} %collective-permute-done.4.rest_1_.edge), custom_call_target="tpu_custom_call" | custom-call | bytes 7864320 | tf_op jit(solution)/shard_map/pack_rest/pallas_call | solution.py:540
  20.3 0.0 copy-start
  20.3 0.1 collective-permute-start.9
  20.4 3.1 %collective-permute-start.8 = (f32[5,96,1024]{2,1,0:T(8,128)S(1)}, f32[5,96,1024]{2,1,0:T(8,128)S(1)}, u32[]{:S(2)}, u32[]{:S(2)}) collective-permute-start(f32[5,96,1024]{2,1,0:T(8,128)S(1)} %get-tuple-element.26), channel_id=1, source_target_pairs={{1,2},{2,1},{5,6},{6,5},{9,10},{10,9},{13,14},{14,13},{17,18},{18,... | collective-permute-start | bytes 5898248 | tf_op jit(solution)/shard_map/ppermute | solution.py:757
  23.4 0.1 collective-permute-start.7
  23.5 0.0 copy-done.3
  23.6 0.0 collective-permute-done.5.inner.outer
  23.6 0.5 collective-permute-start.2
  24.1 0.1 fusion.3.table.rest_4_
  24.2 0.0 copy-done
  24.2 0.0 copy-start.2
  24.3 5.3 %bulk.3.token.held = f32[5,2,256,1024]{3,2,1,0:T(8,128)} custom-call(f32[5,2,256,1024]{3,2,1,0:T(8,128)} %state.15, f32[10,1024]{1,0:T(8,128)S(1)} %collective-permute-done.rest_1_.low, f32[10,1024]{1,0:T(8,128)S(1)} %collective-permute-done.1.rest_2_.high, f32[5,48,1024]{2,1,0:T(8,128)S(1)} %collective-permute-done.5.inner.outer, ...), custom_call_target="tpu_custom_call" | custom-call | flops 29491200 | bytes 4915200 | tf_op jit(solution)/shard_map/bulk/pallas_call | solution.py:578
  29.6 0.0 collective-permute-done.2.inner
  29.6 2.8 %collective-permute-done.3.outer = f32[5,112,1024]{2,1,0:T(8,128)S(1)} collective-permute-done((f32[5,112,1024]{2,1,0:T(8,128)S(1)}, f32[5,112,1024]{2,1,0:T(8,128)S(1)}, u32[]{:S(2)}, u32[]{:S(2)}) %collective-permute-start.3) | collective-permute-done | bytes 2293792 | tf_op jit(solution)/shard_map/ppermute | solution.py:739
  32.4 0.1 broadcast_in_dim.51.factor.rest_0_
  32.5 0.0 copy-done.2
  32.5 5.8 %near.1 = (f32[10,16,1024]{2,1,0:T(8,128)S(1)}, f32[10,16,1024]{2,1,0:T(8,128)S(1)}, f32[16,128]{1,0:T(8,128)S(1)}, f32[5,48,1024]{2,1,0:T(8,128)S(1)}) custom-call(f32[5,2,256,1024]{3,2,1,0:T(8,128)} %state.15, f32[5,2,256,1024]{3,2,1,0:T(8,128)} %state.15, f32[10,1024]{1,0:T(8,128)S(1)} %collective-permute-done.rest_1_.low, ...), custom_call_target="tpu_custom_call" | custom-call | flops 32768000 | bytes 40960000 | tf_op jit(solution)/shard_map/near/pallas_call | solution.py:644
  38.3 3.7 %collective-permute-start.6 = (f32[5,48,1024]{2,1,0:T(8,128)S(1)}, f32[5,48,1024]{2,1,0:T(8,128)S(1)}, u32[]{:S(2)}, u32[]{:S(2)}) collective-permute-start(f32[5,48,1024]{2,1,0:T(8,128)S(1)} %get-tuple-element.25), channel_id=1, source_target_pairs={{1,2},{2,1},{5,6},{6,5},{9,10},{10,9},{13,14},{14,13},{17,18},{18,... | collective-permute-start | bytes 2949128 | tf_op jit(solution)/shard_map/ppermute | solution.py:780
  42.0 1.3 %collective-permute-start.10 = (f32[16,128]{1,0:T(8,128)S(1)}, f32[16,128]{1,0:T(8,128)S(1)}, u32[]{:S(2)}, u32[]{:S(2)}) collective-permute-start(f32[16,128]{1,0:T(8,128)S(1)} %get-tuple-element.27.token), channel_id=1, source_target_pairs={{0,16},{16,0},{1,17},{17,1},{2,18},{18,2},{3,19},{19,3},{4,20},{20... | collective-permute-start | bytes 24584 | tf_op jit(solution)/shard_map/ppermute | solution.py:715
  43.2 0.0 collective-permute-done.9.inner
  43.2 8.6 %bulk.4.held = f32[5,2,256,1024]{3,2,1,0:T(8,128)} custom-call(f32[5,2,256,1024]{3,2,1,0:T(8,128)} %state.15, f32[10,1024]{1,0:T(8,128)S(1)} %collective-permute-done.rest_1_.low, f32[10,1024]{1,0:T(8,128)S(1)} %collective-permute-done.1.rest_2_.high, f32[5,96,1024]{2,1,0:T(8,128)S(1)} %collective-permute-done.9.inner, ...), custom_call_target="tpu_custom_call", output_to_operand_aliasing={{}: (7, {})} | custom-call | flops 58982400 | bytes 9830400 | tf_op jit(solution)/shard_map/bulk/pallas_call | solution.py:578
  51.8 0.0 collective-permute-done.10
  51.8 0.1 add_multiply_fusion.rest_3_
  51.9 1.6 %collective-permute-done.8.outer = f32[5,96,1024]{2,1,0:T(8,128)S(1)} collective-permute-done((f32[5,96,1024]{2,1,0:T(8,128)S(1)}, f32[5,96,1024]{2,1,0:T(8,128)S(1)}, u32[]{:S(2)}, u32[]{:S(2)}) %collective-permute-start.8) | collective-permute-done | bytes 1966112 | tf_op jit(solution)/shard_map/ppermute | solution.py:757
  53.5 0.0 collective-permute-done.7.inner
  53.5 8.7 %bulk.5.held = f32[5,2,256,1024]{3,2,1,0:T(8,128)} custom-call(f32[5,2,256,1024]{3,2,1,0:T(8,128)} %state.15, f32[10,1024]{1,0:T(8,128)S(1)} %collective-permute-done.rest_1_.low, f32[10,1024]{1,0:T(8,128)S(1)} %collective-permute-done.1.rest_2_.high, f32[5,96,1024]{2,1,0:T(8,128)S(1)} %collective-permute-done.7.inner, ...), custom_call_target="tpu_custom_call", output_to_operand_aliasing={{}: (7, {})} | custom-call | flops 58982400 | bytes 9830400 | tf_op jit(solution)/shard_map/bulk/pallas_call | solution.py:578
  62.3 1.8 %collective-permute-done.6.outer = f32[5,48,1024]{2,1,0:T(8,128)S(1)} collective-permute-done((f32[5,48,1024]{2,1,0:T(8,128)S(1)}, f32[5,48,1024]{2,1,0:T(8,128)S(1)}, u32[]{:S(2)}, u32[]{:S(2)}) %collective-permute-start.6) | collective-permute-done | bytes 983072 | tf_op jit(solution)/shard_map/ppermute | solution.py:780
  64.0 2.2 %add_outer.1 = f32[5,2,256,1024]{3,2,1,0:T(8,128)} custom-call(f32[5,48,1024]{2,1,0:T(8,128)S(1)} %collective-permute-done.6.outer, f32[5,2,256,1024]{3,2,1,0:T(8,128)} %bulk.5.held), custom_call_target="tpu_custom_call", output_to_operand_aliasing={{}: (1, {})} | custom-call | flops 1474560 | bytes 3932160 | tf_op jit(solution)/shard_map/add_outer/pallas_call | solution.py:615
  (5 shorter events, 0.1 us)
Async XLA Ops:
  2.1 30.3 %collective-permute-start.3 = (f32[5,112,1024]{2,1,0:T(8,128)S(1)}, f32[5,112,1024]{2,1,0:T(8,128)S(1)}, u32[]{:S(2)}, u32[]{:S(2)}) collective-permute-start(f32[5,112,1024]{2,1,0:T(8,128)S(1)} %get-tuple-element.21), channel_id=1, source_target_pairs={{1,2},{2,1},{5,6},{6,5},{9,10},{10,9},{13,14},{14,13},{17,18},{18,... | collective-permute-start | bytes 6881288 | tf_op jit(solution)/shard_map/ppermute | solution.py:739
  6.6 8.4 %collective-permute-start = (f32[10,1024]{1,0:T(8,128)S(1)}, f32[10,1024]{1,0:T(8,128)S(1)}, u32[]{:S(2)}, u32[]{:S(2)}) collective-permute-start(f32[10,1024]{1,0:T(8,128)S(1)} %get-tuple-element.18), channel_id=1, source_target_pairs={{0,4},{4,8},{8,12},{1,5},{5,9},{9,13},{2,6},{6,10},{10,14},{3,7},{... | collective-permute-start | bytes 122888 | tf_op jit(solution)/shard_map/ppermute | solution.py:741
  9.8 5.3 %collective-permute-start.1 = (f32[10,1024]{1,0:T(8,128)S(1)}, f32[10,1024]{1,0:T(8,128)S(1)}, u32[]{:S(2)}, u32[]{:S(2)}) collective-permute-start(f32[10,1024]{1,0:T(8,128)S(1)} %get-tuple-element.19.token), channel_id=1, source_target_pairs={{4,0},{8,4},{12,8},{5,1},{9,5},{13,9},{6,2},{10,6},{14,10},{7,3},{... | collective-permute-start | bytes 122888 | tf_op jit(solution)/shard_map/ppermute | solution.py:742
  13.7 3.9 %collective-permute-start.4 = (f32[256,128]{1,0:T(8,128)S(1)}, f32[256,128]{1,0:T(8,128)S(1)}, u32[]{:S(2)}, u32[]{:S(2)}) collective-permute-start(f32[256,128]{1,0:T(8,128)S(1)} %get-tuple-element.22.rest_0_), channel_id=1, source_target_pairs={{0,16},{16,0},{1,17},{17,1},{2,18},{18,2},{3,19},{19,3},{4,20},{20... | collective-permute-start | bytes 393224 | tf_op jit(solution)/shard_map/ppermute | solution.py:715
  17.1 0.9 %copy-start.1 = (f32[5,48,1024]{2,1,0:T(8,128)}, f32[5,48,1024]{2,1,0:T(8,128)S(1)}, u32[]{:S(2)}) copy-start(f32[5,48,1024]{2,1,0:T(8,128)S(1)} %get-tuple-element.23.rest_0_) | copy-start | bytes 2949124
  17.1 6.4 %copy-start.3 = (s32[16]{0:T(128)S(1)}, s32[16]{0:T(128)}, u32[]{:S(2)}) copy-start(s32[16]{0:T(128)} %param.4) | copy-start | bytes 196
  17.1 6.5 %collective-permute-start.5 = (f32[5,48,1024]{2,1,0:T(8,128)S(1)}, f32[5,48,1024]{2,1,0:T(8,128)S(1)}, u32[]{:S(2)}, u32[]{:S(2)}) collective-permute-start(f32[5,48,1024]{2,1,0:T(8,128)S(1)} %get-tuple-element.23.rest_0_), channel_id=1, source_target_pairs={{0,1},{1,0},{2,3},{3,2},{4,5},{5,4},{6,7},{7,6},{8,9},{9,8},{10,11... | collective-permute-start | bytes 2949128 | tf_op jit(solution)/shard_map/ppermute | solution.py:759
  20.3 4.0 %copy-start = (f32[5,96,1024]{2,1,0:T(8,128)}, f32[5,96,1024]{2,1,0:T(8,128)S(1)}, u32[]{:S(2)}) copy-start(f32[5,96,1024]{2,1,0:T(8,128)S(1)} %get-tuple-element.24.token) | copy-start | bytes 5898244
  20.3 23.0 %collective-permute-start.9 = (f32[5,96,1024]{2,1,0:T(8,128)S(1)}, f32[5,96,1024]{2,1,0:T(8,128)S(1)}, u32[]{:S(2)}, u32[]{:S(2)}) collective-permute-start(f32[5,96,1024]{2,1,0:T(8,128)S(1)} %get-tuple-element.28), channel_id=1, source_target_pairs={{0,1},{1,0},{2,3},{3,2},{4,5},{5,4},{6,7},{7,6},{8,9},{9,8},{10,11... | collective-permute-start | bytes 5898248 | tf_op jit(solution)/shard_map/ppermute | solution.py:759
  20.4 33.1 %collective-permute-start.8 = (f32[5,96,1024]{2,1,0:T(8,128)S(1)}, f32[5,96,1024]{2,1,0:T(8,128)S(1)}, u32[]{:S(2)}, u32[]{:S(2)}) collective-permute-start(f32[5,96,1024]{2,1,0:T(8,128)S(1)} %get-tuple-element.26), channel_id=1, source_target_pairs={{1,2},{2,1},{5,6},{6,5},{9,10},{10,9},{13,14},{14,13},{17,18},{18,... | collective-permute-start | bytes 5898248 | tf_op jit(solution)/shard_map/ppermute | solution.py:757
  23.4 30.1 %collective-permute-start.7 = (f32[5,96,1024]{2,1,0:T(8,128)S(1)}, f32[5,96,1024]{2,1,0:T(8,128)S(1)}, u32[]{:S(2)}, u32[]{:S(2)}) collective-permute-start(f32[5,96,1024]{2,1,0:T(8,128)S(1)} %get-tuple-element.24.token), channel_id=1, source_target_pairs={{0,1},{1,0},{2,3},{3,2},{4,5},{5,4},{6,7},{7,6},{8,9},{9,8},{10,11... | collective-permute-start | bytes 5898248 | tf_op jit(solution)/shard_map/ppermute | solution.py:759
  23.6 6.0 %collective-permute-start.2 = (f32[5,16,1024]{2,1,0:T(8,128)S(1)}, f32[5,16,1024]{2,1,0:T(8,128)S(1)}, u32[]{:S(2)}, u32[]{:S(2)}) collective-permute-start(f32[5,16,1024]{2,1,0:T(8,128)S(1)} %get-tuple-element.20), channel_id=1, source_target_pairs={{0,1},{1,0},{2,3},{3,2},{4,5},{5,4},{6,7},{7,6},{8,9},{9,8},{10,11... | collective-permute-start | bytes 983048 | tf_op jit(solution)/shard_map/ppermute | solution.py:743
  24.2 8.3 %copy-start.2 = (bf16[384,640]{1,0:T(8,128)(2,1)S(1)}, bf16[384,640]{1,0:T(8,128)(2,1)}, u32[]{:S(2)}) copy-start(bf16[384,640]{1,0:T(8,128)(2,1)} %constant.30.clone.solve) | copy-start | bytes 1474564
  38.3 25.7 %collective-permute-start.6 = (f32[5,48,1024]{2,1,0:T(8,128)S(1)}, f32[5,48,1024]{2,1,0:T(8,128)S(1)}, u32[]{:S(2)}, u32[]{:S(2)}) collective-permute-start(f32[5,48,1024]{2,1,0:T(8,128)S(1)} %get-tuple-element.25), channel_id=1, source_target_pairs={{1,2},{2,1},{5,6},{6,5},{9,10},{10,9},{13,14},{14,13},{17,18},{18,... | collective-permute-start | bytes 2949128 | tf_op jit(solution)/shard_map/ppermute | solution.py:780
  42.0 9.8 %collective-permute-start.10 = (f32[16,128]{1,0:T(8,128)S(1)}, f32[16,128]{1,0:T(8,128)S(1)}, u32[]{:S(2)}, u32[]{:S(2)}) collective-permute-start(f32[16,128]{1,0:T(8,128)S(1)} %get-tuple-element.27.token), channel_id=1, source_target_pairs={{0,16},{16,0},{1,17},{17,1},{2,18},{18,2},{3,19},{19,3},{4,20},{20... | collective-permute-start | bytes 24584 | tf_op jit(solution)/shard_map/ppermute | solution.py:715

commit v17 on v16

--- a/solution.py
+++ b/solution.py
@@ -412,18 +412,25 @@
     return forward, finish
 
 
-def pack_first_kernel(count, state, part, low, high, stage, top, bottom, row_sems, sems):
-    _, _, rows, _ = state.shape
+def pack_first_kernel(count, state, part, stage, sems):
     odd = lax.axis_index("ax") % 2
-    forward, finish = stream([(state.at[:, odd, 0:count, :], stage, part)], sems)
+    for step in stream([(state.at[:, odd, 0:count, :], stage, part)], sems):
+        step()
+
+
+def pack_edges_kernel(state, token, edge, side, low, high, left, right, top, bottom, sems):
+    _, _, rows, cells = state.shape
+    odd = lax.axis_index("ax") % 2
     copies = [
-        pltpu.make_async_copy(state.at[:, :, rows - EIGHT : rows, :], top, row_sems.at[0]),
-        pltpu.make_async_copy(state.at[:, :, 0:EIGHT, :], bottom, row_sems.at[1]),
+        pltpu.make_async_copy(state.at[:, :, rows - EIGHT : rows, :], top, sems.at[0]),
+        pltpu.make_async_copy(state.at[:, :, 0:EIGHT, :], bottom, sems.at[1]),
+        pltpu.make_async_copy(state.at[:, :, :, cells - LANES : cells], left, sems.at[2]),
+        pltpu.make_async_copy(state.at[:, :, :, 0:LANES], right, sems.at[3]),
+        pltpu.make_async_copy(state.at[:, 1 - odd, 0:R_NEAR, :], side, sems.at[4]),
     ]
     for copy in copies:
         copy.start()
-    forward()
-    for copy in copies:
+    for copy in copies[:2]:
         copy.wait()
     for f in range(FIELDS):
         for q in range(PLANES):
@@ -431,20 +438,7 @@
             p = plane_of(odd, q)
             low[k : k + 1, :] = top[f, p, EIGHT - 1 : EIGHT, :]
             high[k : k + 1, :] = bottom[f, p, 0:1, :]
-    finish()
-
-
-def pack_edges_kernel(state, token, edge, side, left, right, sems):
-    _, _, rows, cells = state.shape
-    odd = lax.axis_index("ax") % 2
-    copies = [
-        pltpu.make_async_copy(state.at[:, :, :, cells - LANES : cells], left, sems.at[0]),
-        pltpu.make_async_copy(state.at[:, :, :, 0:LANES], right, sems.at[1]),
-        pltpu.make_async_copy(state.at[:, 1 - odd, 0:R_NEAR, :], side, sems.at[2]),
-    ]
-    for copy in copies:
-        copy.start()
-    for copy in copies[:2]:
+    for copy in copies[2:4]:
         copy.wait()
     lane = lax.broadcasted_iota(jnp.int32, (rows, LANES), 1)
     columns = jnp.ones((rows, LANES), jnp.float32)
@@ -454,7 +448,7 @@
             columns = jnp.where(lane == 4 * f + q, left[f, p, :, LANES - 1 : LANES], columns)
             columns = jnp.where(lane == (4 * f - 1 - q) % LANES, right[f, p, :, 0:1], columns)
     edge[...] = columns
-    copies[2].wait()
+    copies[4].wait()
 
 
 def pack_rest_kernel(parts, tokens, state, *rest):
@@ -493,20 +487,14 @@
 
 
 def pack_first(state, count):
-    fields, planes, _, cells = state.shape
-    vmem = pl.BlockSpec(memory_space=pltpu.VMEM)
-    row = jax.ShapeDtypeStruct((LINES, cells), jnp.float32)
-    rows = pltpu.VMEM((fields, planes, EIGHT, cells), jnp.float32)
+    fields, _, _, cells = state.shape
     return pl.pallas_call(
         functools.partial(pack_first_kernel, count),
         in_specs=[ANY],
-        out_specs=[ANY, vmem, vmem],
-        out_shape=[jax.ShapeDtypeStruct((fields, count, cells), jnp.float32), row, row],
+        out_specs=ANY,
+        out_shape=jax.ShapeDtypeStruct((fields, count, cells), jnp.float32),
         scratch_shapes=[
             pltpu.VMEM((fields, count, cells), jnp.float32),
-            rows,
-            rows,
-            pltpu.SemaphoreType.DMA((2,)),
             pltpu.SemaphoreType.DMA((2 * len(GROUPS),)),
         ],
         compiler_params=PARAMS,
@@ -519,19 +507,23 @@
     fields, planes, rows, cells = state.shape
     vmem = pl.BlockSpec(memory_space=pltpu.VMEM)
     tiles = pltpu.VMEM((fields, planes, rows, LANES), jnp.float32)
+    eight = pltpu.VMEM((fields, planes, EIGHT, cells), jnp.float32)
+    row = jax.ShapeDtypeStruct((LINES, cells), jnp.float32)
     return pl.pallas_call(
         pack_edges_kernel,
         in_specs=[ANY, ANY],
-        out_specs=[vmem, vmem],
+        out_specs=[vmem] * 4,
         out_shape=[
             jax.ShapeDtypeStruct((rows, LANES), jnp.float32),
             jax.ShapeDtypeStruct((fields, R_NEAR, cells), jnp.float32),
+            row,
+            row,
         ],
-        scratch_shapes=[tiles, tiles, pltpu.SemaphoreType.DMA((3,))],
+        scratch_shapes=[tiles, tiles, eight, eight, pltpu.SemaphoreType.DMA((5,))],
         compiler_params=PARAMS,
         cost_estimate=cost(0, fields * planes * rows * LANES * 16),
         name="pack_edges",
-    )(in_hbm(state), token)
+    )(in_hbm(state), in_hbm(token))
 
 
 def pack_rest(state, parts, *tokens):
@@ -735,9 +727,9 @@
     size, spans = chunks(rows)
     count = len(spans)
 
-    part, low, high = pack_first(state, spans[0][1])
+    part = pack_first(state, spans[0][1])
     outer = [lax.ppermute(part, "ax", outer_pairs)]
-    columns, side = pack_edges(state, high)
+    columns, side, low, high = pack_edges(state, part)
     low = lax.ppermute(low, "rad", up)
     high = lax.ppermute(high, "rad", down)
     near_inner = lax.ppermute(side, "ax", inner_pairs)
@@ -788,7 +780,7 @@
     for k in range(passes):
         near_parts = (factor, rhs, local, carry, table) if k == passes - 1 else ()
         out = pass_over(k, ends, out, near_parts=near_parts)
-    return add_outer(counts, outer[2], spans[2], block_rows(spans[2]), out) if count > 2 else out
+    return add_outer(counts, outer[2], spans[2], size, out) if count > 2 else out
 
 
 def solution(mesh):

time: 66.6 us -> 66.3 us (level)
  waiting for transfers between devices: 6.76 us -> 5.89 us
    ppermute x1, waiting for transfers between devices: 2.84 us -> 0.04 us  [body(): outer = [lax.ppermute(part, 'ax', outer_pairs)]]
    ppermute x1, waiting for transfers between devices: 0.14 us -> 2.45 us  [body(): high = lax.ppermute(high, 'rad', down)]
  transfers between devices with their start and end apart: 11 -> 11, of which waited for: 5 -> 3; matrix products, arithmetic and copies ran while one was open for 0% -> 0% of each run, Pallas kernels for 53% -> 54%
where the time goes in v17:
time: 66.3 us; the launch traced here: 65.9 us
  Pallas kernels  39.3 us (59%)
  starting transfers between devices  19.3 us (29%)
  waiting for transfers between devices  5.89 us (9%)
  local copies, waits for them, and re-layouts  0.93 us (1%)
    pallas_call x3, Pallas kernels, bulk(): pl.pallas_call(functools.partial(bulk_kernel, dtheta, rows, span, total_r...  22.6 us
    pallas_call x1, Pallas kernels, near(): pl.pallas_call(functools.partial(near_kernel, dtheta, rows, part[0] if pa...  5.75 us
    ppermute x1, starting transfers between devices, body(): outer = [lax.ppermute(part, 'ax', outer_pairs)]  4.51 us
    pallas_call x2, Pallas kernels, pack_rest(): pl.pallas_call(functools.partial(pack_rest_kernel, parts, len(tokens)), i...  4.17 us
    ppermute x1, starting transfers between devices, body(): outer.append(lax.ppermute(part, 'ax', outer_pairs))  3.64 us
    ppermute x1, starting transfers between devices, body(): outer.append(lax.ppermute(value, 'ax', outer_pairs))  3.3 us
    ppermute x1, starting transfers between devices, body(): low = lax.ppermute(low, 'rad', up)  3.2 us
    pallas_call x1, Pallas kernels, pack_edges(): pl.pallas_call(pack_edges_kernel, in_specs=[ANY, ANY], out_specs=[vmem] *...  2.78 us
  transfers between devices with their start and end apart: 11, of which 3 were waited for; matrix products, arithmetic and copies ran while one was open for 0% of the time, Pallas kernels for 54%

profile of v17, /device:TPU:1, one launch (start us, length us, event | category | flops | bytes accessed | tf_op | source)
XLA Modules:
  0.0 65.9 jit_solution(5739038824942785935)
XLA Ops:
  0.0 1.8 %pack_first.1.token = f32[5,112,1024]{2,1,0:T(8,128)S(1)} custom-call(f32[5,2,256,1024]{3,2,1,0:T(8,128)} %state.15), custom_call_target="tpu_custom_call" | custom-call | bytes 4587520 | tf_op jit(solution)/shard_map/pack_first/pallas_call | solution.py:491
  1.9 0.0 copy-start
  1.9 4.5 %collective-permute-start.3 = (f32[5,112,1024]{2,1,0:T(8,128)S(1)}, f32[5,112,1024]{2,1,0:T(8,128)S(1)}, u32[]{:S(2)}, u32[]{:S(2)}) collective-permute-start(f32[5,112,1024]{2,1,0:T(8,128)S(1)} %pack_first.1.token), channel_id=1, source_target_pairs={{1,2},{2,1},{5,6},{6,5},{9,10},{10,9},{13,14},{14,13},{17,18},{18,... | collective-permute-start | bytes 6881288 | tf_op jit(solution)/shard_map/ppermute | solution.py:731
  6.4 0.0 copy-done
  6.4 2.8 %pack_edges.1 = (f32[256,128]{1,0:T(8,128)S(1)}, f32[5,16,1024]{2,1,0:T(8,128)S(1)}, f32[10,1024]{1,0:T(8,128)S(1)}, f32[10,1024]{1,0:T(8,128)S(1)}) custom-call(f32[5,2,256,1024]{3,2,1,0:T(8,128)} %state.15, f32[5,112,1024]{2,1,0:T(8,128)} %copy-done), custom_call_target="tpu_custom_call" | custom-call | bytes 5242880 | tf_op jit(solution)/shard_map/pack_edges/pallas_call | solution.py:512
  9.2 3.2 %collective-permute-start = (f32[10,1024]{1,0:T(8,128)S(1)}, f32[10,1024]{1,0:T(8,128)S(1)}, u32[]{:S(2)}, u32[]{:S(2)}) collective-permute-start(f32[10,1024]{1,0:T(8,128)S(1)} %get-tuple-element.17), channel_id=1, source_target_pairs={{0,4},{4,8},{8,12},{1,5},{5,9},{9,13},{2,6},{6,10},{10,14},{3,7},{... | collective-permute-start | bytes 122888 | tf_op jit(solution)/shard_map/ppermute | solution.py:733
  12.4 1.3 %collective-permute-start.1 = (f32[10,1024]{1,0:T(8,128)S(1)}, f32[10,1024]{1,0:T(8,128)S(1)}, u32[]{:S(2)}, u32[]{:S(2)}) collective-permute-start(f32[10,1024]{1,0:T(8,128)S(1)} %get-tuple-element.18), channel_id=1, source_target_pairs={{4,0},{8,4},{12,8},{5,1},{9,5},{13,9},{6,2},{10,6},{14,10},{7,3},{... | collective-permute-start | bytes 122888 | tf_op jit(solution)/shard_map/ppermute | solution.py:734
  13.7 1.3 %collective-permute-start.4 = (f32[256,128]{1,0:T(8,128)S(1)}, f32[256,128]{1,0:T(8,128)S(1)}, u32[]{:S(2)}, u32[]{:S(2)}) collective-permute-start(f32[256,128]{1,0:T(8,128)S(1)} %get-tuple-element.20.rest_0_), channel_id=1, source_target_pairs={{0,16},{16,0},{1,17},{17,1},{2,18},{18,2},{3,19},{19,3},{4,20},{20... | collective-permute-start | bytes 393224 | tf_op jit(solution)/shard_map/ppermute | solution.py:707
  15.0 0.0 collective-permute-done.rest_1_.low
  15.0 2.5 %collective-permute-done.1.rest_2_.high = f32[10,1024]{1,0:T(8,128)S(1)} collective-permute-done((f32[10,1024]{1,0:T(8,128)S(1)}, f32[10,1024]{1,0:T(8,128)S(1)}, u32[]{:S(2)}, u32[]{:S(2)}) %collective-permute-start.1) | collective-permute-done | bytes 40992 | tf_op jit(solution)/shard_map/ppermute | solution.py:734
  17.5 1.9 %pack_rest.2 = (f32[5,48,1024]{2,1,0:T(8,128)S(1)}, f32[5,96,1024]{2,1,0:T(8,128)S(1)}) custom-call(f32[5,2,256,1024]{3,2,1,0:T(8,128)} %state.15, f32[256,128]{1,0:T(8,128)S(1)} %get-tuple-element.20.rest_0_, f32[10,1024]{1,0:T(8,128)S(1)} %collective-permute-done.rest_1_.low, f32[10,1024]{1,0:T(8,128)S(1)} %collective-permute-done.1.rest_2_.high), custom_call_target="tpu_custom_call" | custom-call | bytes 5898240 | tf_op jit(solution)/shard_map/pack_rest/pallas_call | solution.py:532
  19.4 0.0 copy-start.2
  19.4 0.0 copy-start.4
  19.4 0.1 collective-permute-start.5
  19.5 0.0 collective-permute-done.4.rest_1_.edge
  19.5 0.8 %copy-done.2 = f32[5,48,1024]{2,1,0:T(8,128)} copy-done((f32[5,48,1024]{2,1,0:T(8,128)}, f32[5,48,1024]{2,1,0:T(8,128)S(1)}, u32[]{:S(2)}) %copy-start.2) | copy-done | bytes 983064
  20.3 2.2 %pack_rest.3 = (f32[5,96,1024]{2,1,0:T(8,128)S(1)}, f32[5,96,1024]{2,1,0:T(8,128)S(1)}) custom-call(f32[5,2,256,1024]{3,2,1,0:T(8,128)} %state.15, f32[5,48,1024]{2,1,0:T(8,128)} %copy-done.2, f32[256,128]{1,0:T(8,128)S(1)} %collective-permute-done.4.rest_1_.edge), custom_call_target="tpu_custom_call" | custom-call | bytes 7864320 | tf_op jit(solution)/shard_map/pack_rest/pallas_call | solution.py:532
  22.6 0.0 copy-start.1
  22.6 0.1 collective-permute-start.9
  22.7 3.3 %collective-permute-start.8 = (f32[5,96,1024]{2,1,0:T(8,128)S(1)}, f32[5,96,1024]{2,1,0:T(8,128)S(1)}, u32[]{:S(2)}, u32[]{:S(2)}) collective-permute-start(f32[5,96,1024]{2,1,0:T(8,128)S(1)} %get-tuple-element.24), channel_id=1, source_target_pairs={{1,2},{2,1},{5,6},{6,5},{9,10},{10,9},{13,14},{14,13},{17,18},{18,... | collective-permute-start | bytes 5898248 | tf_op jit(solution)/shard_map/ppermute | solution.py:749
  26.0 0.1 collective-permute-start.7
  26.1 0.0 copy-done.4
  26.2 0.0 collective-permute-done.5.inner.outer
  26.2 0.5 collective-permute-start.2
  26.7 0.1 fusion.3.table.rest_4_
  26.8 0.0 copy-done.1
  26.8 0.0 copy-start.3
  26.8 5.3 %bulk.3.token.held = f32[5,2,256,1024]{3,2,1,0:T(8,128)} custom-call(f32[5,2,256,1024]{3,2,1,0:T(8,128)} %state.15, f32[10,1024]{1,0:T(8,128)S(1)} %collective-permute-done.rest_1_.low, f32[10,1024]{1,0:T(8,128)S(1)} %collective-permute-done.1.rest_2_.high, f32[5,48,1024]{2,1,0:T(8,128)S(1)} %collective-permute-done.5.inner.outer, ...), custom_call_target="tpu_custom_call" | custom-call | flops 29491200 | bytes 4915200 | tf_op jit(solution)/shard_map/bulk/pallas_call | solution.py:570
  32.1 0.0 collective-permute-done.2.inner
  32.2 0.0 collective-permute-done.3.outer
  32.2 0.1 broadcast_in_dim.51.factor.rest_0_
  32.3 0.0 copy-done.3
  32.3 5.7 %near.1 = (f32[10,16,1024]{2,1,0:T(8,128)S(1)}, f32[10,16,1024]{2,1,0:T(8,128)S(1)}, f32[16,128]{1,0:T(8,128)S(1)}, f32[5,48,1024]{2,1,0:T(8,128)S(1)}) custom-call(f32[5,2,256,1024]{3,2,1,0:T(8,128)} %state.15, f32[5,2,256,1024]{3,2,1,0:T(8,128)} %state.15, f32[10,1024]{1,0:T(8,128)S(1)} %collective-permute-done.rest_1_.low, ...), custom_call_target="tpu_custom_call" | custom-call | flops 32768000 | bytes 40960000 | tf_op jit(solution)/shard_map/near/pallas_call | solution.py:636
  38.0 3.6 %collective-permute-start.6 = (f32[5,48,1024]{2,1,0:T(8,128)S(1)}, f32[5,48,1024]{2,1,0:T(8,128)S(1)}, u32[]{:S(2)}, u32[]{:S(2)}) collective-permute-start(f32[5,48,1024]{2,1,0:T(8,128)S(1)} %get-tuple-element.23), channel_id=1, source_target_pairs={{1,2},{2,1},{5,6},{6,5},{9,10},{10,9},{13,14},{14,13},{17,18},{18,... | collective-permute-start | bytes 2949128 | tf_op jit(solution)/shard_map/ppermute | solution.py:772
  41.7 1.3 %collective-permute-start.10 = (f32[16,128]{1,0:T(8,128)S(1)}, f32[16,128]{1,0:T(8,128)S(1)}, u32[]{:S(2)}, u32[]{:S(2)}) collective-permute-start(f32[16,128]{1,0:T(8,128)S(1)} %get-tuple-element.25.token), channel_id=1, source_target_pairs={{0,16},{16,0},{1,17},{17,1},{2,18},{18,2},{3,19},{19,3},{4,20},{20... | collective-permute-start | bytes 24584 | tf_op jit(solution)/shard_map/ppermute | solution.py:707
  43.0 0.0 collective-permute-done.9.inner
  43.0 8.6 %bulk.4.held = f32[5,2,256,1024]{3,2,1,0:T(8,128)} custom-call(f32[5,2,256,1024]{3,2,1,0:T(8,128)} %state.15, f32[10,1024]{1,0:T(8,128)S(1)} %collective-permute-done.rest_1_.low, f32[10,1024]{1,0:T(8,128)S(1)} %collective-permute-done.1.rest_2_.high, f32[5,96,1024]{2,1,0:T(8,128)S(1)} %collective-permute-done.9.inner, ...), custom_call_target="tpu_custom_call", output_to_operand_aliasing={{}: (7, {})} | custom-call | flops 58982400 | bytes 9830400 | tf_op jit(solution)/shard_map/bulk/pallas_call | solution.py:570
  51.6 0.0 collective-permute-done.10
  51.6 0.1 add_multiply_fusion.rest_3_
  51.6 1.6 %collective-permute-done.8.outer = f32[5,96,1024]{2,1,0:T(8,128)S(1)} collective-permute-done((f32[5,96,1024]{2,1,0:T(8,128)S(1)}, f32[5,96,1024]{2,1,0:T(8,128)S(1)}, u32[]{:S(2)}, u32[]{:S(2)}) %collective-permute-start.8) | collective-permute-done | bytes 1966112 | tf_op jit(solution)/shard_map/ppermute | solution.py:749
  53.3 0.0 collective-permute-done.7.inner
  53.3 8.8 %bulk.5.held = f32[5,2,256,1024]{3,2,1,0:T(8,128)} custom-call(f32[5,2,256,1024]{3,2,1,0:T(8,128)} %state.15, f32[10,1024]{1,0:T(8,128)S(1)} %collective-permute-done.rest_1_.low, f32[10,1024]{1,0:T(8,128)S(1)} %collective-permute-done.1.rest_2_.high, f32[5,96,1024]{2,1,0:T(8,128)S(1)} %collective-permute-done.7.inner, ...), custom_call_target="tpu_custom_call", output_to_operand_aliasing={{}: (7, {})} | custom-call | flops 58982400 | bytes 9830400 | tf_op jit(solution)/shard_map/bulk/pallas_call | solution.py:570
  62.0 1.8 %collective-permute-done.6.outer = f32[5,48,1024]{2,1,0:T(8,128)S(1)} collective-permute-done((f32[5,48,1024]{2,1,0:T(8,128)S(1)}, f32[5,48,1024]{2,1,0:T(8,128)S(1)}, u32[]{:S(2)}, u32[]{:S(2)}) %collective-permute-start.6) | collective-permute-done | bytes 983072 | tf_op jit(solution)/shard_map/ppermute | solution.py:772
  63.8 2.1 %add_outer.1 = f32[5,2,256,1024]{3,2,1,0:T(8,128)} custom-call(f32[5,48,1024]{2,1,0:T(8,128)S(1)} %collective-permute-done.6.outer, f32[5,2,256,1024]{3,2,1,0:T(8,128)} %bulk.5.held), custom_call_target="tpu_custom_call", output_to_operand_aliasing={{}: (1, {})} | custom-call | flops 1474560 | bytes 3932160 | tf_op jit(solution)/shard_map/add_outer/pallas_call | solution.py:607
  (5 shorter events, 0.1 us)
Async XLA Ops:
  1.9 4.5 %copy-start = (f32[5,112,1024]{2,1,0:T(8,128)}, f32[5,112,1024]{2,1,0:T(8,128)S(1)}, u32[]{:S(2)}) copy-start(f32[5,112,1024]{2,1,0:T(8,128)S(1)} %pack_first.1.token) | copy-start | bytes 6881284
  1.9 30.3 %collective-permute-start.3 = (f32[5,112,1024]{2,1,0:T(8,128)S(1)}, f32[5,112,1024]{2,1,0:T(8,128)S(1)}, u32[]{:S(2)}, u32[]{:S(2)}) collective-permute-start(f32[5,112,1024]{2,1,0:T(8,128)S(1)} %pack_first.1.token), channel_id=1, source_target_pairs={{1,2},{2,1},{5,6},{6,5},{9,10},{10,9},{13,14},{14,13},{17,18},{18,... | collective-permute-start | bytes 6881288 | tf_op jit(solution)/shard_map/ppermute | solution.py:731
  9.2 5.8 %collective-permute-start = (f32[10,1024]{1,0:T(8,128)S(1)}, f32[10,1024]{1,0:T(8,128)S(1)}, u32[]{:S(2)}, u32[]{:S(2)}) collective-permute-start(f32[10,1024]{1,0:T(8,128)S(1)} %get-tuple-element.17), channel_id=1, source_target_pairs={{0,4},{4,8},{8,12},{1,5},{5,9},{9,13},{2,6},{6,10},{10,14},{3,7},{... | collective-permute-start | bytes 122888 | tf_op jit(solution)/shard_map/ppermute | solution.py:733
  12.4 5.1 %collective-permute-start.1 = (f32[10,1024]{1,0:T(8,128)S(1)}, f32[10,1024]{1,0:T(8,128)S(1)}, u32[]{:S(2)}, u32[]{:S(2)}) collective-permute-start(f32[10,1024]{1,0:T(8,128)S(1)} %get-tuple-element.18), channel_id=1, source_target_pairs={{4,0},{8,4},{12,8},{5,1},{9,5},{13,9},{6,2},{10,6},{14,10},{7,3},{... | collective-permute-start | bytes 122888 | tf_op jit(solution)/shard_map/ppermute | solution.py:734
  13.7 5.8 %collective-permute-start.4 = (f32[256,128]{1,0:T(8,128)S(1)}, f32[256,128]{1,0:T(8,128)S(1)}, u32[]{:S(2)}, u32[]{:S(2)}) collective-permute-start(f32[256,128]{1,0:T(8,128)S(1)} %get-tuple-element.20.rest_0_), channel_id=1, source_target_pairs={{0,16},{16,0},{1,17},{17,1},{2,18},{18,2},{3,19},{19,3},{4,20},{20... | collective-permute-start | bytes 393224 | tf_op jit(solution)/shard_map/ppermute | solution.py:707
  19.4 0.9 %copy-start.2 = (f32[5,48,1024]{2,1,0:T(8,128)}, f32[5,48,1024]{2,1,0:T(8,128)S(1)}, u32[]{:S(2)}) copy-start(f32[5,48,1024]{2,1,0:T(8,128)S(1)} %get-tuple-element.21.rest_0_) | copy-start | bytes 2949124
  19.4 6.6 %copy-start.4 = (s32[16]{0:T(128)S(1)}, s32[16]{0:T(128)}, u32[]{:S(2)}) copy-start(s32[16]{0:T(128)} %param.4) | copy-start | bytes 196
  19.4 6.7 %collective-permute-start.5 = (f32[5,48,1024]{2,1,0:T(8,128)S(1)}, f32[5,48,1024]{2,1,0:T(8,128)S(1)}, u32[]{:S(2)}, u32[]{:S(2)}) collective-permute-start(f32[5,48,1024]{2,1,0:T(8,128)S(1)} %get-tuple-element.21.rest_0_), channel_id=1, source_target_pairs={{0,1},{1,0},{2,3},{3,2},{4,5},{5,4},{6,7},{7,6},{8,9},{9,8},{10,11... | collective-permute-start | bytes 2949128 | tf_op jit(solution)/shard_map/ppermute | solution.py:751
  22.6 4.2 %copy-start.1 = (f32[5,96,1024]{2,1,0:T(8,128)}, f32[5,96,1024]{2,1,0:T(8,128)S(1)}, u32[]{:S(2)}) copy-start(f32[5,96,1024]{2,1,0:T(8,128)S(1)} %get-tuple-element.22.token) | copy-start | bytes 5898244
  22.6 20.4 %collective-permute-start.9 = (f32[5,96,1024]{2,1,0:T(8,128)S(1)}, f32[5,96,1024]{2,1,0:T(8,128)S(1)}, u32[]{:S(2)}, u32[]{:S(2)}) collective-permute-start(f32[5,96,1024]{2,1,0:T(8,128)S(1)} %get-tuple-element.26), channel_id=1, source_target_pairs={{0,1},{1,0},{2,3},{3,2},{4,5},{5,4},{6,7},{7,6},{8,9},{9,8},{10,11... | collective-permute-start | bytes 5898248 | tf_op jit(solution)/shard_map/ppermute | solution.py:751
  22.7 30.6 %collective-permute-start.8 = (f32[5,96,1024]{2,1,0:T(8,128)S(1)}, f32[5,96,1024]{2,1,0:T(8,128)S(1)}, u32[]{:S(2)}, u32[]{:S(2)}) collective-permute-start(f32[5,96,1024]{2,1,0:T(8,128)S(1)} %get-tuple-element.24), channel_id=1, source_target_pairs={{1,2},{2,1},{5,6},{6,5},{9,10},{10,9},{13,14},{14,13},{17,18},{18,... | collective-permute-start | bytes 5898248 | tf_op jit(solution)/shard_map/ppermute | solution.py:749
  26.0 27.3 %collective-permute-start.7 = (f32[5,96,1024]{2,1,0:T(8,128)S(1)}, f32[5,96,1024]{2,1,0:T(8,128)S(1)}, u32[]{:S(2)}, u32[]{:S(2)}) collective-permute-start(f32[5,96,1024]{2,1,0:T(8,128)S(1)} %get-tuple-element.22.token), channel_id=1, source_target_pairs={{0,1},{1,0},{2,3},{3,2},{4,5},{5,4},{6,7},{7,6},{8,9},{9,8},{10,11... | collective-permute-start | bytes 5898248 | tf_op jit(solution)/shard_map/ppermute | solution.py:751
  26.2 6.0 %collective-permute-start.2 = (f32[5,16,1024]{2,1,0:T(8,128)S(1)}, f32[5,16,1024]{2,1,0:T(8,128)S(1)}, u32[]{:S(2)}, u32[]{:S(2)}) collective-permute-start(f32[5,16,1024]{2,1,0:T(8,128)S(1)} %get-tuple-element.19), channel_id=1, source_target_pairs={{0,1},{1,0},{2,3},{3,2},{4,5},{5,4},{6,7},{7,6},{8,9},{9,8},{10,11... | collective-permute-start | bytes 983048 | tf_op jit(solution)/shard_map/ppermute | solution.py:735
  26.8 5.5 %copy-start.3 = (bf16[384,640]{1,0:T(8,128)(2,1)S(1)}, bf16[384,640]{1,0:T(8,128)(2,1)}, u32[]{:S(2)}) copy-start(bf16[384,640]{1,0:T(8,128)(2,1)} %constant.30.clone.solve) | copy-start | bytes 1474564
  38.0 25.8 %collective-permute-start.6 = (f32[5,48,1024]{2,1,0:T(8,128)S(1)}, f32[5,48,1024]{2,1,0:T(8,128)S(1)}, u32[]{:S(2)}, u32[]{:S(2)}) collective-permute-start(f32[5,48,1024]{2,1,0:T(8,128)S(1)} %get-tuple-element.23), channel_id=1, source_target_pairs={{1,2},{2,1},{5,6},{6,5},{9,10},{10,9},{13,14},{14,13},{17,18},{18,... | collective-permute-start | bytes 2949128 | tf_op jit(solution)/shard_map/ppermute | solution.py:772
  41.7 9.9 %collective-permute-start.10 = (f32[16,128]{1,0:T(8,128)S(1)}, f32[16,128]{1,0:T(8,128)S(1)}, u32[]{:S(2)}, u32[]{:S(2)}) collective-permute-start(f32[16,128]{1,0:T(8,128)S(1)} %get-tuple-element.25.token), channel_id=1, source_target_pairs={{0,16},{16,0},{1,17},{17,1},{2,18},{18,2},{3,19},{19,3},{4,20},{20... | collective-permute-start | bytes 24584 | tf_op jit(solution)/shard_map/ppermute | solution.py:707

commit v18 on v17

--- a/solution.py
+++ b/solution.py
@@ -237,7 +237,7 @@
             pltpu.make_async_copy(near_rows, held.at[:, :, 0:R_NEAR, :], near_sem).wait()
 
 
-def outer_kernel(rows, span, counts, outer, held, out, outer_rows, held_rows, sems):
+def outer_kernel(rows, span, counts, outer, held, out, held_rows, sems):
     flags = place_flags(counts, 0)
     first, end = span
     plane = lax.axis_index("ax") % 2
@@ -247,23 +247,20 @@
         here = pl.ds(k * rows, rows)
         there = pl.ds(first + k * rows, rows)
         ways = [
-            (outer.at[:, here, :], outer_rows.at[:, here, :]),
             (held.at[:, plane, there, :], held_rows.at[:, here, :]),
             (held_rows.at[:, here, :], out.at[:, plane, there, :]),
         ]
-        steps.append([pltpu.make_async_copy(x, y, sems.at[3 * k + i]) for i, (x, y) in enumerate(ways)])
+        steps.append([pltpu.make_async_copy(x, y, sems.at[2 * k + i]) for i, (x, y) in enumerate(ways)])
         steps[-1][0].start()
-        steps[-1][1].start()
-    for k, (come, have, leave) in enumerate(steps):
-        come.wait()
+    for k, (have, leave) in enumerate(steps):
         have.wait()
         for t in range(rows // EIGHT):
             at = pl.ds(k * rows + EIGHT * t, EIGHT)
-            values = outer_flux(flags, [outer_rows[f, at, :] for f in range(FIELDS)])
+            values = outer_flux(flags, [outer[f, at, :] for f in range(FIELDS)])
             for f in range(FIELDS):
                 held_rows[f, at, :] = held_rows[f, at, :] + sign * values[f]
         leave.start()
-    for _, _, leave in steps:
+    for _, leave in steps:
         leave.wait()
 
 
@@ -609,9 +606,9 @@
         grid_spec=pltpu.PrefetchScalarGridSpec(
             num_scalar_prefetch=0,
             grid=(1,),
-            in_specs=[ANY, ANY],
+            in_specs=[pl.BlockSpec(memory_space=pltpu.VMEM), ANY],
             out_specs=ANY,
-            scratch_shapes=[chunk, chunk, pltpu.SemaphoreType.DMA((3 * (count // rows),))],
+            scratch_shapes=[chunk, pltpu.SemaphoreType.DMA((2 * (count // rows),))],
         ),
         out_shape=pltpu.HBM(held.shape, jnp.float32),
         input_output_aliases={1: 0},

time: 66.3 us -> 66.2 us (level)
  no operation moved by 1% of the time
where the time goes in v18:
time: 66.2 us; the launch traced here: 65.8 us
  Pallas kernels  39.2 us (59%)
  starting transfers between devices  19.3 us (29%)
  waiting for transfers between devices  5.89 us (9%)
  local copies, waits for them, and re-layouts  0.93 us (1%)
    pallas_call x3, Pallas kernels, bulk(): pl.pallas_call(functools.partial(bulk_kernel, dtheta, rows, span, total_r...  22.6 us
    pallas_call x1, Pallas kernels, near(): pl.pallas_call(functools.partial(near_kernel, dtheta, rows, part[0] if pa...  5.75 us
    ppermute x1, starting transfers between devices, body(): outer = [lax.ppermute(part, 'ax', outer_pairs)]  4.51 us
    pallas_call x2, Pallas kernels, pack_rest(): pl.pallas_call(functools.partial(pack_rest_kernel, parts, len(tokens)), i...  4.17 us
    ppermute x1, starting transfers between devices, body(): outer.append(lax.ppermute(part, 'ax', outer_pairs))  3.64 us
    ppermute x1, starting transfers between devices, body(): outer.append(lax.ppermute(value, 'ax', outer_pairs))  3.3 us
    ppermute x1, starting transfers between devices, body(): low = lax.ppermute(low, 'rad', up)  3.2 us
    pallas_call x1, Pallas kernels, pack_edges(): pl.pallas_call(pack_edges_kernel, in_specs=[ANY, ANY], out_specs=[vmem] *...  2.78 us
  transfers between devices with their start and end apart: 11, of which 3 were waited for; matrix products, arithmetic and copies ran while one was open for 0% of the time, Pallas kernels for 54%

profile of v18, /device:TPU:1, one launch (start us, length us, event | category | flops | bytes accessed | tf_op | source)
XLA Modules:
  0.0 65.8 jit_solution(11617733849772228620)
XLA Ops:
  0.0 1.8 %pack_first.1.token = f32[5,112,1024]{2,1,0:T(8,128)S(1)} custom-call(f32[5,2,256,1024]{3,2,1,0:T(8,128)} %state.15), custom_call_target="tpu_custom_call" | custom-call | bytes 4587520 | tf_op jit(solution)/shard_map/pack_first/pallas_call | solution.py:488
  1.9 0.0 copy-start
  1.9 4.5 %collective-permute-start.3 = (f32[5,112,1024]{2,1,0:T(8,128)S(1)}, f32[5,112,1024]{2,1,0:T(8,128)S(1)}, u32[]{:S(2)}, u32[]{:S(2)}) collective-permute-start(f32[5,112,1024]{2,1,0:T(8,128)S(1)} %pack_first.1.token), channel_id=1, source_target_pairs={{1,2},{2,1},{5,6},{6,5},{9,10},{10,9},{13,14},{14,13},{17,18},{18,... | collective-permute-start | bytes 6881288 | tf_op jit(solution)/shard_map/ppermute | solution.py:728
  6.4 0.0 copy-done
  6.4 2.8 %pack_edges.1 = (f32[256,128]{1,0:T(8,128)S(1)}, f32[5,16,1024]{2,1,0:T(8,128)S(1)}, f32[10,1024]{1,0:T(8,128)S(1)}, f32[10,1024]{1,0:T(8,128)S(1)}) custom-call(f32[5,2,256,1024]{3,2,1,0:T(8,128)} %state.15, f32[5,112,1024]{2,1,0:T(8,128)} %copy-done), custom_call_target="tpu_custom_call" | custom-call | bytes 5242880 | tf_op jit(solution)/shard_map/pack_edges/pallas_call | solution.py:509
  9.2 3.2 %collective-permute-start = (f32[10,1024]{1,0:T(8,128)S(1)}, f32[10,1024]{1,0:T(8,128)S(1)}, u32[]{:S(2)}, u32[]{:S(2)}) collective-permute-start(f32[10,1024]{1,0:T(8,128)S(1)} %get-tuple-element.17), channel_id=1, source_target_pairs={{0,4},{4,8},{8,12},{1,5},{5,9},{9,13},{2,6},{6,10},{10,14},{3,7},{... | collective-permute-start | bytes 122888 | tf_op jit(solution)/shard_map/ppermute | solution.py:730
  12.4 1.3 %collective-permute-start.1 = (f32[10,1024]{1,0:T(8,128)S(1)}, f32[10,1024]{1,0:T(8,128)S(1)}, u32[]{:S(2)}, u32[]{:S(2)}) collective-permute-start(f32[10,1024]{1,0:T(8,128)S(1)} %get-tuple-element.18), channel_id=1, source_target_pairs={{4,0},{8,4},{12,8},{5,1},{9,5},{13,9},{6,2},{10,6},{14,10},{7,3},{... | collective-permute-start | bytes 122888 | tf_op jit(solution)/shard_map/ppermute | solution.py:731
  13.7 1.3 %collective-permute-start.4 = (f32[256,128]{1,0:T(8,128)S(1)}, f32[256,128]{1,0:T(8,128)S(1)}, u32[]{:S(2)}, u32[]{:S(2)}) collective-permute-start(f32[256,128]{1,0:T(8,128)S(1)} %get-tuple-element.20.rest_0_), channel_id=1, source_target_pairs={{0,16},{16,0},{1,17},{17,1},{2,18},{18,2},{3,19},{19,3},{4,20},{20... | collective-permute-start | bytes 393224 | tf_op jit(solution)/shard_map/ppermute | solution.py:704
  15.0 0.0 collective-permute-done.rest_1_.low
  15.0 2.5 %collective-permute-done.1.rest_2_.high = f32[10,1024]{1,0:T(8,128)S(1)} collective-permute-done((f32[10,1024]{1,0:T(8,128)S(1)}, f32[10,1024]{1,0:T(8,128)S(1)}, u32[]{:S(2)}, u32[]{:S(2)}) %collective-permute-start.1) | collective-permute-done | bytes 40992 | tf_op jit(solution)/shard_map/ppermute | solution.py:731
  17.5 1.9 %pack_rest.2 = (f32[5,48,1024]{2,1,0:T(8,128)S(1)}, f32[5,96,1024]{2,1,0:T(8,128)S(1)}) custom-call(f32[5,2,256,1024]{3,2,1,0:T(8,128)} %state.15, f32[256,128]{1,0:T(8,128)S(1)} %get-tuple-element.20.rest_0_, f32[10,1024]{1,0:T(8,128)S(1)} %collective-permute-done.rest_1_.low, f32[10,1024]{1,0:T(8,128)S(1)} %collective-permute-done.1.rest_2_.high), custom_call_target="tpu_custom_call" | custom-call | bytes 5898240 | tf_op jit(solution)/shard_map/pack_rest/pallas_call | solution.py:529
  19.4 0.0 copy-start.2
  19.4 0.0 copy-start.4
  19.4 0.1 collective-permute-start.5
  19.5 0.0 collective-permute-done.4.rest_1_.edge
  19.5 0.8 %copy-done.2 = f32[5,48,1024]{2,1,0:T(8,128)} copy-done((f32[5,48,1024]{2,1,0:T(8,128)}, f32[5,48,1024]{2,1,0:T(8,128)S(1)}, u32[]{:S(2)}) %copy-start.2) | copy-done | bytes 983064
  20.3 2.2 %pack_rest.3 = (f32[5,96,1024]{2,1,0:T(8,128)S(1)}, f32[5,96,1024]{2,1,0:T(8,128)S(1)}) custom-call(f32[5,2,256,1024]{3,2,1,0:T(8,128)} %state.15, f32[5,48,1024]{2,1,0:T(8,128)} %copy-done.2, f32[256,128]{1,0:T(8,128)S(1)} %collective-permute-done.4.rest_1_.edge), custom_call_target="tpu_custom_call" | custom-call | bytes 7864320 | tf_op jit(solution)/shard_map/pack_rest/pallas_call | solution.py:529
  22.6 0.0 copy-start.1
  22.6 0.1 collective-permute-start.9
  22.7 3.3 %collective-permute-start.8 = (f32[5,96,1024]{2,1,0:T(8,128)S(1)}, f32[5,96,1024]{2,1,0:T(8,128)S(1)}, u32[]{:S(2)}, u32[]{:S(2)}) collective-permute-start(f32[5,96,1024]{2,1,0:T(8,128)S(1)} %get-tuple-element.24), channel_id=1, source_target_pairs={{1,2},{2,1},{5,6},{6,5},{9,10},{10,9},{13,14},{14,13},{17,18},{18,... | collective-permute-start | bytes 5898248 | tf_op jit(solution)/shard_map/ppermute | solution.py:746
  26.0 0.1 collective-permute-start.7
  26.1 0.0 copy-done.4
  26.2 0.0 collective-permute-done.5.inner.outer
  26.2 0.5 collective-permute-start.2
  26.7 0.1 fusion.3.table.rest_4_
  26.8 0.0 copy-done.1
  26.8 0.0 copy-start.3
  26.8 5.3 %bulk.3.token.held = f32[5,2,256,1024]{3,2,1,0:T(8,128)} custom-call(f32[5,2,256,1024]{3,2,1,0:T(8,128)} %state.15, f32[10,1024]{1,0:T(8,128)S(1)} %collective-permute-done.rest_1_.low, f32[10,1024]{1,0:T(8,128)S(1)} %collective-permute-done.1.rest_2_.high, f32[5,48,1024]{2,1,0:T(8,128)S(1)} %collective-permute-done.5.inner.outer, ...), custom_call_target="tpu_custom_call" | custom-call | flops 29491200 | bytes 4915200 | tf_op jit(solution)/shard_map/bulk/pallas_call | solution.py:567
  32.1 0.0 collective-permute-done.2.inner
  32.2 0.0 collective-permute-done.3.outer
  32.2 0.1 broadcast_in_dim.51.factor.rest_0_
  32.3 0.0 copy-done.3
  32.3 5.7 %near.1 = (f32[10,16,1024]{2,1,0:T(8,128)S(1)}, f32[10,16,1024]{2,1,0:T(8,128)S(1)}, f32[16,128]{1,0:T(8,128)S(1)}, f32[5,48,1024]{2,1,0:T(8,128)S(1)}) custom-call(f32[5,2,256,1024]{3,2,1,0:T(8,128)} %state.15, f32[5,2,256,1024]{3,2,1,0:T(8,128)} %state.15, f32[10,1024]{1,0:T(8,128)S(1)} %collective-permute-done.rest_1_.low, ...), custom_call_target="tpu_custom_call" | custom-call | flops 32768000 | bytes 40960000 | tf_op jit(solution)/shard_map/near/pallas_call | solution.py:633
  38.0 3.6 %collective-permute-start.6 = (f32[5,48,1024]{2,1,0:T(8,128)S(1)}, f32[5,48,1024]{2,1,0:T(8,128)S(1)}, u32[]{:S(2)}, u32[]{:S(2)}) collective-permute-start(f32[5,48,1024]{2,1,0:T(8,128)S(1)} %get-tuple-element.23), channel_id=1, source_target_pairs={{1,2},{2,1},{5,6},{6,5},{9,10},{10,9},{13,14},{14,13},{17,18},{18,... | collective-permute-start | bytes 2949128 | tf_op jit(solution)/shard_map/ppermute | solution.py:769
  41.7 1.3 %collective-permute-start.10 = (f32[16,128]{1,0:T(8,128)S(1)}, f32[16,128]{1,0:T(8,128)S(1)}, u32[]{:S(2)}, u32[]{:S(2)}) collective-permute-start(f32[16,128]{1,0:T(8,128)S(1)} %get-tuple-element.25.token), channel_id=1, source_target_pairs={{0,16},{16,0},{1,17},{17,1},{2,18},{18,2},{3,19},{19,3},{4,20},{20... | collective-permute-start | bytes 24584 | tf_op jit(solution)/shard_map/ppermute | solution.py:704
  43.0 0.0 collective-permute-done.9.inner
  43.0 8.6 %bulk.4.held = f32[5,2,256,1024]{3,2,1,0:T(8,128)} custom-call(f32[5,2,256,1024]{3,2,1,0:T(8,128)} %state.15, f32[10,1024]{1,0:T(8,128)S(1)} %collective-permute-done.rest_1_.low, f32[10,1024]{1,0:T(8,128)S(1)} %collective-permute-done.1.rest_2_.high, f32[5,96,1024]{2,1,0:T(8,128)S(1)} %collective-permute-done.9.inner, ...), custom_call_target="tpu_custom_call", output_to_operand_aliasing={{}: (7, {})} | custom-call | flops 58982400 | bytes 9830400 | tf_op jit(solution)/shard_map/bulk/pallas_call | solution.py:567
  51.6 0.0 collective-permute-done.10
  51.6 0.1 add_multiply_fusion.rest_3_
  51.6 1.6 %collective-permute-done.8.outer = f32[5,96,1024]{2,1,0:T(8,128)S(1)} collective-permute-done((f32[5,96,1024]{2,1,0:T(8,128)S(1)}, f32[5,96,1024]{2,1,0:T(8,128)S(1)}, u32[]{:S(2)}, u32[]{:S(2)}) %collective-permute-start.8) | collective-permute-done | bytes 1966112 | tf_op jit(solution)/shard_map/ppermute | solution.py:746
  53.3 0.0 collective-permute-done.7.inner
  53.3 8.8 %bulk.5.held = f32[5,2,256,1024]{3,2,1,0:T(8,128)} custom-call(f32[5,2,256,1024]{3,2,1,0:T(8,128)} %state.15, f32[10,1024]{1,0:T(8,128)S(1)} %collective-permute-done.rest_1_.low, f32[10,1024]{1,0:T(8,128)S(1)} %collective-permute-done.1.rest_2_.high, f32[5,96,1024]{2,1,0:T(8,128)S(1)} %collective-permute-done.7.inner, ...), custom_call_target="tpu_custom_call", output_to_operand_aliasing={{}: (7, {})} | custom-call | flops 58982400 | bytes 9830400 | tf_op jit(solution)/shard_map/bulk/pallas_call | solution.py:567
  62.0 1.8 %collective-permute-done.6.outer = f32[5,48,1024]{2,1,0:T(8,128)S(1)} collective-permute-done((f32[5,48,1024]{2,1,0:T(8,128)S(1)}, f32[5,48,1024]{2,1,0:T(8,128)S(1)}, u32[]{:S(2)}, u32[]{:S(2)}) %collective-permute-start.6) | collective-permute-done | bytes 983072 | tf_op jit(solution)/shard_map/ppermute | solution.py:769
  63.8 2.1 %add_outer.1 = f32[5,2,256,1024]{3,2,1,0:T(8,128)} custom-call(f32[5,48,1024]{2,1,0:T(8,128)S(1)} %collective-permute-done.6.outer, f32[5,2,256,1024]{3,2,1,0:T(8,128)} %bulk.5.held), custom_call_target="tpu_custom_call", output_to_operand_aliasing={{}: (1, {})} | custom-call | flops 1474560 | bytes 3932160 | tf_op jit(solution)/shard_map/add_outer/pallas_call | solution.py:604
  (5 shorter events, 0.1 us)
Async XLA Ops:
  1.9 4.5 %copy-start = (f32[5,112,1024]{2,1,0:T(8,128)}, f32[5,112,1024]{2,1,0:T(8,128)S(1)}, u32[]{:S(2)}) copy-start(f32[5,112,1024]{2,1,0:T(8,128)S(1)} %pack_first.1.token) | copy-start | bytes 6881284
  1.9 30.3 %collective-permute-start.3 = (f32[5,112,1024]{2,1,0:T(8,128)S(1)}, f32[5,112,1024]{2,1,0:T(8,128)S(1)}, u32[]{:S(2)}, u32[]{:S(2)}) collective-permute-start(f32[5,112,1024]{2,1,0:T(8,128)S(1)} %pack_first.1.token), channel_id=1, source_target_pairs={{1,2},{2,1},{5,6},{6,5},{9,10},{10,9},{13,14},{14,13},{17,18},{18,... | collective-permute-start | bytes 6881288 | tf_op jit(solution)/shard_map/ppermute | solution.py:728
  9.2 5.8 %collective-permute-start = (f32[10,1024]{1,0:T(8,128)S(1)}, f32[10,1024]{1,0:T(8,128)S(1)}, u32[]{:S(2)}, u32[]{:S(2)}) collective-permute-start(f32[10,1024]{1,0:T(8,128)S(1)} %get-tuple-element.17), channel_id=1, source_target_pairs={{0,4},{4,8},{8,12},{1,5},{5,9},{9,13},{2,6},{6,10},{10,14},{3,7},{... | collective-permute-start | bytes 122888 | tf_op jit(solution)/shard_map/ppermute | solution.py:730
  12.4 5.1 %collective-permute-start.1 = (f32[10,1024]{1,0:T(8,128)S(1)}, f32[10,1024]{1,0:T(8,128)S(1)}, u32[]{:S(2)}, u32[]{:S(2)}) collective-permute-start(f32[10,1024]{1,0:T(8,128)S(1)} %get-tuple-element.18), channel_id=1, source_target_pairs={{4,0},{8,4},{12,8},{5,1},{9,5},{13,9},{6,2},{10,6},{14,10},{7,3},{... | collective-permute-start | bytes 122888 | tf_op jit(solution)/shard_map/ppermute | solution.py:731
  13.7 5.8 %collective-permute-start.4 = (f32[256,128]{1,0:T(8,128)S(1)}, f32[256,128]{1,0:T(8,128)S(1)}, u32[]{:S(2)}, u32[]{:S(2)}) collective-permute-start(f32[256,128]{1,0:T(8,128)S(1)} %get-tuple-element.20.rest_0_), channel_id=1, source_target_pairs={{0,16},{16,0},{1,17},{17,1},{2,18},{18,2},{3,19},{19,3},{4,20},{20... | collective-permute-start | bytes 393224 | tf_op jit(solution)/shard_map/ppermute | solution.py:704
  19.4 0.9 %copy-start.2 = (f32[5,48,1024]{2,1,0:T(8,128)}, f32[5,48,1024]{2,1,0:T(8,128)S(1)}, u32[]{:S(2)}) copy-start(f32[5,48,1024]{2,1,0:T(8,128)S(1)} %get-tuple-element.21.rest_0_) | copy-start | bytes 2949124
  19.4 6.6 %copy-start.4 = (s32[16]{0:T(128)S(1)}, s32[16]{0:T(128)}, u32[]{:S(2)}) copy-start(s32[16]{0:T(128)} %param.4) | copy-start | bytes 196
  19.4 6.7 %collective-permute-start.5 = (f32[5,48,1024]{2,1,0:T(8,128)S(1)}, f32[5,48,1024]{2,1,0:T(8,128)S(1)}, u32[]{:S(2)}, u32[]{:S(2)}) collective-permute-start(f32[5,48,1024]{2,1,0:T(8,128)S(1)} %get-tuple-element.21.rest_0_), channel_id=1, source_target_pairs={{0,1},{1,0},{2,3},{3,2},{4,5},{5,4},{6,7},{7,6},{8,9},{9,8},{10,11... | collective-permute-start | bytes 2949128 | tf_op jit(solution)/shard_map/ppermute | solution.py:748
  22.6 4.2 %copy-start.1 = (f32[5,96,1024]{2,1,0:T(8,128)}, f32[5,96,1024]{2,1,0:T(8,128)S(1)}, u32[]{:S(2)}) copy-start(f32[5,96,1024]{2,1,0:T(8,128)S(1)} %get-tuple-element.22.token) | copy-start | bytes 5898244
  22.6 20.4 %collective-permute-start.9 = (f32[5,96,1024]{2,1,0:T(8,128)S(1)}, f32[5,96,1024]{2,1,0:T(8,128)S(1)}, u32[]{:S(2)}, u32[]{:S(2)}) collective-permute-start(f32[5,96,1024]{2,1,0:T(8,128)S(1)} %get-tuple-element.26), channel_id=1, source_target_pairs={{0,1},{1,0},{2,3},{3,2},{4,5},{5,4},{6,7},{7,6},{8,9},{9,8},{10,11... | collective-permute-start | bytes 5898248 | tf_op jit(solution)/shard_map/ppermute | solution.py:748
  22.7 30.6 %collective-permute-start.8 = (f32[5,96,1024]{2,1,0:T(8,128)S(1)}, f32[5,96,1024]{2,1,0:T(8,128)S(1)}, u32[]{:S(2)}, u32[]{:S(2)}) collective-permute-start(f32[5,96,1024]{2,1,0:T(8,128)S(1)} %get-tuple-element.24), channel_id=1, source_target_pairs={{1,2},{2,1},{5,6},{6,5},{9,10},{10,9},{13,14},{14,13},{17,18},{18,... | collective-permute-start | bytes 5898248 | tf_op jit(solution)/shard_map/ppermute | solution.py:746
  26.0 27.3 %collective-permute-start.7 = (f32[5,96,1024]{2,1,0:T(8,128)S(1)}, f32[5,96,1024]{2,1,0:T(8,128)S(1)}, u32[]{:S(2)}, u32[]{:S(2)}) collective-permute-start(f32[5,96,1024]{2,1,0:T(8,128)S(1)} %get-tuple-element.22.token), channel_id=1, source_target_pairs={{0,1},{1,0},{2,3},{3,2},{4,5},{5,4},{6,7},{7,6},{8,9},{9,8},{10,11... | collective-permute-start | bytes 5898248 | tf_op jit(solution)/shard_map/ppermute | solution.py:748
  26.2 6.0 %collective-permute-start.2 = (f32[5,16,1024]{2,1,0:T(8,128)S(1)}, f32[5,16,1024]{2,1,0:T(8,128)S(1)}, u32[]{:S(2)}, u32[]{:S(2)}) collective-permute-start(f32[5,16,1024]{2,1,0:T(8,128)S(1)} %get-tuple-element.19), channel_id=1, source_target_pairs={{0,1},{1,0},{2,3},{3,2},{4,5},{5,4},{6,7},{7,6},{8,9},{9,8},{10,11... | collective-permute-start | bytes 983048 | tf_op jit(solution)/shard_map/ppermute | solution.py:732
  26.8 5.5 %copy-start.3 = (bf16[384,640]{1,0:T(8,128)(2,1)S(1)}, bf16[384,640]{1,0:T(8,128)(2,1)}, u32[]{:S(2)}) copy-start(bf16[384,640]{1,0:T(8,128)(2,1)} %constant.30.clone.solve) | copy-start | bytes 1474564
  38.0 25.8 %collective-permute-start.6 = (f32[5,48,1024]{2,1,0:T(8,128)S(1)}, f32[5,48,1024]{2,1,0:T(8,128)S(1)}, u32[]{:S(2)}, u32[]{:S(2)}) collective-permute-start(f32[5,48,1024]{2,1,0:T(8,128)S(1)} %get-tuple-element.23), channel_id=1, source_target_pairs={{1,2},{2,1},{5,6},{6,5},{9,10},{10,9},{13,14},{14,13},{17,18},{18,... | collective-permute-start | bytes 2949128 | tf_op jit(solution)/shard_map/ppermute | solution.py:769
  41.7 9.9 %collective-permute-start.10 = (f32[16,128]{1,0:T(8,128)S(1)}, f32[16,128]{1,0:T(8,128)S(1)}, u32[]{:S(2)}, u32[]{:S(2)}) collective-permute-start(f32[16,128]{1,0:T(8,128)S(1)} %get-tuple-element.25.token), channel_id=1, source_target_pairs={{0,16},{16,0},{1,17},{17,1},{2,18},{18,2},{3,19},{19,3},{4,20},{20... | collective-permute-start | bytes 24584 | tf_op jit(solution)/shard_map/ppermute | solution.py:704
